TPU v7x, 32 devices: a whole 2x2x4 slice. The times are simulated.
32 devices in a mesh: groups: 2 (over y), lat: 16 (over z, x, core).
Axes of the slice: x: 2, y: 2, z: 4, core: 2. Of those that a mesh axis runs over, the one named last changes fastest.
Arguments:
- grad_recon: bfloat16 [4096, 3584], P(('groups', 'lat')), parts along dimension 0, may hold values from -6 to 6
- inputs: bfloat16 [4096, 3584], P(('groups', 'lat')), parts along dimension 0, may hold values from -6 to 6
- decoder: bfloat16 [4096, 3584], P('lat'), may hold values from -0.09375 to 0.09375
- owners: int32 [4096, 4], P(('groups', 'lat')), parts along dimension 0, may hold values from 0 to 15, all different within a row; in each aligned block of 128 rows (0 to 127, 128 to 255, ...) at most 48 rows name the same one
- local_blocks: int32 [4096, 4], P(('groups', 'lat')), parts along dimension 0, may hold values from 0 to 1
- offsets: int32 [4096, 4, 16], P(('groups', 'lat')), parts along dimension 0, may hold values from 0 to 127, as said below
- act_values: bfloat16 [4096, 4, 16], P(('groups', 'lat')), parts along dimension 0, may hold values from 0.049804688 to 3
Outputs:
- decoder_grad: bfloat16 [8192, 3584], P(('groups', 'lat')), parts along dimension 0
- encoder_grad: bfloat16 [3584, 8192], P(None, ('groups', 'lat')), parts along dimension 1
- bias_grad: float32 [8192], P(('groups', 'lat')), parts along dimension 0
- latent_grads: float32 [4096, 64], P(('groups', 'lat')), parts along dimension 0
There are 2 independent parts, one for each index of `groups`. A program takes and returns all parts, laid end to end along the dimension named above; an argument that names none is the same for every part. Nothing has to cross between parts.
Inputs may be any that keep to these rules, and one draw needn't show every extreme that they name: The 4 owners of one row are different; in the rows of one device no owner is named by more than 48 rows, a bound that some block reaches. The 16 offsets of one row and block are different.
All inputs are finite; a program needn't handle non-finite values.
Results may differ from a plain program's by a relative error of at most 0.005.
Values may be sent and summed in bfloat16 or wider, within the bound.
No kernel may reach another device: no remote copies, remote signals or barrier semaphores. Data moves between devices by JAX's collectives and lax.ppermute only.
A program may use at most 128 MiB of HBM per device.

v0:
```python
import jax
import jax.numpy as jnp
from jax import lax
from jax.sharding import PartitionSpec as P

BLOCK = 128


def per_device(grad_recon, inputs, decoder, owners, local_blocks, offsets, act_values):
    token_count = grad_recon.shape[0]
    width = grad_recon.shape[1]
    block_count = owners.shape[1]
    per_block = offsets.shape[2]
    latent_count = decoder.shape[0]
    peer_count = lax.axis_size("lat")
    capacity = max(
        2,
        min(token_count, (3 * token_count * block_count + 2 * peer_count - 1) // (2 * peer_count)),
    )
    pair_count = token_count * block_count
    slot_count = peer_count * capacity
    target = owners.reshape(pair_count)
    one_hot = (target[:, None] == jnp.arange(peer_count, dtype=jnp.int32)[None, :]).astype(
        jnp.int32
    )
    earlier = jnp.cumsum(one_hot, axis=0) - one_hot
    position = jnp.sum(earlier * one_hot, axis=1)
    columns = (local_blocks[:, :, None] * BLOCK + offsets).reshape(pair_count, per_block)
    pair_index = jnp.arange(pair_count, dtype=jnp.int32)
    acts_dense = jnp.zeros((pair_count, latent_count), jnp.bfloat16)
    acts_dense = acts_dense.at[pair_index[:, None], columns].set(
        act_values.reshape(pair_count, per_block)
    )
    slot_pair = jnp.full((slot_count,), pair_count, jnp.int32)
    slot_pair = slot_pair.at[target * capacity + position].set(pair_index)
    filled = slot_pair < pair_count
    safe_pair = jnp.where(filled, slot_pair, 0)
    token_of_slot = safe_pair // block_count
    zero_bf = jnp.zeros((), jnp.bfloat16)
    grad_send = jnp.where(filled[:, None], grad_recon[token_of_slot], zero_bf).reshape(
        peer_count, capacity, width
    )
    input_send = jnp.where(filled[:, None], inputs[token_of_slot], zero_bf).reshape(
        peer_count, capacity, width
    )
    act_send = jnp.where(filled[:, None], acts_dense[safe_pair], zero_bf).reshape(
        peer_count, capacity, latent_count
    )
    grad_recv, input_recv, act_recv = (
        lax.all_to_all(grad_send, "lat", split_axis=0, concat_axis=0, tiled=True),
        lax.all_to_all(input_send, "lat", split_axis=0, concat_axis=0, tiled=True),
        lax.all_to_all(act_send, "lat", split_axis=0, concat_axis=0, tiled=True),
    )
    grad_rows = grad_recv.reshape(slot_count, width)
    input_rows = input_recv.reshape(slot_count, width)
    act_rows = act_recv.reshape(slot_count, latent_count)
    products = lax.dot_general(
        grad_rows, decoder, (((1,), (1,)), ((), ())), preferred_element_type=jnp.float32
    )
    pre_grads = jnp.where(act_rows != 0, products, 0.0)
    bias_grad = jnp.sum(pre_grads, axis=0)
    decoder_grad = lax.dot_general(
        act_rows, grad_rows, (((0,), (0,)), ((), ())), preferred_element_type=jnp.float32
    ).astype(jnp.bfloat16)
    encoder_grad = lax.dot_general(
        input_rows,
        pre_grads.astype(jnp.bfloat16),
        (((0,), (0,)), ((), ())),
        preferred_element_type=jnp.float32,
    ).astype(jnp.bfloat16)
    returning = pre_grads.reshape(peer_count, capacity, latent_count)
    returned = lax.all_to_all(returning, "lat", split_axis=0, concat_axis=0, tiled=True)
    picked_rows = returned[target, position]
    latent_grads = jnp.take_along_axis(picked_rows, columns, axis=1).reshape(
        token_count, block_count * per_block
    )
    return (decoder_grad, encoder_grad, bias_grad, latent_grads)


def solution(mesh):
    placed = (
        P(("groups", "lat"), None),
        P(("groups", "lat"), None),
        P("lat", None),
        P(("groups", "lat"), None),
        P(("groups", "lat"), None),
        P(("groups", "lat"), None, None),
        P(("groups", "lat"), None, None),
    )
    return jax.shard_map(
        per_device,
        mesh=mesh,
        in_specs=placed,
        out_specs=(
            P(("groups", "lat"), None),
            P(None, ("groups", "lat")),
            P(("groups", "lat")),
            P(("groups", "lat"), None),
        ),
        check_vma=False,
    )
```

profile of v0, /device:TPU:0, one launch (start us, length us, event | category | flops | bytes accessed | tf_op | source)
XLA Modules:
  0.0 452.1 jit_solution(8774914615259194728)
XLA Ops:
  0.7 0.9 copy.35
  1.9 1.2 reduce-window.6
  3.1 0.2 slice_reduce_fusion
  3.5 2.4 scatter_custom_fusion
  6.1 0.7 broadcast_multiply_fusion
  6.7 0.8 broadcast_add_fusion
  7.5 0.1 copy.39
  7.7 0.8 shift-left_or_fusion
  8.6 0.7 multiply_reduce_fusion
  9.3 0.7 and_reduce_fusion
  10.2 0.1 reshape.234
  10.3 0.9 copy.43
  11.2 0.1 reshape.236
  11.3 56.6 %scatter_custom_fusion.1 = bf16[131072]{0:T(1024)(128)(2,1)S(1)} fusion(s32[8192]{0:T(1024)S(1)} %reshape.234, bf16[8192]{0:T(1024)(128)(2,1)S(1)} %reshape.236, bf16[]{:T(256)} %constant.25.clone.1), kind=kCustom, calls=%fused_computation.18 | custom fusion | bytes 262146
  68.1 2.7 gather_fusion
  70.7 0.9 broadcast_select_fusion.2
  71.7 7.4 %all-to-all-start = ((bf16[16,48,256]{2,1,0:T(8,128)(2,1)}), bf16[16,48,256]{2,1,0:T(8,128)(2,1)S(1)}, u32[]{:S(2)}, u32[]{:S(2)}) async-start(bf16[16,48,256]{2,1,0:T(8,128)(2,1)} %broadcast_select_fusion.2), calls=%async_computation | async-start | bytes 786432 | tf_op jit(solution)/shard_map/all_to_all | solution.py:52
  79.0 5.5 %gather_fusion.1 = bf16[768,3584]{1,0:T(8,128)(2,1)} fusion(bf16[128,3584]{1,0:T(8,128)(2,1)S(1)} %copy-done.1, s32[1024]{0:T(1024)S(1)} %get-tuple-element.18), kind=kCustom, calls=%fused_computation.1 | custom fusion | bytes 11013120 | tf_op jit(solution)/shard_map/gather | solution.py:40
  84.5 12.3 %gather_fusion.2 = bf16[768,3584]{1,0:T(8,128)(2,1)} fusion(bf16[128,3584]{1,0:T(8,128)(2,1)} %param.8, s32[1024]{0:T(1024)S(1)} %get-tuple-element.18), kind=kCustom, calls=%fused_computation.2 | custom fusion | bytes 11013120 | tf_op jit(solution)/shard_map/gather | solution.py:43
  96.8 9.4 %broadcast_select_fusion = (bf16[16,48,3584]{2,1,0:T(8,128)(2,1)}, bf16[16,48,3584]{2,1,0:T(8,128)(2,1)}) fusion(bf16[16,48,3584]{2,1,0:T(8,128)(2,1)} %bitcast.48, pred[16,48]{1,0:T(8,128)(4,1)S(1)} %broadcast_in_dim.67, bf16[16,48,3584]{2,1,0:T(8,128)(2,1)} %bitcast.47), kind=kLoop, calls=%fused_computation.7 | loop fusion | flops 5505024 | bytes 22020864 | tf_op jit(solution)/shard_map/jit(_where)/select_n | solution.py:43
  106.2 127.5 %all_to_all.20 = bf16[16,48,3584]{2,1,0:T(8,128)(2,1)} all-to-all(bf16[16,48,3584]{2,1,0:T(8,128)(2,1)} %get-tuple-element.15), channel_id=1, replica_groups=mesh['groups'=2,'lat'=16] {'lat'}, dimensions={0} | all-to-all | bytes 11010048 | tf_op jit(solution)/shard_map/all_to_all | solution.py:50
  233.7 4.7 %all-to-all-start.2 = ((bf16[16,48,3584]{2,1,0:T(8,128)(2,1)}), bf16[16,48,3584]{2,1,0:T(8,128)(2,1)}, u32[]{:S(2)}, u32[]{:S(2)}) async-start(bf16[16,48,3584]{2,1,0:T(8,128)(2,1)} %get-tuple-element.14), calls=%async_computation.2 | async-start | bytes 11010048 | tf_op jit(solution)/shard_map/all_to_all | solution.py:51
  238.4 0.1 reshape.220
  238.7 5.6 %fusion.17 = (f32[256]{0:T(256)}, f32[768,256]{1,0:T(8,128)}) fusion(pred[768,256]{1,0:T(8,128)(4,1)S(1)} %bitcast.52, bf16[768,3584]{1,0:T(8,128)(2,1)} %bitcast.45, bf16[256,3584]{1,0:T(8,128)(2,1)S(1)} %copy-done), kind=kOutput, calls=%fused_computation.59 | convolution fusion | flops 1409679104 | bytes 8324096 | tf_op jit(solution)/shard_map/dot_general | solution.py:57
  244.3 94.5 %all-to-all-done.2 = bf16[16,48,3584]{2,1,0:T(8,128)(2,1)} async-done(((bf16[16,48,3584]{2,1,0:T(8,128)(2,1)}), bf16[16,48,3584]{2,1,0:T(8,128)(2,1)}, u32[]{:S(2)}, u32[]{:S(2)}) %all-to-all-start.2) | async-done | bytes 5505056 | tf_op jit(solution)/shard_map/all_to_all | solution.py:51
  338.8 24.9 %all-to-all-start.3 = ((f32[16,48,256]{2,1,0:T(8,128)}), f32[16,48,256]{2,1,0:T(8,128)S(1)}, u32[]{:S(2)}, u32[]{:S(2)}) async-start(f32[16,48,256]{2,1,0:T(8,128)} %bitcast.51), calls=%async_computation.3 | async-start | bytes 1572864 | tf_op jit(solution)/shard_map/all_to_all | solution.py:72
  363.7 5.6 %convolution_convert_fusion = bf16[3584,256]{1,0:T(8,128)(2,1)} fusion(bf16[768,3584]{1,0:T(8,128)(2,1)} %bitcast.8, f32[768,256]{1,0:T(8,128)} %get-tuple-element.17), kind=kOutput, calls=%fused_computation.11 | convolution fusion | flops 1410400256 | bytes 8126464 | tf_op jit(solution)/shard_map/dot_general | solution.py:65
  369.4 5.4 %fusion = bf16[256,3584]{1,0:T(8,128)(2,1)} fusion(bf16[16,48,256]{2,1,0:T(8,128)(2,1)S(1)} %all-to-all-done, bf16[16,48,3584]{2,1,0:T(8,128)(2,1)} %all_to_all.20), kind=kOutput, calls=%fused_computation.10 | convolution fusion | flops 1410203648 | bytes 7733248 | tf_op jit(solution)/shard_map/dot_general | solution.py:62
  374.8 7.7 %all-to-all-done.3 = f32[16,48,256]{2,1,0:T(8,128)S(1)} async-done(((f32[16,48,256]{2,1,0:T(8,128)}), f32[16,48,256]{2,1,0:T(8,128)S(1)}, u32[]{:S(2)}, u32[]{:S(2)}) %all-to-all-start.3) | async-done | bytes 786464 | tf_op jit(solution)/shard_map/all_to_all | solution.py:72
  382.4 3.9 gather_fusion.3
  386.3 65.0 %gather_fusion.4 = f32[8192]{0:T(1024)S(1)} fusion(f32[512,256]{1,0:T(8,128)S(1)} %gather_fusion.3, s32[8192]{0:T(1024)S(1)} %reshape.220), kind=kCustom, calls=%fused_computation.4 | custom fusion | bytes 131072 | tf_op jit(solution)/shard_map/jit(take_along_axis)/gather | solution.py:74
  451.5 0.6 and_select_fusion
  (28 shorter events, 1.2 us)
Async XLA Ops:
  0.6 238.0 %copy-start = (bf16[256,3584]{1,0:T(8,128)(2,1)S(1)}, bf16[256,3584]{1,0:T(8,128)(2,1)}, u32[]{:S(2)}) copy-start(bf16[256,3584]{1,0:T(8,128)(2,1)} %param.9) | copy-start | bytes 5505028
  0.6 78.4 %copy-start.1 = (bf16[128,3584]{1,0:T(8,128)(2,1)S(1)}, bf16[128,3584]{1,0:T(8,128)(2,1)}, u32[]{:S(2)}) copy-start(bf16[128,3584]{1,0:T(8,128)(2,1)} %param.7) | copy-start | bytes 2752516
  71.7 34.5 %all-to-all-start = ((bf16[16,48,256]{2,1,0:T(8,128)(2,1)}), bf16[16,48,256]{2,1,0:T(8,128)(2,1)S(1)}, u32[]{:S(2)}, u32[]{:S(2)}) async-start(bf16[16,48,256]{2,1,0:T(8,128)(2,1)} %broadcast_select_fusion.2), calls=%async_computation | async-start | bytes 786432 | tf_op jit(solution)/shard_map/all_to_all | solution.py:52
  233.7 4.8 %copy-start.2 = (s32[512,16,1]{1,0,2:T(8,128)S(1)}, s32[512,16,1]{1,0,2:T(8,128)}, u32[]{:S(2)}) copy-start(s32[512,16,1]{1,0,2:T(8,128)} %get-tuple-element.8) | copy-start | bytes 98308
  233.7 105.2 %all-to-all-start.2 = ((bf16[16,48,3584]{2,1,0:T(8,128)(2,1)}), bf16[16,48,3584]{2,1,0:T(8,128)(2,1)}, u32[]{:S(2)}, u32[]{:S(2)}) async-start(bf16[16,48,3584]{2,1,0:T(8,128)(2,1)} %get-tuple-element.14), calls=%async_computation.2 | async-start | bytes 11010048 | tf_op jit(solution)/shard_map/all_to_all | solution.py:51
  338.8 43.6 %all-to-all-start.3 = ((f32[16,48,256]{2,1,0:T(8,128)}), f32[16,48,256]{2,1,0:T(8,128)S(1)}, u32[]{:S(2)}, u32[]{:S(2)}) async-start(f32[16,48,256]{2,1,0:T(8,128)} %bitcast.51), calls=%async_computation.3 | async-start | bytes 1572864 | tf_op jit(solution)/shard_map/all_to_all | solution.py:72
where the time goes:
time: 453 us; the launch traced here: 452 us
  local copies, waits for them, and re-layouts  152 us (34%)
  blocking collectives  128 us (28%)
  waiting for transfers between devices  102 us (23%)
  starting transfers between devices  37 us (8%)
  matrix products  16.7 us (4%)
  other arithmetic  16.1 us (4%)
    all_to_all x1, blocking collectives, per_device(): lax.all_to_all(grad_send, 'lat', split_axis=0, concat_axis=0, tiled=True)  128 us
    all_to_all x1, waiting for transfers between devices, per_device(): lax.all_to_all(input_send, 'lat', split_axis=0, concat_axis=0, tiled=True)  94.5 us
    gather x3, local copies, waits for them, and re-layouts, per_device(): jnp.take_along_axis(picked_rows, columns, axis=1)  65.1 us
    unnamed x11, local copies, waits for them, and re-layouts  58.7 us
    all_to_all x1, starting transfers between devices, per_device(): lax.all_to_all(returning, 'lat', split_axis=0, concat_axis=0, tiled=True)  24.9 us
    gather x1, local copies, waits for them, and re-layouts, per_device(): inputs[token_of_slot]  12.3 us
    select_n x1, other arithmetic, per_device(): jnp.where(filled[:, None], inputs[token_of_slot], zero_bf)  9.37 us
  transfers between devices with their start and end apart: 3, of which 2 were waited for; matrix products, arithmetic and copies ran while one was open for 10% of the time, Pallas kernels for 0%

commit v1 on v0

v1 whole, which is shorter than its diff:
```python
import functools

import jax
import jax.numpy as jnp
from jax import lax
from jax.experimental import pallas as pl
from jax.experimental.pallas import tpu as pltpu
from jax.sharding import PartitionSpec as P

BLOCK = 128
PART_BYTES = 9 << 20
HELD_BYTES = 1 << 25


def build_kernel(block_count, per_block, me_ref, meta_ref, acts_ref, cols_ref):
    pairs = block_count * per_block
    meta = meta_ref[0].astype(jnp.float32)
    me = me_ref[0].astype(jnp.float32)
    tokens = meta.shape[1]
    values = jnp.zeros((per_block, tokens), jnp.float32)
    columns = jnp.full((per_block, tokens), -1.0, jnp.float32)
    for i in range(block_count):
        mine = meta[2 * pairs + i : 2 * pairs + i + 1] == me
        values = jnp.where(mine, meta[i * per_block : (i + 1) * per_block], values)
        columns = jnp.where(mine, meta[pairs + i * per_block : pairs + (i + 1) * per_block], columns)
    columns = columns.astype(jnp.int32)
    cols_ref[0] = columns
    row = lax.broadcasted_iota(jnp.int32, (acts_ref.shape[0], tokens), 0)
    dense = jnp.zeros(row.shape, jnp.float32)
    for k in range(per_block):
        dense = jnp.where(row == columns[k : k + 1], values[k : k + 1], dense)
    acts_ref[...] = dense.astype(jnp.bfloat16)


def mask_kernel(per_block, products_ref, cols_ref, pre_ref, lat_ref, bias_ref):
    products = products_ref[...]
    columns = cols_ref[0]
    row = lax.broadcasted_iota(jnp.int32, products.shape, 0)
    kept = jnp.zeros(products.shape, jnp.float32)
    for k in range(per_block):
        hit = row == columns[k : k + 1]
        picked = jnp.where(hit, products, 0.0)
        lat_ref[0, k : k + 1, :] = jnp.sum(picked, axis=0, keepdims=True)
        kept = kept + picked
    pre_ref[...] = kept.astype(jnp.bfloat16)

    @pl.when(pl.program_id(0) == 0)
    def _():
        bias_ref[...] = jnp.zeros_like(bias_ref)

    bias_ref[...] += kept


def column_parts(width, least, row_count):
    lanes = width // BLOCK
    for parts in range(least, lanes + 1):
        if lanes % parts == 0 and row_count * (width // parts) * 2 <= PART_BYTES:
            return parts
    return lanes


def per_device(grad_recon, inputs, decoder, owners, local_blocks, offsets, act_values):
    token_count, width = grad_recon.shape
    block_count = owners.shape[1]
    per_block = offsets.shape[2]
    latent_count = decoder.shape[0]
    peer_count = lax.axis_size("lat")
    pairs = block_count * per_block
    row_count = peer_count * token_count
    me = lax.axis_index("lat").astype(jnp.int32).reshape(1)

    own_t = owners.T
    columns_t = (local_blocks.T[:, None, :] * BLOCK + offsets.transpose(1, 2, 0)).reshape(pairs, token_count)
    acts_t = act_values.transpose(1, 2, 0).reshape(pairs, token_count)
    filler = jnp.zeros((-block_count % 16, token_count), jnp.bfloat16)
    meta = jnp.concatenate([acts_t, columns_t.astype(jnp.bfloat16), own_t.astype(jnp.bfloat16), filler], axis=0)
    meta_all = lax.all_gather(meta, "lat", axis=0)

    parts = column_parts(width, 2, row_count)
    span = width // parts
    depth = max(1, HELD_BYTES // (row_count * span * 2))

    def gathered(rows, p, done):
        piece = rows[:, p * span : (p + 1) * span]
        if len(done) >= depth:
            piece, _ = lax.optimization_barrier((piece, done[-depth]))
        return lax.all_gather(piece, "lat", axis=0, tiled=True)

    acts_dense, cols = pl.pallas_call(
        functools.partial(build_kernel, block_count, per_block),
        grid=(peer_count,),
        in_specs=[
            pl.BlockSpec(memory_space=pltpu.SMEM),
            pl.BlockSpec((1, meta.shape[0], token_count), lambda s: (s, 0, 0)),
        ],
        out_specs=[
            pl.BlockSpec((latent_count, token_count), lambda s: (0, s)),
            pl.BlockSpec((1, per_block, token_count), lambda s: (s, 0, 0)),
        ],
        out_shape=[
            jax.ShapeDtypeStruct((latent_count, row_count), jnp.bfloat16),
            jax.ShapeDtypeStruct((peer_count, per_block, token_count), jnp.int32),
        ],
        cost_estimate=pl.CostEstimate(flops=latent_count * row_count * 48, bytes_accessed=row_count * latent_count * 2, transcendentals=0),
    )(me, meta_all)

    products = None
    decoder_parts = []
    for p in range(parts):
        rows = gathered(grad_recon, p, decoder_parts)
        part = lax.dot_general(acts_dense, rows, (((1,), (0,)), ((), ())), preferred_element_type=jnp.float32).astype(jnp.bfloat16)
        term = lax.dot_general(
            decoder[:, p * span : (p + 1) * span], rows, (((1,), (1,)), ((), ())), preferred_element_type=jnp.float32
        )
        products = term if products is None else products + term
        if depth < 2 * parts:
            part, products = lax.optimization_barrier((part, products))
        decoder_parts.append(part)
    decoder_grad = jnp.concatenate(decoder_parts, axis=1)

    pre_grads, lat, bias_lanes = pl.pallas_call(
        functools.partial(mask_kernel, per_block),
        grid=(peer_count,),
        in_specs=[
            pl.BlockSpec((latent_count, token_count), lambda s: (0, s)),
            pl.BlockSpec((1, per_block, token_count), lambda s: (s, 0, 0)),
        ],
        out_specs=[
            pl.BlockSpec((latent_count, token_count), lambda s: (0, s)),
            pl.BlockSpec((1, per_block, token_count), lambda s: (s, 0, 0)),
            pl.BlockSpec((latent_count, token_count), lambda s: (0, 0)),
        ],
        out_shape=[
            jax.ShapeDtypeStruct((latent_count, row_count), jnp.bfloat16),
            jax.ShapeDtypeStruct((peer_count, per_block, token_count), jnp.float32),
            jax.ShapeDtypeStruct((latent_count, token_count), jnp.float32),
        ],
        cost_estimate=pl.CostEstimate(flops=latent_count * row_count * 64, bytes_accessed=row_count * latent_count * 6, transcendentals=0),
    )(products, cols)
    bias_grad = jnp.sum(bias_lanes, axis=1)

    returned = lax.all_to_all(lat, "lat", split_axis=0, concat_axis=0, tiled=True)
    owner_id = jnp.arange(peer_count, dtype=jnp.int32)[:, None, None, None]
    picked = jnp.where(own_t[None, :, None, :] == owner_id, returned[:, None, :, :], 0.0)
    latent_grads = jnp.sum(picked, axis=0).reshape(pairs, token_count).T

    encoder_parts = []
    for p in range(parts):
        rows = gathered(inputs, p, decoder_parts + encoder_parts)
        encoder_parts.append(
            lax.dot_general(rows, pre_grads, (((0,), (1,)), ((), ())), preferred_element_type=jnp.float32).astype(jnp.bfloat16)
        )
    encoder_grad = jnp.concatenate(encoder_parts, axis=0)
    return (decoder_grad, encoder_grad, bias_grad, latent_grads)


def solution(mesh):
    placed = (
        P(("groups", "lat"), None),
        P(("groups", "lat"), None),
        P("lat", None),
        P(("groups", "lat"), None),
        P(("groups", "lat"), None),
        P(("groups", "lat"), None, None),
        P(("groups", "lat"), None, None),
    )
    return jax.shard_map(
        per_device,
        mesh=mesh,
        in_specs=placed,
        out_specs=(
            P(("groups", "lat"), None),
            P(None, ("groups", "lat")),
            P(("groups", "lat")),
            P(("groups", "lat"), None),
        ),
        check_vma=False,
    )
```

time: 453 us -> 309 us (0.68)
  local copies, waits for them, and re-layouts: 152 us -> 6.82 us
  blocking collectives: 128 us -> 27.8 us
  waiting for transfers between devices: 102 us -> 196 us
  starting transfers between devices: 37 us -> 3.86 us
  Pallas kernels: 0 us -> 21.7 us
  matrix products: 16.7 us -> 34.3 us
  other arithmetic: 16.1 us -> 2.95 us
  between operations: 0.86 us -> 13.9 us
    all_gather x0 -> x4, waiting for transfers between devices: none -> 195 us  [gathered(): return lax.all_gather(piece, 'lat', axis=0, tiled=True)]
    all_to_all x1 -> x0, blocking collectives: 128 us -> none  [per_device(): lax.all_to_all(grad_send, 'lat', split_axis=0, concat_axis=0, tiled=True)]
    all_to_all x3 -> x1, waiting for transfers between devices: 102 us -> 0.01 us  [per_device(): lax.all_to_all(lat, 'lat', split_axis=0, concat_axis=0, tiled=True)]
    gather x7 -> x0, local copies, waits for them, and re-layouts: 89.4 us -> none  [the longest x3 65.1 us: per_device(): jnp.take_along_axis(picked_rows, columns, axis=1)]
    unnamed x11 -> x17, local copies, waits for them, and re-layouts: 58.7 us -> 2.3 us
    all_to_all x3 -> x1, starting transfers between devices: 37 us -> 3.7 us  [per_device(): lax.all_to_all(lat, 'lat', split_axis=0, concat_axis=0, tiled=True)]
    all_gather x0 -> x1, blocking collectives: none -> 27.8 us  [per_device(): meta_all = lax.all_gather(meta, 'lat', axis=0)]
    pallas_call x0 -> x2, Pallas kernels: none -> 21.7 us  [the longest x1 12.3 us: per_device(): pl.pallas_call(functools.partial(mask_kernel, per_block), grid=(peer_coun...]
  transfers between devices with their start and end apart: 3 -> 5, of which waited for: 2 -> 4; matrix products, arithmetic and copies ran while one was open for 10% -> 13% of each run, Pallas kernels for 0% -> 7%
where the time goes in v1:
time: 309 us; the launch traced here: 308 us
  waiting for transfers between devices  196 us (63%)
  matrix products  34.3 us (11%)
  blocking collectives  27.8 us (9%)
  Pallas kernels  21.7 us (7%)
  between operations  13.9 us (4%)
  local copies, waits for them, and re-layouts  6.82 us (2%)
  starting transfers between devices  3.86 us (1%)
    all_gather x4, waiting for transfers between devices, gathered(): return lax.all_gather(piece, 'lat', axis=0, tiled=True)  195 us
    all_gather x1, blocking collectives, per_device(): meta_all = lax.all_gather(meta, 'lat', axis=0)  27.8 us
    dot_general x2, matrix products, per_device(): lax.dot_general(decoder[:, p * span:(p + 1) * span], rows, (((1,), (1,)),...  13.6 us
    pallas_call x1, Pallas kernels, per_device(): pl.pallas_call(functools.partial(mask_kernel, per_block), grid=(peer_coun...  12.3 us
    dot_general x2, matrix products, per_device(): lax.dot_general(acts_dense, rows, (((1,), (0,)), ((), ())), preferred_ele...  10.3 us
    dot_general x2, matrix products, per_device(): lax.dot_general(rows, pre_grads, (((0,), (1,)), ((), ())), preferred_elem...  10.3 us
    pallas_call x1, Pallas kernels, per_device(): pl.pallas_call(functools.partial(build_kernel, block_count, per_block), g...  9.34 us
  transfers between devices with their start and end apart: 5, of which 4 were waited for; matrix products, arithmetic and copies ran while one was open for 13% of the time, Pallas kernels for 7%

profile of v1, /device:TPU:0, one launch (start us, length us, event | category | flops | bytes accessed | tf_op | source)
XLA Modules:
  0.0 307.6 jit_solution(1888166712629969435)
XLA Ops:
  7.2 0.0 all-gather.6.cloned.1.call-start
  7.3 2.3 fusion.7
  9.5 0.0 all-gather.6.cloned.1.call-update
  9.6 0.0 all-gather.8.cloned.1.call-start
  9.6 0.7 all-gather.8.cloned.1.call-update
  10.3 0.0 all-gather.12.cloned.1.call-start
  10.4 2.2 fusion.6
  12.5 0.0 all-gather.12.cloned.1.call-update
  12.5 0.0 all-gather.10.cloned.1.call-start
  12.6 0.5 all-gather.10.cloned.1.call-update
  13.1 0.1 pad.7.clone
  13.3 0.1 maximum_maximum_fusion
  13.4 27.8 %all-gather = bf16[2304,128]{1,0:T(8,128)(2,1)} all-gather(bf16[144,128]{1,0:T(8,128)(2,1)S(1)} %maximum_maximum_fusion), channel_id=2, replica_groups=mesh['groups'=2,'lat'=16] {'lat'}, dimensions={0}, use_global_device_ids=true | all-gather | bytes 626688 | tf_op jit(solution)/shard_map/all_gather | solution.py:77
  41.1 9.3 %shard_map.102 = (bf16[256,2048]{1,0:T(8,128)(2,1)}, s32[16,16,128]{2,1,0:T(8,128)}) custom-call(s32[1]{0:T(128)} %bitcast.me_ref, bf16[16,144,128]{2,1,0:T(8,128)(2,1)} %bitcast.31), custom_call_target="tpu_custom_call" | custom-call | flops 25165824 | bytes 1048576 | tf_op jit(solution)/shard_map/pallas_call | solution.py:89
  50.5 33.4 %all-gather.6.cloned.1.call-done = bf16[2048,1792]{1,0:T(8,128)(2,1)} async-done(((bf16[128,1792]{1,0:T(8,128)(2,1)}), bf16[2048,1792]{1,0:T(8,128)(2,1)}) %all-gather.6.cloned.1.call-update) | async-done | bytes 7340048 | tf_op jit(solution)/shard_map/all_gather | solution.py:87
  83.9 6.5 %fusion.3 = f32[256,2048]{1,0:T(8,128)} fusion(bf16[2048,1792]{1,0:T(8,128)(2,1)} %all-gather.6.cloned.1.call-done, bf16[256,3584]{1,0:T(8,128)(2,1)S(1)} %copy-done.5), kind=kOutput, calls=%fused_computation.10 | convolution fusion | flops 1879048192 | bytes 10354688 | tf_op jit(solution)/shard_map/dot_general | solution.py:112
  90.4 62.5 %all-gather.8.cloned.1.call-done = bf16[2048,1792]{1,0:T(8,128)(2,1)} async-done(((bf16[128,1792]{1,0:T(8,128)(2,1)}), bf16[2048,1792]{1,0:T(8,128)(2,1)}) %all-gather.8.cloned.1.call-update) | async-done | bytes 7340048 | tf_op jit(solution)/shard_map/all_gather | solution.py:87
  152.9 7.1 %convolution_add_fusion.products_ref = f32[256,2048]{1,0:T(8,128)} fusion(f32[256,2048]{1,0:T(8,128)} %fusion.3, bf16[2048,1792]{1,0:T(8,128)(2,1)} %all-gather.8.cloned.1.call-done, bf16[256,3584]{1,0:T(8,128)(2,1)S(1)} %copy-done.5), kind=kOutput, calls=%fused_computation | convolution fusion | flops 1879572480 | bytes 12451840 | tf_op jit(solution)/shard_map/dot_general | solution.py:112
  160.0 12.3 %shard_map.103 = (bf16[256,2048]{1,0:T(8,128)(2,1)}, f32[16,16,128]{2,1,0:T(8,128)}, f32[256,128]{1,0:T(8,128)}) custom-call(f32[256,2048]{1,0:T(8,128)} %convolution_add_fusion.products_ref, s32[16,16,128]{2,1,0:T(8,128)} %get-tuple-element.10.cols_ref), custom_call_target="tpu_custom_call" | custom-call | flops 33554432 | bytes 3145728 | tf_op jit(solution)/shard_map/pallas_call | solution.py:121
  172.3 3.7 %all-to-all-start = ((f32[16,16,128]{2,1,0:T(8,128)}), f32[16,16,128]{2,1,0:T(8,128)S(1)}, u32[]{:S(2)}, u32[]{:S(2)}) async-start(f32[16,16,128]{2,1,0:T(8,128)} %get-tuple-element.13), calls=%async_computation | async-start | bytes 262144 | tf_op jit(solution)/shard_map/all_to_all | solution.py:142
  176.1 5.2 %convolution_convert_fusion.2 = bf16[256,1792]{1,0:T(8,128)(2,1)S(1)} fusion(bf16[256,2048]{1,0:T(8,128)(2,1)S(1)} %copy-done.7, bf16[2048,1792]{1,0:T(8,128)(2,1)} %all-gather.8.cloned.1.call-done), kind=kOutput, calls=%fused_computation.3 | convolution fusion | flops 1879506944 | bytes 9306112 | tf_op jit(solution)/shard_map/dot_general | solution.py:111
  181.3 5.2 %convolution_convert_fusion.3 = bf16[256,1792]{1,0:T(8,128)(2,1)S(1)} fusion(bf16[256,2048]{1,0:T(8,128)(2,1)S(1)} %copy-done.7, bf16[2048,1792]{1,0:T(8,128)(2,1)} %all-gather.6.cloned.1.call-done), kind=kOutput, calls=%fused_computation.4 | convolution fusion | flops 1879506944 | bytes 9306112 | tf_op jit(solution)/shard_map/dot_general | solution.py:111
  186.4 1.4 pad_maximum_fusion
  187.8 35.5 %all-gather.12.cloned.1.call-done = bf16[2048,1792]{1,0:T(8,128)(2,1)} async-done(((bf16[128,1792]{1,0:T(8,128)(2,1)}), bf16[2048,1792]{1,0:T(8,128)(2,1)}) %all-gather.12.cloned.1.call-update) | async-done | bytes 7340048 | tf_op jit(solution)/shard_map/all_gather | solution.py:87
  223.2 5.2 %fusion.1 = bf16[1792,256]{0,1:T(8,128)(2,1)S(1)} fusion(bf16[256,2048]{1,0:T(8,128)(2,1)S(1)} %copy-done.6, bf16[2048,1792]{1,0:T(8,128)(2,1)} %all-gather.12.cloned.1.call-done), kind=kOutput, calls=%fused_computation.6 | convolution fusion | flops 1879506944 | bytes 9306112 | tf_op jit(solution)/shard_map/dot_general | solution.py:151
  228.4 63.7 %all-gather.10.cloned.1.call-done = bf16[2048,1792]{1,0:T(8,128)(2,1)} async-done(((bf16[128,1792]{1,0:T(8,128)(2,1)}), bf16[2048,1792]{1,0:T(8,128)(2,1)}) %all-gather.10.cloned.1.call-update) | async-done | bytes 7340048 | tf_op jit(solution)/shard_map/all_gather | solution.py:87
  292.1 5.2 %fusion = bf16[1792,256]{0,1:T(8,128)(2,1)S(1)} fusion(bf16[256,2048]{1,0:T(8,128)(2,1)S(1)} %copy-done.6, bf16[2048,1792]{1,0:T(8,128)(2,1)} %all-gather.10.cloned.1.call-done), kind=kOutput, calls=%fused_computation.5 | convolution fusion | flops 1879506944 | bytes 9306112 | tf_op jit(solution)/shard_map/dot_general | solution.py:151
  297.3 0.1 pad_maximum_fusion.1
  297.4 2.3 copy.12
  299.7 0.7 reduce_sum.18
  300.4 0.0 all-to-all-done
  300.4 0.7 select_reduce_fusion
  (21 shorter events, 0.1 us)
Async XLA Ops:
  7.2 6.1 %copy-start.3 = (s32[128,4]{0,1:T(4,128)S(1)}, s32[128,4]{0,1:T(4,128)}, u32[]{:S(2)}) copy-start(s32[128,4]{0,1:T(4,128)} %param.10) | copy-start | bytes 6148
  7.2 6.0 %copy-start.4 = (s32[128,4]{0,1:T(4,128)S(1)}, s32[128,4]{0,1:T(4,128)}, u32[]{:S(2)}) copy-start(s32[128,4]{0,1:T(4,128)} %param.11) | copy-start | bytes 6148
  7.2 6.1 %copy-start.1 = (s32[128,4,16]{0,2,1:T(8,128)S(1)}, s32[128,4,16]{0,2,1:T(8,128)}, u32[]{:S(2)}) copy-start(s32[128,4,16]{0,2,1:T(8,128)} %param.12) | copy-start | bytes 98308
  7.2 6.1 %copy-start.2 = (bf16[128,4,16]{0,2,1:T(8,128)(2,1)S(1)}, bf16[128,4,16]{0,2,1:T(8,128)(2,1)}, u32[]{:S(2)}) copy-start(bf16[128,4,16]{0,2,1:T(8,128)(2,1)} %param.13) | copy-start | bytes 49156
  7.2 76.7 %copy-start.5 = (bf16[256,3584]{1,0:T(8,128)(2,1)S(1)}, bf16[256,3584]{1,0:T(8,128)(2,1)}, u32[]{:S(2)}) copy-start(bf16[256,3584]{1,0:T(8,128)(2,1)} %param.9) | copy-start | bytes 5505028
  7.2 76.7 %all-gather.6.cloned.1.call-start = ((), (), s32[]{:S(2)}) async-start(), calls=%async_computation.1 | async-start | bytes 7798784 | tf_op jit(solution)/shard_map/all_gather | solution.py:87
  9.6 143.3 %all-gather.8.cloned.1.call-start = ((), (), s32[]{:S(2)}) async-start(), calls=%async_computation.2 | async-start | bytes 7798784 | tf_op jit(solution)/shard_map/all_gather | solution.py:87
  10.3 212.9 %all-gather.12.cloned.1.call-start = ((), (), s32[]{:S(2)}) async-start(), calls=%async_computation.4 | async-start | bytes 7798784 | tf_op jit(solution)/shard_map/all_gather | solution.py:87
  12.5 279.6 %all-gather.10.cloned.1.call-start = ((), (), s32[]{:S(2)}) async-start(), calls=%async_computation.3 | async-start | bytes 7798784 | tf_op jit(solution)/shard_map/all_gather | solution.py:87
  90.4 85.7 %copy-start.7 = (bf16[256,2048]{1,0:T(8,128)(2,1)S(1)}, bf16[256,2048]{1,0:T(8,128)(2,1)}, u32[]{:S(2)}) copy-start(bf16[256,2048]{1,0:T(8,128)(2,1)} %get-tuple-element.9) | copy-start | bytes 3145732
  172.3 128.0 %all-to-all-start = ((f32[16,16,128]{2,1,0:T(8,128)}), f32[16,16,128]{2,1,0:T(8,128)S(1)}, u32[]{:S(2)}, u32[]{:S(2)}) async-start(f32[16,16,128]{2,1,0:T(8,128)} %get-tuple-element.13), calls=%async_computation | async-start | bytes 262144 | tf_op jit(solution)/shard_map/all_to_all | solution.py:142
  186.4 36.8 %copy-start.6 = (bf16[256,2048]{1,0:T(8,128)(2,1)S(1)}, bf16[256,2048]{1,0:T(8,128)(2,1)}, u32[]{:S(2)}) copy-start(bf16[256,2048]{1,0:T(8,128)(2,1)} %get-tuple-element.11) | copy-start | bytes 3145732
  297.3 2.4 copy-start
Sparse Core Ops, SparseCore 0:
  10.9 72.9 all-gather.5
  86.2 66.6 all-gather.7
  155.2 68.0 all-gather.11
  225.4 66.6 all-gather.9

commit v2 on v1

v2 whole, which is shorter than its diff:
```python
import functools

import jax
import jax.numpy as jnp
import numpy as np
from jax import lax
from jax.experimental import pallas as pl
from jax.experimental.pallas import tpu as pltpu
from jax.sharding import PartitionSpec as P

BLOCK = 128
PART_BYTES = 9 << 20
HELD_BYTES = 1 << 25
RING_BYTES = 1 << 26
VMEM_BYTES = 48 << 20


def ring_tables(peer_count):
    chips = peer_count // 2
    ring = [chip for chip in range(chips) if chip % 2 == 0] + [chip for chip in reversed(range(chips)) if chip % 2]
    place = {chip: spot for spot, chip in enumerate(ring)}
    sources = np.zeros((peer_count, chips, 4), np.int32)
    first_step = np.zeros((peer_count, 2, chips), np.int32)
    for device in range(peer_count):
        chip, core = divmod(device, 2)
        sign = 1 - 2 * core
        for step in range(chips):
            ahead, behind = ring[(place[chip] - sign * step) % chips], ring[(place[chip] + sign * step) % chips]
            sources[device, step] = (2 * ahead + core, 2 * ahead + 1 - core, 2 * behind + 1 - core, 2 * behind + core)
            first_step[device, 0, ahead] = step
            first_step[device, 1, behind] = step
    up = [(2 * ring[i], 2 * ring[(i + 1) % chips]) for i in range(chips)]
    down = [(2 * ring[i], 2 * ring[(i - 1) % chips]) for i in range(chips)]
    up_1, down_1 = [(a + 1, b + 1) for a, b in up], [(a + 1, b + 1) for a, b in down]
    swap = [(i, i ^ 1) for i in range(peer_count)]
    return sources, first_step, up + down_1, down + up_1, swap


def join_rows(parts, rows_ref):
    half = parts[0].shape[0]
    for i, part in enumerate(parts):
        rows_ref[i * half : (i + 1) * half, :] = part[...]


def grad_kernel(has_total, last, per_block, *refs):
    order_ref, meta_ref, decoder_ref = refs[:3]
    parts = refs[3:7]
    refs = refs[7:]
    total_ref = None
    if has_total:
        total_ref, refs = refs[0], refs[1:]
    out_ref, pre_ref, lat_ref, bias_ref, rows_ref, acts_ref = refs
    join_rows(parts, rows_ref)
    latents, width = decoder_ref.shape
    tokens = rows_ref.shape[0] // 2
    products = lax.dot_general(decoder_ref[...], rows_ref[...], (((1,), (1,)), ((), ())), preferred_element_type=jnp.float32)
    low = lax.broadcasted_iota(jnp.int32, (2 * per_block, tokens), 1) < tokens // 2
    row = lax.broadcasted_iota(jnp.int32, (latents, tokens), 0)
    bias = jnp.zeros((latents, tokens), jnp.float32)
    for tile in range(2):
        meta = jnp.where(
            low,
            meta_ref[order_ref[2 * tile]].astype(jnp.float32),
            meta_ref[order_ref[2 * tile + 1]].astype(jnp.float32),
        )
        columns = meta[:per_block].astype(jnp.int32)
        values = meta[per_block:]
        here = products[:, tile * tokens : (tile + 1) * tokens]
        kept = jnp.zeros((latents, tokens), jnp.float32)
        dense = jnp.zeros((latents, tokens), jnp.float32)
        for k in range(per_block):
            hit = row == columns[k : k + 1]
            picked = jnp.where(hit, here, 0.0)
            lat_ref[tile, k : k + 1, :] = jnp.sum(picked, axis=0, keepdims=True)
            kept = kept + picked
            dense = jnp.where(hit, values[k : k + 1], dense)
        bias = bias + kept
        pre_ref[:, tile * tokens : (tile + 1) * tokens] = kept.astype(jnp.bfloat16)
        acts_ref[:, tile * tokens : (tile + 1) * tokens] = dense.astype(jnp.bfloat16)
    bias_ref[...] = bias
    acts = acts_ref[...]
    span = 512 if width % 512 == 0 else BLOCK

    def column(i, _):
        at = pl.ds(pl.multiple_of(i * span, span), span)
        term = lax.dot_general(acts, rows_ref[:, at], (((1,), (0,)), ((), ())), preferred_element_type=jnp.float32)
        if has_total:
            term = term + total_ref[:, at]
        out_ref[:, at] = term.astype(out_ref.dtype)
        return 0

    lax.fori_loop(0, width // span, column, 0)


def input_kernel(has_total, last, *refs):
    pre_ref = refs[0]
    parts = refs[1:5]
    refs = refs[5:]
    total_ref = None
    if has_total:
        total_ref, refs = refs[0], refs[1:]
    out_ref, rows_ref = refs
    join_rows(parts, rows_ref)
    width = rows_ref.shape[1]
    pre = pre_ref[...]
    span = 512 if width % 512 == 0 else BLOCK

    def column(i, _):
        at = pl.ds(pl.multiple_of(i * span, span), span)
        term = lax.dot_general(rows_ref[:, at], pre, (((0,), (1,)), ((), ())), preferred_element_type=jnp.float32)
        if has_total:
            term = term + total_ref[at, :]
        out_ref[at, :] = term.astype(out_ref.dtype)
        return 0

    lax.fori_loop(0, width // span, column, 0)


def ring_rows(rows, down_up):
    up, down, swap, chips = down_up
    half = rows.shape[0] // 2
    low, high = rows[:half], rows[half:]
    steps = []
    for step in range(chips):
        if step:
            low = lax.ppermute(low, "lat", up)
            high = lax.ppermute(high, "lat", down)
        other_low = lax.ppermute(low, "lat", swap)
        other_high = lax.ppermute(high, "lat", swap)
        steps.append((low, other_high, other_low, high))
    return steps


def by_ring(grad_recon, inputs, decoder, owners, local_blocks, offsets, act_values):
    token_count, width = grad_recon.shape
    block_count = owners.shape[1]
    per_block = offsets.shape[2]
    latent_count = decoder.shape[0]
    peer_count = lax.axis_size("lat")
    chips = peer_count // 2
    me = lax.axis_index("lat")
    sources, first_step, up, down, swap = ring_tables(peer_count)
    order = jnp.asarray(sources)[me]
    step_of = jnp.asarray(first_step)[me]

    own_t = owners.T
    columns_t = (local_blocks.T[:, None, :] * BLOCK + offsets.transpose(1, 2, 0)).astype(jnp.float32)
    values_t = act_values.transpose(1, 2, 0).astype(jnp.float32)
    peers = jnp.arange(peer_count, dtype=jnp.int32)
    sent_columns = jnp.full((peer_count, per_block, token_count), -1.0, jnp.float32)
    sent_values = jnp.zeros((peer_count, per_block, token_count), jnp.float32)
    for i in range(block_count):
        named = own_t[i][None, None, :] == peers[:, None, None]
        sent_columns = jnp.where(named, columns_t[i][None], sent_columns)
        sent_values = jnp.where(named, values_t[i][None], sent_values)
    meta = jnp.concatenate([sent_columns, sent_values], axis=1).astype(jnp.bfloat16)
    meta = lax.all_to_all(meta, "lat", split_axis=0, concat_axis=0, tiled=True)

    grad_steps = ring_rows(grad_recon, (up, down, swap, chips))
    input_steps = ring_rows(inputs, (up, down, swap, chips))
    params = pltpu.CompilerParams(vmem_limit_bytes=VMEM_BYTES)
    whole = pl.BlockSpec(memory_space=pltpu.VMEM)
    scalars = pl.BlockSpec(memory_space=pltpu.SMEM)
    step_tokens = 2 * token_count
    work = 2 * latent_count * width * step_tokens

    total, pres, lats, biases = None, [], [], []
    for step, parts in enumerate(grad_steps):
        last = step == chips - 1
        operands = [order[step], meta, decoder, *parts] + ([] if total is None else [total])
        total, pre, lat, bias = pl.pallas_call(
            functools.partial(grad_kernel, total is not None, last, per_block),
            in_specs=[scalars] + [whole] * (len(operands) - 1),
            out_specs=[whole] * 4,
            out_shape=[
                jax.ShapeDtypeStruct((latent_count, width), jnp.bfloat16 if last else jnp.float32),
                jax.ShapeDtypeStruct((latent_count, step_tokens), jnp.bfloat16),
                jax.ShapeDtypeStruct((2, per_block, token_count), jnp.float32),
                jax.ShapeDtypeStruct((latent_count, token_count), jnp.float32),
            ],
            scratch_shapes=[
                pltpu.VMEM((step_tokens, width), jnp.bfloat16),
                pltpu.VMEM((latent_count, step_tokens), jnp.bfloat16),
            ],
            compiler_params=params,
            cost_estimate=pl.CostEstimate(flops=2 * work, bytes_accessed=12 * latent_count * width, transcendentals=0),
            name="grad_step",
        )(*operands)
        pres.append(pre)
        lats.append(lat)
        biases.append(bias)
    decoder_grad = total
    bias_grad = jnp.sum(functools.reduce(jnp.add, biases), axis=1)

    lat = jnp.stack(lats)
    ahead, behind = lat[:, 0][step_of[0]], lat[:, 1][step_of[1]]
    low = (jnp.arange(token_count) < token_count // 2)[None, None, :]
    same, other = jnp.where(low, ahead, behind), jnp.where(low, behind, ahead)
    even = me % 2 == 0
    lat = jnp.stack([jnp.where(even, same, other), jnp.where(even, other, same)], axis=1)
    returned = lax.all_to_all(
        lat.reshape(peer_count, per_block, token_count), "lat", split_axis=0, concat_axis=0, tiled=True
    )
    latent_grads = pick_returned(returned, own_t)

    total = None
    for step, parts in enumerate(input_steps):
        last = step == chips - 1
        operands = [pres[step], *parts] + ([] if total is None else [total])
        total = pl.pallas_call(
            functools.partial(input_kernel, total is not None, last),
            in_specs=[whole] * len(operands),
            out_specs=whole,
            out_shape=jax.ShapeDtypeStruct((width, latent_count), jnp.bfloat16 if last else jnp.float32),
            scratch_shapes=[pltpu.VMEM((step_tokens, width), jnp.bfloat16)],
            compiler_params=params,
            cost_estimate=pl.CostEstimate(flops=work, bytes_accessed=10 * latent_count * width, transcendentals=0),
            name="input_step",
        )(*operands)
    return (decoder_grad, total, bias_grad, latent_grads)


def pick_returned(returned, own_t):
    owner_id = jnp.arange(returned.shape[0], dtype=jnp.int32)[:, None, None, None]
    picked = jnp.where(own_t[None, :, None, :] == owner_id, returned[:, None, :, :], 0.0)
    return jnp.sum(picked, axis=0).reshape(-1, own_t.shape[1]).T


def build_kernel(block_count, per_block, me_ref, meta_ref, acts_ref, cols_ref):
    pairs = block_count * per_block
    meta = meta_ref[0].astype(jnp.float32)
    me = me_ref[0].astype(jnp.float32)
    tokens = meta.shape[1]
    values = jnp.zeros((per_block, tokens), jnp.float32)
    columns = jnp.full((per_block, tokens), -1.0, jnp.float32)
    for i in range(block_count):
        mine = meta[2 * pairs + i : 2 * pairs + i + 1] == me
        values = jnp.where(mine, meta[i * per_block : (i + 1) * per_block], values)
        columns = jnp.where(mine, meta[pairs + i * per_block : pairs + (i + 1) * per_block], columns)
    columns = columns.astype(jnp.int32)
    cols_ref[0] = columns
    row = lax.broadcasted_iota(jnp.int32, (acts_ref.shape[0], tokens), 0)
    dense = jnp.zeros(row.shape, jnp.float32)
    for k in range(per_block):
        dense = jnp.where(row == columns[k : k + 1], values[k : k + 1], dense)
    acts_ref[...] = dense.astype(jnp.bfloat16)


def mask_kernel(per_block, products_ref, cols_ref, pre_ref, lat_ref, bias_ref):
    products = products_ref[...]
    columns = cols_ref[0]
    row = lax.broadcasted_iota(jnp.int32, products.shape, 0)
    kept = jnp.zeros(products.shape, jnp.float32)
    for k in range(per_block):
        picked = jnp.where(row == columns[k : k + 1], products, 0.0)
        lat_ref[0, k : k + 1, :] = jnp.sum(picked, axis=0, keepdims=True)
        kept = kept + picked
    pre_ref[...] = kept.astype(jnp.bfloat16)

    @pl.when(pl.program_id(0) == 0)
    def _():
        bias_ref[...] = jnp.zeros_like(bias_ref)

    bias_ref[...] += kept


def column_parts(width, row_count):
    lanes = width // BLOCK
    for parts in range(2, lanes + 1):
        if lanes % parts == 0 and row_count * (width // parts) * 2 <= PART_BYTES:
            return parts
    return lanes


def by_gather(grad_recon, inputs, decoder, owners, local_blocks, offsets, act_values):
    token_count, width = grad_recon.shape
    block_count = owners.shape[1]
    per_block = offsets.shape[2]
    latent_count = decoder.shape[0]
    peer_count = lax.axis_size("lat")
    pairs = block_count * per_block
    row_count = peer_count * token_count
    me = lax.axis_index("lat").astype(jnp.int32).reshape(1)

    own_t = owners.T
    columns_t = (local_blocks.T[:, None, :] * BLOCK + offsets.transpose(1, 2, 0)).reshape(pairs, token_count)
    acts_t = act_values.transpose(1, 2, 0).reshape(pairs, token_count)
    filler = jnp.zeros((-block_count % 16, token_count), jnp.bfloat16)
    meta = jnp.concatenate([acts_t, columns_t.astype(jnp.bfloat16), own_t.astype(jnp.bfloat16), filler], axis=0)
    meta_all = lax.all_gather(meta, "lat", axis=0)

    parts = column_parts(width, row_count)
    span = width // parts
    depth = max(1, HELD_BYTES // (row_count * span * 2))

    def gathered(rows, p, done):
        piece = rows[:, p * span : (p + 1) * span]
        if len(done) >= depth:
            piece, _ = lax.optimization_barrier((piece, done[-depth]))
        return lax.all_gather(piece, "lat", axis=0, tiled=True)

    tile = pl.BlockSpec((latent_count, token_count), lambda s: (0, s))
    picks = pl.BlockSpec((1, per_block, token_count), lambda s: (s, 0, 0))
    acts_dense, cols = pl.pallas_call(
        functools.partial(build_kernel, block_count, per_block),
        grid=(peer_count,),
        in_specs=[
            pl.BlockSpec(memory_space=pltpu.SMEM),
            pl.BlockSpec((1, meta.shape[0], token_count), lambda s: (s, 0, 0)),
        ],
        out_specs=[tile, picks],
        out_shape=[
            jax.ShapeDtypeStruct((latent_count, row_count), jnp.bfloat16),
            jax.ShapeDtypeStruct((peer_count, per_block, token_count), jnp.int32),
        ],
        name="build",
    )(me, meta_all)

    products = None
    decoder_parts = []
    for p in range(parts):
        rows = gathered(grad_recon, p, decoder_parts)
        part = lax.dot_general(
            acts_dense, rows, (((1,), (0,)), ((), ())), preferred_element_type=jnp.float32
        ).astype(jnp.bfloat16)
        term = lax.dot_general(
            decoder[:, p * span : (p + 1) * span], rows, (((1,), (1,)), ((), ())), preferred_element_type=jnp.float32
        )
        products = term if products is None else products + term
        if depth < 2 * parts:
            part, products = lax.optimization_barrier((part, products))
        decoder_parts.append(part)
    decoder_grad = jnp.concatenate(decoder_parts, axis=1)

    pre_grads, lat, bias_lanes = pl.pallas_call(
        functools.partial(mask_kernel, per_block),
        grid=(peer_count,),
        in_specs=[tile, picks],
        out_specs=[tile, picks, pl.BlockSpec((latent_count, token_count), lambda s: (0, 0))],
        out_shape=[
            jax.ShapeDtypeStruct((latent_count, row_count), jnp.bfloat16),
            jax.ShapeDtypeStruct((peer_count, per_block, token_count), jnp.float32),
            jax.ShapeDtypeStruct((latent_count, token_count), jnp.float32),
        ],
        name="mask",
    )(products, cols)
    bias_grad = jnp.sum(bias_lanes, axis=1)
    returned = lax.all_to_all(lat, "lat", split_axis=0, concat_axis=0, tiled=True)
    latent_grads = pick_returned(returned, own_t)

    encoder_parts = []
    for p in range(parts):
        rows = gathered(inputs, p, decoder_parts + encoder_parts)
        encoder_parts.append(
            lax.dot_general(rows, pre_grads, (((0,), (1,)), ((), ())), preferred_element_type=jnp.float32).astype(
                jnp.bfloat16
            )
        )
    return (decoder_grad, jnp.concatenate(encoder_parts, axis=0), bias_grad, latent_grads)


def per_device(grad_recon, *others):
    row_bytes = lax.axis_size("lat") * grad_recon.size * grad_recon.dtype.itemsize
    way = by_ring if 2 * row_bytes <= RING_BYTES and lax.axis_size("lat") % 2 == 0 else by_gather
    return way(grad_recon, *others)


def solution(mesh):
    rows = P(("groups", "lat"), None)
    entries = P(("groups", "lat"), None, None)
    return jax.shard_map(
        per_device,
        mesh=mesh,
        in_specs=(rows, rows, P("lat", None), rows, rows, entries, entries),
        out_specs=(rows, P(None, ("groups", "lat")), P(("groups", "lat")), rows),
        check_vma=False,
    )
```

time: 309 us -> 220 us (0.71)
  waiting for transfers between devices: 196 us -> 22.6 us
  Pallas kernels: 21.7 us -> 88 us
  starting transfers between devices: 3.86 us -> 62.2 us
  local copies, waits for them, and re-layouts: 6.82 us -> 43.2 us
  matrix products: 34.3 us -> 0 us
  blocking collectives: 27.8 us -> 0 us
  between operations: 13.9 us -> 1.37 us
    all_gather x4 -> x0, waiting for transfers between devices: 195 us -> none  [gathered(): return lax.all_gather(piece, 'lat', axis=0, tiled=True)]
    pallas_call x2 -> x16, Pallas kernels: 21.7 us -> 88 us  [the longest x8 55.9 us: by_ring(): pl.pallas_call(functools.partial(grad_kernel, total is not None, last, pe...]
    ppermute x0 -> x60, starting transfers between devices: none -> 52.6 us  [the longest x14 26 us: ring_rows(): low = lax.ppermute(low, 'lat', up)]
    unnamed x17 -> x157, local copies, waits for them, and re-layouts: 2.3 us -> 37.4 us
    dot_general x6 -> x0, matrix products: 34.3 us -> none  [the longest x2 13.6 us: per_device(): lax.dot_general(decoder[:, p * span:(p + 1) * span], rows, (((1,), (1,)),...]
    all_gather x1 -> x0, blocking collectives: 27.8 us -> none  [per_device(): meta_all = lax.all_gather(meta, 'lat', axis=0)]
    ppermute x0 -> x60, waiting for transfers between devices: none -> 22.6 us  [the longest x14 19.9 us: ring_rows(): high = lax.ppermute(high, 'lat', down)]
    all_to_all x1 -> x2, starting transfers between devices: 3.7 us -> 9.57 us  [the longest x1 6.06 us: by_ring(): meta = lax.all_to_all(meta, 'lat', split_axis=0, concat_axis=0, tiled=True)]
  transfers between devices with their start and end apart: 5 -> 62, of which waited for: 4 -> 13; matrix products, arithmetic and copies ran while one was open for 13% -> 3% of each run, Pallas kernels for 7% -> 40%
where the time goes in v2:
time: 220 us; the launch traced here: 219 us
  Pallas kernels  88 us (40%)
  starting transfers between devices  62.2 us (28%)
  local copies, waits for them, and re-layouts  43.2 us (20%)
  waiting for transfers between devices  22.6 us (10%)
  other arithmetic  2.21 us (1%)
    pallas_call x8, Pallas kernels, by_ring(): pl.pallas_call(functools.partial(grad_kernel, total is not None, last, pe...  55.9 us
    unnamed x157, local copies, waits for them, and re-layouts  37.4 us
    pallas_call x8, Pallas kernels, by_ring(): pl.pallas_call(functools.partial(input_kernel, total is not None, last),...  32.1 us
    ppermute x14, starting transfers between devices, ring_rows(): low = lax.ppermute(low, 'lat', up)  26 us
    ppermute x14, starting transfers between devices, ring_rows(): high = lax.ppermute(high, 'lat', down)  20.5 us
    ppermute x14, waiting for transfers between devices, ring_rows(): high = lax.ppermute(high, 'lat', down)  19.9 us
    all_to_all x1, starting transfers between devices, by_ring(): meta = lax.all_to_all(meta, 'lat', split_axis=0, concat_axis=0, tiled=True)  6.06 us
  transfers between devices with their start and end apart: 62, of which 13 were waited for; matrix products, arithmetic and copies ran while one was open for 3% of the time, Pallas kernels for 40%

profile of v2, /device:TPU:0, one launch (start us, length us, event | category | flops | bytes accessed | tf_op | source)
XLA Modules:
  0.0 219.5 jit_solution(4532740277454781712)
XLA Ops:
  2.6 2.6 %collective-permute-start.7 = (bf16[64,3584]{1,0:T(8,128)(2,1)S(1)}, bf16[64,3584]{1,0:T(8,128)(2,1)S(1)}, u32[]{:S(2)}, u32[]{:S(2)}) collective-permute-start(bf16[64,3584]{1,0:T(8,128)(2,1)S(1)} %get-tuple-element.70.refs_6_), channel_id=1, source_target_pairs={{0,2},{4,0},{8,4},{12,8},{14,12},{10,14},{6,10},{2,6},{1,5},{5,9},... | collective-permute-start | bytes 1376264 | tf_op jit(solution)/shard_map/ppermute | solution.py:127
  11.4 3.7 %collective-permute-done.7.refs_6_ = bf16[64,3584]{1,0:T(8,128)(2,1)S(1)} collective-permute-done((bf16[64,3584]{1,0:T(8,128)(2,1)S(1)}, bf16[64,3584]{1,0:T(8,128)(2,1)S(1)}, u32[]{:S(2)}, u32[]{:S(2)}) %collective-permute-start.7) | collective-permute-done | bytes 458784 | tf_op jit(solution)/shard_map/ppermute | solution.py:127
  15.0 2.8 %collective-permute-start.30 = (bf16[64,3584]{1,0:T(8,128)(2,1)S(1)}, bf16[64,3584]{1,0:T(8,128)(2,1)S(1)}, u32[]{:S(2)}, u32[]{:S(2)}) collective-permute-start(bf16[64,3584]{1,0:T(8,128)(2,1)S(1)} %get-tuple-element.69.refs_1_), channel_id=1, source_target_pairs={{0,4},{4,8},{8,12},{12,14},{14,10},{10,6},{6,2},{2,0},{1,3},{5,1},... | collective-permute-start | bytes 1376264 | tf_op jit(solution)/shard_map/ppermute | solution.py:126
  24.9 2.8 %collective-permute-start.1 = (bf16[64,3584]{1,0:T(8,128)(2,1)S(1)}, bf16[64,3584]{1,0:T(8,128)(2,1)S(1)}, u32[]{:S(2)}, u32[]{:S(2)}) collective-permute-start(bf16[64,3584]{1,0:T(8,128)(2,1)S(1)} %collective-permute-done.refs_3_), channel_id=1, source_target_pairs={{0,4},{4,8},{8,12},{12,14},{14,10},{10,6},{6,2},{2,0},{1,3},{5,1},... | collective-permute-start | bytes 1376264 | tf_op jit(solution)/shard_map/ppermute | solution.py:126
  29.4 2.2 collective-permute-start.38
  34.7 2.8 %collective-permute-start.31 = (bf16[64,3584]{1,0:T(8,128)(2,1)S(1)}, bf16[64,3584]{1,0:T(8,128)(2,1)}, u32[]{:S(2)}, u32[]{:S(2)}) collective-permute-start(bf16[64,3584]{1,0:T(8,128)(2,1)S(1)} %collective-permute-done.30.refs_1_), channel_id=1, source_target_pairs={{0,4},{4,8},{8,12},{12,14},{14,10},{10,6},{6,2},{2,0},{1,3},{5,1},... | collective-permute-start | bytes 1376264 | tf_op jit(solution)/shard_map/ppermute | solution.py:126
  39.4 2.0 collective-permute-start.9
  44.6 2.8 %collective-permute-start.2 = (bf16[64,3584]{1,0:T(8,128)(2,1)S(1)}, bf16[64,3584]{1,0:T(8,128)(2,1)S(1)}, u32[]{:S(2)}, u32[]{:S(2)}) collective-permute-start(bf16[64,3584]{1,0:T(8,128)(2,1)S(1)} %collective-permute-done.1.refs_3_), channel_id=1, source_target_pairs={{0,4},{4,8},{8,12},{12,14},{14,10},{10,6},{6,2},{2,0},{1,3},{5,1},... | collective-permute-start | bytes 1376264 | tf_op jit(solution)/shard_map/ppermute | solution.py:126
  52.2 2.3 %collective-permute-done.9.refs_6_ = bf16[64,3584]{1,0:T(8,128)(2,1)} collective-permute-done((bf16[64,3584]{1,0:T(8,128)(2,1)S(1)}, bf16[64,3584]{1,0:T(8,128)(2,1)}, u32[]{:S(2)}, u32[]{:S(2)}) %collective-permute-start.9) | collective-permute-done | bytes 458784 | tf_op jit(solution)/shard_map/ppermute | solution.py:127
  54.5 2.8 %collective-permute-start.32 = (bf16[64,3584]{1,0:T(8,128)(2,1)}, bf16[64,3584]{1,0:T(8,128)(2,1)}, u32[]{:S(2)}, u32[]{:S(2)}) collective-permute-start(bf16[64,3584]{1,0:T(8,128)(2,1)} %collective-permute-done.31.refs_1_), channel_id=1, source_target_pairs={{0,4},{4,8},{8,12},{12,14},{14,10},{10,6},{6,2},{2,0},{1,3},{5,1},... | collective-permute-start | bytes 1376264 | tf_op jit(solution)/shard_map/ppermute | solution.py:126
  59.8 6.1 %all-to-all-start = ((bf16[16,32,128]{2,1,0:T(8,128)(2,1)}), bf16[16,32,128]{2,1,0:T(8,128)(2,1)S(1)}, u32[]{:S(2)}, u32[]{:S(2)}) async-start(bf16[16,32,128]{2,1,0:T(8,128)(2,1)} %pad_maximum_fusion), calls=%async_computation | async-start | bytes 262144 | tf_op jit(solution)/shard_map/all_to_all | solution.py:157
  66.6 2.0 collective-permute-start.10
  73.3 7.3 %collective-permute-done.10.refs_6_ = bf16[64,3584]{1,0:T(8,128)(2,1)} collective-permute-done((bf16[64,3584]{1,0:T(8,128)(2,1)}, bf16[64,3584]{1,0:T(8,128)(2,1)}, u32[]{:S(2)}, u32[]{:S(2)}) %collective-permute-start.10) | collective-permute-done | bytes 458784 | tf_op jit(solution)/shard_map/ppermute | solution.py:127
  80.6 2.6 %collective-permute-start.33 = (bf16[64,3584]{1,0:T(8,128)(2,1)}, bf16[64,3584]{1,0:T(8,128)(2,1)}, u32[]{:S(2)}, u32[]{:S(2)}) collective-permute-start(bf16[64,3584]{1,0:T(8,128)(2,1)} %collective-permute-done.32.refs_1_), channel_id=1, source_target_pairs={{0,4},{4,8},{8,12},{12,14},{14,10},{10,6},{6,2},{2,0},{1,3},{5,1},... | collective-permute-start | bytes 1376264 | tf_op jit(solution)/shard_map/ppermute | solution.py:126
  87.7 5.6 %grad_step.8 = (f32[256,3584]{1,0:T(8,128)}, bf16[256,256]{1,0:T(8,128)(2,1)S(1)}, f32[2,16,128]{2,1,0:T(8,128)S(1)}, f32[256,128]{1,0:T(8,128)S(1)}) custom-call(s32[4]{0:T(128)S(1)} %get-tuple-element.86.refs_0_, bf16[16,32,128]{2,1,0:T(8,128)(2,1)S(1)} %all-to-all-done.refs_1_, bf16[256,3584]{1,0:T(8,128)(2,1)S(1)} %copy-done, ...), custom_call_target="tpu_custom_call" | custom-call | flops 939524096 | bytes 11010048 | tf_op jit(solution)/shard_map/grad_step/pallas_call | solution.py:171
  94.0 2.0 input_step.8.refs_5_
  99.6 7.2 %grad_step.9 = (f32[256,3584]{1,0:T(8,128)}, bf16[256,256]{1,0:T(8,128)(2,1)S(1)}, f32[2,16,128]{2,1,0:T(8,128)S(1)}, f32[256,128]{1,0:T(8,128)S(1)}) custom-call(s32[4]{0:T(128)S(1)} %get-tuple-element.87.refs_0_, bf16[16,32,128]{2,1,0:T(8,128)(2,1)S(1)} %all-to-all-done.refs_1_, bf16[256,3584]{1,0:T(8,128)(2,1)S(1)} %copy-done, ...), custom_call_target="tpu_custom_call" | custom-call | flops 939524096 | bytes 11010048 | tf_op jit(solution)/shard_map/grad_step/pallas_call | solution.py:171
  109.7 4.2 %input_step.9.refs_5_ = f32[3584,256]{1,0:T(8,128)S(1)} custom-call(bf16[256,256]{1,0:T(8,128)(2,1)S(1)} %get-tuple-element.50.refs_0_, bf16[64,3584]{1,0:T(8,128)(2,1)S(1)} %copy-done.14, bf16[64,3584]{1,0:T(8,128)(2,1)S(1)} %copy-done.30, bf16[64,3584]{1,0:T(8,128)(2,1)S(1)} %copy-done.38, bf16[64,3584]{1,0:T(8,128)(2,1)S(1)} %copy-done.12, ...), custom_call_target="tpu_custom_call" | custom-call | flops 469762048 | bytes 9175040 | tf_op jit(solution)/shard_map/input_step/pallas_call | solution.py:210
  115.8 7.1 %grad_step.10 = (f32[256,3584]{1,0:T(8,128)}, bf16[256,256]{1,0:T(8,128)(2,1)S(1)}, f32[2,16,128]{2,1,0:T(8,128)S(1)}, f32[256,128]{1,0:T(8,128)S(1)}) custom-call(s32[4]{0:T(128)S(1)} %get-tuple-element.88.refs_0_, bf16[16,32,128]{2,1,0:T(8,128)(2,1)S(1)} %all-to-all-done.refs_1_, bf16[256,3584]{1,0:T(8,128)(2,1)S(1)} %copy-done, ...), custom_call_target="tpu_custom_call" | custom-call | flops 939524096 | bytes 11010048 | tf_op jit(solution)/shard_map/grad_step/pallas_call | solution.py:171
  123.6 4.7 %input_step.10.refs_5_ = f32[3584,256]{1,0:T(8,128)S(1)} custom-call(bf16[256,256]{1,0:T(8,128)(2,1)S(1)} %get-tuple-element.49.refs_0_, bf16[64,3584]{1,0:T(8,128)(2,1)} %collective-permute-done.31.refs_1_, bf16[64,3584]{1,0:T(8,128)(2,1)} %collective-permute-done.54.refs_2_, bf16[64,3584]{1,0:T(8,128)(2,1)} %collective-permute-done.55.refs_3_, ...), custom_call_target="tpu_custom_call" | custom-call | flops 469762048 | bytes 9175040 | tf_op jit(solution)/shard_map/input_step/pallas_call | solution.py:210
  134.1 7.4 %grad_step.11 = (f32[256,3584]{1,0:T(8,128)}, bf16[256,256]{1,0:T(8,128)(2,1)S(1)}, f32[2,16,128]{2,1,0:T(8,128)S(1)}, f32[256,128]{1,0:T(8,128)S(1)}) custom-call(s32[4]{0:T(128)S(1)} %get-tuple-element.89.refs_0_, bf16[16,32,128]{2,1,0:T(8,128)(2,1)S(1)} %all-to-all-done.refs_1_, bf16[256,3584]{1,0:T(8,128)(2,1)S(1)} %copy-done, ...), custom_call_target="tpu_custom_call" | custom-call | flops 939524096 | bytes 11010048 | tf_op jit(solution)/shard_map/grad_step/pallas_call | solution.py:171
  141.6 2.2 %collective-permute-done.12.refs_6_ = bf16[64,3584]{1,0:T(8,128)(2,1)S(1)} collective-permute-done((bf16[64,3584]{1,0:T(8,128)(2,1)}, bf16[64,3584]{1,0:T(8,128)(2,1)S(1)}, u32[]{:S(2)}, u32[]{:S(2)}) %collective-permute-start.12) | collective-permute-done | bytes 458784 | tf_op jit(solution)/shard_map/ppermute | solution.py:127
  145.8 4.4 %input_step.11.refs_5_ = f32[3584,256]{1,0:T(8,128)S(1)} custom-call(bf16[256,256]{1,0:T(8,128)(2,1)S(1)} %get-tuple-element.48.refs_0_, bf16[64,3584]{1,0:T(8,128)(2,1)} %collective-permute-done.32.refs_1_, bf16[64,3584]{1,0:T(8,128)(2,1)S(1)} %copy-done.44, bf16[64,3584]{1,0:T(8,128)(2,1)S(1)} %copy-done.46, ...), custom_call_target="tpu_custom_call" | custom-call | flops 469762048 | bytes 9175040 | tf_op jit(solution)/shard_map/input_step/pallas_call | solution.py:210
  152.1 7.7 %grad_step.12 = (f32[256,3584]{1,0:T(8,128)}, bf16[256,256]{1,0:T(8,128)(2,1)S(1)}, f32[2,16,128]{2,1,0:T(8,128)S(1)}, f32[256,128]{1,0:T(8,128)S(1)}) custom-call(s32[4]{0:T(128)S(1)} %get-tuple-element.90.refs_0_, bf16[16,32,128]{2,1,0:T(8,128)(2,1)S(1)} %all-to-all-done.refs_1_, bf16[256,3584]{1,0:T(8,128)(2,1)S(1)} %copy-done, ...), custom_call_target="tpu_custom_call" | custom-call | flops 939524096 | bytes 11010048 | tf_op jit(solution)/shard_map/grad_step/pallas_call | solution.py:171
  160.5 4.4 %input_step.12.refs_5_ = f32[3584,256]{1,0:T(8,128)S(1)} custom-call(bf16[256,256]{1,0:T(8,128)(2,1)S(1)} %get-tuple-element.47.refs_0_, bf16[64,3584]{1,0:T(8,128)(2,1)} %collective-permute-done.33.refs_1_, bf16[64,3584]{1,0:T(8,128)(2,1)S(1)} %collective-permute-done.50.refs_2_, bf16[64,3584]{1,0:T(8,128)(2,1)S(1)} %collective-permute-done.51.refs_3_, ...), custom_call_target="tpu_custom_call" | custom-call | flops 469762048 | bytes 9175040 | tf_op jit(solution)/shard_map/input_step/pallas_call | solution.py:210
  168.6 7.3 %grad_step.13 = (f32[256,3584]{1,0:T(8,128)}, bf16[256,256]{1,0:T(8,128)(2,1)S(1)}, f32[2,16,128]{2,1,0:T(8,128)S(1)}, f32[256,128]{1,0:T(8,128)S(1)}) custom-call(s32[4]{0:T(128)S(1)} %get-tuple-element.91.refs_0_, bf16[16,32,128]{2,1,0:T(8,128)(2,1)S(1)} %all-to-all-done.refs_1_, bf16[256,3584]{1,0:T(8,128)(2,1)S(1)} %copy-done, ...), custom_call_target="tpu_custom_call" | custom-call | flops 939524096 | bytes 11010048 | tf_op jit(solution)/shard_map/grad_step/pallas_call | solution.py:171
  179.2 7.1 %grad_step.14 = (f32[256,3584]{1,0:T(8,128)}, bf16[256,256]{1,0:T(8,128)(2,1)S(1)}, f32[2,16,128]{2,1,0:T(8,128)S(1)}, f32[256,128]{1,0:T(8,128)S(1)}) custom-call(s32[4]{0:T(128)S(1)} %get-tuple-element.92.refs_0_, bf16[16,32,128]{2,1,0:T(8,128)(2,1)S(1)} %all-to-all-done.refs_1_, bf16[256,3584]{1,0:T(8,128)(2,1)S(1)} %copy-done, ...), custom_call_target="tpu_custom_call" | custom-call | flops 939524096 | bytes 11010048 | tf_op jit(solution)/shard_map/grad_step/pallas_call | solution.py:171
  188.1 6.5 %grad_step.15 = (bf16[256,3584]{1,0:T(8,128)(2,1)}, bf16[256,256]{1,0:T(8,128)(2,1)S(1)}, f32[2,16,128]{2,1,0:T(8,128)S(1)}, f32[256,128]{1,0:T(8,128)S(1)}) custom-call(s32[4]{0:T(128)S(1)} %get-tuple-element.93.refs_0_, bf16[16,32,128]{2,1,0:T(8,128)(2,1)S(1)} %all-to-all-done.refs_1_, bf16[256,3584]{1,0:T(8,128)(2,1)S(1)} %copy-done, ...), custom_call_target="tpu_custom_call" | custom-call | flops 939524096 | bytes 11010048 | tf_op jit(solution)/shard_map/grad_step/pallas_call | solution.py:171
  199.1 3.5 %all-to-all-start.1 = ((f32[16,16,128]{2,1,0:T(8,128)}), f32[16,16,128]{2,1,0:T(8,128)S(1)}, u32[]{:S(2)}, u32[]{:S(2)}) async-start(f32[16,16,128]{2,1,0:T(8,128)} %bitcast.40), calls=%async_computation.1 | async-start | bytes 262144 | tf_op jit(solution)/shard_map/all_to_all | solution.py:201
  203.6 4.4 %input_step.13.refs_5_ = f32[3584,256]{1,0:T(8,128)S(1)} custom-call(bf16[256,256]{1,0:T(8,128)(2,1)S(1)} %get-tuple-element.46.refs_0_, bf16[64,3584]{1,0:T(8,128)(2,1)} %collective-permute-done.34.refs_1_, bf16[64,3584]{1,0:T(8,128)(2,1)S(1)} %copy-done.50, bf16[64,3584]{1,0:T(8,128)(2,1)} %collective-permute-done.49.refs_3_, ...), custom_call_target="tpu_custom_call" | custom-call | flops 469762048 | bytes 9175040 | tf_op jit(solution)/shard_map/input_step/pallas_call | solution.py:210
  209.9 4.7 %input_step.14.refs_5_ = f32[3584,256]{1,0:T(8,128)S(1)} custom-call(bf16[256,256]{1,0:T(8,128)(2,1)S(1)} %copy-done.52, bf16[64,3584]{1,0:T(8,128)(2,1)} %collective-permute-done.35.refs_1_, bf16[64,3584]{1,0:T(8,128)(2,1)} %collective-permute-done.46.refs_2_, bf16[64,3584]{1,0:T(8,128)(2,1)} %collective-permute-done.47.refs_3_, ...), custom_call_target="tpu_custom_call" | custom-call | flops 469762048 | bytes 9175040 | tf_op jit(solution)/shard_map/input_step/pallas_call | solution.py:210
  214.7 3.3 %input_step.15 = bf16[3584,256]{1,0:T(8,128)(2,1)} custom-call(bf16[256,256]{1,0:T(8,128)(2,1)S(1)} %copy-done.54, bf16[64,3584]{1,0:T(8,128)(2,1)S(1)} %collective-permute-done.36.refs_1_, bf16[64,3584]{1,0:T(8,128)(2,1)S(1)} %collective-permute-done.44.refs_2_, bf16[64,3584]{1,0:T(8,128)(2,1)S(1)} %collective-permute-done.45.refs_3_, ...), custom_call_target="tpu_custom_call" | custom-call | flops 469762048 | bytes 9175040 | tf_op jit(solution)/shard_map/input_step/pallas_call | solution.py:210
  (291 shorter events, 79.7 us)
Async XLA Ops:
  10.3 14.6 %collective-permute-start.37 = (bf16[64,3584]{1,0:T(8,128)(2,1)S(1)}, bf16[64,3584]{1,0:T(8,128)(2,1)S(1)}, u32[]{:S(2)}, u32[]{:S(2)}) collective-permute-start(bf16[64,3584]{1,0:T(8,128)(2,1)S(1)} %get-tuple-element.68.refs_4_), channel_id=1, source_target_pairs={{0,2},{4,0},{8,4},{12,8},{14,12},{10,14},{6,10},{2,6},{1,5},{5,9},... | collective-permute-start | bytes 1376264 | tf_op jit(solution)/shard_map/ppermute | solution.py:127
  29.4 15.3 %collective-permute-start.38 = (bf16[64,3584]{1,0:T(8,128)(2,1)S(1)}, bf16[64,3584]{1,0:T(8,128)(2,1)}, u32[]{:S(2)}, u32[]{:S(2)}) collective-permute-start(bf16[64,3584]{1,0:T(8,128)(2,1)S(1)} %collective-permute-done.37.refs_4_), channel_id=1, source_target_pairs={{0,2},{4,0},{8,4},{12,8},{14,12},{10,14},{6,10},{2,6},{1,5},{5,9},... | collective-permute-start | bytes 1376264 | tf_op jit(solution)/shard_map/ppermute | solution.py:127
  39.4 15.0 %collective-permute-start.9 = (bf16[64,3584]{1,0:T(8,128)(2,1)S(1)}, bf16[64,3584]{1,0:T(8,128)(2,1)}, u32[]{:S(2)}, u32[]{:S(2)}) collective-permute-start(bf16[64,3584]{1,0:T(8,128)(2,1)S(1)} %collective-permute-done.8.refs_6_), channel_id=1, source_target_pairs={{0,2},{4,0},{8,4},{12,8},{14,12},{10,14},{6,10},{2,6},{1,5},{5,9},... | collective-permute-start | bytes 1376264 | tf_op jit(solution)/shard_map/ppermute | solution.py:127
  48.6 18.0 %collective-permute-start.54 = (bf16[64,3584]{1,0:T(8,128)(2,1)}, bf16[64,3584]{1,0:T(8,128)(2,1)}, u32[]{:S(2)}, u32[]{:S(2)}) collective-permute-start(bf16[64,3584]{1,0:T(8,128)(2,1)} %collective-permute-done.38.refs_4_), channel_id=1, source_target_pairs={{0,1},{1,0},{2,3},{3,2},{4,5},{5,4},{6,7},{7,6},{8,9},{9,8},{10,11... | collective-permute-start | bytes 1376264 | tf_op jit(solution)/shard_map/ppermute | solution.py:129
  49.3 19.2 %collective-permute-start.39 = (bf16[64,3584]{1,0:T(8,128)(2,1)}, bf16[64,3584]{1,0:T(8,128)(2,1)}, u32[]{:S(2)}, u32[]{:S(2)}) collective-permute-start(bf16[64,3584]{1,0:T(8,128)(2,1)} %collective-permute-done.38.refs_4_), channel_id=1, source_target_pairs={{0,2},{4,0},{8,4},{12,8},{14,12},{10,14},{6,10},{2,6},{1,5},{5,9},... | collective-permute-start | bytes 1376264 | tf_op jit(solution)/shard_map/ppermute | solution.py:127
  52.0 16.6 %collective-permute-start.55 = (bf16[64,3584]{1,0:T(8,128)(2,1)}, bf16[64,3584]{1,0:T(8,128)(2,1)}, u32[]{:S(2)}, u32[]{:S(2)}) collective-permute-start(bf16[64,3584]{1,0:T(8,128)(2,1)} %collective-permute-done.31.refs_1_), channel_id=1, source_target_pairs={{0,1},{1,0},{2,3},{3,2},{4,5},{5,4},{6,7},{7,6},{8,9},{9,8},{10,11... | collective-permute-start | bytes 1376264 | tf_op jit(solution)/shard_map/ppermute | solution.py:128
  54.5 15.4 %collective-permute-start.32 = (bf16[64,3584]{1,0:T(8,128)(2,1)}, bf16[64,3584]{1,0:T(8,128)(2,1)}, u32[]{:S(2)}, u32[]{:S(2)}) collective-permute-start(bf16[64,3584]{1,0:T(8,128)(2,1)} %collective-permute-done.31.refs_1_), channel_id=1, source_target_pairs={{0,4},{4,8},{8,12},{12,14},{14,10},{10,6},{6,2},{2,0},{1,3},{5,1},... | collective-permute-start | bytes 1376264 | tf_op jit(solution)/shard_map/ppermute | solution.py:126
  59.8 25.8 %all-to-all-start = ((bf16[16,32,128]{2,1,0:T(8,128)(2,1)}), bf16[16,32,128]{2,1,0:T(8,128)(2,1)S(1)}, u32[]{:S(2)}, u32[]{:S(2)}) async-start(bf16[16,32,128]{2,1,0:T(8,128)(2,1)} %pad_maximum_fusion), calls=%async_computation | async-start | bytes 262144 | tf_op jit(solution)/shard_map/all_to_all | solution.py:157
  68.6 14.6 %collective-permute-start.3 = (bf16[64,3584]{1,0:T(8,128)(2,1)}, bf16[64,3584]{1,0:T(8,128)(2,1)}, u32[]{:S(2)}, u32[]{:S(2)}) collective-permute-start(bf16[64,3584]{1,0:T(8,128)(2,1)} %copy-done.25), channel_id=1, source_target_pairs={{0,4},{4,8},{8,12},{12,14},{14,10},{10,6},{6,2},{2,0},{1,3},{5,1},... | collective-permute-start | bytes 1376264 | tf_op jit(solution)/shard_map/ppermute | solution.py:126
  71.9 26.1 %collective-permute-start.40 = (bf16[64,3584]{1,0:T(8,128)(2,1)}, bf16[64,3584]{1,0:T(8,128)(2,1)}, u32[]{:S(2)}, u32[]{:S(2)}) collective-permute-start(bf16[64,3584]{1,0:T(8,128)(2,1)} %collective-permute-done.39.refs_4_), channel_id=1, source_target_pairs={{0,2},{4,0},{8,4},{12,8},{14,12},{10,14},{6,10},{2,6},{1,5},{5,9},... | collective-permute-start | bytes 1376264 | tf_op jit(solution)/shard_map/ppermute | solution.py:127
  80.6 18.7 %collective-permute-start.33 = (bf16[64,3584]{1,0:T(8,128)(2,1)}, bf16[64,3584]{1,0:T(8,128)(2,1)}, u32[]{:S(2)}, u32[]{:S(2)}) collective-permute-start(bf16[64,3584]{1,0:T(8,128)(2,1)} %collective-permute-done.32.refs_1_), channel_id=1, source_target_pairs={{0,4},{4,8},{8,12},{12,14},{14,10},{10,6},{6,2},{2,0},{1,3},{5,1},... | collective-permute-start | bytes 1376264 | tf_op jit(solution)/shard_map/ppermute | solution.py:126
  83.2 24.2 %collective-permute-start.20 = (bf16[64,3584]{1,0:T(8,128)(2,1)}, bf16[64,3584]{1,0:T(8,128)(2,1)}, u32[]{:S(2)}, u32[]{:S(2)}) collective-permute-start(bf16[64,3584]{1,0:T(8,128)(2,1)} %collective-permute-done.10.refs_6_), channel_id=1, source_target_pairs={{0,1},{1,0},{2,3},{3,2},{4,5},{5,4},{6,7},{7,6},{8,9},{9,8},{10,11... | collective-permute-start | bytes 1376264 | tf_op jit(solution)/shard_map/ppermute | solution.py:129
  84.0 24.9 %collective-permute-start.11 = (bf16[64,3584]{1,0:T(8,128)(2,1)}, bf16[64,3584]{1,0:T(8,128)(2,1)}, u32[]{:S(2)}, u32[]{:S(2)}) collective-permute-start(bf16[64,3584]{1,0:T(8,128)(2,1)} %collective-permute-done.10.refs_6_), channel_id=1, source_target_pairs={{0,2},{4,0},{8,4},{12,8},{14,12},{10,14},{6,10},{2,6},{1,5},{5,9},... | collective-permute-start | bytes 1376264 | tf_op jit(solution)/shard_map/ppermute | solution.py:127
  85.6 23.3 %collective-permute-start.21 = (bf16[64,3584]{1,0:T(8,128)(2,1)}, bf16[64,3584]{1,0:T(8,128)(2,1)}, u32[]{:S(2)}, u32[]{:S(2)}) collective-permute-start(bf16[64,3584]{1,0:T(8,128)(2,1)} %collective-permute-done.3.refs_3_), channel_id=1, source_target_pairs={{0,1},{1,0},{2,3},{3,2},{4,5},{5,4},{6,7},{7,6},{8,9},{9,8},{10,11... | collective-permute-start | bytes 1376264 | tf_op jit(solution)/shard_map/ppermute | solution.py:128
  97.9 32.3 %collective-permute-start.4 = (bf16[64,3584]{1,0:T(8,128)(2,1)}, bf16[64,3584]{1,0:T(8,128)(2,1)S(1)}, u32[]{:S(2)}, u32[]{:S(2)}) collective-permute-start(bf16[64,3584]{1,0:T(8,128)(2,1)} %collective-permute-done.3.refs_3_), channel_id=1, source_target_pairs={{0,4},{4,8},{8,12},{12,14},{14,10},{10,6},{6,2},{2,0},{1,3},{5,1},... | collective-permute-start | bytes 1376264 | tf_op jit(solution)/shard_map/ppermute | solution.py:126
  99.3 32.3 %collective-permute-start.50 = (bf16[64,3584]{1,0:T(8,128)(2,1)}, bf16[64,3584]{1,0:T(8,128)(2,1)S(1)}, u32[]{:S(2)}, u32[]{:S(2)}) collective-permute-start(bf16[64,3584]{1,0:T(8,128)(2,1)} %collective-permute-done.40.refs_4_), channel_id=1, source_target_pairs={{0,1},{1,0},{2,3},{3,2},{4,5},{5,4},{6,7},{7,6},{8,9},{9,8},{10,11... | collective-permute-start | bytes 1376264 | tf_op jit(solution)/shard_map/ppermute | solution.py:129
  107.4 24.9 %collective-permute-start.41 = (bf16[64,3584]{1,0:T(8,128)(2,1)}, bf16[64,3584]{1,0:T(8,128)(2,1)S(1)}, u32[]{:S(2)}, u32[]{:S(2)}) collective-permute-start(bf16[64,3584]{1,0:T(8,128)(2,1)} %collective-permute-done.40.refs_4_), channel_id=1, source_target_pairs={{0,2},{4,0},{8,4},{12,8},{14,12},{10,14},{6,10},{2,6},{1,5},{5,9},... | collective-permute-start | bytes 1376264 | tf_op jit(solution)/shard_map/ppermute | solution.py:127
  108.9 23.4 %collective-permute-start.51 = (bf16[64,3584]{1,0:T(8,128)(2,1)}, bf16[64,3584]{1,0:T(8,128)(2,1)S(1)}, u32[]{:S(2)}, u32[]{:S(2)}) collective-permute-start(bf16[64,3584]{1,0:T(8,128)(2,1)} %collective-permute-done.33.refs_1_), channel_id=1, source_target_pairs={{0,1},{1,0},{2,3},{3,2},{4,5},{5,4},{6,7},{7,6},{8,9},{9,8},{10,11... | collective-permute-start | bytes 1376264 | tf_op jit(solution)/shard_map/ppermute | solution.py:128
  108.9 23.9 %collective-permute-start.34 = (bf16[64,3584]{1,0:T(8,128)(2,1)}, bf16[64,3584]{1,0:T(8,128)(2,1)}, u32[]{:S(2)}, u32[]{:S(2)}) collective-permute-start(bf16[64,3584]{1,0:T(8,128)(2,1)} %collective-permute-done.33.refs_1_), channel_id=1, source_target_pairs={{0,4},{4,8},{8,12},{12,14},{14,10},{10,6},{6,2},{2,0},{1,3},{5,1},... | collective-permute-start | bytes 1376264 | tf_op jit(solution)/shard_map/ppermute | solution.py:126
  132.3 34.4 %collective-permute-start.18 = (bf16[64,3584]{1,0:T(8,128)(2,1)}, bf16[64,3584]{1,0:T(8,128)(2,1)S(1)}, u32[]{:S(2)}, u32[]{:S(2)}) collective-permute-start(bf16[64,3584]{1,0:T(8,128)(2,1)} %collective-permute-done.11.refs_6_), channel_id=1, source_target_pairs={{0,1},{1,0},{2,3},{3,2},{4,5},{5,4},{6,7},{7,6},{8,9},{9,8},{10,11... | collective-permute-start | bytes 1376264 | tf_op jit(solution)/shard_map/ppermute | solution.py:129
  132.3 35.8 %collective-permute-start.19 = (bf16[64,3584]{1,0:T(8,128)(2,1)S(1)}, bf16[64,3584]{1,0:T(8,128)(2,1)S(1)}, u32[]{:S(2)}, u32[]{:S(2)}) collective-permute-start(bf16[64,3584]{1,0:T(8,128)(2,1)S(1)} %collective-permute-done.4.refs_3_), channel_id=1, source_target_pairs={{0,1},{1,0},{2,3},{3,2},{4,5},{5,4},{6,7},{7,6},{8,9},{9,8},{10,11... | collective-permute-start | bytes 1376264 | tf_op jit(solution)/shard_map/ppermute | solution.py:128
  132.8 35.3 %collective-permute-start.42 = (bf16[64,3584]{1,0:T(8,128)(2,1)S(1)}, bf16[64,3584]{1,0:T(8,128)(2,1)}, u32[]{:S(2)}, u32[]{:S(2)}) collective-permute-start(bf16[64,3584]{1,0:T(8,128)(2,1)S(1)} %collective-permute-done.41.refs_4_), channel_id=1, source_target_pairs={{0,2},{4,0},{8,4},{12,8},{14,12},{10,14},{6,10},{2,6},{1,5},{5,9},... | collective-permute-start | bytes 1376264 | tf_op jit(solution)/shard_map/ppermute | solution.py:127
  143.8 32.8 %collective-permute-start.13 = (bf16[64,3584]{1,0:T(8,128)(2,1)S(1)}, bf16[64,3584]{1,0:T(8,128)(2,1)S(1)}, u32[]{:S(2)}, u32[]{:S(2)}) collective-permute-start(bf16[64,3584]{1,0:T(8,128)(2,1)S(1)} %collective-permute-done.12.refs_6_), channel_id=1, source_target_pairs={{0,2},{4,0},{8,4},{12,8},{14,12},{10,14},{6,10},{2,6},{1,5},{5,9},... | collective-permute-start | bytes 1376264 | tf_op jit(solution)/shard_map/ppermute | solution.py:127
  145.0 31.6 %collective-permute-start.6 = (bf16[64,3584]{1,0:T(8,128)(2,1)S(1)}, bf16[64,3584]{1,0:T(8,128)(2,1)S(1)}, u32[]{:S(2)}, u32[]{:S(2)}) collective-permute-start(bf16[64,3584]{1,0:T(8,128)(2,1)S(1)} %collective-permute-done.5.refs_3_), channel_id=1, source_target_pairs={{0,4},{4,8},{8,12},{12,14},{14,10},{10,6},{6,2},{2,0},{1,3},{5,1},... | collective-permute-start | bytes 1376264 | tf_op jit(solution)/shard_map/ppermute | solution.py:126
  177.1 18.8 %collective-permute-start.48 = (bf16[64,3584]{1,0:T(8,128)(2,1)S(1)}, bf16[64,3584]{1,0:T(8,128)(2,1)S(1)}, u32[]{:S(2)}, u32[]{:S(2)}) collective-permute-start(bf16[64,3584]{1,0:T(8,128)(2,1)S(1)} %collective-permute-done.41.refs_4_), channel_id=1, source_target_pairs={{0,1},{1,0},{2,3},{3,2},{4,5},{5,4},{6,7},{7,6},{8,9},{9,8},{10,11... | collective-permute-start | bytes 1376264 | tf_op jit(solution)/shard_map/ppermute | solution.py:129
  177.2 19.6 %collective-permute-start.43 = (bf16[64,3584]{1,0:T(8,128)(2,1)}, bf16[64,3584]{1,0:T(8,128)(2,1)S(1)}, u32[]{:S(2)}, u32[]{:S(2)}) collective-permute-start(bf16[64,3584]{1,0:T(8,128)(2,1)} %collective-permute-done.42.refs_4_), channel_id=1, source_target_pairs={{0,2},{4,0},{8,4},{12,8},{14,12},{10,14},{6,10},{2,6},{1,5},{5,9},... | collective-permute-start | bytes 1376264 | tf_op jit(solution)/shard_map/ppermute | solution.py:127
  177.8 19.4 %collective-permute-start.36 = (bf16[64,3584]{1,0:T(8,128)(2,1)}, bf16[64,3584]{1,0:T(8,128)(2,1)S(1)}, u32[]{:S(2)}, u32[]{:S(2)}) collective-permute-start(bf16[64,3584]{1,0:T(8,128)(2,1)} %collective-permute-done.35.refs_1_), channel_id=1, source_target_pairs={{0,4},{4,8},{8,12},{12,14},{14,10},{10,6},{6,2},{2,0},{1,3},{5,1},... | collective-permute-start | bytes 1376264 | tf_op jit(solution)/shard_map/ppermute | solution.py:126
  187.6 15.0 %collective-permute-start.49 = (bf16[64,3584]{1,0:T(8,128)(2,1)}, bf16[64,3584]{1,0:T(8,128)(2,1)}, u32[]{:S(2)}, u32[]{:S(2)}) collective-permute-start(bf16[64,3584]{1,0:T(8,128)(2,1)} %collective-permute-done.34.refs_1_), channel_id=1, source_target_pairs={{0,1},{1,0},{2,3},{3,2},{4,5},{5,4},{6,7},{7,6},{8,9},{9,8},{10,11... | collective-permute-start | bytes 1376264 | tf_op jit(solution)/shard_map/ppermute | solution.py:128
  187.6 22.3 %collective-permute-start.46 = (bf16[64,3584]{1,0:T(8,128)(2,1)}, bf16[64,3584]{1,0:T(8,128)(2,1)}, u32[]{:S(2)}, u32[]{:S(2)}) collective-permute-start(bf16[64,3584]{1,0:T(8,128)(2,1)} %collective-permute-done.42.refs_4_), channel_id=1, source_target_pairs={{0,1},{1,0},{2,3},{3,2},{4,5},{5,4},{6,7},{7,6},{8,9},{9,8},{10,11... | collective-permute-start | bytes 1376264 | tf_op jit(solution)/shard_map/ppermute | solution.py:129
  196.7 17.9 %collective-permute-start.44 = (bf16[64,3584]{1,0:T(8,128)(2,1)S(1)}, bf16[64,3584]{1,0:T(8,128)(2,1)S(1)}, u32[]{:S(2)}, u32[]{:S(2)}) collective-permute-start(bf16[64,3584]{1,0:T(8,128)(2,1)S(1)} %collective-permute-done.43.refs_4_), channel_id=1, source_target_pairs={{0,1},{1,0},{2,3},{3,2},{4,5},{5,4},{6,7},{7,6},{8,9},{9,8},{10,11... | collective-permute-start | bytes 1376264 | tf_op jit(solution)/shard_map/ppermute | solution.py:129
  197.2 17.5 %collective-permute-start.45 = (bf16[64,3584]{1,0:T(8,128)(2,1)S(1)}, bf16[64,3584]{1,0:T(8,128)(2,1)S(1)}, u32[]{:S(2)}, u32[]{:S(2)}) collective-permute-start(bf16[64,3584]{1,0:T(8,128)(2,1)S(1)} %collective-permute-done.36.refs_1_), channel_id=1, source_target_pairs={{0,1},{1,0},{2,3},{3,2},{4,5},{5,4},{6,7},{7,6},{8,9},{9,8},{10,11... | collective-permute-start | bytes 1376264 | tf_op jit(solution)/shard_map/ppermute | solution.py:128
  199.1 19.7 %all-to-all-start.1 = ((f32[16,16,128]{2,1,0:T(8,128)}), f32[16,16,128]{2,1,0:T(8,128)S(1)}, u32[]{:S(2)}, u32[]{:S(2)}) async-start(f32[16,16,128]{2,1,0:T(8,128)} %bitcast.40), calls=%async_computation.1 | async-start | bytes 262144 | tf_op jit(solution)/shard_map/all_to_all | solution.py:201
  (105 other events, 830.4 us)

commit v3 on v1

v3 whole, which is shorter than its diff:
```python
import functools

import jax
import jax.numpy as jnp
import numpy as np
from jax import lax
from jax.experimental import pallas as pl
from jax.experimental.pallas import tpu as pltpu
from jax.sharding import PartitionSpec as P

BLOCK = 128
PART_BYTES = 9 << 20
HELD_BYTES = 1 << 25
RING_BYTES = 1 << 26
VMEM_BYTES = 20 << 20


def ring_tables(peer_count):
    chips = peer_count // 2
    ring = [chip for chip in range(chips) if chip % 2 == 0] + [chip for chip in reversed(range(chips)) if chip % 2]
    place = {chip: spot for spot, chip in enumerate(ring)}
    sources = np.zeros((peer_count, chips, 2), np.int32)
    spot_of = np.zeros((peer_count, peer_count), np.int32)
    for device in range(peer_count):
        chip, core = divmod(device, 2)
        for step in range(chips):
            hop = (step + 1) // 2
            other = ring[(place[chip] + (-hop if step % 2 else hop)) % chips]
            sources[device, step] = (2 * other + core, 2 * other + 1 - core)
            spot_of[device, 2 * other + core] = 2 * step
            spot_of[device, 2 * other + 1 - core] = 2 * step + 1
    up = [(2 * ring[i] + c, 2 * ring[(i + 1) % chips] + c) for i in range(chips) for c in range(2)]
    down = [(b, a) for a, b in up]
    swap = [(i, i ^ 1) for i in range(peer_count)]
    return sources, spot_of, up, down, swap


def product_kernel(per_block, order_ref, meta_ref, decoder_ref, mine_ref, theirs_ref, acts_ref, pre_ref, lat_ref, bias_ref):
    latents, width = decoder_ref.shape
    tokens = mine_ref.shape[0]
    span = 512 if width % 512 == 0 else BLOCK
    products = jnp.zeros((latents, 2 * tokens), jnp.float32)
    for at in range(0, width, span):
        rows = jnp.concatenate([mine_ref[:, at : at + span], theirs_ref[:, at : at + span]], axis=0)
        products += lax.dot_general(
            decoder_ref[:, at : at + span], rows, (((1,), (1,)), ((), ())), preferred_element_type=jnp.float32
        )
    row = lax.broadcasted_iota(jnp.int32, (8, tokens), 0)
    for tile in range(2):
        meta = meta_ref[order_ref[tile]].astype(jnp.float32)
        columns = [jnp.broadcast_to(meta[k : k + 1], (8, tokens)).astype(jnp.int32) for k in range(per_block)]
        values = [jnp.broadcast_to(meta[per_block + k : per_block + k + 1], (8, tokens)) for k in range(per_block)]
        sums = [jnp.zeros((8, tokens), jnp.float32) for _ in range(per_block)]
        at = slice(tile * tokens, (tile + 1) * tokens)
        for block in range(0, latents, 16):
            kept_both, dense_both = [], []
            for base in (block, block + 8):
                here = products[base : base + 8, at]
                kept = jnp.zeros((8, tokens), jnp.float32)
                dense = jnp.zeros((8, tokens), jnp.float32)
                for k in range(per_block):
                    hit = columns[k] == row + base
                    picked = jnp.where(hit, here, 0.0)
                    sums[k] = sums[k] + picked
                    kept = kept + picked
                    dense = jnp.where(hit, values[k], dense)
                if tile == 0:
                    bias_ref[base : base + 8, :] = kept
                else:
                    bias_ref[base : base + 8, :] += kept
                kept_both.append(kept)
                dense_both.append(dense)
            pre_ref[block : block + 16, at] = jnp.concatenate(kept_both, axis=0).astype(jnp.bfloat16)
            acts_ref[block : block + 16, at] = jnp.concatenate(dense_both, axis=0).astype(jnp.bfloat16)
        for k in range(per_block):
            lat_ref[tile, k : k + 1, :] = jnp.sum(sums[k], axis=0, keepdims=True)


def decoder_kernel(steps, *refs):
    acts, rows, out_ref = refs[:steps], refs[steps : 3 * steps], refs[3 * steps]
    total = jnp.zeros(out_ref.shape, jnp.float32)
    for s in range(steps):
        both = jnp.concatenate([rows[2 * s][...], rows[2 * s + 1][...]], axis=0)
        total += jnp.dot(acts[s][...], both, preferred_element_type=jnp.float32)
    out_ref[...] = total.astype(out_ref.dtype)


def encoder_kernel(steps, *refs):
    pres, rows, refs = refs[:steps], refs[steps : 3 * steps], refs[3 * steps :]
    out_ref = refs[-1]
    total = refs[0][...] if len(refs) == 2 else jnp.zeros(out_ref.shape, jnp.float32)
    for s in range(steps):
        both = jnp.concatenate([rows[2 * s][...], rows[2 * s + 1][...]], axis=0)
        total += lax.dot_general(both, pres[s][...], (((0,), (1,)), ((), ())), preferred_element_type=jnp.float32)
    out_ref[...] = total.astype(out_ref.dtype)


def after(value, *others):
    return lax.optimization_barrier((value, *others))[0]


def by_ring(grad_recon, inputs, decoder, owners, local_blocks, offsets, act_values):
    token_count, width = grad_recon.shape
    block_count = owners.shape[1]
    per_block = offsets.shape[2]
    latent_count = decoder.shape[0]
    peer_count = lax.axis_size("lat")
    chips = peer_count // 2
    me = lax.axis_index("lat")
    sources, spot_of, up, down, swap = ring_tables(peer_count)
    order = jnp.asarray(sources)[me]
    spots = jnp.asarray(spot_of)[me]

    own_t = owners.T
    columns_t = (local_blocks.T[:, None, :] * BLOCK + offsets.transpose(1, 2, 0)).astype(jnp.float32)
    values_t = act_values.transpose(1, 2, 0).astype(jnp.float32)
    peers = jnp.arange(peer_count, dtype=jnp.int32)
    sent_columns = jnp.full((peer_count, per_block, token_count), -1.0, jnp.float32)
    sent_values = jnp.zeros((peer_count, per_block, token_count), jnp.float32)
    for i in range(block_count):
        named = own_t[i][None, None, :] == peers[:, None, None]
        sent_columns = jnp.where(named, columns_t[i][None], sent_columns)
        sent_values = jnp.where(named, values_t[i][None], sent_values)
    meta = jnp.concatenate([sent_columns, sent_values], axis=1).astype(jnp.bfloat16)
    meta = lax.all_to_all(meta, "lat", split_axis=0, concat_axis=0, tiled=True)

    whole = pl.BlockSpec(memory_space=pltpu.VMEM)
    scalars = pl.BlockSpec(memory_space=pltpu.SMEM)
    step_tokens = 2 * token_count
    work = 2 * latent_count * width * step_tokens
    params = pltpu.CompilerParams(vmem_limit_bytes=VMEM_BYTES)

    def products(step, rows):
        return pl.pallas_call(
            functools.partial(product_kernel, per_block),
            in_specs=[scalars] + [whole] * 4,
            out_specs=[whole] * 4,
            out_shape=[
                jax.ShapeDtypeStruct((latent_count, step_tokens), jnp.bfloat16),
                jax.ShapeDtypeStruct((latent_count, step_tokens), jnp.bfloat16),
                jax.ShapeDtypeStruct((2, per_block, token_count), jnp.float32),
                jax.ShapeDtypeStruct((latent_count, token_count), jnp.float32),
            ],
            compiler_params=params,
            cost_estimate=pl.CostEstimate(flops=work, bytes_accessed=2 * step_tokens * width, transcendentals=0),
            name="products",
        )(order[step], meta, decoder, *rows)

    span = 512 if width % 512 == 0 else BLOCK
    rows_block = pl.BlockSpec((token_count, span), lambda i: (0, i))

    def decoder_sum(acts, rows):
        return pl.pallas_call(
            functools.partial(decoder_kernel, len(acts)),
            grid=(width // span,),
            in_specs=[whole] * len(acts) + [rows_block] * (2 * len(acts)),
            out_specs=pl.BlockSpec((latent_count, span), lambda i: (0, i)),
            out_shape=jax.ShapeDtypeStruct((latent_count, width), jnp.bfloat16),
            compiler_params=params,
            cost_estimate=pl.CostEstimate(
                flops=work * len(acts), bytes_accessed=2 * len(acts) * step_tokens * width, transcendentals=0
            ),
            name="decoder_sum",
        )(*acts, *[part for pair in rows for part in pair])

    def encoder_sum(pres, rows, total, dtype):
        block = pl.BlockSpec((span, latent_count), lambda i: (i, 0))
        totals = [] if total is None else [total]
        return pl.pallas_call(
            functools.partial(encoder_kernel, len(pres)),
            grid=(width // span,),
            in_specs=[whole] * len(pres) + [rows_block] * (2 * len(pres)) + [block] * len(totals),
            out_specs=block,
            out_shape=jax.ShapeDtypeStruct((width, latent_count), dtype),
            compiler_params=params,
            cost_estimate=pl.CostEstimate(
                flops=work * len(pres), bytes_accessed=2 * len(pres) * step_tokens * width, transcendentals=0
            ),
            name="encoder_sum",
        )(*pres, *[part for pair in rows for part in pair], *totals)

    def other(rows):
        return lax.ppermute(rows, "lat", swap)

    grads, ins, done = [None] * chips, [None] * chips, [None] * chips
    held = {("g", True): grad_recon, ("g", False): grad_recon, ("i", True): inputs, ("i", False): inputs}

    def hop(kind, number, *first):
        for upward in (True, False):
            step = 2 * number - 1 if upward else 2 * number
            antipode = 2 * number == chips
            if antipode and upward != (kind == "g"):
                continue
            rows = held[kind, upward]
            if first:
                rows = after(rows, *first)
            rows = lax.ppermute(rows, "lat", up if upward else down)
            held[kind, upward] = rows
            (grads if kind == "g" else ins)[chips - 1 if antipode else step] = (rows, other(rows))

    def compute(*steps):
        for step in steps:
            done[step] = products(step, grads[step])

    hops = chips // 2
    grads[0] = (grad_recon, other(grad_recon))
    ins[0] = (inputs, other(inputs))
    hop("g", 1)
    hop("i", 1)
    compute(0)
    for number in range(2, hops + 1):
        earlier = [done[step][3] for step in range(max(0, 2 * number - 5), 2 * number - 3)]
        hop("g", number, *earlier)
        compute(2 * number - 3, 2 * number - 2)
        if number < hops:
            hop("i", number, *earlier)
    compute(chips - 1)
    hop("i", hops, done[chips - 2][3])
    acts, pres, lats, biases = zip(*done)

    lat = jnp.concatenate(lats, axis=0)[spots]
    returned = lax.all_to_all(lat, "lat", split_axis=0, concat_axis=0, tiled=True)
    latent_grads = pick_returned(returned, own_t)
    decoder_grad = decoder_sum(acts, grads)
    bias_grad = jnp.sum(functools.reduce(jnp.add, biases), axis=1)

    early = [0] + list(range(1, chips - 3)) + [chips - 2]
    late = [chips - 3, chips - 1]
    total = encoder_sum([pres[s] for s in early], [ins[s] for s in early], None, jnp.float32)
    encoder_grad = encoder_sum([pres[s] for s in late], [ins[s] for s in late], total, jnp.bfloat16)
    return (decoder_grad, encoder_grad, bias_grad, latent_grads)


def pick_returned(returned, own_t):
    owner_id = jnp.arange(returned.shape[0], dtype=jnp.int32)[:, None, None, None]
    picked = jnp.where(own_t[None, :, None, :] == owner_id, returned[:, None, :, :], 0.0)
    return jnp.sum(picked, axis=0).reshape(-1, own_t.shape[1]).T


def build_kernel(block_count, per_block, me_ref, meta_ref, acts_ref, cols_ref):
    pairs = block_count * per_block
    meta = meta_ref[0].astype(jnp.float32)
    me = me_ref[0].astype(jnp.float32)
    tokens = meta.shape[1]
    values = jnp.zeros((per_block, tokens), jnp.float32)
    columns = jnp.full((per_block, tokens), -1.0, jnp.float32)
    for i in range(block_count):
        mine = meta[2 * pairs + i : 2 * pairs + i + 1] == me
        values = jnp.where(mine, meta[i * per_block : (i + 1) * per_block], values)
        columns = jnp.where(mine, meta[pairs + i * per_block : pairs + (i + 1) * per_block], columns)
    columns = columns.astype(jnp.int32)
    cols_ref[0] = columns
    row = lax.broadcasted_iota(jnp.int32, (acts_ref.shape[0], tokens), 0)
    dense = jnp.zeros(row.shape, jnp.float32)
    for k in range(per_block):
        dense = jnp.where(row == columns[k : k + 1], values[k : k + 1], dense)
    acts_ref[...] = dense.astype(jnp.bfloat16)


def mask_kernel(per_block, products_ref, cols_ref, pre_ref, lat_ref, bias_ref):
    products = products_ref[...]
    columns = cols_ref[0]
    row = lax.broadcasted_iota(jnp.int32, products.shape, 0)
    kept = jnp.zeros(products.shape, jnp.float32)
    for k in range(per_block):
        picked = jnp.where(row == columns[k : k + 1], products, 0.0)
        lat_ref[0, k : k + 1, :] = jnp.sum(picked, axis=0, keepdims=True)
        kept = kept + picked
    pre_ref[...] = kept.astype(jnp.bfloat16)

    @pl.when(pl.program_id(0) == 0)
    def _():
        bias_ref[...] = jnp.zeros_like(bias_ref)

    bias_ref[...] += kept


def column_parts(width, row_count):
    lanes = width // BLOCK
    for parts in range(2, lanes + 1):
        if lanes % parts == 0 and row_count * (width // parts) * 2 <= PART_BYTES:
            return parts
    return lanes


def by_gather(grad_recon, inputs, decoder, owners, local_blocks, offsets, act_values):
    token_count, width = grad_recon.shape
    block_count = owners.shape[1]
    per_block = offsets.shape[2]
    latent_count = decoder.shape[0]
    peer_count = lax.axis_size("lat")
    pairs = block_count * per_block
    row_count = peer_count * token_count
    me = lax.axis_index("lat").astype(jnp.int32).reshape(1)

    own_t = owners.T
    columns_t = (local_blocks.T[:, None, :] * BLOCK + offsets.transpose(1, 2, 0)).reshape(pairs, token_count)
    acts_t = act_values.transpose(1, 2, 0).reshape(pairs, token_count)
    filler = jnp.zeros((-block_count % 16, token_count), jnp.bfloat16)
    meta = jnp.concatenate([acts_t, columns_t.astype(jnp.bfloat16), own_t.astype(jnp.bfloat16), filler], axis=0)
    meta_all = lax.all_gather(meta, "lat", axis=0)

    parts = column_parts(width, row_count)
    span = width // parts
    depth = max(1, HELD_BYTES // (row_count * span * 2))

    def gathered(rows, p, done):
        piece = rows[:, p * span : (p + 1) * span]
        if len(done) >= depth:
            piece, _ = lax.optimization_barrier((piece, done[-depth]))
        return lax.all_gather(piece, "lat", axis=0, tiled=True)

    tile = pl.BlockSpec((latent_count, token_count), lambda s: (0, s))
    picks = pl.BlockSpec((1, per_block, token_count), lambda s: (s, 0, 0))
    acts_dense, cols = pl.pallas_call(
        functools.partial(build_kernel, block_count, per_block),
        grid=(peer_count,),
        in_specs=[
            pl.BlockSpec(memory_space=pltpu.SMEM),
            pl.BlockSpec((1, meta.shape[0], token_count), lambda s: (s, 0, 0)),
        ],
        out_specs=[tile, picks],
        out_shape=[
            jax.ShapeDtypeStruct((latent_count, row_count), jnp.bfloat16),
            jax.ShapeDtypeStruct((peer_count, per_block, token_count), jnp.int32),
        ],
        name="build",
    )(me, meta_all)

    products = None
    decoder_parts = []
    for p in range(parts):
        rows = gathered(grad_recon, p, decoder_parts)
        part = lax.dot_general(
            acts_dense, rows, (((1,), (0,)), ((), ())), preferred_element_type=jnp.float32
        ).astype(jnp.bfloat16)
        term = lax.dot_general(
            decoder[:, p * span : (p + 1) * span], rows, (((1,), (1,)), ((), ())), preferred_element_type=jnp.float32
        )
        products = term if products is None else products + term
        if depth < 2 * parts:
            part, products = lax.optimization_barrier((part, products))
        decoder_parts.append(part)
    decoder_grad = jnp.concatenate(decoder_parts, axis=1)

    pre_grads, lat, bias_lanes = pl.pallas_call(
        functools.partial(mask_kernel, per_block),
        grid=(peer_count,),
        in_specs=[tile, picks],
        out_specs=[tile, picks, pl.BlockSpec((latent_count, token_count), lambda s: (0, 0))],
        out_shape=[
            jax.ShapeDtypeStruct((latent_count, row_count), jnp.bfloat16),
            jax.ShapeDtypeStruct((peer_count, per_block, token_count), jnp.float32),
            jax.ShapeDtypeStruct((latent_count, token_count), jnp.float32),
        ],
        name="mask",
    )(products, cols)
    bias_grad = jnp.sum(bias_lanes, axis=1)
    returned = lax.all_to_all(lat, "lat", split_axis=0, concat_axis=0, tiled=True)
    latent_grads = pick_returned(returned, own_t)

    encoder_parts = []
    for p in range(parts):
        rows = gathered(inputs, p, decoder_parts + encoder_parts)
        encoder_parts.append(
            lax.dot_general(rows, pre_grads, (((0,), (1,)), ((), ())), preferred_element_type=jnp.float32).astype(
                jnp.bfloat16
            )
        )
    return (decoder_grad, jnp.concatenate(encoder_parts, axis=0), bias_grad, latent_grads)


def per_device(grad_recon, *others):
    row_bytes = lax.axis_size("lat") * grad_recon.size * grad_recon.dtype.itemsize
    way = by_ring if 2 * row_bytes <= RING_BYTES and lax.axis_size("lat") % 4 == 0 else by_gather
    return way(grad_recon, *others)


def solution(mesh):
    rows = P(("groups", "lat"), None)
    entries = P(("groups", "lat"), None, None)
    return jax.shard_map(
        per_device,
        mesh=mesh,
        in_specs=(rows, rows, P("lat", None), rows, rows, entries, entries),
        out_specs=(rows, P(None, ("groups", "lat")), P(("groups", "lat")), rows),
        check_vma=False,
    )
```

time: 309 us -> 222 us (0.72)
  waiting for transfers between devices: 196 us -> 110 us
  matrix products: 34.3 us -> 0 us
  local copies, waits for them, and re-layouts: 6.82 us -> 36.6 us
  blocking collectives: 27.8 us -> 0 us
  starting transfers between devices: 3.86 us -> 27.8 us
  Pallas kernels: 21.7 us -> 39.3 us
  between operations: 13.9 us -> 1.15 us
    all_gather x4 -> x0, waiting for transfers between devices: 195 us -> none  [gathered(): return lax.all_gather(piece, 'lat', axis=0, tiled=True)]
    ppermute x0 -> x30, waiting for transfers between devices: none -> 93.5 us  [the longest x14 93.5 us: hop(): rows = lax.ppermute(rows, 'lat', up if upward else down)]
    dot_general x6 -> x0, matrix products: 34.3 us -> none  [the longest x2 13.6 us: per_device(): lax.dot_general(decoder[:, p * span:(p + 1) * span], rows, (((1,), (1,)),...]
    unnamed x17 -> x121, local copies, waits for them, and re-layouts: 2.3 us -> 31.6 us
    all_gather x1 -> x0, blocking collectives: 27.8 us -> none  [per_device(): meta_all = lax.all_gather(meta, 'lat', axis=0)]
    pallas_call x2 -> x11, Pallas kernels: 21.7 us -> 39.3 us  [the longest x8 17.9 us: products(): pl.pallas_call(functools.partial(product_kernel, per_block), in_specs=[sc...]
    ppermute x0 -> x30, starting transfers between devices: none -> 17.2 us  [the longest x14 14.4 us: hop(): rows = lax.ppermute(rows, 'lat', up if upward else down)]
    all_to_all x1 -> x2, waiting for transfers between devices: 0.01 us -> 16.4 us  [the longest x1 16.4 us: by_ring(): meta = lax.all_to_all(meta, 'lat', split_axis=0, concat_axis=0, tiled=True)]
  transfers between devices with their start and end apart: 5 -> 32, of which waited for: 4 -> 8; matrix products, arithmetic and copies ran while one was open for 13% -> 7% of each run, Pallas kernels for 7% -> 15%
where the time goes in v3:
time: 222 us; the launch traced here: 221 us
  waiting for transfers between devices  110 us (50%)
  Pallas kernels  39.3 us (18%)
  local copies, waits for them, and re-layouts  36.6 us (16%)
  starting transfers between devices  27.8 us (13%)
  other arithmetic  5.93 us (3%)
    ppermute x14, waiting for transfers between devices, hop(): rows = lax.ppermute(rows, 'lat', up if upward else down)  93.5 us
    unnamed x121, local copies, waits for them, and re-layouts  31.6 us
    pallas_call x8, Pallas kernels, products(): pl.pallas_call(functools.partial(product_kernel, per_block), in_specs=[sc...  17.9 us
    all_to_all x1, waiting for transfers between devices, by_ring(): meta = lax.all_to_all(meta, 'lat', split_axis=0, concat_axis=0, tiled=True)  16.4 us
    ppermute x14, starting transfers between devices, hop(): rows = lax.ppermute(rows, 'lat', up if upward else down)  14.4 us
    pallas_call x2, Pallas kernels, encoder_sum(): pl.pallas_call(functools.partial(encoder_kernel, len(pres)), grid=(width...  13.3 us
    pallas_call x1, Pallas kernels, decoder_sum(): pl.pallas_call(functools.partial(decoder_kernel, len(acts)), grid=(width...  8.03 us
    all_to_all x1, starting transfers between devices, by_ring(): meta = lax.all_to_all(meta, 'lat', split_axis=0, concat_axis=0, tiled=True)  6.48 us
  transfers between devices with their start and end apart: 32, of which 8 were waited for; matrix products, arithmetic and copies ran while one was open for 7% of the time, Pallas kernels for 15%

profile of v3, /device:TPU:0, one launch (start us, length us, event | category | flops | bytes accessed | tf_op | source)
XLA Modules:
  0.0 220.7 jit_solution(12592078913830737127)
XLA Ops:
  1.1 2.6 %collective-permute-start.1 = (bf16[128,3584]{1,0:T(8,128)(2,1)}, bf16[128,3584]{1,0:T(8,128)(2,1)S(1)}, u32[]{:S(2)}, u32[]{:S(2)}) collective-permute-start(bf16[128,3584]{1,0:T(8,128)(2,1)} %refs_8_.1), channel_id=1, source_target_pairs={{0,4},{1,5},{4,8},{5,9},{8,12},{9,13},{12,14},{13,15},{14,10},{15,... | collective-permute-start | bytes 2752520 | tf_op jit(solution)/shard_map/ppermute | solution.py:197
  3.8 2.0 collective-permute-start.15
  8.9 16.3 %collective-permute-done.1.mine_ref.refs_10_ = bf16[128,3584]{1,0:T(8,128)(2,1)S(1)} collective-permute-done((bf16[128,3584]{1,0:T(8,128)(2,1)}, bf16[128,3584]{1,0:T(8,128)(2,1)S(1)}, u32[]{:S(2)}, u32[]{:S(2)}) %collective-permute-start.1) | collective-permute-done | bytes 917536 | tf_op jit(solution)/shard_map/ppermute | solution.py:197
  25.9 6.5 %all-to-all-start = ((bf16[16,32,128]{2,1,0:T(8,128)(2,1)}), bf16[16,32,128]{2,1,0:T(8,128)(2,1)S(1)}, u32[]{:S(2)}, u32[]{:S(2)}) async-start(bf16[16,32,128]{2,1,0:T(8,128)(2,1)} %pad_maximum_fusion), calls=%async_computation | async-start | bytes 262144 | tf_op jit(solution)/shard_map/all_to_all | solution.py:125
  33.5 16.4 %all-to-all-done.meta_ref = bf16[16,32,128]{2,1,0:T(8,128)(2,1)S(1)} async-done(((bf16[16,32,128]{2,1,0:T(8,128)(2,1)}), bf16[16,32,128]{2,1,0:T(8,128)(2,1)S(1)}, u32[]{:S(2)}, u32[]{:S(2)}) %all-to-all-start) | async-done | bytes 131104 | tf_op jit(solution)/shard_map/all_to_all | solution.py:125
  49.8 1.5 copy-done
  52.5 2.0 products.8
  55.4 1.9 collective-permute-start.7
  57.5 1.9 collective-permute-start.20
  59.4 19.1 %collective-permute-done.5.mine_ref.refs_14_ = bf16[128,3584]{1,0:T(8,128)(2,1)S(1)} collective-permute-done((bf16[128,3584]{1,0:T(8,128)(2,1)S(1)}, bf16[128,3584]{1,0:T(8,128)(2,1)S(1)}, u32[]{:S(2)}, u32[]{:S(2)}) %collective-permute-start.5) | collective-permute-done | bytes 917536 | tf_op jit(solution)/shard_map/ppermute | solution.py:197
  78.4 3.0 %products.9 = (bf16[256,256]{1,0:T(8,128)(2,1)S(1)}, bf16[256,256]{1,0:T(8,128)(2,1)S(1)}, f32[2,16,128]{2,1,0:T(8,128)S(1)}, f32[256,128]{1,0:T(8,128)S(1)}) custom-call(s32[2]{0:T(128)S(1)} %get-tuple-element.104.order_ref, bf16[16,32,128]{2,1,0:T(8,128)(2,1)S(1)} %all-to-all-done.meta_ref, bf16[256,3584]{1,0:T(8,128)(2,1)S(1)} %copy-done.1, ...), custom_call_target="tpu_custom_call" | custom-call | flops 469762048 | bytes 1835008 | tf_op jit(solution)/shard_map/products/pallas_call | solution.py:134
  81.5 2.7 %products.10 = (bf16[256,256]{1,0:T(8,128)(2,1)S(1)}, bf16[256,256]{1,0:T(8,128)(2,1)S(1)}, f32[2,16,128]{2,1,0:T(8,128)S(1)}, f32[256,128]{1,0:T(8,128)S(1)}) custom-call(s32[2]{0:T(128)S(1)} %get-tuple-element.103.order_ref, bf16[16,32,128]{2,1,0:T(8,128)(2,1)S(1)} %all-to-all-done.meta_ref, bf16[256,3584]{1,0:T(8,128)(2,1)S(1)} %copy-done.1, ...), custom_call_target="tpu_custom_call" | custom-call | flops 469762048 | bytes 1835008 | tf_op jit(solution)/shard_map/products/pallas_call | solution.py:134
  84.8 12.3 %collective-permute-done.16.refs_12_ = bf16[128,3584]{1,0:T(8,128)(2,1)S(1)} collective-permute-done((bf16[128,3584]{1,0:T(8,128)(2,1)}, bf16[128,3584]{1,0:T(8,128)(2,1)S(1)}, u32[]{:S(2)}, u32[]{:S(2)}) %collective-permute-start.16) | collective-permute-done | bytes 917536 | tf_op jit(solution)/shard_map/ppermute | solution.py:197
  97.2 1.3 collective-permute-start.11
  100.0 1.3 collective-permute-start.21
  101.3 19.1 %collective-permute-done.11.mine_ref.refs_20_ = bf16[128,3584]{1,0:T(8,128)(2,1)S(1)} collective-permute-done((bf16[128,3584]{1,0:T(8,128)(2,1)S(1)}, bf16[128,3584]{1,0:T(8,128)(2,1)S(1)}, u32[]{:S(2)}, u32[]{:S(2)}) %collective-permute-start.11) | collective-permute-done | bytes 917536 | tf_op jit(solution)/shard_map/ppermute | solution.py:197
  120.5 1.3 collective-permute-done.9.mine_ref.refs_18_
  121.8 2.0 products.11
  124.5 2.0 products.12
  127.9 13.6 %collective-permute-done.17.refs_2_ = bf16[128,3584]{1,0:T(8,128)(2,1)} collective-permute-done((bf16[128,3584]{1,0:T(8,128)(2,1)S(1)}, bf16[128,3584]{1,0:T(8,128)(2,1)}, u32[]{:S(2)}, u32[]{:S(2)}) %collective-permute-start.17) | collective-permute-done | bytes 917536 | tf_op jit(solution)/shard_map/ppermute | solution.py:197
  143.5 2.0 products.14
  147.6 11.8 %collective-permute-done.13.mine_ref.refs_22_ = bf16[128,3584]{1,0:T(8,128)(2,1)S(1)} collective-permute-done((bf16[128,3584]{1,0:T(8,128)(2,1)S(1)}, bf16[128,3584]{1,0:T(8,128)(2,1)S(1)}, u32[]{:S(2)}, u32[]{:S(2)}) %collective-permute-start.13) | collective-permute-done | bytes 917536 | tf_op jit(solution)/shard_map/ppermute | solution.py:197
  161.8 2.0 products.13
  164.5 6.6 %encoder_sum.2.refs_6_ = f32[3584,256]{1,0:T(8,128)S(1)} custom-call(bf16[256,256]{1,0:T(8,128)(2,1)S(1)} %get-tuple-element.72.refs_0_, bf16[256,256]{1,0:T(8,128)(2,1)S(1)} %get-tuple-element.73.refs_1_, bf16[256,256]{1,0:T(8,128)(2,1)S(1)} %get-tuple-element.74.refs_2_, bf16[256,256]{1,0:T(8,128)(2,1)S(1)} %get-tuple-element.75.refs_3_, ...), custom_call_target="tpu_custom_call" | custom-call | flops 2818572288 | bytes 11010048 | tf_op jit(solution)/shard_map/encoder_sum/pallas_call | solution.py:169
  173.0 2.0 products.15
  178.5 2.1 gather_fusion
  180.6 4.2 %all-to-all-start.1 = ((f32[16,16,128]{2,1,0:T(8,128)}), f32[16,16,128]{2,1,0:T(8,128)}, u32[]{:S(2)}, u32[]{:S(2)}) async-start(f32[16,16,128]{2,1,0:T(8,128)} %gather_fusion), calls=%async_computation.1 | async-start | bytes 262144 | tf_op jit(solution)/shard_map/all_to_all | solution.py:222
  187.2 1.2 copy-done.11
  200.6 8.0 %decoder_sum.1 = bf16[256,3584]{1,0:T(8,128)(2,1)} custom-call(bf16[256,256]{1,0:T(8,128)(2,1)S(1)} %get-tuple-element.46.refs_0_, bf16[256,256]{1,0:T(8,128)(2,1)S(1)} %get-tuple-element.47.refs_1_, bf16[256,256]{1,0:T(8,128)(2,1)S(1)} %get-tuple-element.48.refs_2_, bf16[256,256]{1,0:T(8,128)(2,1)S(1)} %get-tuple-element.51.refs_3_, ...), custom_call_target="tpu_custom_call" | custom-call | flops 3758096384 | bytes 14680064 | tf_op jit(solution)/shard_map/decoder_sum/pallas_call | solution.py:153
  209.4 1.6 select_reduce_fusion
  211.0 2.0 copy-done.3
  213.9 6.7 %encoder_sum.3 = bf16[3584,256]{1,0:T(8,128)(2,1)} custom-call(bf16[256,256]{1,0:T(8,128)(2,1)S(1)} %copy-done.32, bf16[256,256]{1,0:T(8,128)(2,1)S(1)} %copy-done.36, bf16[128,3584]{1,0:T(8,128)(2,1)} %collective-permute-done.17.refs_2_, bf16[128,3584]{1,0:T(8,128)(2,1)} %collective-permute-done.18.refs_3_, ...), custom_call_target="tpu_custom_call" | custom-call | flops 939524096 | bytes 3670016 | tf_op jit(solution)/shard_map/encoder_sum/pallas_call | solution.py:169
  (181 shorter events, 40.4 us)
Async XLA Ops:
  0.6 49.2 %collective-permute-start = (bf16[128,3584]{1,0:T(8,128)(2,1)}, bf16[128,3584]{1,0:T(8,128)(2,1)S(1)}, u32[]{:S(2)}, u32[]{:S(2)}) collective-permute-start(bf16[128,3584]{1,0:T(8,128)(2,1)} %refs_8_.1), channel_id=1, source_target_pairs={{0,1},{1,0},{2,3},{3,2},{4,5},{5,4},{6,7},{7,6},{8,9},{9,8},{10,11... | collective-permute-start | bytes 2752520 | tf_op jit(solution)/shard_map/ppermute | solution.py:183
  1.1 24.0 %collective-permute-start.1 = (bf16[128,3584]{1,0:T(8,128)(2,1)}, bf16[128,3584]{1,0:T(8,128)(2,1)S(1)}, u32[]{:S(2)}, u32[]{:S(2)}) collective-permute-start(bf16[128,3584]{1,0:T(8,128)(2,1)} %refs_8_.1), channel_id=1, source_target_pairs={{0,4},{1,5},{4,8},{5,9},{8,12},{9,13},{12,14},{13,15},{14,10},{15,... | collective-permute-start | bytes 2752520 | tf_op jit(solution)/shard_map/ppermute | solution.py:197
  3.8 29.3 %collective-permute-start.3 = (bf16[128,3584]{1,0:T(8,128)(2,1)}, bf16[128,3584]{1,0:T(8,128)(2,1)S(1)}, u32[]{:S(2)}, u32[]{:S(2)}) collective-permute-start(bf16[128,3584]{1,0:T(8,128)(2,1)} %refs_8_.1), channel_id=1, source_target_pairs={{4,0},{5,1},{8,4},{9,5},{12,8},{13,9},{14,12},{15,13},{10,14},{11,... | collective-permute-start | bytes 2752520 | tf_op jit(solution)/shard_map/ppermute | solution.py:197
  3.8 51.6 %collective-permute-start.15 = (bf16[128,3584]{1,0:T(8,128)(2,1)}, bf16[128,3584]{1,0:T(8,128)(2,1)}, u32[]{:S(2)}, u32[]{:S(2)}) collective-permute-start(bf16[128,3584]{1,0:T(8,128)(2,1)} %refs_6_.1), channel_id=1, source_target_pairs={{0,4},{1,5},{4,8},{5,9},{8,12},{9,13},{12,14},{13,15},{14,10},{15,... | collective-permute-start | bytes 2752520 | tf_op jit(solution)/shard_map/ppermute | solution.py:197
  5.8 51.4 %collective-permute-start.19 = (bf16[128,3584]{1,0:T(8,128)(2,1)}, bf16[128,3584]{1,0:T(8,128)(2,1)}, u32[]{:S(2)}, u32[]{:S(2)}) collective-permute-start(bf16[128,3584]{1,0:T(8,128)(2,1)} %refs_6_.1), channel_id=1, source_target_pairs={{4,0},{5,1},{8,4},{9,5},{12,8},{13,9},{14,12},{15,13},{10,14},{11,... | collective-permute-start | bytes 2752520 | tf_op jit(solution)/shard_map/ppermute | solution.py:197
  25.1 32.1 %collective-permute-start.2 = (bf16[128,3584]{1,0:T(8,128)(2,1)S(1)}, bf16[128,3584]{1,0:T(8,128)(2,1)}, u32[]{:S(2)}, u32[]{:S(2)}) collective-permute-start(bf16[128,3584]{1,0:T(8,128)(2,1)S(1)} %collective-permute-done.1.mine_ref.refs_10_), channel_id=1, source_target_pairs={{0,1},{1,0},{2,3},{3,2},{4,5},{5,4},{6,7},{7,6},{8,9},{9,8},{10,11... | collective-permute-start | bytes 2752520 | tf_op jit(solution)/shard_map/ppermute | solution.py:183
  25.9 24.0 %all-to-all-start = ((bf16[16,32,128]{2,1,0:T(8,128)(2,1)}), bf16[16,32,128]{2,1,0:T(8,128)(2,1)S(1)}, u32[]{:S(2)}, u32[]{:S(2)}) async-start(bf16[16,32,128]{2,1,0:T(8,128)(2,1)} %pad_maximum_fusion), calls=%async_computation | async-start | bytes 262144 | tf_op jit(solution)/shard_map/all_to_all | solution.py:125
  33.1 24.4 %collective-permute-start.4 = (bf16[128,3584]{1,0:T(8,128)(2,1)S(1)}, bf16[128,3584]{1,0:T(8,128)(2,1)}, u32[]{:S(2)}, u32[]{:S(2)}) collective-permute-start(bf16[128,3584]{1,0:T(8,128)(2,1)S(1)} %collective-permute-done.3.mine_ref.refs_12_), channel_id=1, source_target_pairs={{0,1},{1,0},{2,3},{3,2},{4,5},{5,4},{6,7},{7,6},{8,9},{9,8},{10,11... | collective-permute-start | bytes 2752520 | tf_op jit(solution)/shard_map/ppermute | solution.py:183
  55.2 23.2 %collective-permute-start.5 = (bf16[128,3584]{1,0:T(8,128)(2,1)S(1)}, bf16[128,3584]{1,0:T(8,128)(2,1)S(1)}, u32[]{:S(2)}, u32[]{:S(2)}) collective-permute-start(bf16[128,3584]{1,0:T(8,128)(2,1)S(1)} %collective-permute-done.1.mine_ref.refs_10_), channel_id=1, source_target_pairs={{0,4},{1,5},{4,8},{5,9},{8,12},{9,13},{12,14},{13,15},{14,10},{15,... | collective-permute-start | bytes 2752520 | tf_op jit(solution)/shard_map/ppermute | solution.py:197
  55.4 28.9 %collective-permute-start.7 = (bf16[128,3584]{1,0:T(8,128)(2,1)S(1)}, bf16[128,3584]{1,0:T(8,128)(2,1)S(1)}, u32[]{:S(2)}, u32[]{:S(2)}) collective-permute-start(bf16[128,3584]{1,0:T(8,128)(2,1)S(1)} %collective-permute-done.3.mine_ref.refs_12_), channel_id=1, source_target_pairs={{4,0},{5,1},{8,4},{9,5},{12,8},{13,9},{14,12},{15,13},{10,14},{11,... | collective-permute-start | bytes 2752520 | tf_op jit(solution)/shard_map/ppermute | solution.py:197
  57.3 27.2 %collective-permute-start.24 = (bf16[128,3584]{1,0:T(8,128)(2,1)S(1)}, bf16[128,3584]{1,0:T(8,128)(2,1)S(1)}, u32[]{:S(2)}, u32[]{:S(2)}) collective-permute-start(bf16[128,3584]{1,0:T(8,128)(2,1)S(1)} %copy-done.28), channel_id=1, source_target_pairs={{0,1},{1,0},{2,3},{3,2},{4,5},{5,4},{6,7},{7,6},{8,9},{9,8},{10,11... | collective-permute-start | bytes 2752520 | tf_op jit(solution)/shard_map/ppermute | solution.py:183
  57.3 39.9 %collective-permute-start.16 = (bf16[128,3584]{1,0:T(8,128)(2,1)}, bf16[128,3584]{1,0:T(8,128)(2,1)S(1)}, u32[]{:S(2)}, u32[]{:S(2)}) collective-permute-start(bf16[128,3584]{1,0:T(8,128)(2,1)} %collective-permute-done.15.refs_8_), channel_id=1, source_target_pairs={{0,4},{1,5},{4,8},{5,9},{8,12},{9,13},{12,14},{13,15},{14,10},{15,... | collective-permute-start | bytes 2752520 | tf_op jit(solution)/shard_map/ppermute | solution.py:197
  57.5 41.0 %collective-permute-start.20 = (bf16[128,3584]{1,0:T(8,128)(2,1)}, bf16[128,3584]{1,0:T(8,128)(2,1)S(1)}, u32[]{:S(2)}, u32[]{:S(2)}) collective-permute-start(bf16[128,3584]{1,0:T(8,128)(2,1)} %collective-permute-done.19.refs_10_), channel_id=1, source_target_pairs={{4,0},{5,1},{8,4},{9,5},{12,8},{13,9},{14,12},{15,13},{10,14},{11,... | collective-permute-start | bytes 2752520 | tf_op jit(solution)/shard_map/ppermute | solution.py:197
  78.4 20.8 %collective-permute-start.25 = (bf16[128,3584]{1,0:T(8,128)(2,1)}, bf16[128,3584]{1,0:T(8,128)(2,1)S(1)}, u32[]{:S(2)}, u32[]{:S(2)}) collective-permute-start(bf16[128,3584]{1,0:T(8,128)(2,1)} %collective-permute-done.15.refs_8_), channel_id=1, source_target_pairs={{0,1},{1,0},{2,3},{3,2},{4,5},{5,4},{6,7},{7,6},{8,9},{9,8},{10,11... | collective-permute-start | bytes 2752520 | tf_op jit(solution)/shard_map/ppermute | solution.py:183
  84.3 15.0 %collective-permute-start.6 = (bf16[128,3584]{1,0:T(8,128)(2,1)S(1)}, bf16[128,3584]{1,0:T(8,128)(2,1)S(1)}, u32[]{:S(2)}, u32[]{:S(2)}) collective-permute-start(bf16[128,3584]{1,0:T(8,128)(2,1)S(1)} %collective-permute-done.5.mine_ref.refs_14_), channel_id=1, source_target_pairs={{0,1},{1,0},{2,3},{3,2},{4,5},{5,4},{6,7},{7,6},{8,9},{9,8},{10,11... | collective-permute-start | bytes 2752520 | tf_op jit(solution)/shard_map/ppermute | solution.py:183
  84.5 15.6 %collective-permute-start.8 = (bf16[128,3584]{1,0:T(8,128)(2,1)S(1)}, bf16[128,3584]{1,0:T(8,128)(2,1)S(1)}, u32[]{:S(2)}, u32[]{:S(2)}) collective-permute-start(bf16[128,3584]{1,0:T(8,128)(2,1)S(1)} %collective-permute-done.7.mine_ref.refs_16_), channel_id=1, source_target_pairs={{0,1},{1,0},{2,3},{3,2},{4,5},{5,4},{6,7},{7,6},{8,9},{9,8},{10,11... | collective-permute-start | bytes 2752520 | tf_op jit(solution)/shard_map/ppermute | solution.py:183
  97.2 23.3 %collective-permute-start.11 = (bf16[128,3584]{1,0:T(8,128)(2,1)S(1)}, bf16[128,3584]{1,0:T(8,128)(2,1)S(1)}, u32[]{:S(2)}, u32[]{:S(2)}) collective-permute-start(bf16[128,3584]{1,0:T(8,128)(2,1)S(1)} %collective-permute-done.7.mine_ref.refs_16_), channel_id=1, source_target_pairs={{4,0},{5,1},{8,4},{9,5},{12,8},{13,9},{14,12},{15,13},{10,14},{11,... | collective-permute-start | bytes 2752520 | tf_op jit(solution)/shard_map/ppermute | solution.py:197
  98.5 23.3 %collective-permute-start.9 = (bf16[128,3584]{1,0:T(8,128)(2,1)S(1)}, bf16[128,3584]{1,0:T(8,128)(2,1)S(1)}, u32[]{:S(2)}, u32[]{:S(2)}) collective-permute-start(bf16[128,3584]{1,0:T(8,128)(2,1)S(1)} %collective-permute-done.5.mine_ref.refs_14_), channel_id=1, source_target_pairs={{0,4},{1,5},{4,8},{5,9},{8,12},{9,13},{12,14},{13,15},{14,10},{15,... | collective-permute-start | bytes 2752520 | tf_op jit(solution)/shard_map/ppermute | solution.py:197
  99.2 27.9 %collective-permute-start.26 = (bf16[128,3584]{1,0:T(8,128)(2,1)}, bf16[128,3584]{1,0:T(8,128)(2,1)S(1)}, u32[]{:S(2)}, u32[]{:S(2)}) collective-permute-start(bf16[128,3584]{1,0:T(8,128)(2,1)} %collective-permute-done.19.refs_10_), channel_id=1, source_target_pairs={{0,1},{1,0},{2,3},{3,2},{4,5},{5,4},{6,7},{7,6},{8,9},{9,8},{10,11... | collective-permute-start | bytes 2752520 | tf_op jit(solution)/shard_map/ppermute | solution.py:183
  99.2 42.3 %collective-permute-start.17 = (bf16[128,3584]{1,0:T(8,128)(2,1)S(1)}, bf16[128,3584]{1,0:T(8,128)(2,1)}, u32[]{:S(2)}, u32[]{:S(2)}) collective-permute-start(bf16[128,3584]{1,0:T(8,128)(2,1)S(1)} %collective-permute-done.16.refs_12_), channel_id=1, source_target_pairs={{0,4},{1,5},{4,8},{5,9},{8,12},{9,13},{12,14},{13,15},{14,10},{15,... | collective-permute-start | bytes 2752520 | tf_op jit(solution)/shard_map/ppermute | solution.py:197
  100.0 41.5 %collective-permute-start.21 = (bf16[128,3584]{1,0:T(8,128)(2,1)S(1)}, bf16[128,3584]{1,0:T(8,128)(2,1)S(1)}, u32[]{:S(2)}, u32[]{:S(2)}) collective-permute-start(bf16[128,3584]{1,0:T(8,128)(2,1)S(1)} %collective-permute-done.20.refs_14_), channel_id=1, source_target_pairs={{4,0},{5,1},{8,4},{9,5},{12,8},{13,9},{14,12},{15,13},{10,14},{11,... | collective-permute-start | bytes 2752520 | tf_op jit(solution)/shard_map/ppermute | solution.py:197
  120.5 21.6 %collective-permute-start.12 = (bf16[128,3584]{1,0:T(8,128)(2,1)S(1)}, bf16[128,3584]{1,0:T(8,128)(2,1)S(1)}, u32[]{:S(2)}, u32[]{:S(2)}) collective-permute-start(bf16[128,3584]{1,0:T(8,128)(2,1)S(1)} %collective-permute-done.11.mine_ref.refs_20_), channel_id=1, source_target_pairs={{0,1},{1,0},{2,3},{3,2},{4,5},{5,4},{6,7},{7,6},{8,9},{9,8},{10,11... | collective-permute-start | bytes 2752520 | tf_op jit(solution)/shard_map/ppermute | solution.py:183
  121.7 24.5 %collective-permute-start.10 = (bf16[128,3584]{1,0:T(8,128)(2,1)S(1)}, bf16[128,3584]{1,0:T(8,128)(2,1)S(1)}, u32[]{:S(2)}, u32[]{:S(2)}) collective-permute-start(bf16[128,3584]{1,0:T(8,128)(2,1)S(1)} %collective-permute-done.9.mine_ref.refs_18_), channel_id=1, source_target_pairs={{0,1},{1,0},{2,3},{3,2},{4,5},{5,4},{6,7},{7,6},{8,9},{9,8},{10,11... | collective-permute-start | bytes 2752520 | tf_op jit(solution)/shard_map/ppermute | solution.py:183
  127.2 32.2 %collective-permute-start.13 = (bf16[128,3584]{1,0:T(8,128)(2,1)S(1)}, bf16[128,3584]{1,0:T(8,128)(2,1)S(1)}, u32[]{:S(2)}, u32[]{:S(2)}) collective-permute-start(bf16[128,3584]{1,0:T(8,128)(2,1)S(1)} %collective-permute-done.9.mine_ref.refs_18_), channel_id=1, source_target_pairs={{0,4},{1,5},{4,8},{5,9},{8,12},{9,13},{12,14},{13,15},{14,10},{15,... | collective-permute-start | bytes 2752520 | tf_op jit(solution)/shard_map/ppermute | solution.py:197
  141.5 22.4 %collective-permute-start.27 = (bf16[128,3584]{1,0:T(8,128)(2,1)S(1)}, bf16[128,3584]{1,0:T(8,128)(2,1)S(1)}, u32[]{:S(2)}, u32[]{:S(2)}) collective-permute-start(bf16[128,3584]{1,0:T(8,128)(2,1)S(1)} %collective-permute-done.16.refs_12_), channel_id=1, source_target_pairs={{0,1},{1,0},{2,3},{3,2},{4,5},{5,4},{6,7},{7,6},{8,9},{9,8},{10,11... | collective-permute-start | bytes 2752520 | tf_op jit(solution)/shard_map/ppermute | solution.py:183
  141.5 23.0 %collective-permute-start.28 = (bf16[128,3584]{1,0:T(8,128)(2,1)S(1)}, bf16[128,3584]{1,0:T(8,128)(2,1)S(1)}, u32[]{:S(2)}, u32[]{:S(2)}) collective-permute-start(bf16[128,3584]{1,0:T(8,128)(2,1)S(1)} %collective-permute-done.20.refs_14_), channel_id=1, source_target_pairs={{0,1},{1,0},{2,3},{3,2},{4,5},{5,4},{6,7},{7,6},{8,9},{9,8},{10,11... | collective-permute-start | bytes 2752520 | tf_op jit(solution)/shard_map/ppermute | solution.py:183
  142.0 22.5 %collective-permute-start.29 = (bf16[128,3584]{1,0:T(8,128)(2,1)S(1)}, bf16[128,3584]{1,0:T(8,128)(2,1)S(1)}, u32[]{:S(2)}, u32[]{:S(2)}) collective-permute-start(bf16[128,3584]{1,0:T(8,128)(2,1)S(1)} %collective-permute-done.21.refs_16_), channel_id=1, source_target_pairs={{0,1},{1,0},{2,3},{3,2},{4,5},{5,4},{6,7},{7,6},{8,9},{9,8},{10,11... | collective-permute-start | bytes 2752520 | tf_op jit(solution)/shard_map/ppermute | solution.py:183
  146.2 24.9 %collective-permute-start.22 = (bf16[128,3584]{1,0:T(8,128)(2,1)S(1)}, bf16[128,3584]{1,0:T(8,128)(2,1)}, u32[]{:S(2)}, u32[]{:S(2)}) collective-permute-start(bf16[128,3584]{1,0:T(8,128)(2,1)S(1)} %collective-permute-done.21.refs_16_), channel_id=1, source_target_pairs={{4,0},{5,1},{8,4},{9,5},{12,8},{13,9},{14,12},{15,13},{10,14},{11,... | collective-permute-start | bytes 2752520 | tf_op jit(solution)/shard_map/ppermute | solution.py:197
  159.4 13.6 %collective-permute-start.14 = (bf16[128,3584]{1,0:T(8,128)(2,1)S(1)}, bf16[128,3584]{1,0:T(8,128)(2,1)S(1)}, u32[]{:S(2)}, u32[]{:S(2)}) collective-permute-start(bf16[128,3584]{1,0:T(8,128)(2,1)S(1)} %collective-permute-done.13.mine_ref.refs_22_), channel_id=1, source_target_pairs={{0,1},{1,0},{2,3},{3,2},{4,5},{5,4},{6,7},{7,6},{8,9},{9,8},{10,11... | collective-permute-start | bytes 2752520 | tf_op jit(solution)/shard_map/ppermute | solution.py:183
  163.9 47.0 %collective-permute-start.18 = (bf16[128,3584]{1,0:T(8,128)(2,1)}, bf16[128,3584]{1,0:T(8,128)(2,1)}, u32[]{:S(2)}, u32[]{:S(2)}) collective-permute-start(bf16[128,3584]{1,0:T(8,128)(2,1)} %collective-permute-done.17.refs_2_), channel_id=1, source_target_pairs={{0,1},{1,0},{2,3},{3,2},{4,5},{5,4},{6,7},{7,6},{8,9},{9,8},{10,11... | collective-permute-start | bytes 2752520 | tf_op jit(solution)/shard_map/ppermute | solution.py:183
  171.1 39.8 %collective-permute-start.23 = (bf16[128,3584]{1,0:T(8,128)(2,1)}, bf16[128,3584]{1,0:T(8,128)(2,1)}, u32[]{:S(2)}, u32[]{:S(2)}) collective-permute-start(bf16[128,3584]{1,0:T(8,128)(2,1)} %collective-permute-done.22.refs_4_), channel_id=1, source_target_pairs={{0,1},{1,0},{2,3},{3,2},{4,5},{5,4},{6,7},{7,6},{8,9},{9,8},{10,11... | collective-permute-start | bytes 2752520 | tf_op jit(solution)/shard_map/ppermute | solution.py:183
  180.6 28.7 %all-to-all-start.1 = ((f32[16,16,128]{2,1,0:T(8,128)}), f32[16,16,128]{2,1,0:T(8,128)}, u32[]{:S(2)}, u32[]{:S(2)}) async-start(f32[16,16,128]{2,1,0:T(8,128)} %gather_fusion), calls=%async_computation.1 | async-start | bytes 262144 | tf_op jit(solution)/shard_map/all_to_all | solution.py:222
  (57 other events, 533.3 us)

commit v4 on v3

--- a/solution.py
+++ b/solution.py
@@ -12,7 +12,7 @@
 PART_BYTES = 9 << 20
 HELD_BYTES = 1 << 25
 RING_BYTES = 1 << 26
-VMEM_BYTES = 20 << 20
+VMEM_BYTES = 24 << 20
 
 
 def ring_tables(peer_count):
@@ -20,31 +20,39 @@
     ring = [chip for chip in range(chips) if chip % 2 == 0] + [chip for chip in reversed(range(chips)) if chip % 2]
     place = {chip: spot for spot, chip in enumerate(ring)}
     sources = np.zeros((peer_count, chips, 2), np.int32)
-    spot_of = np.zeros((peer_count, peer_count), np.int32)
     for device in range(peer_count):
         chip, core = divmod(device, 2)
-        for step in range(chips):
-            hop = (step + 1) // 2
-            other = ring[(place[chip] + (-hop if step % 2 else hop)) % chips]
-            sources[device, step] = (2 * other + core, 2 * other + 1 - core)
-            spot_of[device, 2 * other + core] = 2 * step
-            spot_of[device, 2 * other + 1 - core] = 2 * step + 1
-    up = [(2 * ring[i] + c, 2 * ring[(i + 1) % chips] + c) for i in range(chips) for c in range(2)]
-    down = [(b, a) for a, b in up]
+        sign = 1 - 2 * core
+        for hop in range(chips):
+            behind, ahead = ring[(place[chip] - sign * hop) % chips], ring[(place[chip] + sign * hop) % chips]
+            sources[device, hop] = (2 * behind + core, 2 * ahead + 1 - core)
+    onward = [(2 * ring[i], 2 * ring[(i + 1) % chips]) for i in range(chips)]
+    onward += [(2 * ring[i] + 1, 2 * ring[(i - 1) % chips] + 1) for i in range(chips)]
     swap = [(i, i ^ 1) for i in range(peer_count)]
-    return sources, spot_of, up, down, swap
-
-
-def product_kernel(per_block, order_ref, meta_ref, decoder_ref, mine_ref, theirs_ref, acts_ref, pre_ref, lat_ref, bias_ref):
-    latents, width = decoder_ref.shape
+    return sources, onward, swap
+
+
+def product_kernel(per_block, order_ref, meta_ref, decoder_ref, mine_ref, theirs_ref, *refs):
+    acts_ref, pre_ref, lat_ref, bias_ref, rows_ref, sems = refs[-6:]
     tokens = mine_ref.shape[0]
-    span = 512 if width % 512 == 0 else BLOCK
-    products = jnp.zeros((latents, 2 * tokens), jnp.float32)
-    for at in range(0, width, span):
-        rows = jnp.concatenate([mine_ref[:, at : at + span], theirs_ref[:, at : at + span]], axis=0)
-        products += lax.dot_general(
-            decoder_ref[:, at : at + span], rows, (((1,), (1,)), ((), ())), preferred_element_type=jnp.float32
-        )
+    copies = [
+        pltpu.make_async_copy(source, rows_ref.at[pl.ds(i * tokens, tokens)], sems.at[i])
+        for i, source in enumerate((mine_ref, theirs_ref))
+    ]
+    for copy in copies:
+        copy.start()
+    if len(refs) == 8:
+        lat_ref[...] = refs[0][...]
+        bias_ref[...] = refs[1][...]
+    else:
+        lat_ref[...] = jnp.zeros_like(lat_ref)
+        bias_ref[...] = jnp.zeros_like(bias_ref)
+    latents = decoder_ref.shape[0]
+    for copy in copies:
+        copy.wait()
+    products = lax.dot_general(
+        decoder_ref[...], rows_ref[...], (((1,), (1,)), ((), ())), preferred_element_type=jnp.float32
+    )
     row = lax.broadcasted_iota(jnp.int32, (8, tokens), 0)
     for tile in range(2):
         meta = meta_ref[order_ref[tile]].astype(jnp.float32)
@@ -64,35 +72,54 @@
                     sums[k] = sums[k] + picked
                     kept = kept + picked
                     dense = jnp.where(hit, values[k], dense)
-                if tile == 0:
-                    bias_ref[base : base + 8, :] = kept
-                else:
-                    bias_ref[base : base + 8, :] += kept
+                bias_ref[base : base + 8, :] += kept
                 kept_both.append(kept)
                 dense_both.append(dense)
             pre_ref[block : block + 16, at] = jnp.concatenate(kept_both, axis=0).astype(jnp.bfloat16)
             acts_ref[block : block + 16, at] = jnp.concatenate(dense_both, axis=0).astype(jnp.bfloat16)
+        source = order_ref[tile]
         for k in range(per_block):
-            lat_ref[tile, k : k + 1, :] = jnp.sum(sums[k], axis=0, keepdims=True)
-
-
-def decoder_kernel(steps, *refs):
-    acts, rows, out_ref = refs[:steps], refs[steps : 3 * steps], refs[3 * steps]
-    total = jnp.zeros(out_ref.shape, jnp.float32)
-    for s in range(steps):
-        both = jnp.concatenate([rows[2 * s][...], rows[2 * s + 1][...]], axis=0)
-        total += jnp.dot(acts[s][...], both, preferred_element_type=jnp.float32)
-    out_ref[...] = total.astype(out_ref.dtype)
-
-
-def encoder_kernel(steps, *refs):
+            lat_ref[source, k : k + 1, :] = jnp.sum(sums[k], axis=0, keepdims=True)
+
+
+def decoder_kernel(steps, span, *refs):
+    acts, rows, out_ref = refs[:steps], refs[steps : 3 * steps], refs[-1]
+
+    def body(*blocks):
+        total = jnp.zeros(blocks[-1].shape, jnp.float32)
+        for s in range(steps):
+            both = jnp.concatenate([blocks[2 * s][...], blocks[2 * s + 1][...]], axis=0)
+            total += jnp.dot(acts[s][...], both, preferred_element_type=jnp.float32)
+        blocks[-1][...] = total.astype(out_ref.dtype)
+
+    tokens, width = rows[0].shape
+    pltpu.emit_pipeline(
+        body,
+        grid=(width // span,),
+        in_specs=[pl.BlockSpec((tokens, span), lambda i: (0, i))] * (2 * steps),
+        out_specs=[pl.BlockSpec((out_ref.shape[0], span), lambda i: (0, i))],
+    )(*rows, out_ref)
+
+
+def encoder_kernel(steps, span, *refs):
     pres, rows, refs = refs[:steps], refs[steps : 3 * steps], refs[3 * steps :]
     out_ref = refs[-1]
-    total = refs[0][...] if len(refs) == 2 else jnp.zeros(out_ref.shape, jnp.float32)
-    for s in range(steps):
-        both = jnp.concatenate([rows[2 * s][...], rows[2 * s + 1][...]], axis=0)
-        total += lax.dot_general(both, pres[s][...], (((0,), (1,)), ((), ())), preferred_element_type=jnp.float32)
-    out_ref[...] = total.astype(out_ref.dtype)
+
+    def body(*blocks):
+        total = blocks[2 * steps][...] if len(refs) == 2 else jnp.zeros(blocks[-1].shape, jnp.float32)
+        for s in range(steps):
+            both = jnp.concatenate([blocks[2 * s][...], blocks[2 * s + 1][...]], axis=0)
+            total += lax.dot_general(both, pres[s][...], (((0,), (1,)), ((), ())), preferred_element_type=jnp.float32)
+        blocks[-1][...] = total.astype(out_ref.dtype)
+
+    tokens, width = rows[0].shape
+    sums = pl.BlockSpec((span, out_ref.shape[1]), lambda i: (i, 0))
+    pltpu.emit_pipeline(
+        body,
+        grid=(width // span,),
+        in_specs=[pl.BlockSpec((tokens, span), lambda i: (0, i))] * (2 * steps) + [sums] * (len(refs) - 1),
+        out_specs=[sums],
+    )(*rows, *refs)
 
 
 def after(value, *others):
@@ -107,9 +134,8 @@
     peer_count = lax.axis_size("lat")
     chips = peer_count // 2
     me = lax.axis_index("lat")
-    sources, spot_of, up, down, swap = ring_tables(peer_count)
+    sources, onward, swap = ring_tables(peer_count)
     order = jnp.asarray(sources)[me]
-    spots = jnp.asarray(spot_of)[me]
 
     own_t = owners.T
     columns_t = (local_blocks.T[:, None, :] * BLOCK + offsets.transpose(1, 2, 0)).astype(jnp.float32)
@@ -126,108 +152,88 @@
 
     whole = pl.BlockSpec(memory_space=pltpu.VMEM)
     scalars = pl.BlockSpec(memory_space=pltpu.SMEM)
+    far = pl.BlockSpec(memory_space=pltpu.HBM)
     step_tokens = 2 * token_count
-    work = 2 * latent_count * width * step_tokens
+    light = pl.CostEstimate(flops=1, bytes_accessed=1, transcendentals=0)
     params = pltpu.CompilerParams(vmem_limit_bytes=VMEM_BYTES)
 
-    def products(step, rows):
+    def products(step, rows, totals):
         return pl.pallas_call(
             functools.partial(product_kernel, per_block),
-            in_specs=[scalars] + [whole] * 4,
+            in_specs=[scalars, whole, whole, far, far] + [whole] * len(totals),
             out_specs=[whole] * 4,
             out_shape=[
                 jax.ShapeDtypeStruct((latent_count, step_tokens), jnp.bfloat16),
                 jax.ShapeDtypeStruct((latent_count, step_tokens), jnp.bfloat16),
-                jax.ShapeDtypeStruct((2, per_block, token_count), jnp.float32),
+                jax.ShapeDtypeStruct((peer_count, per_block, token_count), jnp.float32),
                 jax.ShapeDtypeStruct((latent_count, token_count), jnp.float32),
             ],
+            scratch_shapes=[pltpu.VMEM((step_tokens, width), jnp.bfloat16), pltpu.SemaphoreType.DMA((2,))],
             compiler_params=params,
-            cost_estimate=pl.CostEstimate(flops=work, bytes_accessed=2 * step_tokens * width, transcendentals=0),
+            cost_estimate=light,
             name="products",
-        )(order[step], meta, decoder, *rows)
+        )(order[step], meta, decoder, *rows, *totals)
 
     span = 512 if width % 512 == 0 else BLOCK
-    rows_block = pl.BlockSpec((token_count, span), lambda i: (0, i))
 
     def decoder_sum(acts, rows):
+        steps = len(acts)
         return pl.pallas_call(
-            functools.partial(decoder_kernel, len(acts)),
-            grid=(width // span,),
-            in_specs=[whole] * len(acts) + [rows_block] * (2 * len(acts)),
-            out_specs=pl.BlockSpec((latent_count, span), lambda i: (0, i)),
+            functools.partial(decoder_kernel, steps, span),
+            in_specs=[whole] * steps + [far] * (2 * steps),
+            out_specs=far,
             out_shape=jax.ShapeDtypeStruct((latent_count, width), jnp.bfloat16),
             compiler_params=params,
-            cost_estimate=pl.CostEstimate(
-                flops=work * len(acts), bytes_accessed=2 * len(acts) * step_tokens * width, transcendentals=0
-            ),
+            cost_estimate=light,
             name="decoder_sum",
         )(*acts, *[part for pair in rows for part in pair])
 
-    def encoder_sum(pres, rows, total, dtype):
-        block = pl.BlockSpec((span, latent_count), lambda i: (i, 0))
-        totals = [] if total is None else [total]
+    def encoder_sum(pres, rows, partial, dtype):
+        steps = len(pres)
+        partials = [] if partial is None else [partial]
         return pl.pallas_call(
-            functools.partial(encoder_kernel, len(pres)),
-            grid=(width // span,),
-            in_specs=[whole] * len(pres) + [rows_block] * (2 * len(pres)) + [block] * len(totals),
-            out_specs=block,
+            functools.partial(encoder_kernel, steps, span),
+            in_specs=[whole] * steps + [far] * (2 * steps + len(partials)),
+            out_specs=far,
             out_shape=jax.ShapeDtypeStruct((width, latent_count), dtype),
             compiler_params=params,
-            cost_estimate=pl.CostEstimate(
-                flops=work * len(pres), bytes_accessed=2 * len(pres) * step_tokens * width, transcendentals=0
-            ),
+            cost_estimate=light,
             name="encoder_sum",
-        )(*pres, *[part for pair in rows for part in pair], *totals)
-
-    def other(rows):
-        return lax.ppermute(rows, "lat", swap)
-
-    grads, ins, done = [None] * chips, [None] * chips, [None] * chips
-    held = {("g", True): grad_recon, ("g", False): grad_recon, ("i", True): inputs, ("i", False): inputs}
-
-    def hop(kind, number, *first):
-        for upward in (True, False):
-            step = 2 * number - 1 if upward else 2 * number
-            antipode = 2 * number == chips
-            if antipode and upward != (kind == "g"):
-                continue
-            rows = held[kind, upward]
-            if first:
-                rows = after(rows, *first)
-            rows = lax.ppermute(rows, "lat", up if upward else down)
-            held[kind, upward] = rows
-            (grads if kind == "g" else ins)[chips - 1 if antipode else step] = (rows, other(rows))
-
-    def compute(*steps):
-        for step in steps:
-            done[step] = products(step, grads[step])
-
-    hops = chips // 2
-    grads[0] = (grad_recon, other(grad_recon))
-    ins[0] = (inputs, other(inputs))
-    hop("g", 1)
-    hop("i", 1)
-    compute(0)
-    for number in range(2, hops + 1):
-        earlier = [done[step][3] for step in range(max(0, 2 * number - 5), 2 * number - 3)]
-        hop("g", number, *earlier)
-        compute(2 * number - 3, 2 * number - 2)
-        if number < hops:
-            hop("i", number, *earlier)
-    compute(chips - 1)
-    hop("i", hops, done[chips - 2][3])
-    acts, pres, lats, biases = zip(*done)
-
-    lat = jnp.concatenate(lats, axis=0)[spots]
-    returned = lax.all_to_all(lat, "lat", split_axis=0, concat_axis=0, tiled=True)
+        )(*pres, *[part for pair in rows for part in pair], *partials)
+
+    acts, pres, totals = [], [], ()
+    grads, ins = [], [inputs]
+
+    def send(rows, way, *first):
+        return lax.ppermute(after(rows, *first) if first else rows, "lat", way)
+
+    def compute(rows):
+        nonlocal totals
+        grads.append(rows)
+        acts_here, pre_here, *totals = products(len(acts), rows, totals)
+        acts.append(acts_here)
+        pres.append(pre_here)
+
+    arriving = send(grad_recon, onward)
+    compute((grad_recon, send(grad_recon, swap)))
+    partial = None
+    for hop in range(1, chips):
+        grad = arriving
+        if hop < chips - 1:
+            arriving = send(grad, onward, *((meta,) if hop == 1 else (totals[1],)))
+        theirs = send(grad, swap, *(() if partial is None else (partial,)))
+        moved = send(ins[hop - 1], onward, *((theirs,) if hop == 1 else (ins[hop - 2][1],)), *(totals if hop == chips - 1 else ()))
+        compute((grad, theirs))
+        ins[hop - 1] = (ins[hop - 1], send(ins[hop - 1], swap))
+        ins.append(moved)
+        if hop == chips - 2:
+            partial = encoder_sum(pres[: hop - 1], ins[: hop - 1], None, jnp.float32)
+    returned = lax.all_to_all(totals[0], "lat", split_axis=0, concat_axis=0, tiled=True)
     latent_grads = pick_returned(returned, own_t)
     decoder_grad = decoder_sum(acts, grads)
-    bias_grad = jnp.sum(functools.reduce(jnp.add, biases), axis=1)
-
-    early = [0] + list(range(1, chips - 3)) + [chips - 2]
-    late = [chips - 3, chips - 1]
-    total = encoder_sum([pres[s] for s in early], [ins[s] for s in early], None, jnp.float32)
-    encoder_grad = encoder_sum([pres[s] for s in late], [ins[s] for s in late], total, jnp.bfloat16)
+    ins[-1] = (ins[-1], send(ins[-1], swap, decoder_grad))
+    bias_grad = jnp.sum(totals[1], axis=1)
+    encoder_grad = encoder_sum(pres[chips - 3 :], ins[chips - 3 :], partial, jnp.bfloat16)
     return (decoder_grad, encoder_grad, bias_grad, latent_grads)
 
 

time: 222 us -> 193 us (0.87)
  local copies, waits for them, and re-layouts: 36.6 us -> 11.5 us
  starting transfers between devices: 27.8 us -> 14.8 us
  waiting for transfers between devices: 110 us -> 117 us
  Pallas kernels: 39.3 us -> 44.6 us
  other arithmetic: 5.93 us -> 3.59 us
    unnamed x121 -> x28, local copies, waits for them, and re-layouts: 31.6 us -> 9.24 us
    ppermute x30, starting transfers between devices: 17.2 us -> 4.76 us  [send(): return lax.ppermute(after(rows, *first) if first else rows, 'lat', way)]
    all_to_all x1, waiting for transfers between devices: 16.4 us -> 7.52 us  [by_ring(): meta = lax.all_to_all(meta, 'lat', split_axis=0, concat_axis=0, tiled=True)]
    ppermute x30, waiting for transfers between devices: 93.5 us -> 102 us  [send(): return lax.ppermute(after(rows, *first) if first else rows, 'lat', way)]
    all_to_all x1, waiting for transfers between devices: 0.01 us -> 7.19 us  [by_ring(): lax.all_to_all(totals[0], 'lat', split_axis=0, concat_axis=0, tiled=True)]
    pallas_call x8, Pallas kernels: 17.9 us -> 21.8 us  [products(): pl.pallas_call(functools.partial(product_kernel, per_block), in_specs=[sc...]
  transfers between devices with their start and end apart: 32 -> 32, of which waited for: 8 -> 16; matrix products, arithmetic and copies ran while one was open for 7% -> 3% of each run, Pallas kernels for 15% -> 20%
where the time goes in v4:
time: 193 us; the launch traced here: 192 us
  waiting for transfers between devices  117 us (61%)
  Pallas kernels  44.6 us (23%)
  starting transfers between devices  14.8 us (8%)
  local copies, waits for them, and re-layouts  11.5 us (6%)
  other arithmetic  3.59 us (2%)
    ppermute x30, waiting for transfers between devices, send(): return lax.ppermute(after(rows, *first) if first else rows, 'lat', way)  102 us
    pallas_call x8, Pallas kernels, products(): pl.pallas_call(functools.partial(product_kernel, per_block), in_specs=[sc...  21.8 us
    pallas_call x2, Pallas kernels, encoder_sum(): pl.pallas_call(functools.partial(encoder_kernel, steps, span), in_specs=[...  13.9 us
    unnamed x28, local copies, waits for them, and re-layouts  9.24 us
    pallas_call x1, Pallas kernels, decoder_sum(): pl.pallas_call(functools.partial(decoder_kernel, steps, span), in_specs=[...  8.91 us
    all_to_all x1, waiting for transfers between devices, by_ring(): meta = lax.all_to_all(meta, 'lat', split_axis=0, concat_axis=0, tiled=True)  7.52 us
    all_to_all x1, waiting for transfers between devices, by_ring(): lax.all_to_all(totals[0], 'lat', split_axis=0, concat_axis=0, tiled=True)  7.19 us
    all_to_all x1, starting transfers between devices, by_ring(): meta = lax.all_to_all(meta, 'lat', split_axis=0, concat_axis=0, tiled=True)  6.54 us
  transfers between devices with their start and end apart: 32, of which 16 were waited for; matrix products, arithmetic and copies ran while one was open for 3% of the time, Pallas kernels for 20%

profile of v4, /device:TPU:0, one launch (start us, length us, event | category | flops | bytes accessed | tf_op | source)
XLA Modules:
  0.0 192.2 jit_solution(8119189612108716716)
XLA Ops:
  0.6 3.1 %collective-permute-start.1 = (bf16[128,3584]{1,0:T(8,128)(2,1)}, bf16[128,3584]{1,0:T(8,128)(2,1)S(1)}, u32[]{:S(2)}, u32[]{:S(2)}) collective-permute-start(bf16[128,3584]{1,0:T(8,128)(2,1)} %refs_8_.1), channel_id=1, source_target_pairs={{0,4},{4,8},{8,12},{12,14},{14,10},{10,6},{6,2},{2,0},{1,3},{5,1},... | collective-permute-start | bytes 2752520 | tf_op jit(solution)/shard_map/ppermute | solution.py:208
  6.0 9.2 %collective-permute-done.1.mine_ref.refs_10_ = bf16[128,3584]{1,0:T(8,128)(2,1)S(1)} collective-permute-done((bf16[128,3584]{1,0:T(8,128)(2,1)}, bf16[128,3584]{1,0:T(8,128)(2,1)S(1)}, u32[]{:S(2)}, u32[]{:S(2)}) %collective-permute-start.1) | collective-permute-done | bytes 917536 | tf_op jit(solution)/shard_map/ppermute | solution.py:208
  16.7 6.5 %all-to-all-start = ((bf16[16,32,128]{2,1,0:T(8,128)(2,1)}), bf16[16,32,128]{2,1,0:T(8,128)(2,1)S(1)}, u32[]{:S(2)}, u32[]{:S(2)}) async-start(bf16[16,32,128]{2,1,0:T(8,128)(2,1)} %pad_maximum_fusion), calls=%async_computation | async-start | bytes 262144 | tf_op jit(solution)/shard_map/all_to_all | solution.py:151
  23.7 7.5 %all-to-all-done.meta_ref = bf16[16,32,128]{2,1,0:T(8,128)(2,1)S(1)} async-done(((bf16[16,32,128]{2,1,0:T(8,128)(2,1)}), bf16[16,32,128]{2,1,0:T(8,128)(2,1)S(1)}, u32[]{:S(2)}, u32[]{:S(2)}) %all-to-all-start) | async-done | bytes 131104 | tf_op jit(solution)/shard_map/all_to_all | solution.py:151
  33.0 1.5 copy-done
  35.7 3.5 %products.8 = (bf16[256,256]{1,0:T(8,128)(2,1)S(1)}, bf16[256,256]{1,0:T(8,128)(2,1)S(1)}, f32[16,16,128]{2,1,0:T(8,128)S(1)}, f32[256,128]{1,0:T(8,128)S(1)}) custom-call(s32[2]{0:T(128)S(1)} %get-tuple-element.115.order_ref, bf16[16,32,128]{2,1,0:T(8,128)(2,1)S(1)} %all-to-all-done.meta_ref, bf16[256,3584]{1,0:T(8,128)(2,1)S(1)} %copy-done, ...), custom_call_target="tpu_custom_call" | custom-call | flops 1 | bytes 1 | tf_op jit(solution)/shard_map/products/pallas_call | solution.py:161
  39.2 2.5 %products.9 = (bf16[256,256]{1,0:T(8,128)(2,1)S(1)}, bf16[256,256]{1,0:T(8,128)(2,1)S(1)}, f32[16,16,128]{2,1,0:T(8,128)S(1)}, f32[256,128]{1,0:T(8,128)S(1)}) custom-call(s32[2]{0:T(128)S(1)} %get-tuple-element.114.order_ref, bf16[16,32,128]{2,1,0:T(8,128)(2,1)S(1)} %all-to-all-done.meta_ref, bf16[256,3584]{1,0:T(8,128)(2,1)S(1)} %copy-done.1, ...), custom_call_target="tpu_custom_call" | custom-call | flops 1 | bytes 1 | tf_op jit(solution)/shard_map/products/pallas_call | solution.py:161
  41.7 2.9 %collective-permute-done.3.mine_ref.refs_12_ = bf16[128,3584]{1,0:T(8,128)(2,1)S(1)} collective-permute-done((bf16[128,3584]{1,0:T(8,128)(2,1)S(1)}, bf16[128,3584]{1,0:T(8,128)(2,1)S(1)}, u32[]{:S(2)}, u32[]{:S(2)}) %collective-permute-start.3) | collective-permute-done | bytes 917536 | tf_op jit(solution)/shard_map/ppermute | solution.py:208
  44.6 9.9 %collective-permute-done.15.refs_7_ = bf16[128,3584]{1,0:T(8,128)(2,1)} collective-permute-done((bf16[128,3584]{1,0:T(8,128)(2,1)}, bf16[128,3584]{1,0:T(8,128)(2,1)}, u32[]{:S(2)}, u32[]{:S(2)}) %collective-permute-start.15) | collective-permute-done | bytes 917536 | tf_op jit(solution)/shard_map/ppermute | solution.py:208
  54.5 9.7 %collective-permute-done.5.mine_ref.refs_14_ = bf16[128,3584]{1,0:T(8,128)(2,1)S(1)} collective-permute-done((bf16[128,3584]{1,0:T(8,128)(2,1)S(1)}, bf16[128,3584]{1,0:T(8,128)(2,1)S(1)}, u32[]{:S(2)}, u32[]{:S(2)}) %collective-permute-start.5) | collective-permute-done | bytes 917536 | tf_op jit(solution)/shard_map/ppermute | solution.py:208
  64.3 2.5 %products.10 = (bf16[256,256]{1,0:T(8,128)(2,1)S(1)}, bf16[256,256]{1,0:T(8,128)(2,1)S(1)}, f32[16,16,128]{2,1,0:T(8,128)S(1)}, f32[256,128]{1,0:T(8,128)S(1)}) custom-call(s32[2]{0:T(128)S(1)} %get-tuple-element.113.order_ref, bf16[16,32,128]{2,1,0:T(8,128)(2,1)S(1)} %all-to-all-done.meta_ref, bf16[256,3584]{1,0:T(8,128)(2,1)S(1)} %copy-done.1, ...), custom_call_target="tpu_custom_call" | custom-call | flops 1 | bytes 1 | tf_op jit(solution)/shard_map/products/pallas_call | solution.py:161
  66.9 7.2 %collective-permute-done.17.refs_9_ = bf16[128,3584]{1,0:T(8,128)(2,1)S(1)} collective-permute-done((bf16[128,3584]{1,0:T(8,128)(2,1)}, bf16[128,3584]{1,0:T(8,128)(2,1)S(1)}, u32[]{:S(2)}, u32[]{:S(2)}) %collective-permute-start.17) | collective-permute-done | bytes 917536 | tf_op jit(solution)/shard_map/ppermute | solution.py:208
  74.1 2.5 %products.11 = (bf16[256,256]{1,0:T(8,128)(2,1)S(1)}, bf16[256,256]{1,0:T(8,128)(2,1)S(1)}, f32[16,16,128]{2,1,0:T(8,128)S(1)}, f32[256,128]{1,0:T(8,128)S(1)}) custom-call(s32[2]{0:T(128)S(1)} %get-tuple-element.112.order_ref, bf16[16,32,128]{2,1,0:T(8,128)(2,1)S(1)} %all-to-all-done.meta_ref, bf16[256,3584]{1,0:T(8,128)(2,1)S(1)} %copy-done.1, ...), custom_call_target="tpu_custom_call" | custom-call | flops 1 | bytes 1 | tf_op jit(solution)/shard_map/products/pallas_call | solution.py:161
  76.6 7.3 %collective-permute-done.7.mine_ref.refs_16_ = bf16[128,3584]{1,0:T(8,128)(2,1)S(1)} collective-permute-done((bf16[128,3584]{1,0:T(8,128)(2,1)S(1)}, bf16[128,3584]{1,0:T(8,128)(2,1)S(1)}, u32[]{:S(2)}, u32[]{:S(2)}) %collective-permute-start.7) | collective-permute-done | bytes 917536 | tf_op jit(solution)/shard_map/ppermute | solution.py:208
  83.9 9.8 %collective-permute-done.19.refs_11_ = bf16[128,3584]{1,0:T(8,128)(2,1)S(1)} collective-permute-done((bf16[128,3584]{1,0:T(8,128)(2,1)S(1)}, bf16[128,3584]{1,0:T(8,128)(2,1)S(1)}, u32[]{:S(2)}, u32[]{:S(2)}) %collective-permute-start.19) | collective-permute-done | bytes 917536 | tf_op jit(solution)/shard_map/ppermute | solution.py:208
  93.8 9.8 %collective-permute-done.9.mine_ref.refs_18_ = bf16[128,3584]{1,0:T(8,128)(2,1)S(1)} collective-permute-done((bf16[128,3584]{1,0:T(8,128)(2,1)S(1)}, bf16[128,3584]{1,0:T(8,128)(2,1)S(1)}, u32[]{:S(2)}, u32[]{:S(2)}) %collective-permute-start.9) | collective-permute-done | bytes 917536 | tf_op jit(solution)/shard_map/ppermute | solution.py:208
  103.6 2.5 %products.12 = (bf16[256,256]{1,0:T(8,128)(2,1)S(1)}, bf16[256,256]{1,0:T(8,128)(2,1)S(1)}, f32[16,16,128]{2,1,0:T(8,128)S(1)}, f32[256,128]{1,0:T(8,128)S(1)}) custom-call(s32[2]{0:T(128)S(1)} %get-tuple-element.111.order_ref, bf16[16,32,128]{2,1,0:T(8,128)(2,1)S(1)} %all-to-all-done.meta_ref, bf16[256,3584]{1,0:T(8,128)(2,1)S(1)} %copy-done.1, ...), custom_call_target="tpu_custom_call" | custom-call | flops 1 | bytes 1 | tf_op jit(solution)/shard_map/products/pallas_call | solution.py:161
  106.2 7.2 %collective-permute-done.21.refs_13_ = bf16[128,3584]{1,0:T(8,128)(2,1)S(1)} collective-permute-done((bf16[128,3584]{1,0:T(8,128)(2,1)S(1)}, bf16[128,3584]{1,0:T(8,128)(2,1)S(1)}, u32[]{:S(2)}, u32[]{:S(2)}) %collective-permute-start.21) | collective-permute-done | bytes 917536 | tf_op jit(solution)/shard_map/ppermute | solution.py:208
  113.4 2.5 %products.13 = (bf16[256,256]{1,0:T(8,128)(2,1)S(1)}, bf16[256,256]{1,0:T(8,128)(2,1)S(1)}, f32[16,16,128]{2,1,0:T(8,128)S(1)}, f32[256,128]{1,0:T(8,128)S(1)}) custom-call(s32[2]{0:T(128)S(1)} %get-tuple-element.110.order_ref, bf16[16,32,128]{2,1,0:T(8,128)(2,1)S(1)} %all-to-all-done.meta_ref, bf16[256,3584]{1,0:T(8,128)(2,1)S(1)} %copy-done.1, ...), custom_call_target="tpu_custom_call" | custom-call | flops 1 | bytes 1 | tf_op jit(solution)/shard_map/products/pallas_call | solution.py:161
  116.0 7.3 %collective-permute-done.11.mine_ref.refs_20_ = bf16[128,3584]{1,0:T(8,128)(2,1)S(1)} collective-permute-done((bf16[128,3584]{1,0:T(8,128)(2,1)S(1)}, bf16[128,3584]{1,0:T(8,128)(2,1)S(1)}, u32[]{:S(2)}, u32[]{:S(2)}) %collective-permute-start.11) | collective-permute-done | bytes 917536 | tf_op jit(solution)/shard_map/ppermute | solution.py:208
  123.3 9.8 %collective-permute-done.24.refs_3_ = bf16[128,3584]{1,0:T(8,128)(2,1)S(1)} collective-permute-done((bf16[128,3584]{1,0:T(8,128)(2,1)S(1)}, bf16[128,3584]{1,0:T(8,128)(2,1)S(1)}, u32[]{:S(2)}, u32[]{:S(2)}) %collective-permute-start.24) | collective-permute-done | bytes 917536 | tf_op jit(solution)/shard_map/ppermute | solution.py:208
  133.1 7.0 %encoder_sum.2.refs_9_ = f32[3584,256]{1,0:T(8,128)S(1)} custom-call(bf16[256,256]{1,0:T(8,128)(2,1)S(1)} %get-tuple-element.76.refs_0_, bf16[256,256]{1,0:T(8,128)(2,1)S(1)} %get-tuple-element.77.refs_1_, bf16[256,256]{1,0:T(8,128)(2,1)S(1)} %get-tuple-element.78.refs_2_, bf16[256,256]{1,0:T(8,128)(2,1)S(1)} %get-tuple-element.79.refs_3_, ...), custom_call_target="tpu_custom_call" | custom-call | flops 1 | bytes 1 | tf_op jit(solution)/shard_map/encoder_sum/pallas_call | solution.py:194
  140.1 2.8 %collective-permute-done.13.mine_ref.refs_22_ = bf16[128,3584]{1,0:T(8,128)(2,1)S(1)} collective-permute-done((bf16[128,3584]{1,0:T(8,128)(2,1)S(1)}, bf16[128,3584]{1,0:T(8,128)(2,1)S(1)}, u32[]{:S(2)}, u32[]{:S(2)}) %collective-permute-start.13) | collective-permute-done | bytes 917536 | tf_op jit(solution)/shard_map/ppermute | solution.py:208
  142.9 2.5 %products.14 = (bf16[256,256]{1,0:T(8,128)(2,1)S(1)}, bf16[256,256]{1,0:T(8,128)(2,1)S(1)}, f32[16,16,128]{2,1,0:T(8,128)S(1)}, f32[256,128]{1,0:T(8,128)S(1)}) custom-call(s32[2]{0:T(128)S(1)} %get-tuple-element.109.order_ref, bf16[16,32,128]{2,1,0:T(8,128)(2,1)S(1)} %all-to-all-done.meta_ref, bf16[256,3584]{1,0:T(8,128)(2,1)S(1)} %copy-done.1, ...), custom_call_target="tpu_custom_call" | custom-call | flops 1 | bytes 1 | tf_op jit(solution)/shard_map/products/pallas_call | solution.py:161
  145.5 7.4 %collective-permute-done.26.refs_5_ = bf16[128,3584]{1,0:T(8,128)(2,1)} collective-permute-done((bf16[128,3584]{1,0:T(8,128)(2,1)S(1)}, bf16[128,3584]{1,0:T(8,128)(2,1)}, u32[]{:S(2)}, u32[]{:S(2)}) %collective-permute-start.26) | collective-permute-done | bytes 917536 | tf_op jit(solution)/shard_map/ppermute | solution.py:208
  152.9 3.2 %products.15 = (bf16[256,256]{1,0:T(8,128)(2,1)S(1)}, bf16[256,256]{1,0:T(8,128)(2,1)S(1)}, f32[16,16,128]{2,1,0:T(8,128)}, f32[256,128]{1,0:T(8,128)S(1)}) custom-call(s32[2]{0:T(128)S(1)} %get-tuple-element.108.order_ref, bf16[16,32,128]{2,1,0:T(8,128)(2,1)S(1)} %all-to-all-done.meta_ref, bf16[256,3584]{1,0:T(8,128)(2,1)S(1)} %copy-done.1, ...), custom_call_target="tpu_custom_call" | custom-call | flops 1 | bytes 1 | tf_op jit(solution)/shard_map/products/pallas_call | solution.py:161
  156.1 8.9 %decoder_sum.1 = bf16[256,3584]{1,0:T(8,128)(2,1)} custom-call(bf16[256,256]{1,0:T(8,128)(2,1)S(1)} %get-tuple-element.51.refs_0_, bf16[256,256]{1,0:T(8,128)(2,1)S(1)} %get-tuple-element.54.refs_1_, bf16[256,256]{1,0:T(8,128)(2,1)S(1)} %get-tuple-element.58.refs_2_, bf16[256,256]{1,0:T(8,128)(2,1)S(1)} %get-tuple-element.62.refs_3_, ...), custom_call_target="tpu_custom_call" | custom-call | flops 1 | bytes 1 | tf_op jit(solution)/shard_map/decoder_sum/pallas_call | solution.py:181
  165.0 1.5 collective-permute-done.28.refs_7_
  166.6 3.5 %all-to-all-start.1 = ((f32[16,16,128]{2,1,0:T(8,128)}), f32[16,16,128]{2,1,0:T(8,128)S(1)}, u32[]{:S(2)}, u32[]{:S(2)}) async-start(f32[16,16,128]{2,1,0:T(8,128)} %get-tuple-element.97), calls=%async_computation.1 | async-start | bytes 262144 | tf_op jit(solution)/shard_map/all_to_all | solution.py:231
  170.8 7.2 %all-to-all-done.1 = f32[16,16,128]{2,1,0:T(8,128)S(1)} async-done(((f32[16,16,128]{2,1,0:T(8,128)}), f32[16,16,128]{2,1,0:T(8,128)S(1)}, u32[]{:S(2)}, u32[]{:S(2)}) %all-to-all-start.1) | async-done | bytes 131104 | tf_op jit(solution)/shard_map/all_to_all | solution.py:231
  179.6 2.0 %copy-done.3 = f32[3584,256]{1,0:T(8,128)S(1)} copy-done((f32[3584,256]{1,0:T(8,128)S(1)}, f32[3584,256]{1,0:T(8,128)}, u32[]{:S(2)}) %copy-start.3) | copy-done | bytes 3670040
  185.2 7.0 %encoder_sum.3 = bf16[3584,256]{1,0:T(8,128)(2,1)} custom-call(bf16[256,256]{1,0:T(8,128)(2,1)S(1)} %get-tuple-element.89.refs_0_, bf16[256,256]{1,0:T(8,128)(2,1)S(1)} %get-tuple-element.90.refs_1_, bf16[256,256]{1,0:T(8,128)(2,1)S(1)} %get-tuple-element.91.refs_2_, bf16[128,3584]{1,0:T(8,128)(2,1)S(1)} %copy-done.8, bf16[128,3584]{1,0:T(8,128)(2,1)S(1)} %copy-done.10, ...), custom_call_target="tpu_custom_call" | custom-call | flops 1 | bytes 1 | tf_op jit(solution)/shard_map/encoder_sum/pallas_call | solution.py:194
  (84 shorter events, 13.3 us)
Async XLA Ops:
  0.6 14.6 %collective-permute-start.1 = (bf16[128,3584]{1,0:T(8,128)(2,1)}, bf16[128,3584]{1,0:T(8,128)(2,1)S(1)}, u32[]{:S(2)}, u32[]{:S(2)}) collective-permute-start(bf16[128,3584]{1,0:T(8,128)(2,1)} %refs_8_.1), channel_id=1, source_target_pairs={{0,4},{4,8},{8,12},{12,14},{14,10},{10,6},{6,2},{2,0},{1,3},{5,1},... | collective-permute-start | bytes 2752520 | tf_op jit(solution)/shard_map/ppermute | solution.py:208
  15.2 16.0 %collective-permute-start.2 = (bf16[128,3584]{1,0:T(8,128)(2,1)S(1)}, bf16[128,3584]{1,0:T(8,128)(2,1)S(1)}, u32[]{:S(2)}, u32[]{:S(2)}) collective-permute-start(bf16[128,3584]{1,0:T(8,128)(2,1)S(1)} %collective-permute-done.1.mine_ref.refs_10_), channel_id=1, source_target_pairs={{0,1},{1,0},{2,3},{3,2},{4,5},{5,4},{6,7},{7,6},{8,9},{9,8},{10,11... | collective-permute-start | bytes 2752520 | tf_op jit(solution)/shard_map/ppermute | solution.py:208
  16.7 14.5 %all-to-all-start = ((bf16[16,32,128]{2,1,0:T(8,128)(2,1)}), bf16[16,32,128]{2,1,0:T(8,128)(2,1)S(1)}, u32[]{:S(2)}, u32[]{:S(2)}) async-start(bf16[16,32,128]{2,1,0:T(8,128)(2,1)} %pad_maximum_fusion), calls=%async_computation | async-start | bytes 262144 | tf_op jit(solution)/shard_map/all_to_all | solution.py:151
  23.3 9.7 %collective-permute-start = (bf16[128,3584]{1,0:T(8,128)(2,1)}, bf16[128,3584]{1,0:T(8,128)(2,1)}, u32[]{:S(2)}, u32[]{:S(2)}) collective-permute-start(bf16[128,3584]{1,0:T(8,128)(2,1)} %refs_8_.1), channel_id=1, source_target_pairs={{0,1},{1,0},{2,3},{3,2},{4,5},{5,4},{6,7},{7,6},{8,9},{9,8},{10,11... | collective-permute-start | bytes 2752520 | tf_op jit(solution)/shard_map/ppermute | solution.py:208
  31.2 13.4 %collective-permute-start.3 = (bf16[128,3584]{1,0:T(8,128)(2,1)S(1)}, bf16[128,3584]{1,0:T(8,128)(2,1)S(1)}, u32[]{:S(2)}, u32[]{:S(2)}) collective-permute-start(bf16[128,3584]{1,0:T(8,128)(2,1)S(1)} %collective-permute-done.1.mine_ref.refs_10_), channel_id=1, source_target_pairs={{0,4},{4,8},{8,12},{12,14},{14,10},{10,6},{6,2},{2,0},{1,3},{5,1},... | collective-permute-start | bytes 2752520 | tf_op jit(solution)/shard_map/ppermute | solution.py:208
  31.2 13.4 %collective-permute-start.14 = (bf16[128,3584]{1,0:T(8,128)(2,1)}, bf16[128,3584]{1,0:T(8,128)(2,1)}, u32[]{:S(2)}, u32[]{:S(2)}) collective-permute-start(bf16[128,3584]{1,0:T(8,128)(2,1)} %refs_5_.1), channel_id=1, source_target_pairs={{0,1},{1,0},{2,3},{3,2},{4,5},{5,4},{6,7},{7,6},{8,9},{9,8},{10,11... | collective-permute-start | bytes 2752520 | tf_op jit(solution)/shard_map/ppermute | solution.py:208
  31.2 23.3 %collective-permute-start.15 = (bf16[128,3584]{1,0:T(8,128)(2,1)}, bf16[128,3584]{1,0:T(8,128)(2,1)}, u32[]{:S(2)}, u32[]{:S(2)}) collective-permute-start(bf16[128,3584]{1,0:T(8,128)(2,1)} %refs_5_.1), channel_id=1, source_target_pairs={{0,4},{4,8},{8,12},{12,14},{14,10},{10,6},{6,2},{2,0},{1,3},{5,1},... | collective-permute-start | bytes 2752520 | tf_op jit(solution)/shard_map/ppermute | solution.py:208
  44.6 19.7 %collective-permute-start.5 = (bf16[128,3584]{1,0:T(8,128)(2,1)S(1)}, bf16[128,3584]{1,0:T(8,128)(2,1)S(1)}, u32[]{:S(2)}, u32[]{:S(2)}) collective-permute-start(bf16[128,3584]{1,0:T(8,128)(2,1)S(1)} %collective-permute-done.3.mine_ref.refs_12_), channel_id=1, source_target_pairs={{0,4},{4,8},{8,12},{12,14},{14,10},{10,6},{6,2},{2,0},{1,3},{5,1},... | collective-permute-start | bytes 2752520 | tf_op jit(solution)/shard_map/ppermute | solution.py:208
  44.6 19.7 %collective-permute-start.4 = (bf16[128,3584]{1,0:T(8,128)(2,1)S(1)}, bf16[128,3584]{1,0:T(8,128)(2,1)S(1)}, u32[]{:S(2)}, u32[]{:S(2)}) collective-permute-start(bf16[128,3584]{1,0:T(8,128)(2,1)S(1)} %collective-permute-done.3.mine_ref.refs_12_), channel_id=1, source_target_pairs={{0,1},{1,0},{2,3},{3,2},{4,5},{5,4},{6,7},{7,6},{8,9},{9,8},{10,11... | collective-permute-start | bytes 2752520 | tf_op jit(solution)/shard_map/ppermute | solution.py:208
  54.5 12.3 %collective-permute-start.16 = (bf16[128,3584]{1,0:T(8,128)(2,1)}, bf16[128,3584]{1,0:T(8,128)(2,1)S(1)}, u32[]{:S(2)}, u32[]{:S(2)}) collective-permute-start(bf16[128,3584]{1,0:T(8,128)(2,1)} %collective-permute-done.15.refs_7_), channel_id=1, source_target_pairs={{0,1},{1,0},{2,3},{3,2},{4,5},{5,4},{6,7},{7,6},{8,9},{9,8},{10,11... | collective-permute-start | bytes 2752520 | tf_op jit(solution)/shard_map/ppermute | solution.py:208
  54.5 19.6 %collective-permute-start.17 = (bf16[128,3584]{1,0:T(8,128)(2,1)}, bf16[128,3584]{1,0:T(8,128)(2,1)S(1)}, u32[]{:S(2)}, u32[]{:S(2)}) collective-permute-start(bf16[128,3584]{1,0:T(8,128)(2,1)} %collective-permute-done.15.refs_7_), channel_id=1, source_target_pairs={{0,4},{4,8},{8,12},{12,14},{14,10},{10,6},{6,2},{2,0},{1,3},{5,1},... | collective-permute-start | bytes 2752520 | tf_op jit(solution)/shard_map/ppermute | solution.py:208
  64.3 9.8 %collective-permute-start.6 = (bf16[128,3584]{1,0:T(8,128)(2,1)S(1)}, bf16[128,3584]{1,0:T(8,128)(2,1)S(1)}, u32[]{:S(2)}, u32[]{:S(2)}) collective-permute-start(bf16[128,3584]{1,0:T(8,128)(2,1)S(1)} %collective-permute-done.5.mine_ref.refs_14_), channel_id=1, source_target_pairs={{0,1},{1,0},{2,3},{3,2},{4,5},{5,4},{6,7},{7,6},{8,9},{9,8},{10,11... | collective-permute-start | bytes 2752520 | tf_op jit(solution)/shard_map/ppermute | solution.py:208
  66.8 17.1 %collective-permute-start.7 = (bf16[128,3584]{1,0:T(8,128)(2,1)S(1)}, bf16[128,3584]{1,0:T(8,128)(2,1)S(1)}, u32[]{:S(2)}, u32[]{:S(2)}) collective-permute-start(bf16[128,3584]{1,0:T(8,128)(2,1)S(1)} %collective-permute-done.5.mine_ref.refs_14_), channel_id=1, source_target_pairs={{0,4},{4,8},{8,12},{12,14},{14,10},{10,6},{6,2},{2,0},{1,3},{5,1},... | collective-permute-start | bytes 2752520 | tf_op jit(solution)/shard_map/ppermute | solution.py:208
  74.1 9.8 %collective-permute-start.18 = (bf16[128,3584]{1,0:T(8,128)(2,1)S(1)}, bf16[128,3584]{1,0:T(8,128)(2,1)S(1)}, u32[]{:S(2)}, u32[]{:S(2)}) collective-permute-start(bf16[128,3584]{1,0:T(8,128)(2,1)S(1)} %collective-permute-done.17.refs_9_), channel_id=1, source_target_pairs={{0,1},{1,0},{2,3},{3,2},{4,5},{5,4},{6,7},{7,6},{8,9},{9,8},{10,11... | collective-permute-start | bytes 2752520 | tf_op jit(solution)/shard_map/ppermute | solution.py:208
  74.1 19.7 %collective-permute-start.19 = (bf16[128,3584]{1,0:T(8,128)(2,1)S(1)}, bf16[128,3584]{1,0:T(8,128)(2,1)S(1)}, u32[]{:S(2)}, u32[]{:S(2)}) collective-permute-start(bf16[128,3584]{1,0:T(8,128)(2,1)S(1)} %collective-permute-done.17.refs_9_), channel_id=1, source_target_pairs={{0,4},{4,8},{8,12},{12,14},{14,10},{10,6},{6,2},{2,0},{1,3},{5,1},... | collective-permute-start | bytes 2752520 | tf_op jit(solution)/shard_map/ppermute | solution.py:208
  83.9 19.7 %collective-permute-start.9 = (bf16[128,3584]{1,0:T(8,128)(2,1)S(1)}, bf16[128,3584]{1,0:T(8,128)(2,1)S(1)}, u32[]{:S(2)}, u32[]{:S(2)}) collective-permute-start(bf16[128,3584]{1,0:T(8,128)(2,1)S(1)} %collective-permute-done.7.mine_ref.refs_16_), channel_id=1, source_target_pairs={{0,4},{4,8},{8,12},{12,14},{14,10},{10,6},{6,2},{2,0},{1,3},{5,1},... | collective-permute-start | bytes 2752520 | tf_op jit(solution)/shard_map/ppermute | solution.py:208
  83.9 19.7 %collective-permute-start.8 = (bf16[128,3584]{1,0:T(8,128)(2,1)S(1)}, bf16[128,3584]{1,0:T(8,128)(2,1)S(1)}, u32[]{:S(2)}, u32[]{:S(2)}) collective-permute-start(bf16[128,3584]{1,0:T(8,128)(2,1)S(1)} %collective-permute-done.7.mine_ref.refs_16_), channel_id=1, source_target_pairs={{0,1},{1,0},{2,3},{3,2},{4,5},{5,4},{6,7},{7,6},{8,9},{9,8},{10,11... | collective-permute-start | bytes 2752520 | tf_op jit(solution)/shard_map/ppermute | solution.py:208
  93.8 12.4 %collective-permute-start.20 = (bf16[128,3584]{1,0:T(8,128)(2,1)S(1)}, bf16[128,3584]{1,0:T(8,128)(2,1)S(1)}, u32[]{:S(2)}, u32[]{:S(2)}) collective-permute-start(bf16[128,3584]{1,0:T(8,128)(2,1)S(1)} %collective-permute-done.19.refs_11_), channel_id=1, source_target_pairs={{0,1},{1,0},{2,3},{3,2},{4,5},{5,4},{6,7},{7,6},{8,9},{9,8},{10,11... | collective-permute-start | bytes 2752520 | tf_op jit(solution)/shard_map/ppermute | solution.py:208
  93.8 19.7 %collective-permute-start.21 = (bf16[128,3584]{1,0:T(8,128)(2,1)S(1)}, bf16[128,3584]{1,0:T(8,128)(2,1)S(1)}, u32[]{:S(2)}, u32[]{:S(2)}) collective-permute-start(bf16[128,3584]{1,0:T(8,128)(2,1)S(1)} %collective-permute-done.19.refs_11_), channel_id=1, source_target_pairs={{0,4},{4,8},{8,12},{12,14},{14,10},{10,6},{6,2},{2,0},{1,3},{5,1},... | collective-permute-start | bytes 2752520 | tf_op jit(solution)/shard_map/ppermute | solution.py:208
  103.6 9.8 %collective-permute-start.10 = (bf16[128,3584]{1,0:T(8,128)(2,1)S(1)}, bf16[128,3584]{1,0:T(8,128)(2,1)S(1)}, u32[]{:S(2)}, u32[]{:S(2)}) collective-permute-start(bf16[128,3584]{1,0:T(8,128)(2,1)S(1)} %collective-permute-done.9.mine_ref.refs_18_), channel_id=1, source_target_pairs={{0,1},{1,0},{2,3},{3,2},{4,5},{5,4},{6,7},{7,6},{8,9},{9,8},{10,11... | collective-permute-start | bytes 2752520 | tf_op jit(solution)/shard_map/ppermute | solution.py:208
  106.1 17.1 %collective-permute-start.11 = (bf16[128,3584]{1,0:T(8,128)(2,1)S(1)}, bf16[128,3584]{1,0:T(8,128)(2,1)S(1)}, u32[]{:S(2)}, u32[]{:S(2)}) collective-permute-start(bf16[128,3584]{1,0:T(8,128)(2,1)S(1)} %collective-permute-done.9.mine_ref.refs_18_), channel_id=1, source_target_pairs={{0,4},{4,8},{8,12},{12,14},{14,10},{10,6},{6,2},{2,0},{1,3},{5,1},... | collective-permute-start | bytes 2752520 | tf_op jit(solution)/shard_map/ppermute | solution.py:208
  113.4 9.8 %collective-permute-start.22 = (bf16[128,3584]{1,0:T(8,128)(2,1)S(1)}, bf16[128,3584]{1,0:T(8,128)(2,1)S(1)}, u32[]{:S(2)}, u32[]{:S(2)}) collective-permute-start(bf16[128,3584]{1,0:T(8,128)(2,1)S(1)} %collective-permute-done.21.refs_13_), channel_id=1, source_target_pairs={{0,1},{1,0},{2,3},{3,2},{4,5},{5,4},{6,7},{7,6},{8,9},{9,8},{10,11... | collective-permute-start | bytes 2752520 | tf_op jit(solution)/shard_map/ppermute | solution.py:208
  113.4 19.7 %collective-permute-start.24 = (bf16[128,3584]{1,0:T(8,128)(2,1)S(1)}, bf16[128,3584]{1,0:T(8,128)(2,1)S(1)}, u32[]{:S(2)}, u32[]{:S(2)}) collective-permute-start(bf16[128,3584]{1,0:T(8,128)(2,1)S(1)} %collective-permute-done.21.refs_13_), channel_id=1, source_target_pairs={{0,4},{4,8},{8,12},{12,14},{14,10},{10,6},{6,2},{2,0},{1,3},{5,1},... | collective-permute-start | bytes 2752520 | tf_op jit(solution)/shard_map/ppermute | solution.py:208
  123.2 19.7 %collective-permute-start.13 = (bf16[128,3584]{1,0:T(8,128)(2,1)S(1)}, bf16[128,3584]{1,0:T(8,128)(2,1)S(1)}, u32[]{:S(2)}, u32[]{:S(2)}) collective-permute-start(bf16[128,3584]{1,0:T(8,128)(2,1)S(1)} %collective-permute-done.11.mine_ref.refs_20_), channel_id=1, source_target_pairs={{0,4},{4,8},{8,12},{12,14},{14,10},{10,6},{6,2},{2,0},{1,3},{5,1},... | collective-permute-start | bytes 2752520 | tf_op jit(solution)/shard_map/ppermute | solution.py:208
  123.2 19.7 %collective-permute-start.12 = (bf16[128,3584]{1,0:T(8,128)(2,1)S(1)}, bf16[128,3584]{1,0:T(8,128)(2,1)S(1)}, u32[]{:S(2)}, u32[]{:S(2)}) collective-permute-start(bf16[128,3584]{1,0:T(8,128)(2,1)S(1)} %collective-permute-done.11.mine_ref.refs_20_), channel_id=1, source_target_pairs={{0,1},{1,0},{2,3},{3,2},{4,5},{5,4},{6,7},{7,6},{8,9},{9,8},{10,11... | collective-permute-start | bytes 2752520 | tf_op jit(solution)/shard_map/ppermute | solution.py:208
  133.1 12.4 %collective-permute-start.25 = (bf16[128,3584]{1,0:T(8,128)(2,1)S(1)}, bf16[128,3584]{1,0:T(8,128)(2,1)S(1)}, u32[]{:S(2)}, u32[]{:S(2)}) collective-permute-start(bf16[128,3584]{1,0:T(8,128)(2,1)S(1)} %collective-permute-done.24.refs_3_), channel_id=1, source_target_pairs={{0,1},{1,0},{2,3},{3,2},{4,5},{5,4},{6,7},{7,6},{8,9},{9,8},{10,11... | collective-permute-start | bytes 2752520 | tf_op jit(solution)/shard_map/ppermute | solution.py:208
  133.1 19.8 %collective-permute-start.26 = (bf16[128,3584]{1,0:T(8,128)(2,1)S(1)}, bf16[128,3584]{1,0:T(8,128)(2,1)}, u32[]{:S(2)}, u32[]{:S(2)}) collective-permute-start(bf16[128,3584]{1,0:T(8,128)(2,1)S(1)} %collective-permute-done.24.refs_3_), channel_id=1, source_target_pairs={{0,4},{4,8},{8,12},{12,14},{14,10},{10,6},{6,2},{2,0},{1,3},{5,1},... | collective-permute-start | bytes 2752520 | tf_op jit(solution)/shard_map/ppermute | solution.py:208
  142.9 9.9 %collective-permute-start.23 = (bf16[128,3584]{1,0:T(8,128)(2,1)S(1)}, bf16[128,3584]{1,0:T(8,128)(2,1)S(1)}, u32[]{:S(2)}, u32[]{:S(2)}) collective-permute-start(bf16[128,3584]{1,0:T(8,128)(2,1)S(1)} %collective-permute-done.13.mine_ref.refs_22_), channel_id=1, source_target_pairs={{0,1},{1,0},{2,3},{3,2},{4,5},{5,4},{6,7},{7,6},{8,9},{9,8},{10,11... | collective-permute-start | bytes 2752520 | tf_op jit(solution)/shard_map/ppermute | solution.py:208
  152.8 13.7 %collective-permute-start.28 = (bf16[128,3584]{1,0:T(8,128)(2,1)}, bf16[128,3584]{1,0:T(8,128)(2,1)}, u32[]{:S(2)}, u32[]{:S(2)}) collective-permute-start(bf16[128,3584]{1,0:T(8,128)(2,1)} %collective-permute-done.26.refs_5_), channel_id=1, source_target_pairs={{0,4},{4,8},{8,12},{12,14},{14,10},{10,6},{6,2},{2,0},{1,3},{5,1},... | collective-permute-start | bytes 2752520 | tf_op jit(solution)/shard_map/ppermute | solution.py:208
  152.8 25.8 %collective-permute-start.27 = (bf16[128,3584]{1,0:T(8,128)(2,1)}, bf16[128,3584]{1,0:T(8,128)(2,1)}, u32[]{:S(2)}, u32[]{:S(2)}) collective-permute-start(bf16[128,3584]{1,0:T(8,128)(2,1)} %collective-permute-done.26.refs_5_), channel_id=1, source_target_pairs={{0,1},{1,0},{2,3},{3,2},{4,5},{5,4},{6,7},{7,6},{8,9},{9,8},{10,11... | collective-permute-start | bytes 2752520 | tf_op jit(solution)/shard_map/ppermute | solution.py:208
  166.6 12.1 %collective-permute-start.29 = (bf16[128,3584]{1,0:T(8,128)(2,1)}, bf16[128,3584]{1,0:T(8,128)(2,1)S(1)}, u32[]{:S(2)}, u32[]{:S(2)}) collective-permute-start(bf16[128,3584]{1,0:T(8,128)(2,1)} %collective-permute-done.28.refs_7_), channel_id=1, source_target_pairs={{0,1},{1,0},{2,3},{3,2},{4,5},{5,4},{6,7},{7,6},{8,9},{9,8},{10,11... | collective-permute-start | bytes 2752520 | tf_op jit(solution)/shard_map/ppermute | solution.py:208
  166.6 11.4 %all-to-all-start.1 = ((f32[16,16,128]{2,1,0:T(8,128)}), f32[16,16,128]{2,1,0:T(8,128)S(1)}, u32[]{:S(2)}, u32[]{:S(2)}) async-start(f32[16,16,128]{2,1,0:T(8,128)} %get-tuple-element.97), calls=%async_computation.1 | async-start | bytes 262144 | tf_op jit(solution)/shard_map/all_to_all | solution.py:231
  (14 other events, 72.5 us)

commit v5 on v4

--- a/solution.py
+++ b/solution.py
@@ -32,27 +32,24 @@
     return sources, onward, swap
 
 
-def product_kernel(per_block, order_ref, meta_ref, decoder_ref, mine_ref, theirs_ref, *refs):
-    acts_ref, pre_ref, lat_ref, bias_ref, rows_ref, sems = refs[-6:]
-    tokens = mine_ref.shape[0]
-    copies = [
-        pltpu.make_async_copy(source, rows_ref.at[pl.ds(i * tokens, tokens)], sems.at[i])
-        for i, source in enumerate((mine_ref, theirs_ref))
-    ]
-    for copy in copies:
-        copy.start()
-    if len(refs) == 8:
-        lat_ref[...] = refs[0][...]
-        bias_ref[...] = refs[1][...]
-    else:
+def grad_kernel(per_block, order_ref, meta_ref, decoder_ref, mine_ref, theirs_ref, *refs):
+    total_ref, lat_ref, bias_ref, pre_ref, acts_ref = refs[-5:]
+    first = len(refs) == 5
+    if first:
         lat_ref[...] = jnp.zeros_like(lat_ref)
         bias_ref[...] = jnp.zeros_like(bias_ref)
-    latents = decoder_ref.shape[0]
-    for copy in copies:
-        copy.wait()
-    products = lax.dot_general(
-        decoder_ref[...], rows_ref[...], (((1,), (1,)), ((), ())), preferred_element_type=jnp.float32
-    )
+    else:
+        lat_ref[...] = refs[1][...]
+        bias_ref[...] = refs[2][...]
+    latents, width = decoder_ref.shape
+    tokens = mine_ref.shape[0]
+    span = column_span(width)
+    products = jnp.zeros((latents, 2 * tokens), jnp.float32)
+    for at in range(0, width, span):
+        rows = jnp.concatenate([mine_ref[:, at : at + span], theirs_ref[:, at : at + span]], axis=0)
+        products += lax.dot_general(
+            decoder_ref[:, at : at + span], rows, (((1,), (1,)), ((), ())), preferred_element_type=jnp.float32
+        )
     row = lax.broadcasted_iota(jnp.int32, (8, tokens), 0)
     for tile in range(2):
         meta = meta_ref[order_ref[tile]].astype(jnp.float32)
@@ -80,46 +77,28 @@
         source = order_ref[tile]
         for k in range(per_block):
             lat_ref[source, k : k + 1, :] = jnp.sum(sums[k], axis=0, keepdims=True)
-
-
-def decoder_kernel(steps, span, *refs):
-    acts, rows, out_ref = refs[:steps], refs[steps : 3 * steps], refs[-1]
-
-    def body(*blocks):
-        total = jnp.zeros(blocks[-1].shape, jnp.float32)
-        for s in range(steps):
-            both = jnp.concatenate([blocks[2 * s][...], blocks[2 * s + 1][...]], axis=0)
-            total += jnp.dot(acts[s][...], both, preferred_element_type=jnp.float32)
-        blocks[-1][...] = total.astype(out_ref.dtype)
-
-    tokens, width = rows[0].shape
-    pltpu.emit_pipeline(
-        body,
-        grid=(width // span,),
-        in_specs=[pl.BlockSpec((tokens, span), lambda i: (0, i))] * (2 * steps),
-        out_specs=[pl.BlockSpec((out_ref.shape[0], span), lambda i: (0, i))],
-    )(*rows, out_ref)
-
-
-def encoder_kernel(steps, span, *refs):
-    pres, rows, refs = refs[:steps], refs[steps : 3 * steps], refs[3 * steps :]
-    out_ref = refs[-1]
-
-    def body(*blocks):
-        total = blocks[2 * steps][...] if len(refs) == 2 else jnp.zeros(blocks[-1].shape, jnp.float32)
-        for s in range(steps):
-            both = jnp.concatenate([blocks[2 * s][...], blocks[2 * s + 1][...]], axis=0)
-            total += lax.dot_general(both, pres[s][...], (((0,), (1,)), ((), ())), preferred_element_type=jnp.float32)
-        blocks[-1][...] = total.astype(out_ref.dtype)
-
-    tokens, width = rows[0].shape
-    sums = pl.BlockSpec((span, out_ref.shape[1]), lambda i: (i, 0))
-    pltpu.emit_pipeline(
-        body,
-        grid=(width // span,),
-        in_specs=[pl.BlockSpec((tokens, span), lambda i: (0, i))] * (2 * steps) + [sums] * (len(refs) - 1),
-        out_specs=[sums],
-    )(*rows, *refs)
+    for at in range(0, width, span):
+        rows = jnp.concatenate([mine_ref[:, at : at + span], theirs_ref[:, at : at + span]], axis=0)
+        term = jnp.dot(acts_ref[...], rows, preferred_element_type=jnp.float32)
+        if not first:
+            term += refs[0][:, at : at + span]
+        total_ref[:, at : at + span] = term.astype(total_ref.dtype)
+
+
+def input_kernel(pre_ref, mine_ref, theirs_ref, *refs):
+    total_ref = refs[-1]
+    width = mine_ref.shape[1]
+    span = column_span(width)
+    for at in range(0, width, span):
+        rows = jnp.concatenate([mine_ref[:, at : at + span], theirs_ref[:, at : at + span]], axis=0)
+        term = lax.dot_general(rows, pre_ref[...], (((0,), (1,)), ((), ())), preferred_element_type=jnp.float32)
+        if len(refs) == 2:
+            term += refs[0][at : at + span, :]
+        total_ref[at : at + span, :] = term.astype(total_ref.dtype)
+
+
+def column_span(width):
+    return 512 if width % 512 == 0 else BLOCK
 
 
 def after(value, *others):
@@ -152,89 +131,75 @@
 
     whole = pl.BlockSpec(memory_space=pltpu.VMEM)
     scalars = pl.BlockSpec(memory_space=pltpu.SMEM)
-    far = pl.BlockSpec(memory_space=pltpu.HBM)
     step_tokens = 2 * token_count
     light = pl.CostEstimate(flops=1, bytes_accessed=1, transcendentals=0)
     params = pltpu.CompilerParams(vmem_limit_bytes=VMEM_BYTES)
 
-    def products(step, rows, totals):
+    def near(value):
+        return pltpu.with_memory_space_constraint(value, pltpu.VMEM)
+
+    def grad_step(hop, rows, totals):
+        last = hop == chips - 1
+        sums = (latent_count, width)
         return pl.pallas_call(
-            functools.partial(product_kernel, per_block),
-            in_specs=[scalars, whole, whole, far, far] + [whole] * len(totals),
+            functools.partial(grad_kernel, per_block),
+            in_specs=[scalars] + [whole] * (4 + len(totals)),
             out_specs=[whole] * 4,
             out_shape=[
-                jax.ShapeDtypeStruct((latent_count, step_tokens), jnp.bfloat16),
-                jax.ShapeDtypeStruct((latent_count, step_tokens), jnp.bfloat16),
-                jax.ShapeDtypeStruct((peer_count, per_block, token_count), jnp.float32),
-                jax.ShapeDtypeStruct((latent_count, token_count), jnp.float32),
+                jax.ShapeDtypeStruct(sums, jnp.bfloat16) if last else pltpu.VMEM(sums, jnp.float32),
+                pltpu.VMEM((peer_count, per_block, token_count), jnp.float32),
+                pltpu.VMEM((latent_count, token_count), jnp.float32),
+                pltpu.VMEM((latent_count, step_tokens), jnp.bfloat16),
             ],
-            scratch_shapes=[pltpu.VMEM((step_tokens, width), jnp.bfloat16), pltpu.SemaphoreType.DMA((2,))],
+            scratch_shapes=[pltpu.VMEM((latent_count, step_tokens), jnp.bfloat16)],
+            input_output_aliases={5 + i: i for i in range(1 if last else 0, len(totals))},
             compiler_params=params,
             cost_estimate=light,
-            name="products",
-        )(order[step], meta, decoder, *rows, *totals)
-
-    span = 512 if width % 512 == 0 else BLOCK
-
-    def decoder_sum(acts, rows):
-        steps = len(acts)
+            name="grad_step",
+        )(order[hop], near(meta), near(decoder), near(rows[0]), near(rows[1]), *map(near, totals))
+
+    def input_step(hop, rows, total):
+        last = hop == chips - 1
+        sums = (width, latent_count)
+        totals = () if total is None else (total,)
         return pl.pallas_call(
-            functools.partial(decoder_kernel, steps, span),
-            in_specs=[whole] * steps + [far] * (2 * steps),
-            out_specs=far,
-            out_shape=jax.ShapeDtypeStruct((latent_count, width), jnp.bfloat16),
+            input_kernel,
+            in_specs=[whole] * (3 + len(totals)),
+            out_specs=whole,
+            out_shape=jax.ShapeDtypeStruct(sums, jnp.bfloat16) if last else pltpu.VMEM(sums, jnp.float32),
+            input_output_aliases={3: 0} if totals and not last else {},
             compiler_params=params,
             cost_estimate=light,
-            name="decoder_sum",
-        )(*acts, *[part for pair in rows for part in pair])
-
-    def encoder_sum(pres, rows, partial, dtype):
-        steps = len(pres)
-        partials = [] if partial is None else [partial]
-        return pl.pallas_call(
-            functools.partial(encoder_kernel, steps, span),
-            in_specs=[whole] * steps + [far] * (2 * steps + len(partials)),
-            out_specs=far,
-            out_shape=jax.ShapeDtypeStruct((width, latent_count), dtype),
-            compiler_params=params,
-            cost_estimate=light,
-            name="encoder_sum",
-        )(*pres, *[part for pair in rows for part in pair], *partials)
-
-    acts, pres, totals = [], [], ()
-    grads, ins = [], [inputs]
+            name="input_step",
+        )(near(pres[hop]), near(rows[0]), near(rows[1]), *map(near, totals))
 
     def send(rows, way, *first):
         return lax.ppermute(after(rows, *first) if first else rows, "lat", way)
 
-    def compute(rows):
+    pres, totals, encoder_total = [], (), None
+
+    def use_grads(rows):
         nonlocal totals
-        grads.append(rows)
-        acts_here, pre_here, *totals = products(len(acts), rows, totals)
-        acts.append(acts_here)
-        pres.append(pre_here)
-
-    arriving = send(grad_recon, onward)
-    compute((grad_recon, send(grad_recon, swap)))
-    partial = None
+        *totals, pre = grad_step(len(pres), rows, totals)
+        pres.append(pre)
+
+    grad, inward = send(grad_recon, onward), send(inputs, onward)
+    use_grads((grad_recon, send(grad_recon, swap)))
+    encoder_total = input_step(0, (inputs, send(inputs, swap, meta)), None)
+    grad_next = send(grad, onward, meta)
     for hop in range(1, chips):
-        grad = arriving
+        use_grads((grad, send(grad, swap)))
+        pair = (inward, send(inward, swap, *((totals[2], encoder_total) if hop == chips - 1 else ())))
         if hop < chips - 1:
-            arriving = send(grad, onward, *((meta,) if hop == 1 else (totals[1],)))
-        theirs = send(grad, swap, *(() if partial is None else (partial,)))
-        moved = send(ins[hop - 1], onward, *((theirs,) if hop == 1 else (ins[hop - 2][1],)), *(totals if hop == chips - 1 else ()))
-        compute((grad, theirs))
-        ins[hop - 1] = (ins[hop - 1], send(ins[hop - 1], swap))
-        ins.append(moved)
-        if hop == chips - 2:
-            partial = encoder_sum(pres[: hop - 1], ins[: hop - 1], None, jnp.float32)
-    returned = lax.all_to_all(totals[0], "lat", split_axis=0, concat_axis=0, tiled=True)
-    latent_grads = pick_returned(returned, own_t)
-    decoder_grad = decoder_sum(acts, grads)
-    ins[-1] = (ins[-1], send(ins[-1], swap, decoder_grad))
-    bias_grad = jnp.sum(totals[1], axis=1)
-    encoder_grad = encoder_sum(pres[chips - 3 :], ins[chips - 3 :], partial, jnp.bfloat16)
-    return (decoder_grad, encoder_grad, bias_grad, latent_grads)
+            inward = send(inward, onward, totals[2])
+        encoder_total = input_step(hop, pair, encoder_total)
+        grad = grad_next
+        if hop < chips - 2:
+            grad_next = send(grad, onward, encoder_total)
+    decoder_grad, lat, bias = totals
+    returned = lax.all_to_all(lat, "lat", split_axis=0, concat_axis=0, tiled=True)
+    latent_grads = pick_returned(after(returned, encoder_total), own_t)
+    return (decoder_grad, encoder_total, jnp.sum(bias, axis=1), latent_grads)
 
 
 def pick_returned(returned, own_t):

time: 193 us -> 170 us (0.88)
  waiting for transfers between devices: 117 us -> 81.9 us
  starting transfers between devices: 14.8 us -> 33.4 us
  local copies, waits for them, and re-layouts: 11.5 us -> 7.02 us
    ppermute x30, waiting for transfers between devices: 102 us -> 71.4 us  [send(): return lax.ppermute(after(rows, *first) if first else rows, 'lat', way)]
    ppermute x30, starting transfers between devices: 4.76 us -> 23.3 us  [send(): return lax.ppermute(after(rows, *first) if first else rows, 'lat', way)]
    unnamed x28 -> x14, local copies, waits for them, and re-layouts: 9.24 us -> 4.74 us
    all_to_all x1, waiting for transfers between devices: 7.19 us -> 3.22 us  [by_ring(): lax.all_to_all(lat, 'lat', split_axis=0, concat_axis=0, tiled=True)]
    pallas_call x11 -> x16, Pallas kernels: 44.6 us -> 42.7 us  [the longest x8 31.8 us: grad_step(): pl.pallas_call(functools.partial(grad_kernel, per_block), in_specs=[scala...]
  transfers between devices with their start and end apart: 32 -> 32, of which waited for: 16 -> 15; matrix products, arithmetic and copies ran while one was open for 3% -> 3% of each run, Pallas kernels for 20% -> 25%
where the time goes in v5:
time: 170 us; the launch traced here: 169 us
  waiting for transfers between devices  81.9 us (48%)
  Pallas kernels  42.7 us (25%)
  starting transfers between devices  33.4 us (20%)
  local copies, waits for them, and re-layouts  7.02 us (4%)
  other arithmetic  3.59 us (2%)
    ppermute x30, waiting for transfers between devices, send(): return lax.ppermute(after(rows, *first) if first else rows, 'lat', way)  71.4 us
    pallas_call x8, Pallas kernels, grad_step(): pl.pallas_call(functools.partial(grad_kernel, per_block), in_specs=[scala...  31.8 us
    ppermute x30, starting transfers between devices, send(): return lax.ppermute(after(rows, *first) if first else rows, 'lat', way)  23.3 us
    pallas_call x8, Pallas kernels, input_step(): pl.pallas_call(input_kernel, in_specs=[whole] * (3 + len(totals)), out_sp...  10.9 us
    all_to_all x1, waiting for transfers between devices, by_ring(): meta = lax.all_to_all(meta, 'lat', split_axis=0, concat_axis=0, tiled=True)  7.23 us
    all_to_all x1, starting transfers between devices, by_ring(): meta = lax.all_to_all(meta, 'lat', split_axis=0, concat_axis=0, tiled=True)  6.54 us
    unnamed x14, local copies, waits for them, and re-layouts  4.74 us
    all_to_all x1, starting transfers between devices, by_ring(): lax.all_to_all(lat, 'lat', split_axis=0, concat_axis=0, tiled=True)  3.51 us
  transfers between devices with their start and end apart: 32, of which 15 were waited for; matrix products, arithmetic and copies ran while one was open for 3% of the time, Pallas kernels for 25%

profile of v5, /device:TPU:0, one launch (start us, length us, event | category | flops | bytes accessed | tf_op | source)
XLA Modules:
  0.0 169.4 jit_solution(11348385208959057345)
XLA Ops:
  0.6 3.1 %collective-permute-start = (bf16[128,3584]{1,0:T(8,128)(2,1)}, bf16[128,3584]{1,0:T(8,128)(2,1)S(1)}, u32[]{:S(2)}, u32[]{:S(2)}) collective-permute-start(bf16[128,3584]{1,0:T(8,128)(2,1)} %mine_ref.2), channel_id=1, source_target_pairs={{0,4},{4,8},{8,12},{12,14},{14,10},{10,6},{6,2},{2,0},{1,3},{5,1},... | collective-permute-start | bytes 2752520 | tf_op jit(solution)/shard_map/ppermute | solution.py:177
  7.6 7.6 %collective-permute-done.mine_ref = bf16[128,3584]{1,0:T(8,128)(2,1)S(1)} collective-permute-done((bf16[128,3584]{1,0:T(8,128)(2,1)}, bf16[128,3584]{1,0:T(8,128)(2,1)S(1)}, u32[]{:S(2)}, u32[]{:S(2)}) %collective-permute-start) | collective-permute-done | bytes 917536 | tf_op jit(solution)/shard_map/ppermute | solution.py:177
  16.7 6.5 %all-to-all-start = ((bf16[16,32,128]{2,1,0:T(8,128)(2,1)}), bf16[16,32,128]{2,1,0:T(8,128)(2,1)S(1)}, u32[]{:S(2)}, u32[]{:S(2)}) async-start(bf16[16,32,128]{2,1,0:T(8,128)(2,1)} %pad_maximum_fusion), calls=%async_computation | async-start | bytes 262144 | tf_op jit(solution)/shard_map/all_to_all | solution.py:130
  24.0 7.2 %all-to-all-done.meta_ref = bf16[16,32,128]{2,1,0:T(8,128)(2,1)S(1)} async-done(((bf16[16,32,128]{2,1,0:T(8,128)(2,1)}), bf16[16,32,128]{2,1,0:T(8,128)(2,1)S(1)}, u32[]{:S(2)}, u32[]{:S(2)}) %all-to-all-start) | async-done | bytes 131104 | tf_op jit(solution)/shard_map/all_to_all | solution.py:130
  34.4 3.3 %grad_step.8 = (f32[256,3584]{1,0:T(8,128)S(1)}, f32[16,16,128]{2,1,0:T(8,128)}, f32[256,128]{1,0:T(8,128)S(1)}, bf16[256,256]{1,0:T(8,128)(2,1)S(1)}) custom-call(s32[2]{0:T(128)S(1)} %get-tuple-element.113.order_ref, bf16[16,32,128]{2,1,0:T(8,128)(2,1)S(1)} %all-to-all-done.meta_ref, bf16[256,3584]{1,0:T(8,128)(2,1)S(1)} %copy-done.2, ...), custom_call_target="tpu_custom_call" | custom-call | flops 1 | bytes 1 | tf_op jit(solution)/shard_map/grad_step/pallas_call | solution.py:144
  37.7 4.3 %grad_step.9 = (f32[256,3584]{1,0:T(8,128)S(1)}, f32[16,16,128]{2,1,0:T(8,128)}, f32[256,128]{1,0:T(8,128)S(1)}, bf16[256,256]{1,0:T(8,128)(2,1)S(1)}) custom-call(s32[2]{0:T(128)S(1)} %get-tuple-element.114.order_ref, bf16[16,32,128]{2,1,0:T(8,128)(2,1)S(1)} %all-to-all-done.meta_ref, ...), custom_call_target="tpu_custom_call", output_to_operand_aliasing={{0}: (5, {}), {1}: (6, {}), {2}: (7, {})} | custom-call | flops 1 | bytes 1 | tf_op jit(solution)/shard_map/grad_step/pallas_call | solution.py:144
  46.8 8.6 %collective-permute-done.9.mine_ref = bf16[128,3584]{1,0:T(8,128)(2,1)S(1)} collective-permute-done((bf16[128,3584]{1,0:T(8,128)(2,1)S(1)}, bf16[128,3584]{1,0:T(8,128)(2,1)S(1)}, u32[]{:S(2)}, u32[]{:S(2)}) %collective-permute-start.9) | collective-permute-done | bytes 917536 | tf_op jit(solution)/shard_map/ppermute | solution.py:177
  55.4 3.9 %grad_step.10 = (f32[256,3584]{1,0:T(8,128)S(1)}, f32[16,16,128]{2,1,0:T(8,128)}, f32[256,128]{1,0:T(8,128)S(1)}, bf16[256,256]{1,0:T(8,128)(2,1)S(1)}) custom-call(s32[2]{0:T(128)S(1)} %get-tuple-element.112.order_ref, bf16[16,32,128]{2,1,0:T(8,128)(2,1)S(1)} %all-to-all-done.meta_ref, ...), custom_call_target="tpu_custom_call", output_to_operand_aliasing={{0}: (5, {}), {1}: (6, {}), {2}: (7, {})} | custom-call | flops 1 | bytes 1 | tf_op jit(solution)/shard_map/grad_step/pallas_call | solution.py:144
  61.0 4.2 %collective-permute-done.7.mine_ref = bf16[128,3584]{1,0:T(8,128)(2,1)S(1)} collective-permute-done((bf16[128,3584]{1,0:T(8,128)(2,1)S(1)}, bf16[128,3584]{1,0:T(8,128)(2,1)S(1)}, u32[]{:S(2)}, u32[]{:S(2)}) %collective-permute-start.7) | collective-permute-done | bytes 917536 | tf_op jit(solution)/shard_map/ppermute | solution.py:177
  66.6 2.0 %collective-permute-start.11 = (bf16[128,3584]{1,0:T(8,128)(2,1)S(1)}, bf16[128,3584]{1,0:T(8,128)(2,1)S(1)}, u32[]{:S(2)}, u32[]{:S(2)}) collective-permute-start(bf16[128,3584]{1,0:T(8,128)(2,1)S(1)} %collective-permute-done.7.mine_ref), channel_id=1, source_target_pairs={{0,4},{4,8},{8,12},{12,14},{14,10},{10,6},{6,2},{2,0},{1,3},{5,1},... | collective-permute-start | bytes 2752520 | tf_op jit(solution)/shard_map/ppermute | solution.py:177
  68.6 6.4 %collective-permute-done.13.mine_ref = bf16[128,3584]{1,0:T(8,128)(2,1)S(1)} collective-permute-done((bf16[128,3584]{1,0:T(8,128)(2,1)S(1)}, bf16[128,3584]{1,0:T(8,128)(2,1)S(1)}, u32[]{:S(2)}, u32[]{:S(2)}) %collective-permute-start.13) | collective-permute-done | bytes 917536 | tf_op jit(solution)/shard_map/ppermute | solution.py:177
  75.1 3.9 %grad_step.11 = (f32[256,3584]{1,0:T(8,128)S(1)}, f32[16,16,128]{2,1,0:T(8,128)}, f32[256,128]{1,0:T(8,128)S(1)}, bf16[256,256]{1,0:T(8,128)(2,1)S(1)}) custom-call(s32[2]{0:T(128)S(1)} %get-tuple-element.111.order_ref, bf16[16,32,128]{2,1,0:T(8,128)(2,1)S(1)} %all-to-all-done.meta_ref, ...), custom_call_target="tpu_custom_call", output_to_operand_aliasing={{0}: (5, {}), {1}: (6, {}), {2}: (7, {})} | custom-call | flops 1 | bytes 1 | tf_op jit(solution)/shard_map/grad_step/pallas_call | solution.py:144
  80.7 4.2 %collective-permute-done.11.mine_ref = bf16[128,3584]{1,0:T(8,128)(2,1)S(1)} collective-permute-done((bf16[128,3584]{1,0:T(8,128)(2,1)S(1)}, bf16[128,3584]{1,0:T(8,128)(2,1)S(1)}, u32[]{:S(2)}, u32[]{:S(2)}) %collective-permute-start.11) | collective-permute-done | bytes 917536 | tf_op jit(solution)/shard_map/ppermute | solution.py:177
  86.3 1.8 %collective-permute-start.15 = (bf16[128,3584]{1,0:T(8,128)(2,1)S(1)}, bf16[128,3584]{1,0:T(8,128)(2,1)S(1)}, u32[]{:S(2)}, u32[]{:S(2)}) collective-permute-start(bf16[128,3584]{1,0:T(8,128)(2,1)S(1)} %collective-permute-done.11.mine_ref), channel_id=1, source_target_pairs={{0,4},{4,8},{8,12},{12,14},{14,10},{10,6},{6,2},{2,0},{1,3},{5,1},... | collective-permute-start | bytes 2752520 | tf_op jit(solution)/shard_map/ppermute | solution.py:177
  88.1 6.6 %collective-permute-done.17.mine_ref = bf16[128,3584]{1,0:T(8,128)(2,1)S(1)} collective-permute-done((bf16[128,3584]{1,0:T(8,128)(2,1)S(1)}, bf16[128,3584]{1,0:T(8,128)(2,1)S(1)}, u32[]{:S(2)}, u32[]{:S(2)}) %collective-permute-start.17) | collective-permute-done | bytes 917536 | tf_op jit(solution)/shard_map/ppermute | solution.py:177
  94.7 3.9 %grad_step.12 = (f32[256,3584]{1,0:T(8,128)S(1)}, f32[16,16,128]{2,1,0:T(8,128)}, f32[256,128]{1,0:T(8,128)S(1)}, bf16[256,256]{1,0:T(8,128)(2,1)S(1)}) custom-call(s32[2]{0:T(128)S(1)} %get-tuple-element.110.order_ref, bf16[16,32,128]{2,1,0:T(8,128)(2,1)S(1)} %all-to-all-done.meta_ref, ...), custom_call_target="tpu_custom_call", output_to_operand_aliasing={{0}: (5, {}), {1}: (6, {}), {2}: (7, {})} | custom-call | flops 1 | bytes 1 | tf_op jit(solution)/shard_map/grad_step/pallas_call | solution.py:144
  98.6 1.7 %collective-permute-start.21 = (bf16[128,3584]{1,0:T(8,128)(2,1)S(1)}, bf16[128,3584]{1,0:T(8,128)(2,1)S(1)}, u32[]{:S(2)}, u32[]{:S(2)}) collective-permute-start(bf16[128,3584]{1,0:T(8,128)(2,1)S(1)} %collective-permute-done.17.mine_ref), channel_id=1, source_target_pairs={{0,4},{4,8},{8,12},{12,14},{14,10},{10,6},{6,2},{2,0},{1,3},{5,1},... | collective-permute-start | bytes 2752520 | tf_op jit(solution)/shard_map/ppermute | solution.py:177
  100.4 4.2 %collective-permute-done.15.mine_ref = bf16[128,3584]{1,0:T(8,128)(2,1)S(1)} collective-permute-done((bf16[128,3584]{1,0:T(8,128)(2,1)S(1)}, bf16[128,3584]{1,0:T(8,128)(2,1)S(1)}, u32[]{:S(2)}, u32[]{:S(2)}) %collective-permute-start.15) | collective-permute-done | bytes 917536 | tf_op jit(solution)/shard_map/ppermute | solution.py:177
  106.0 1.8 %collective-permute-start.19 = (bf16[128,3584]{1,0:T(8,128)(2,1)S(1)}, bf16[128,3584]{1,0:T(8,128)(2,1)S(1)}, u32[]{:S(2)}, u32[]{:S(2)}) collective-permute-start(bf16[128,3584]{1,0:T(8,128)(2,1)S(1)} %collective-permute-done.15.mine_ref), channel_id=1, source_target_pairs={{0,4},{4,8},{8,12},{12,14},{14,10},{10,6},{6,2},{2,0},{1,3},{5,1},... | collective-permute-start | bytes 2752520 | tf_op jit(solution)/shard_map/ppermute | solution.py:177
  107.7 6.6 %collective-permute-done.21.mine_ref = bf16[128,3584]{1,0:T(8,128)(2,1)S(1)} collective-permute-done((bf16[128,3584]{1,0:T(8,128)(2,1)S(1)}, bf16[128,3584]{1,0:T(8,128)(2,1)S(1)}, u32[]{:S(2)}, u32[]{:S(2)}) %collective-permute-start.21) | collective-permute-done | bytes 917536 | tf_op jit(solution)/shard_map/ppermute | solution.py:177
  114.4 3.9 %grad_step.13 = (f32[256,3584]{1,0:T(8,128)S(1)}, f32[16,16,128]{2,1,0:T(8,128)}, f32[256,128]{1,0:T(8,128)S(1)}, bf16[256,256]{1,0:T(8,128)(2,1)S(1)}) custom-call(s32[2]{0:T(128)S(1)} %get-tuple-element.109.order_ref, bf16[16,32,128]{2,1,0:T(8,128)(2,1)S(1)} %all-to-all-done.meta_ref, ...), custom_call_target="tpu_custom_call", output_to_operand_aliasing={{0}: (5, {}), {1}: (6, {}), {2}: (7, {})} | custom-call | flops 1 | bytes 1 | tf_op jit(solution)/shard_map/grad_step/pallas_call | solution.py:144
  120.0 4.2 %collective-permute-done.19.mine_ref = bf16[128,3584]{1,0:T(8,128)(2,1)S(1)} collective-permute-done((bf16[128,3584]{1,0:T(8,128)(2,1)S(1)}, bf16[128,3584]{1,0:T(8,128)(2,1)S(1)}, u32[]{:S(2)}, u32[]{:S(2)}) %collective-permute-start.19) | collective-permute-done | bytes 917536 | tf_op jit(solution)/shard_map/ppermute | solution.py:177
  125.6 2.0 %collective-permute-start.23 = (bf16[128,3584]{1,0:T(8,128)(2,1)S(1)}, bf16[128,3584]{1,0:T(8,128)(2,1)S(1)}, u32[]{:S(2)}, u32[]{:S(2)}) collective-permute-start(bf16[128,3584]{1,0:T(8,128)(2,1)S(1)} %collective-permute-done.19.mine_ref), channel_id=1, source_target_pairs={{0,4},{4,8},{8,12},{12,14},{14,10},{10,6},{6,2},{2,0},{1,3},{5,1},... | collective-permute-start | bytes 2752520 | tf_op jit(solution)/shard_map/ppermute | solution.py:177
  127.6 6.4 %collective-permute-done.26.mine_ref = bf16[128,3584]{1,0:T(8,128)(2,1)S(1)} collective-permute-done((bf16[128,3584]{1,0:T(8,128)(2,1)S(1)}, bf16[128,3584]{1,0:T(8,128)(2,1)S(1)}, u32[]{:S(2)}, u32[]{:S(2)}) %collective-permute-start.26) | collective-permute-done | bytes 917536 | tf_op jit(solution)/shard_map/ppermute | solution.py:177
  134.0 3.9 %grad_step.14 = (f32[256,3584]{1,0:T(8,128)S(1)}, f32[16,16,128]{2,1,0:T(8,128)}, f32[256,128]{1,0:T(8,128)S(1)}, bf16[256,256]{1,0:T(8,128)(2,1)S(1)}) custom-call(s32[2]{0:T(128)S(1)} %get-tuple-element.108.order_ref, bf16[16,32,128]{2,1,0:T(8,128)(2,1)S(1)} %all-to-all-done.meta_ref, ...), custom_call_target="tpu_custom_call", output_to_operand_aliasing={{0}: (5, {}), {1}: (6, {}), {2}: (7, {})} | custom-call | flops 1 | bytes 1 | tf_op jit(solution)/shard_map/grad_step/pallas_call | solution.py:144
  138.0 5.9 %collective-permute-done.23.mine_ref = bf16[128,3584]{1,0:T(8,128)(2,1)S(1)} collective-permute-done((bf16[128,3584]{1,0:T(8,128)(2,1)S(1)}, bf16[128,3584]{1,0:T(8,128)(2,1)S(1)}, u32[]{:S(2)}, u32[]{:S(2)}) %collective-permute-start.23) | collective-permute-done | bytes 917536 | tf_op jit(solution)/shard_map/ppermute | solution.py:177
  147.0 4.7 %grad_step.15 = (bf16[256,3584]{1,0:T(8,128)(2,1)}, f32[16,16,128]{2,1,0:T(8,128)}, f32[256,128]{1,0:T(8,128)S(1)}, bf16[256,256]{1,0:T(8,128)(2,1)S(1)}) custom-call(s32[2]{0:T(128)S(1)} %get-tuple-element.115.order_ref, bf16[16,32,128]{2,1,0:T(8,128)(2,1)S(1)} %all-to-all-done.meta_ref, ...), custom_call_target="tpu_custom_call", output_to_operand_aliasing={{1}: (6, {}), {2}: (7, {})} | custom-call | flops 1 | bytes 1 | tf_op jit(solution)/shard_map/grad_step/pallas_call | solution.py:144
  151.7 5.5 %collective-permute-done.27.mine_ref = bf16[128,3584]{1,0:T(8,128)(2,1)S(1)} collective-permute-done((bf16[128,3584]{1,0:T(8,128)(2,1)S(1)}, bf16[128,3584]{1,0:T(8,128)(2,1)S(1)}, u32[]{:S(2)}, u32[]{:S(2)}) %collective-permute-start.27) | collective-permute-done | bytes 917536 | tf_op jit(solution)/shard_map/ppermute | solution.py:177
  157.3 3.5 %all-to-all-start.1 = ((f32[16,16,128]{2,1,0:T(8,128)}), f32[16,16,128]{2,1,0:T(8,128)S(1)}, u32[]{:S(2)}, u32[]{:S(2)}) async-start(f32[16,16,128]{2,1,0:T(8,128)} %get-tuple-element.96), calls=%async_computation.1 | async-start | bytes 262144 | tf_op jit(solution)/shard_map/all_to_all | solution.py:200
  161.5 2.0 %copy-done.1 = f32[3584,256]{1,0:T(8,128)S(1)} copy-done((f32[3584,256]{1,0:T(8,128)S(1)}, f32[3584,256]{1,0:T(8,128)}, u32[]{:S(2)}) %copy-start.1) | copy-done | bytes 3670040
  163.5 1.9 %input_step.15 = bf16[3584,256]{1,0:T(8,128)(2,1)} custom-call(bf16[256,256]{1,0:T(8,128)(2,1)S(1)} %get-tuple-element.90.pre_ref, bf16[128,3584]{1,0:T(8,128)(2,1)S(1)} %collective-permute-done.27.mine_ref, bf16[128,3584]{1,0:T(8,128)(2,1)S(1)} %collective-permute-done.29.theirs_ref, f32[3584,256]{1,0:T(8,128)S(1)} %copy-done.1), custom_call_target="tpu_custom_call" | custom-call | flops 1 | bytes 1 | tf_op jit(solution)/shard_map/input_step/pallas_call | solution.py:165
  165.5 3.2 %all-to-all-done.1 = f32[16,16,128]{2,1,0:T(8,128)S(1)} async-done(((f32[16,16,128]{2,1,0:T(8,128)}), f32[16,16,128]{2,1,0:T(8,128)S(1)}, u32[]{:S(2)}, u32[]{:S(2)}) %all-to-all-start.1) | async-done | bytes 131104 | tf_op jit(solution)/shard_map/all_to_all | solution.py:200
  (75 shorter events, 29.4 us)
Async XLA Ops:
  0.6 14.6 %collective-permute-start = (bf16[128,3584]{1,0:T(8,128)(2,1)}, bf16[128,3584]{1,0:T(8,128)(2,1)S(1)}, u32[]{:S(2)}, u32[]{:S(2)}) collective-permute-start(bf16[128,3584]{1,0:T(8,128)(2,1)} %mine_ref.2), channel_id=1, source_target_pairs={{0,4},{4,8},{8,12},{12,14},{14,10},{10,6},{6,2},{2,0},{1,3},{5,1},... | collective-permute-start | bytes 2752520 | tf_op jit(solution)/shard_map/ppermute | solution.py:177
  3.7 28.0 %collective-permute-start.3 = (bf16[128,3584]{1,0:T(8,128)(2,1)}, bf16[128,3584]{1,0:T(8,128)(2,1)S(1)}, u32[]{:S(2)}, u32[]{:S(2)}) collective-permute-start(bf16[128,3584]{1,0:T(8,128)(2,1)} %mine_ref.2), channel_id=1, source_target_pairs={{0,1},{1,0},{2,3},{3,2},{4,5},{5,4},{6,7},{7,6},{8,9},{9,8},{10,11... | collective-permute-start | bytes 2752520 | tf_op jit(solution)/shard_map/ppermute | solution.py:177
  3.7 27.5 %collective-permute-start.4 = (bf16[128,3584]{1,0:T(8,128)(2,1)}, bf16[128,3584]{1,0:T(8,128)(2,1)S(1)}, u32[]{:S(2)}, u32[]{:S(2)}) collective-permute-start(bf16[128,3584]{1,0:T(8,128)(2,1)} %mine_ref.3), channel_id=1, source_target_pairs={{0,4},{4,8},{8,12},{12,14},{14,10},{10,6},{6,2},{2,0},{1,3},{5,1},... | collective-permute-start | bytes 2752520 | tf_op jit(solution)/shard_map/ppermute | solution.py:177
  15.2 22.5 %collective-permute-start.2 = (bf16[128,3584]{1,0:T(8,128)(2,1)S(1)}, bf16[128,3584]{1,0:T(8,128)(2,1)}, u32[]{:S(2)}, u32[]{:S(2)}) collective-permute-start(bf16[128,3584]{1,0:T(8,128)(2,1)S(1)} %collective-permute-done.mine_ref), channel_id=1, source_target_pairs={{0,1},{1,0},{2,3},{3,2},{4,5},{5,4},{6,7},{7,6},{8,9},{9,8},{10,11... | collective-permute-start | bytes 2752520 | tf_op jit(solution)/shard_map/ppermute | solution.py:177
  16.7 14.5 %all-to-all-start = ((bf16[16,32,128]{2,1,0:T(8,128)(2,1)}), bf16[16,32,128]{2,1,0:T(8,128)(2,1)S(1)}, u32[]{:S(2)}, u32[]{:S(2)}) async-start(bf16[16,32,128]{2,1,0:T(8,128)(2,1)} %pad_maximum_fusion), calls=%async_computation | async-start | bytes 262144 | tf_op jit(solution)/shard_map/all_to_all | solution.py:130
  31.2 13.4 %collective-permute-start.6 = (bf16[128,3584]{1,0:T(8,128)(2,1)}, bf16[128,3584]{1,0:T(8,128)(2,1)S(1)}, u32[]{:S(2)}, u32[]{:S(2)}) collective-permute-start(bf16[128,3584]{1,0:T(8,128)(2,1)} %mine_ref.3), channel_id=1, source_target_pairs={{0,1},{1,0},{2,3},{3,2},{4,5},{5,4},{6,7},{7,6},{8,9},{9,8},{10,11... | collective-permute-start | bytes 2752520 | tf_op jit(solution)/shard_map/ppermute | solution.py:177
  31.2 13.4 %collective-permute-start.1 = (bf16[128,3584]{1,0:T(8,128)(2,1)S(1)}, bf16[128,3584]{1,0:T(8,128)(2,1)S(1)}, u32[]{:S(2)}, u32[]{:S(2)}) collective-permute-start(bf16[128,3584]{1,0:T(8,128)(2,1)S(1)} %collective-permute-done.mine_ref), channel_id=1, source_target_pairs={{0,4},{4,8},{8,12},{12,14},{14,10},{10,6},{6,2},{2,0},{1,3},{5,1},... | collective-permute-start | bytes 2752520 | tf_op jit(solution)/shard_map/ppermute | solution.py:177
  31.2 14.1 %collective-permute-start.5 = (bf16[128,3584]{1,0:T(8,128)(2,1)S(1)}, bf16[128,3584]{1,0:T(8,128)(2,1)S(1)}, u32[]{:S(2)}, u32[]{:S(2)}) collective-permute-start(bf16[128,3584]{1,0:T(8,128)(2,1)S(1)} %collective-permute-done.4.mine_ref), channel_id=1, source_target_pairs={{0,1},{1,0},{2,3},{3,2},{4,5},{5,4},{6,7},{7,6},{8,9},{9,8},{10,11... | collective-permute-start | bytes 2752520 | tf_op jit(solution)/shard_map/ppermute | solution.py:177
  42.0 13.4 %collective-permute-start.9 = (bf16[128,3584]{1,0:T(8,128)(2,1)S(1)}, bf16[128,3584]{1,0:T(8,128)(2,1)S(1)}, u32[]{:S(2)}, u32[]{:S(2)}) collective-permute-start(bf16[128,3584]{1,0:T(8,128)(2,1)S(1)} %collective-permute-done.4.mine_ref), channel_id=1, source_target_pairs={{0,4},{4,8},{8,12},{12,14},{14,10},{10,6},{6,2},{2,0},{1,3},{5,1},... | collective-permute-start | bytes 2752520 | tf_op jit(solution)/shard_map/ppermute | solution.py:177
  44.6 10.8 %collective-permute-start.8 = (bf16[128,3584]{1,0:T(8,128)(2,1)S(1)}, bf16[128,3584]{1,0:T(8,128)(2,1)S(1)}, u32[]{:S(2)}, u32[]{:S(2)}) collective-permute-start(bf16[128,3584]{1,0:T(8,128)(2,1)S(1)} %collective-permute-done.1.mine_ref), channel_id=1, source_target_pairs={{0,1},{1,0},{2,3},{3,2},{4,5},{5,4},{6,7},{7,6},{8,9},{9,8},{10,11... | collective-permute-start | bytes 2752520 | tf_op jit(solution)/shard_map/ppermute | solution.py:177
  46.7 18.5 %collective-permute-start.7 = (bf16[128,3584]{1,0:T(8,128)(2,1)S(1)}, bf16[128,3584]{1,0:T(8,128)(2,1)S(1)}, u32[]{:S(2)}, u32[]{:S(2)}) collective-permute-start(bf16[128,3584]{1,0:T(8,128)(2,1)S(1)} %collective-permute-done.1.mine_ref), channel_id=1, source_target_pairs={{0,4},{4,8},{8,12},{12,14},{14,10},{10,6},{6,2},{2,0},{1,3},{5,1},... | collective-permute-start | bytes 2752520 | tf_op jit(solution)/shard_map/ppermute | solution.py:177
  55.4 9.8 %collective-permute-start.10 = (bf16[128,3584]{1,0:T(8,128)(2,1)S(1)}, bf16[128,3584]{1,0:T(8,128)(2,1)S(1)}, u32[]{:S(2)}, u32[]{:S(2)}) collective-permute-start(bf16[128,3584]{1,0:T(8,128)(2,1)S(1)} %collective-permute-done.9.mine_ref), channel_id=1, source_target_pairs={{0,1},{1,0},{2,3},{3,2},{4,5},{5,4},{6,7},{7,6},{8,9},{9,8},{10,11... | collective-permute-start | bytes 2752520 | tf_op jit(solution)/shard_map/ppermute | solution.py:177
  59.3 15.8 %collective-permute-start.13 = (bf16[128,3584]{1,0:T(8,128)(2,1)S(1)}, bf16[128,3584]{1,0:T(8,128)(2,1)S(1)}, u32[]{:S(2)}, u32[]{:S(2)}) collective-permute-start(bf16[128,3584]{1,0:T(8,128)(2,1)S(1)} %collective-permute-done.9.mine_ref), channel_id=1, source_target_pairs={{0,4},{4,8},{8,12},{12,14},{14,10},{10,6},{6,2},{2,0},{1,3},{5,1},... | collective-permute-start | bytes 2752520 | tf_op jit(solution)/shard_map/ppermute | solution.py:177
  65.2 9.8 %collective-permute-start.12 = (bf16[128,3584]{1,0:T(8,128)(2,1)S(1)}, bf16[128,3584]{1,0:T(8,128)(2,1)S(1)}, u32[]{:S(2)}, u32[]{:S(2)}) collective-permute-start(bf16[128,3584]{1,0:T(8,128)(2,1)S(1)} %collective-permute-done.7.mine_ref), channel_id=1, source_target_pairs={{0,1},{1,0},{2,3},{3,2},{4,5},{5,4},{6,7},{7,6},{8,9},{9,8},{10,11... | collective-permute-start | bytes 2752520 | tf_op jit(solution)/shard_map/ppermute | solution.py:177
  66.6 18.3 %collective-permute-start.11 = (bf16[128,3584]{1,0:T(8,128)(2,1)S(1)}, bf16[128,3584]{1,0:T(8,128)(2,1)S(1)}, u32[]{:S(2)}, u32[]{:S(2)}) collective-permute-start(bf16[128,3584]{1,0:T(8,128)(2,1)S(1)} %collective-permute-done.7.mine_ref), channel_id=1, source_target_pairs={{0,4},{4,8},{8,12},{12,14},{14,10},{10,6},{6,2},{2,0},{1,3},{5,1},... | collective-permute-start | bytes 2752520 | tf_op jit(solution)/shard_map/ppermute | solution.py:177
  75.1 9.8 %collective-permute-start.14 = (bf16[128,3584]{1,0:T(8,128)(2,1)S(1)}, bf16[128,3584]{1,0:T(8,128)(2,1)S(1)}, u32[]{:S(2)}, u32[]{:S(2)}) collective-permute-start(bf16[128,3584]{1,0:T(8,128)(2,1)S(1)} %collective-permute-done.13.mine_ref), channel_id=1, source_target_pairs={{0,1},{1,0},{2,3},{3,2},{4,5},{5,4},{6,7},{7,6},{8,9},{9,8},{10,11... | collective-permute-start | bytes 2752520 | tf_op jit(solution)/shard_map/ppermute | solution.py:177
  79.0 15.7 %collective-permute-start.17 = (bf16[128,3584]{1,0:T(8,128)(2,1)S(1)}, bf16[128,3584]{1,0:T(8,128)(2,1)S(1)}, u32[]{:S(2)}, u32[]{:S(2)}) collective-permute-start(bf16[128,3584]{1,0:T(8,128)(2,1)S(1)} %collective-permute-done.13.mine_ref), channel_id=1, source_target_pairs={{0,4},{4,8},{8,12},{12,14},{14,10},{10,6},{6,2},{2,0},{1,3},{5,1},... | collective-permute-start | bytes 2752520 | tf_op jit(solution)/shard_map/ppermute | solution.py:177
  84.9 9.8 %collective-permute-start.16 = (bf16[128,3584]{1,0:T(8,128)(2,1)S(1)}, bf16[128,3584]{1,0:T(8,128)(2,1)S(1)}, u32[]{:S(2)}, u32[]{:S(2)}) collective-permute-start(bf16[128,3584]{1,0:T(8,128)(2,1)S(1)} %collective-permute-done.11.mine_ref), channel_id=1, source_target_pairs={{0,1},{1,0},{2,3},{3,2},{4,5},{5,4},{6,7},{7,6},{8,9},{9,8},{10,11... | collective-permute-start | bytes 2752520 | tf_op jit(solution)/shard_map/ppermute | solution.py:177
  86.3 18.3 %collective-permute-start.15 = (bf16[128,3584]{1,0:T(8,128)(2,1)S(1)}, bf16[128,3584]{1,0:T(8,128)(2,1)S(1)}, u32[]{:S(2)}, u32[]{:S(2)}) collective-permute-start(bf16[128,3584]{1,0:T(8,128)(2,1)S(1)} %collective-permute-done.11.mine_ref), channel_id=1, source_target_pairs={{0,4},{4,8},{8,12},{12,14},{14,10},{10,6},{6,2},{2,0},{1,3},{5,1},... | collective-permute-start | bytes 2752520 | tf_op jit(solution)/shard_map/ppermute | solution.py:177
  94.7 9.8 %collective-permute-start.18 = (bf16[128,3584]{1,0:T(8,128)(2,1)S(1)}, bf16[128,3584]{1,0:T(8,128)(2,1)S(1)}, u32[]{:S(2)}, u32[]{:S(2)}) collective-permute-start(bf16[128,3584]{1,0:T(8,128)(2,1)S(1)} %collective-permute-done.17.mine_ref), channel_id=1, source_target_pairs={{0,1},{1,0},{2,3},{3,2},{4,5},{5,4},{6,7},{7,6},{8,9},{9,8},{10,11... | collective-permute-start | bytes 2752520 | tf_op jit(solution)/shard_map/ppermute | solution.py:177
  98.6 15.7 %collective-permute-start.21 = (bf16[128,3584]{1,0:T(8,128)(2,1)S(1)}, bf16[128,3584]{1,0:T(8,128)(2,1)S(1)}, u32[]{:S(2)}, u32[]{:S(2)}) collective-permute-start(bf16[128,3584]{1,0:T(8,128)(2,1)S(1)} %collective-permute-done.17.mine_ref), channel_id=1, source_target_pairs={{0,4},{4,8},{8,12},{12,14},{14,10},{10,6},{6,2},{2,0},{1,3},{5,1},... | collective-permute-start | bytes 2752520 | tf_op jit(solution)/shard_map/ppermute | solution.py:177
  104.5 9.8 %collective-permute-start.20 = (bf16[128,3584]{1,0:T(8,128)(2,1)S(1)}, bf16[128,3584]{1,0:T(8,128)(2,1)S(1)}, u32[]{:S(2)}, u32[]{:S(2)}) collective-permute-start(bf16[128,3584]{1,0:T(8,128)(2,1)S(1)} %collective-permute-done.15.mine_ref), channel_id=1, source_target_pairs={{0,1},{1,0},{2,3},{3,2},{4,5},{5,4},{6,7},{7,6},{8,9},{9,8},{10,11... | collective-permute-start | bytes 2752520 | tf_op jit(solution)/shard_map/ppermute | solution.py:177
  106.0 18.3 %collective-permute-start.19 = (bf16[128,3584]{1,0:T(8,128)(2,1)S(1)}, bf16[128,3584]{1,0:T(8,128)(2,1)S(1)}, u32[]{:S(2)}, u32[]{:S(2)}) collective-permute-start(bf16[128,3584]{1,0:T(8,128)(2,1)S(1)} %collective-permute-done.15.mine_ref), channel_id=1, source_target_pairs={{0,4},{4,8},{8,12},{12,14},{14,10},{10,6},{6,2},{2,0},{1,3},{5,1},... | collective-permute-start | bytes 2752520 | tf_op jit(solution)/shard_map/ppermute | solution.py:177
  114.4 9.8 %collective-permute-start.22 = (bf16[128,3584]{1,0:T(8,128)(2,1)S(1)}, bf16[128,3584]{1,0:T(8,128)(2,1)S(1)}, u32[]{:S(2)}, u32[]{:S(2)}) collective-permute-start(bf16[128,3584]{1,0:T(8,128)(2,1)S(1)} %collective-permute-done.21.mine_ref), channel_id=1, source_target_pairs={{0,1},{1,0},{2,3},{3,2},{4,5},{5,4},{6,7},{7,6},{8,9},{9,8},{10,11... | collective-permute-start | bytes 2752520 | tf_op jit(solution)/shard_map/ppermute | solution.py:177
  118.3 15.7 %collective-permute-start.26 = (bf16[128,3584]{1,0:T(8,128)(2,1)S(1)}, bf16[128,3584]{1,0:T(8,128)(2,1)S(1)}, u32[]{:S(2)}, u32[]{:S(2)}) collective-permute-start(bf16[128,3584]{1,0:T(8,128)(2,1)S(1)} %collective-permute-done.21.mine_ref), channel_id=1, source_target_pairs={{0,4},{4,8},{8,12},{12,14},{14,10},{10,6},{6,2},{2,0},{1,3},{5,1},... | collective-permute-start | bytes 2752520 | tf_op jit(solution)/shard_map/ppermute | solution.py:177
  124.2 9.8 %collective-permute-start.25 = (bf16[128,3584]{1,0:T(8,128)(2,1)S(1)}, bf16[128,3584]{1,0:T(8,128)(2,1)S(1)}, u32[]{:S(2)}, u32[]{:S(2)}) collective-permute-start(bf16[128,3584]{1,0:T(8,128)(2,1)S(1)} %collective-permute-done.19.mine_ref), channel_id=1, source_target_pairs={{0,1},{1,0},{2,3},{3,2},{4,5},{5,4},{6,7},{7,6},{8,9},{9,8},{10,11... | collective-permute-start | bytes 2752520 | tf_op jit(solution)/shard_map/ppermute | solution.py:177
  125.6 18.3 %collective-permute-start.23 = (bf16[128,3584]{1,0:T(8,128)(2,1)S(1)}, bf16[128,3584]{1,0:T(8,128)(2,1)S(1)}, u32[]{:S(2)}, u32[]{:S(2)}) collective-permute-start(bf16[128,3584]{1,0:T(8,128)(2,1)S(1)} %collective-permute-done.19.mine_ref), channel_id=1, source_target_pairs={{0,4},{4,8},{8,12},{12,14},{14,10},{10,6},{6,2},{2,0},{1,3},{5,1},... | collective-permute-start | bytes 2752520 | tf_op jit(solution)/shard_map/ppermute | solution.py:177
  134.0 11.6 %collective-permute-start.28 = (bf16[128,3584]{1,0:T(8,128)(2,1)S(1)}, bf16[128,3584]{1,0:T(8,128)(2,1)S(1)}, u32[]{:S(2)}, u32[]{:S(2)}) collective-permute-start(bf16[128,3584]{1,0:T(8,128)(2,1)S(1)} %collective-permute-done.26.mine_ref), channel_id=1, source_target_pairs={{0,1},{1,0},{2,3},{3,2},{4,5},{5,4},{6,7},{7,6},{8,9},{9,8},{10,11... | collective-permute-start | bytes 2752520 | tf_op jit(solution)/shard_map/ppermute | solution.py:177
  143.9 3.2 %collective-permute-start.24 = (bf16[128,3584]{1,0:T(8,128)(2,1)S(1)}, bf16[128,3584]{1,0:T(8,128)(2,1)S(1)}, u32[]{:S(2)}, u32[]{:S(2)}) collective-permute-start(bf16[128,3584]{1,0:T(8,128)(2,1)S(1)} %collective-permute-done.23.mine_ref), channel_id=1, source_target_pairs={{0,1},{1,0},{2,3},{3,2},{4,5},{5,4},{6,7},{7,6},{8,9},{9,8},{10,11... | collective-permute-start | bytes 2752520 | tf_op jit(solution)/shard_map/ppermute | solution.py:177
  143.9 13.4 %collective-permute-start.27 = (bf16[128,3584]{1,0:T(8,128)(2,1)S(1)}, bf16[128,3584]{1,0:T(8,128)(2,1)S(1)}, u32[]{:S(2)}, u32[]{:S(2)}) collective-permute-start(bf16[128,3584]{1,0:T(8,128)(2,1)S(1)} %collective-permute-done.26.mine_ref), channel_id=1, source_target_pairs={{0,4},{4,8},{8,12},{12,14},{14,10},{10,6},{6,2},{2,0},{1,3},{5,1},... | collective-permute-start | bytes 2752520 | tf_op jit(solution)/shard_map/ppermute | solution.py:177
  157.3 4.2 %collective-permute-start.29 = (bf16[128,3584]{1,0:T(8,128)(2,1)S(1)}, bf16[128,3584]{1,0:T(8,128)(2,1)S(1)}, u32[]{:S(2)}, u32[]{:S(2)}) collective-permute-start(bf16[128,3584]{1,0:T(8,128)(2,1)S(1)} %collective-permute-done.27.mine_ref), channel_id=1, source_target_pairs={{0,1},{1,0},{2,3},{3,2},{4,5},{5,4},{6,7},{7,6},{8,9},{9,8},{10,11... | collective-permute-start | bytes 2752520 | tf_op jit(solution)/shard_map/ppermute | solution.py:177
  157.3 11.4 %all-to-all-start.1 = ((f32[16,16,128]{2,1,0:T(8,128)}), f32[16,16,128]{2,1,0:T(8,128)S(1)}, u32[]{:S(2)}, u32[]{:S(2)}) async-start(f32[16,16,128]{2,1,0:T(8,128)} %get-tuple-element.96), calls=%async_computation.1 | async-start | bytes 262144 | tf_op jit(solution)/shard_map/all_to_all | solution.py:200
  (7 other events, 40.2 us)

commit v6 on v5

--- a/solution.py
+++ b/solution.py
@@ -13,6 +13,7 @@
 HELD_BYTES = 1 << 25
 RING_BYTES = 1 << 26
 VMEM_BYTES = 24 << 20
+LAG = 4
 
 
 def ring_tables(peer_count):
@@ -29,18 +30,34 @@
     onward = [(2 * ring[i], 2 * ring[(i + 1) % chips]) for i in range(chips)]
     onward += [(2 * ring[i] + 1, 2 * ring[(i - 1) % chips] + 1) for i in range(chips)]
     swap = [(i, i ^ 1) for i in range(peer_count)]
-    return sources, onward, swap
+    backward = [(b, a) for a, b in onward]
+    return sources, onward, backward, swap
+
+
+def meta_kernel(owners_ref, blocks_ref, offsets_ref, values_ref, meta_ref):
+    count, per_block, tokens = offsets_ref.shape
+    columns = [
+        (jnp.broadcast_to(blocks_ref[i : i + 1, :], (per_block, tokens)) * BLOCK + offsets_ref[i]).astype(jnp.float32)
+        for i in range(count)
+    ]
+    values = [values_ref[i].astype(jnp.float32) for i in range(count)]
+    named = [jnp.broadcast_to(owners_ref[i : i + 1, :], (per_block, tokens)) for i in range(count)]
+    for owner in range(meta_ref.shape[0]):
+        told_columns = jnp.full((per_block, tokens), -1.0, jnp.float32)
+        told_values = jnp.zeros((per_block, tokens), jnp.float32)
+        for i in range(count):
+            mine = named[i] == owner
+            told_columns = jnp.where(mine, columns[i], told_columns)
+            told_values = jnp.where(mine, values[i], told_values)
+        meta_ref[owner, :per_block, :] = told_columns.astype(jnp.bfloat16)
+        meta_ref[owner, per_block:, :] = told_values.astype(jnp.bfloat16)
 
 
 def grad_kernel(per_block, order_ref, meta_ref, decoder_ref, mine_ref, theirs_ref, *refs):
-    total_ref, lat_ref, bias_ref, pre_ref, acts_ref = refs[-5:]
-    first = len(refs) == 5
-    if first:
-        lat_ref[...] = jnp.zeros_like(lat_ref)
-        bias_ref[...] = jnp.zeros_like(bias_ref)
-    else:
-        lat_ref[...] = refs[1][...]
-        bias_ref[...] = refs[2][...]
+    total_ref, bias_ref, lat_ref, pre_ref, acts_ref, bias_sum = refs[-6:]
+    first, last = len(refs) == 6, bias_ref.shape[0] == 1
+    bias_sum[...] = jnp.zeros_like(bias_sum) if first else refs[1][...]
+    lat_ref[...] = jnp.zeros_like(lat_ref) if first else refs[2][...]
     latents, width = decoder_ref.shape
     tokens = mine_ref.shape[0]
     span = column_span(width)
@@ -69,7 +86,7 @@
                     sums[k] = sums[k] + picked
                     kept = kept + picked
                     dense = jnp.where(hit, values[k], dense)
-                bias_ref[base : base + 8, :] += kept
+                bias_sum[base : base + 8, :] += kept
                 kept_both.append(kept)
                 dense_both.append(dense)
             pre_ref[block : block + 16, at] = jnp.concatenate(kept_both, axis=0).astype(jnp.bfloat16)
@@ -83,6 +100,7 @@
         if not first:
             term += refs[0][:, at : at + span]
         total_ref[:, at : at + span] = term.astype(total_ref.dtype)
+    bias_ref[...] = jnp.sum(bias_sum[...].T, axis=0, keepdims=True) if last else bias_sum[...]
 
 
 def input_kernel(pre_ref, mine_ref, theirs_ref, *refs):
@@ -113,53 +131,52 @@
     peer_count = lax.axis_size("lat")
     chips = peer_count // 2
     me = lax.axis_index("lat")
-    sources, onward, swap = ring_tables(peer_count)
+    sources, onward, backward, swap = ring_tables(peer_count)
     order = jnp.asarray(sources)[me]
-
     own_t = owners.T
-    columns_t = (local_blocks.T[:, None, :] * BLOCK + offsets.transpose(1, 2, 0)).astype(jnp.float32)
-    values_t = act_values.transpose(1, 2, 0).astype(jnp.float32)
-    peers = jnp.arange(peer_count, dtype=jnp.int32)
-    sent_columns = jnp.full((peer_count, per_block, token_count), -1.0, jnp.float32)
-    sent_values = jnp.zeros((peer_count, per_block, token_count), jnp.float32)
-    for i in range(block_count):
-        named = own_t[i][None, None, :] == peers[:, None, None]
-        sent_columns = jnp.where(named, columns_t[i][None], sent_columns)
-        sent_values = jnp.where(named, values_t[i][None], sent_values)
-    meta = jnp.concatenate([sent_columns, sent_values], axis=1).astype(jnp.bfloat16)
-    meta = lax.all_to_all(meta, "lat", split_axis=0, concat_axis=0, tiled=True)
-
     whole = pl.BlockSpec(memory_space=pltpu.VMEM)
     scalars = pl.BlockSpec(memory_space=pltpu.SMEM)
     step_tokens = 2 * token_count
     light = pl.CostEstimate(flops=1, bytes_accessed=1, transcendentals=0)
     params = pltpu.CompilerParams(vmem_limit_bytes=VMEM_BYTES)
 
+    meta = pl.pallas_call(
+        meta_kernel,
+        in_specs=[whole] * 4,
+        out_specs=whole,
+        out_shape=jax.ShapeDtypeStruct((peer_count, 2 * per_block, token_count), jnp.bfloat16),
+        compiler_params=params,
+        cost_estimate=light,
+        name="meta",
+    )(own_t, local_blocks.T, offsets.transpose(1, 2, 0), act_values.transpose(1, 2, 0))
+    meta = lax.all_to_all(meta, "lat", split_axis=0, concat_axis=0, tiled=True)
+
     def near(value):
         return pltpu.with_memory_space_constraint(value, pltpu.VMEM)
 
-    def grad_step(hop, rows, totals):
-        last = hop == chips - 1
-        sums = (latent_count, width)
+    def grad_step(hop, rows, totals, last):
+        sums, lanes = (latent_count, width), (latent_count, token_count)
         return pl.pallas_call(
             functools.partial(grad_kernel, per_block),
             in_specs=[scalars] + [whole] * (4 + len(totals)),
             out_specs=[whole] * 4,
             out_shape=[
                 jax.ShapeDtypeStruct(sums, jnp.bfloat16) if last else pltpu.VMEM(sums, jnp.float32),
-                pltpu.VMEM((peer_count, per_block, token_count), jnp.float32),
-                pltpu.VMEM((latent_count, token_count), jnp.float32),
+                jax.ShapeDtypeStruct((1, latent_count), jnp.float32) if last else pltpu.VMEM(lanes, jnp.float32),
+                jax.ShapeDtypeStruct((peer_count, per_block, token_count), jnp.float32),
                 pltpu.VMEM((latent_count, step_tokens), jnp.bfloat16),
             ],
-            scratch_shapes=[pltpu.VMEM((latent_count, step_tokens), jnp.bfloat16)],
-            input_output_aliases={5 + i: i for i in range(1 if last else 0, len(totals))},
+            scratch_shapes=[
+                pltpu.VMEM((latent_count, step_tokens), jnp.bfloat16),
+                pltpu.VMEM(lanes, jnp.float32),
+            ],
+            input_output_aliases={} if last or not totals else {5: 0, 6: 1},
             compiler_params=params,
             cost_estimate=light,
             name="grad_step",
         )(order[hop], near(meta), near(decoder), near(rows[0]), near(rows[1]), *map(near, totals))
 
-    def input_step(hop, rows, total):
-        last = hop == chips - 1
+    def input_step(pre, rows, total, last):
         sums = (width, latent_count)
         totals = () if total is None else (total,)
         return pl.pallas_call(
@@ -171,35 +188,60 @@
             compiler_params=params,
             cost_estimate=light,
             name="input_step",
-        )(near(pres[hop]), near(rows[0]), near(rows[1]), *map(near, totals))
+        )(near(pre), near(rows[0]), near(rows[1]), *map(near, totals))
 
     def send(rows, way, *first):
         return lax.ppermute(after(rows, *first) if first else rows, "lat", way)
 
-    pres, totals, encoder_total = [], (), None
-
-    def use_grads(rows):
-        nonlocal totals
-        *totals, pre = grad_step(len(pres), rows, totals)
-        pres.append(pre)
-
-    grad, inward = send(grad_recon, onward), send(inputs, onward)
-    use_grads((grad_recon, send(grad_recon, swap)))
-    encoder_total = input_step(0, (inputs, send(inputs, swap, meta)), None)
-    grad_next = send(grad, onward, meta)
-    for hop in range(1, chips):
-        use_grads((grad, send(grad, swap)))
-        pair = (inward, send(inward, swap, *((totals[2], encoder_total) if hop == chips - 1 else ())))
-        if hop < chips - 1:
-            inward = send(inward, onward, totals[2])
-        encoder_total = input_step(hop, pair, encoder_total)
-        grad = grad_next
-        if hop < chips - 2:
-            grad_next = send(grad, onward, encoder_total)
-    decoder_grad, lat, bias = totals
-    returned = lax.all_to_all(lat, "lat", split_axis=0, concat_axis=0, tiled=True)
-    latent_grads = pick_returned(after(returned, encoder_total), own_t)
-    return (decoder_grad, encoder_total, jnp.sum(bias, axis=1), latent_grads)
+    half = chips // 2
+    later = [("inputs", 1)]
+    for hop in range(1, half):
+        later += [("inputs", hop + 1), ("inputs", -hop)]
+    turns = []
+    for hop in range(1, half + 1):
+        turns += [("grads", hop)] + ([("grads", -hop)] if hop < half else []) + [later.pop(0)]
+    turns += later
+    pres, totals, encoder_grad = {}, (), None
+
+    def use(kind, hop, rows, last=False):
+        nonlocal totals, encoder_grad
+        if kind == "grads":
+            *totals, pres[hop] = grad_step(hop, rows, totals, last)
+            return totals[1]
+        encoder_grad = input_step(pres[hop], rows, encoder_grad, last)
+        return encoder_grad
+
+    held = {(kind, way): rows for kind, rows in (("grads", grad_recon), ("inputs", inputs)) for way in (True, False)}
+    own_grads, own_inputs = send(grad_recon, swap), send(inputs, swap, meta)
+    marks = []
+    last_grads = max(turn for turn, (kind, _) in enumerate(turns) if kind == "grads")
+    returned = None
+
+    def arrive(turn):
+        nonlocal returned
+        kind, hop = turns[turn]
+        last = turn in (last_grads, len(turns) - 1)
+        ready = (meta,) if turn < 2 else (marks[turn - 2],)
+        if turn == len(turns) - 1:
+            ready += (returned,)
+        marks.append(use(kind, hop % chips, (arrived[turn], send(arrived[turn], swap, *ready)), last))
+        if turn == last_grads:
+            returned = lax.all_to_all(totals[2], "lat", split_axis=0, concat_axis=0, tiled=True)
+
+    use("grads", 0, (grad_recon, own_grads))
+    use("inputs", 0, (inputs, own_inputs))
+    arrived = []
+    for turn, (kind, hop) in enumerate(turns):
+        if turn >= LAG:
+            arrive(turn - LAG)
+        ready = () if turn < 3 else (meta,) if turn < LAG else (marks[turn - LAG],)
+        rows = send(held[kind, hop > 0], onward if hop > 0 else backward, *ready)
+        held[kind, hop > 0] = rows
+        arrived.append(rows)
+    for turn in range(len(turns) - LAG, len(turns)):
+        arrive(turn)
+    latent_grads = pick_returned(after(returned, encoder_grad), own_t)
+    return (totals[0], encoder_grad, totals[1].reshape(latent_count), latent_grads)
 
 
 def pick_returned(returned, own_t):

time: 170 us -> 165 us (0.971)
  starting transfers between devices: 33.4 us -> 23.2 us
  local copies, waits for them, and re-layouts: 7.02 us -> 12.1 us
  waiting for transfers between devices: 81.9 us -> 85.6 us
  other arithmetic: 3.59 us -> 0.7 us
    ppermute x30, starting transfers between devices: 23.3 us -> 13.3 us  [send(): return lax.ppermute(after(rows, *first) if first else rows, 'lat', way)]
    all_to_all x1, waiting for transfers between devices: 7.23 us -> 16.4 us  [by_ring(): meta = lax.all_to_all(meta, 'lat', split_axis=0, concat_axis=0, tiled=True)]
    unnamed x14 -> x26, local copies, waits for them, and re-layouts: 4.74 us -> 11.4 us
    pallas_call x8, Pallas kernels: 31.8 us -> 26.4 us  [grad_step(): pl.pallas_call(functools.partial(grad_kernel, per_block), in_specs=[scala...]
    pallas_call x8, Pallas kernels: 10.9 us -> 14.3 us  [input_step(): pl.pallas_call(input_kernel, in_specs=[whole] * (3 + len(totals)), out_sp...]
    ppermute x30, waiting for transfers between devices: 71.4 us -> 68.5 us  [send(): return lax.ppermute(after(rows, *first) if first else rows, 'lat', way)]
    all_to_all x1, waiting for transfers between devices: 3.22 us -> 0.68 us  [arrive(): lax.all_to_all(totals[2], 'lat', split_axis=0, concat_axis=0, tiled=True)]
  transfers between devices with their start and end apart: 32 -> 32, of which waited for: 15 -> 11; matrix products, arithmetic and copies ran while one was open for 3% -> 0% of each run, Pallas kernels for 25% -> 23%
where the time goes in v6:
time: 165 us; the launch traced here: 164 us
  waiting for transfers between devices  85.6 us (52%)
  Pallas kernels  41.4 us (25%)
  starting transfers between devices  23.2 us (14%)
  local copies, waits for them, and re-layouts  12.1 us (7%)
    ppermute x30, waiting for transfers between devices, send(): return lax.ppermute(after(rows, *first) if first else rows, 'lat', way)  68.5 us
    pallas_call x8, Pallas kernels, grad_step(): pl.pallas_call(functools.partial(grad_kernel, per_block), in_specs=[scala...  26.4 us
    all_to_all x1, waiting for transfers between devices, by_ring(): meta = lax.all_to_all(meta, 'lat', split_axis=0, concat_axis=0, tiled=True)  16.4 us
    pallas_call x8, Pallas kernels, input_step(): pl.pallas_call(input_kernel, in_specs=[whole] * (3 + len(totals)), out_sp...  14.3 us
    ppermute x30, starting transfers between devices, send(): return lax.ppermute(after(rows, *first) if first else rows, 'lat', way)  13.3 us
    unnamed x26, local copies, waits for them, and re-layouts  11.4 us
    all_to_all x1, starting transfers between devices, by_ring(): meta = lax.all_to_all(meta, 'lat', split_axis=0, concat_axis=0, tiled=True)  6.36 us
    all_to_all x1, starting transfers between devices, arrive(): lax.all_to_all(totals[2], 'lat', split_axis=0, concat_axis=0, tiled=True)  3.51 us
  transfers between devices with their start and end apart: 32, of which 11 were waited for; matrix products, arithmetic and copies ran while one was open for 0% of the time, Pallas kernels for 23%

profile of v6, /device:TPU:0, one launch (start us, length us, event | category | flops | bytes accessed | tf_op | source)
XLA Modules:
  0.0 163.9 jit_solution(5401130292792306988)
XLA Ops:
  0.6 3.1 %collective-permute-start = (bf16[128,3584]{1,0:T(8,128)(2,1)}, bf16[128,3584]{1,0:T(8,128)(2,1)}, u32[]{:S(2)}, u32[]{:S(2)}) collective-permute-start(bf16[128,3584]{1,0:T(8,128)(2,1)} %mine_ref.2), channel_id=1, source_target_pairs={{0,4},{4,8},{8,12},{12,14},{14,10},{10,6},{6,2},{2,0},{1,3},{5,1},... | collective-permute-start | bytes 2752520 | tf_op jit(solution)/shard_map/ppermute | solution.py:194
  7.3 6.4 %all-to-all-start = ((bf16[16,32,128]{2,1,0:T(8,128)(2,1)}), bf16[16,32,128]{2,1,0:T(8,128)(2,1)S(1)}, u32[]{:S(2)}, u32[]{:S(2)}) async-start(bf16[16,32,128]{2,1,0:T(8,128)(2,1)} %meta.1), calls=%async_computation | async-start | bytes 262144 | tf_op jit(solution)/shard_map/all_to_all | solution.py:152
  14.0 16.4 %all-to-all-done.meta_ref = bf16[16,32,128]{2,1,0:T(8,128)(2,1)S(1)} async-done(((bf16[16,32,128]{2,1,0:T(8,128)(2,1)}), bf16[16,32,128]{2,1,0:T(8,128)(2,1)S(1)}, u32[]{:S(2)}, u32[]{:S(2)}) %all-to-all-start) | async-done | bytes 131104 | tf_op jit(solution)/shard_map/all_to_all | solution.py:152
  31.0 1.7 %collective-permute-start.1 = (bf16[128,3584]{1,0:T(8,128)(2,1)}, bf16[128,3584]{1,0:T(8,128)(2,1)S(1)}, u32[]{:S(2)}, u32[]{:S(2)}) collective-permute-start(bf16[128,3584]{1,0:T(8,128)(2,1)} %collective-permute-done.mine_ref), channel_id=1, source_target_pairs={{0,4},{4,8},{8,12},{12,14},{14,10},{10,6},{6,2},{2,0},{1,3},{5,1},... | collective-permute-start | bytes 2752520 | tf_op jit(solution)/shard_map/ppermute | solution.py:194
  33.6 1.5 copy-done.4
  36.3 3.3 %grad_step.8 = (f32[256,3584]{1,0:T(8,128)S(1)}, f32[256,128]{1,0:T(8,128)S(1)}, f32[16,16,128]{2,1,0:T(8,128)S(1)}, bf16[256,256]{1,0:T(8,128)(2,1)S(1)}) custom-call(s32[2]{0:T(128)S(1)} %get-tuple-element.121.order_ref, bf16[16,32,128]{2,1,0:T(8,128)(2,1)S(1)} %all-to-all-done.meta_ref, bf16[256,3584]{1,0:T(8,128)(2,1)S(1)} %copy-done.4, ...), custom_call_target="tpu_custom_call" | custom-call | flops 1 | bytes 1 | tf_op jit(solution)/shard_map/grad_step/pallas_call | solution.py:159
  39.6 3.8 %grad_step.9 = (f32[256,3584]{1,0:T(8,128)S(1)}, f32[256,128]{1,0:T(8,128)S(1)}, f32[16,16,128]{2,1,0:T(8,128)S(1)}, bf16[256,256]{1,0:T(8,128)(2,1)S(1)}) custom-call(s32[2]{0:T(128)S(1)} %get-tuple-element.122.order_ref, bf16[16,32,128]{2,1,0:T(8,128)(2,1)S(1)} %all-to-all-done.meta_ref, ...), custom_call_target="tpu_custom_call", output_to_operand_aliasing={{0}: (5, {}), {1}: (6, {})} | custom-call | flops 1 | bytes 1 | tf_op jit(solution)/shard_map/grad_step/pallas_call | solution.py:159
  44.2 3.6 %grad_step.10 = (f32[256,3584]{1,0:T(8,128)S(1)}, f32[256,128]{1,0:T(8,128)S(1)}, f32[16,16,128]{2,1,0:T(8,128)S(1)}, bf16[256,256]{1,0:T(8,128)(2,1)S(1)}) custom-call(s32[2]{0:T(128)S(1)} %get-tuple-element.119.order_ref, bf16[16,32,128]{2,1,0:T(8,128)(2,1)S(1)} %all-to-all-done.meta_ref, ...), custom_call_target="tpu_custom_call", output_to_operand_aliasing={{0}: (5, {}), {1}: (6, {})} | custom-call | flops 1 | bytes 1 | tf_op jit(solution)/shard_map/grad_step/pallas_call | solution.py:159
  47.8 12.8 %collective-permute-done.1.mine_ref = bf16[128,3584]{1,0:T(8,128)(2,1)S(1)} collective-permute-done((bf16[128,3584]{1,0:T(8,128)(2,1)}, bf16[128,3584]{1,0:T(8,128)(2,1)S(1)}, u32[]{:S(2)}, u32[]{:S(2)}) %collective-permute-start.1) | collective-permute-done | bytes 917536 | tf_op jit(solution)/shard_map/ppermute | solution.py:194
  61.4 1.4 input_step.9.refs_0_
  63.7 1.5 collective-permute-start.7
  65.1 2.9 %grad_step.11 = (f32[256,3584]{1,0:T(8,128)S(1)}, f32[256,128]{1,0:T(8,128)S(1)}, f32[16,16,128]{2,1,0:T(8,128)S(1)}, bf16[256,256]{1,0:T(8,128)(2,1)S(1)}) custom-call(s32[2]{0:T(128)S(1)} %get-tuple-element.120.order_ref, bf16[16,32,128]{2,1,0:T(8,128)(2,1)S(1)} %all-to-all-done.meta_ref, ...), custom_call_target="tpu_custom_call", output_to_operand_aliasing={{0}: (5, {}), {1}: (6, {})} | custom-call | flops 1 | bytes 1 | tf_op jit(solution)/shard_map/grad_step/pallas_call | solution.py:159
  68.0 6.0 %collective-permute-done.11.mine_ref = bf16[128,3584]{1,0:T(8,128)(2,1)S(1)} collective-permute-done((bf16[128,3584]{1,0:T(8,128)(2,1)S(1)}, bf16[128,3584]{1,0:T(8,128)(2,1)S(1)}, u32[]{:S(2)}, u32[]{:S(2)}) %collective-permute-start.11) | collective-permute-done | bytes 917536 | tf_op jit(solution)/shard_map/ppermute | solution.py:194
  74.1 2.9 %grad_step.12 = (f32[256,3584]{1,0:T(8,128)S(1)}, f32[256,128]{1,0:T(8,128)S(1)}, f32[16,16,128]{2,1,0:T(8,128)S(1)}, bf16[256,256]{1,0:T(8,128)(2,1)S(1)}) custom-call(s32[2]{0:T(128)S(1)} %get-tuple-element.116.order_ref, bf16[16,32,128]{2,1,0:T(8,128)(2,1)S(1)} %all-to-all-done.meta_ref, ...), custom_call_target="tpu_custom_call", output_to_operand_aliasing={{0}: (5, {}), {1}: (6, {})} | custom-call | flops 1 | bytes 1 | tf_op jit(solution)/shard_map/grad_step/pallas_call | solution.py:159
  77.0 13.6 %collective-permute-done.7.mine_ref = bf16[128,3584]{1,0:T(8,128)(2,1)S(1)} collective-permute-done((bf16[128,3584]{1,0:T(8,128)(2,1)S(1)}, bf16[128,3584]{1,0:T(8,128)(2,1)S(1)}, u32[]{:S(2)}, u32[]{:S(2)}) %collective-permute-start.7) | collective-permute-done | bytes 917536 | tf_op jit(solution)/shard_map/ppermute | solution.py:194
  90.6 1.4 input_step.10.refs_0_
  94.1 2.9 %grad_step.13 = (f32[256,3584]{1,0:T(8,128)S(1)}, f32[256,128]{1,0:T(8,128)S(1)}, f32[16,16,128]{2,1,0:T(8,128)S(1)}, bf16[256,256]{1,0:T(8,128)(2,1)S(1)}) custom-call(s32[2]{0:T(128)S(1)} %get-tuple-element.117.order_ref, bf16[16,32,128]{2,1,0:T(8,128)(2,1)S(1)} %all-to-all-done.meta_ref, ...), custom_call_target="tpu_custom_call", output_to_operand_aliasing={{0}: (5, {}), {1}: (6, {})} | custom-call | flops 1 | bytes 1 | tf_op jit(solution)/shard_map/grad_step/pallas_call | solution.py:159
  97.0 14.5 %collective-permute-done.20.mine_ref = bf16[128,3584]{1,0:T(8,128)(2,1)S(1)} collective-permute-done((bf16[128,3584]{1,0:T(8,128)(2,1)S(1)}, bf16[128,3584]{1,0:T(8,128)(2,1)S(1)}, u32[]{:S(2)}, u32[]{:S(2)}) %collective-permute-start.20) | collective-permute-done | bytes 917536 | tf_op jit(solution)/shard_map/ppermute | solution.py:194
  111.5 2.9 %grad_step.14 = (f32[256,3584]{1,0:T(8,128)S(1)}, f32[256,128]{1,0:T(8,128)S(1)}, f32[16,16,128]{2,1,0:T(8,128)S(1)}, bf16[256,256]{1,0:T(8,128)(2,1)S(1)}) custom-call(s32[2]{0:T(128)S(1)} %get-tuple-element.118.order_ref, bf16[16,32,128]{2,1,0:T(8,128)(2,1)S(1)} %all-to-all-done.meta_ref, ...), custom_call_target="tpu_custom_call", output_to_operand_aliasing={{0}: (5, {}), {1}: (6, {})} | custom-call | flops 1 | bytes 1 | tf_op jit(solution)/shard_map/grad_step/pallas_call | solution.py:159
  115.0 1.8 %collective-permute-start.21 = (bf16[128,3584]{1,0:T(8,128)(2,1)S(1)}, bf16[128,3584]{1,0:T(8,128)(2,1)S(1)}, u32[]{:S(2)}, u32[]{:S(2)}) collective-permute-start(bf16[128,3584]{1,0:T(8,128)(2,1)S(1)} %collective-permute-done.20.mine_ref), channel_id=1, source_target_pairs={{4,0},{8,4},{12,8},{14,12},{10,14},{6,10},{2,6},{0,2},{3,1},{1,5},... | collective-permute-start | bytes 2752520 | tf_op jit(solution)/shard_map/ppermute | solution.py:194
  118.2 13.6 %collective-permute-done.24.mine_ref = bf16[128,3584]{1,0:T(8,128)(2,1)S(1)} collective-permute-done((bf16[128,3584]{1,0:T(8,128)(2,1)S(1)}, bf16[128,3584]{1,0:T(8,128)(2,1)S(1)}, u32[]{:S(2)}, u32[]{:S(2)}) %collective-permute-start.24) | collective-permute-done | bytes 917536 | tf_op jit(solution)/shard_map/ppermute | solution.py:194
  131.8 4.1 %grad_step.15 = (bf16[256,3584]{1,0:T(8,128)(2,1)}, f32[1,256]{1,0:T(1,128)}, f32[16,16,128]{2,1,0:T(8,128)}, bf16[256,256]{1,0:T(8,128)(2,1)S(1)}) custom-call(s32[2]{0:T(128)S(1)} %get-tuple-element.123.order_ref, bf16[16,32,128]{2,1,0:T(8,128)(2,1)S(1)} %all-to-all-done.meta_ref, bf16[256,3584]{1,0:T(8,128)(2,1)S(1)} %copy-done.5, ...), custom_call_target="tpu_custom_call" | custom-call | flops 1 | bytes 1 | tf_op jit(solution)/shard_map/grad_step/pallas_call | solution.py:159
  136.5 1.6 collective-permute-start.22
  138.0 3.5 %all-to-all-start.1 = ((f32[16,16,128]{2,1,0:T(8,128)}), f32[16,16,128]{2,1,0:T(8,128)S(1)}, u32[]{:S(2)}, u32[]{:S(2)}) async-start(f32[16,16,128]{2,1,0:T(8,128)} %get-tuple-element.111), calls=%async_computation.1 | async-start | bytes 262144 | tf_op jit(solution)/shard_map/all_to_all | solution.py:229
  141.6 2.0 %copy-done.1 = f32[3584,256]{1,0:T(8,128)S(1)} copy-done((f32[3584,256]{1,0:T(8,128)S(1)}, f32[3584,256]{1,0:T(8,128)}, u32[]{:S(2)}) %copy-start.1) | copy-done | bytes 3670040
  143.6 2.5 %input_step.12.refs_0_ = f32[3584,256]{1,0:T(8,128)S(1)} custom-call(bf16[256,256]{1,0:T(8,128)(2,1)S(1)} %get-tuple-element.106.pre_ref, bf16[128,3584]{1,0:T(8,128)(2,1)S(1)} %collective-permute-done.24.mine_ref, bf16[128,3584]{1,0:T(8,128)(2,1)} %collective-permute-done.26.theirs_ref, f32[3584,256]{1,0:T(8,128)S(1)} %copy-done.1), custom_call_target="tpu_custom_call", output_to_operand_aliasing={{}: (3, {})} | custom-call | flops 1 | bytes 1 | tf_op jit(solution)/shard_map/input_step/pallas_call | solution.py:182
  146.1 5.4 %collective-permute-done.28.mine_ref = bf16[128,3584]{1,0:T(8,128)(2,1)S(1)} collective-permute-done((bf16[128,3584]{1,0:T(8,128)(2,1)S(1)}, bf16[128,3584]{1,0:T(8,128)(2,1)S(1)}, u32[]{:S(2)}, u32[]{:S(2)}) %collective-permute-start.28) | collective-permute-done | bytes 917536 | tf_op jit(solution)/shard_map/ppermute | solution.py:194
  151.5 2.5 %input_step.13.refs_0_ = f32[3584,256]{1,0:T(8,128)S(1)} custom-call(bf16[256,256]{1,0:T(8,128)(2,1)S(1)} %get-tuple-element.105.pre_ref, bf16[128,3584]{1,0:T(8,128)(2,1)S(1)} %collective-permute-done.21.mine_ref, bf16[128,3584]{1,0:T(8,128)(2,1)} %collective-permute-done.23.theirs_ref, ...), custom_call_target="tpu_custom_call", output_to_operand_aliasing={{}: (3, {})} | custom-call | flops 1 | bytes 1 | tf_op jit(solution)/shard_map/input_step/pallas_call | solution.py:182
  154.0 1.8 %copy-done.2 = f32[3584,256]{1,0:T(8,128)} copy-done((f32[3584,256]{1,0:T(8,128)}, f32[3584,256]{1,0:T(8,128)S(1)}, u32[]{:S(2)}) %copy-start.2) | copy-done | bytes 3670040
  156.6 2.0 %copy-done.3 = f32[3584,256]{1,0:T(8,128)S(1)} copy-done((f32[3584,256]{1,0:T(8,128)S(1)}, f32[3584,256]{1,0:T(8,128)}, u32[]{:S(2)}) %copy-start.3) | copy-done | bytes 3670040
  158.6 1.4 input_step.14.refs_0_
  160.1 3.1 %input_step.15 = bf16[3584,256]{1,0:T(8,128)(2,1)} custom-call(bf16[256,256]{1,0:T(8,128)(2,1)S(1)} %get-tuple-element.100.pre_ref, bf16[128,3584]{1,0:T(8,128)(2,1)} %collective-permute-done.22.mine_ref, bf16[128,3584]{1,0:T(8,128)(2,1)S(1)} %collective-permute-done.27.theirs_ref, f32[3584,256]{1,0:T(8,128)S(1)} %input_step.14.refs_0_), custom_call_target="tpu_custom_call" | custom-call | flops 1 | bytes 1 | tf_op jit(solution)/shard_map/input_step/pallas_call | solution.py:182
  (79 shorter events, 15.1 us)
Async XLA Ops:
  0.6 29.8 %collective-permute-start = (bf16[128,3584]{1,0:T(8,128)(2,1)}, bf16[128,3584]{1,0:T(8,128)(2,1)}, u32[]{:S(2)}, u32[]{:S(2)}) collective-permute-start(bf16[128,3584]{1,0:T(8,128)(2,1)} %mine_ref.2), channel_id=1, source_target_pairs={{0,4},{4,8},{8,12},{12,14},{14,10},{10,6},{6,2},{2,0},{1,3},{5,1},... | collective-permute-start | bytes 2752520 | tf_op jit(solution)/shard_map/ppermute | solution.py:194
  3.7 27.0 %collective-permute-start.8 = (bf16[128,3584]{1,0:T(8,128)(2,1)}, bf16[128,3584]{1,0:T(8,128)(2,1)S(1)}, u32[]{:S(2)}, u32[]{:S(2)}) collective-permute-start(bf16[128,3584]{1,0:T(8,128)(2,1)} %mine_ref.2), channel_id=1, source_target_pairs={{4,0},{8,4},{12,8},{14,12},{10,14},{6,10},{2,6},{0,2},{3,1},{1,5},... | collective-permute-start | bytes 2752520 | tf_op jit(solution)/shard_map/ppermute | solution.py:194
  7.3 23.2 %all-to-all-start = ((bf16[16,32,128]{2,1,0:T(8,128)(2,1)}), bf16[16,32,128]{2,1,0:T(8,128)(2,1)S(1)}, u32[]{:S(2)}, u32[]{:S(2)}) async-start(bf16[16,32,128]{2,1,0:T(8,128)(2,1)} %meta.1), calls=%async_computation | async-start | bytes 262144 | tf_op jit(solution)/shard_map/all_to_all | solution.py:152
  13.6 19.8 %collective-permute-start.3 = (bf16[128,3584]{1,0:T(8,128)(2,1)}, bf16[128,3584]{1,0:T(8,128)(2,1)}, u32[]{:S(2)}, u32[]{:S(2)}) collective-permute-start(bf16[128,3584]{1,0:T(8,128)(2,1)} %mine_ref.2), channel_id=1, source_target_pairs={{0,1},{1,0},{2,3},{3,2},{4,5},{5,4},{6,7},{7,6},{8,9},{9,8},{10,11... | collective-permute-start | bytes 2752520 | tf_op jit(solution)/shard_map/ppermute | solution.py:194
  30.5 9.1 %collective-permute-start.2 = (bf16[128,3584]{1,0:T(8,128)(2,1)}, bf16[128,3584]{1,0:T(8,128)(2,1)}, u32[]{:S(2)}, u32[]{:S(2)}) collective-permute-start(bf16[128,3584]{1,0:T(8,128)(2,1)} %collective-permute-done.mine_ref), channel_id=1, source_target_pairs={{0,1},{1,0},{2,3},{3,2},{4,5},{5,4},{6,7},{7,6},{8,9},{9,8},{10,11... | collective-permute-start | bytes 2752520 | tf_op jit(solution)/shard_map/ppermute | solution.py:194
  30.6 13.6 %collective-permute-start.4 = (bf16[128,3584]{1,0:T(8,128)(2,1)}, bf16[128,3584]{1,0:T(8,128)(2,1)S(1)}, u32[]{:S(2)}, u32[]{:S(2)}) collective-permute-start(bf16[128,3584]{1,0:T(8,128)(2,1)} %mine_ref.3), channel_id=1, source_target_pairs={{0,4},{4,8},{8,12},{12,14},{14,10},{10,6},{6,2},{2,0},{1,3},{5,1},... | collective-permute-start | bytes 2752520 | tf_op jit(solution)/shard_map/ppermute | solution.py:194
  30.7 13.6 %collective-permute-start.9 = (bf16[128,3584]{1,0:T(8,128)(2,1)S(1)}, bf16[128,3584]{1,0:T(8,128)(2,1)}, u32[]{:S(2)}, u32[]{:S(2)}) collective-permute-start(bf16[128,3584]{1,0:T(8,128)(2,1)S(1)} %collective-permute-done.8.mine_ref), channel_id=1, source_target_pairs={{0,1},{1,0},{2,3},{3,2},{4,5},{5,4},{6,7},{7,6},{8,9},{9,8},{10,11... | collective-permute-start | bytes 2752520 | tf_op jit(solution)/shard_map/ppermute | solution.py:194
  31.0 29.7 %collective-permute-start.1 = (bf16[128,3584]{1,0:T(8,128)(2,1)}, bf16[128,3584]{1,0:T(8,128)(2,1)S(1)}, u32[]{:S(2)}, u32[]{:S(2)}) collective-permute-start(bf16[128,3584]{1,0:T(8,128)(2,1)} %collective-permute-done.mine_ref), channel_id=1, source_target_pairs={{0,4},{4,8},{8,12},{12,14},{14,10},{10,6},{6,2},{2,0},{1,3},{5,1},... | collective-permute-start | bytes 2752520 | tf_op jit(solution)/shard_map/ppermute | solution.py:194
  33.4 27.3 %collective-permute-start.6 = (bf16[128,3584]{1,0:T(8,128)(2,1)}, bf16[128,3584]{1,0:T(8,128)(2,1)S(1)}, u32[]{:S(2)}, u32[]{:S(2)}) collective-permute-start(bf16[128,3584]{1,0:T(8,128)(2,1)} %mine_ref.3), channel_id=1, source_target_pairs={{0,1},{1,0},{2,3},{3,2},{4,5},{5,4},{6,7},{7,6},{8,9},{9,8},{10,11... | collective-permute-start | bytes 2752520 | tf_op jit(solution)/shard_map/ppermute | solution.py:194
  44.2 17.2 %collective-permute-start.5 = (bf16[128,3584]{1,0:T(8,128)(2,1)S(1)}, bf16[128,3584]{1,0:T(8,128)(2,1)S(1)}, u32[]{:S(2)}, u32[]{:S(2)}) collective-permute-start(bf16[128,3584]{1,0:T(8,128)(2,1)S(1)} %collective-permute-done.4.mine_ref), channel_id=1, source_target_pairs={{0,1},{1,0},{2,3},{3,2},{4,5},{5,4},{6,7},{7,6},{8,9},{9,8},{10,11... | collective-permute-start | bytes 2752520 | tf_op jit(solution)/shard_map/ppermute | solution.py:194
  44.2 19.1 %collective-permute-start.14 = (bf16[128,3584]{1,0:T(8,128)(2,1)S(1)}, bf16[128,3584]{1,0:T(8,128)(2,1)S(1)}, u32[]{:S(2)}, u32[]{:S(2)}) collective-permute-start(bf16[128,3584]{1,0:T(8,128)(2,1)S(1)} %collective-permute-done.8.mine_ref), channel_id=1, source_target_pairs={{4,0},{8,4},{12,8},{14,12},{10,14},{6,10},{2,6},{0,2},{3,1},{1,5},... | collective-permute-start | bytes 2752520 | tf_op jit(solution)/shard_map/ppermute | solution.py:194
  60.7 4.5 %collective-permute-start.10 = (bf16[128,3584]{1,0:T(8,128)(2,1)S(1)}, bf16[128,3584]{1,0:T(8,128)(2,1)S(1)}, u32[]{:S(2)}, u32[]{:S(2)}) collective-permute-start(bf16[128,3584]{1,0:T(8,128)(2,1)S(1)} %collective-permute-done.1.mine_ref), channel_id=1, source_target_pairs={{0,1},{1,0},{2,3},{3,2},{4,5},{5,4},{6,7},{7,6},{8,9},{9,8},{10,11... | collective-permute-start | bytes 2752520 | tf_op jit(solution)/shard_map/ppermute | solution.py:194
  60.7 13.4 %collective-permute-start.11 = (bf16[128,3584]{1,0:T(8,128)(2,1)S(1)}, bf16[128,3584]{1,0:T(8,128)(2,1)S(1)}, u32[]{:S(2)}, u32[]{:S(2)}) collective-permute-start(bf16[128,3584]{1,0:T(8,128)(2,1)S(1)} %collective-permute-done.4.mine_ref), channel_id=1, source_target_pairs={{0,4},{4,8},{8,12},{12,14},{14,10},{10,6},{6,2},{2,0},{1,3},{5,1},... | collective-permute-start | bytes 2752520 | tf_op jit(solution)/shard_map/ppermute | solution.py:194
  63.3 10.8 %collective-permute-start.17 = (bf16[128,3584]{1,0:T(8,128)(2,1)S(1)}, bf16[128,3584]{1,0:T(8,128)(2,1)S(1)}, u32[]{:S(2)}, u32[]{:S(2)}) collective-permute-start(bf16[128,3584]{1,0:T(8,128)(2,1)S(1)} %collective-permute-done.14.mine_ref), channel_id=1, source_target_pairs={{0,1},{1,0},{2,3},{3,2},{4,5},{5,4},{6,7},{7,6},{8,9},{9,8},{10,11... | collective-permute-start | bytes 2752520 | tf_op jit(solution)/shard_map/ppermute | solution.py:194
  63.7 26.9 %collective-permute-start.7 = (bf16[128,3584]{1,0:T(8,128)(2,1)S(1)}, bf16[128,3584]{1,0:T(8,128)(2,1)S(1)}, u32[]{:S(2)}, u32[]{:S(2)}) collective-permute-start(bf16[128,3584]{1,0:T(8,128)(2,1)S(1)} %collective-permute-done.1.mine_ref), channel_id=1, source_target_pairs={{0,4},{4,8},{8,12},{12,14},{14,10},{10,6},{6,2},{2,0},{1,3},{5,1},... | collective-permute-start | bytes 2752520 | tf_op jit(solution)/shard_map/ppermute | solution.py:194
  74.1 16.5 %collective-permute-start.12 = (bf16[128,3584]{1,0:T(8,128)(2,1)S(1)}, bf16[128,3584]{1,0:T(8,128)(2,1)S(1)}, u32[]{:S(2)}, u32[]{:S(2)}) collective-permute-start(bf16[128,3584]{1,0:T(8,128)(2,1)S(1)} %collective-permute-done.11.mine_ref), channel_id=1, source_target_pairs={{0,1},{1,0},{2,3},{3,2},{4,5},{5,4},{6,7},{7,6},{8,9},{9,8},{10,11... | collective-permute-start | bytes 2752520 | tf_op jit(solution)/shard_map/ppermute | solution.py:194
  74.1 19.2 %collective-permute-start.15 = (bf16[128,3584]{1,0:T(8,128)(2,1)S(1)}, bf16[128,3584]{1,0:T(8,128)(2,1)S(1)}, u32[]{:S(2)}, u32[]{:S(2)}) collective-permute-start(bf16[128,3584]{1,0:T(8,128)(2,1)S(1)} %collective-permute-done.14.mine_ref), channel_id=1, source_target_pairs={{4,0},{8,4},{12,8},{14,12},{10,14},{6,10},{2,6},{0,2},{3,1},{1,5},... | collective-permute-start | bytes 2752520 | tf_op jit(solution)/shard_map/ppermute | solution.py:194
  90.6 3.6 %collective-permute-start.18 = (bf16[128,3584]{1,0:T(8,128)(2,1)S(1)}, bf16[128,3584]{1,0:T(8,128)(2,1)S(1)}, u32[]{:S(2)}, u32[]{:S(2)}) collective-permute-start(bf16[128,3584]{1,0:T(8,128)(2,1)S(1)} %collective-permute-done.7.mine_ref), channel_id=1, source_target_pairs={{0,1},{1,0},{2,3},{3,2},{4,5},{5,4},{6,7},{7,6},{8,9},{9,8},{10,11... | collective-permute-start | bytes 2752520 | tf_op jit(solution)/shard_map/ppermute | solution.py:194
  90.6 20.9 %collective-permute-start.20 = (bf16[128,3584]{1,0:T(8,128)(2,1)S(1)}, bf16[128,3584]{1,0:T(8,128)(2,1)S(1)}, u32[]{:S(2)}, u32[]{:S(2)}) collective-permute-start(bf16[128,3584]{1,0:T(8,128)(2,1)S(1)} %copy-done.7), channel_id=1, source_target_pairs={{4,0},{8,4},{12,8},{14,12},{10,14},{6,10},{2,6},{0,2},{3,1},{1,5},... | collective-permute-start | bytes 2752520 | tf_op jit(solution)/shard_map/ppermute | solution.py:194
  93.3 18.2 %collective-permute-start.16 = (bf16[128,3584]{1,0:T(8,128)(2,1)S(1)}, bf16[128,3584]{1,0:T(8,128)(2,1)S(1)}, u32[]{:S(2)}, u32[]{:S(2)}) collective-permute-start(bf16[128,3584]{1,0:T(8,128)(2,1)S(1)} %collective-permute-done.15.mine_ref), channel_id=1, source_target_pairs={{0,1},{1,0},{2,3},{3,2},{4,5},{5,4},{6,7},{7,6},{8,9},{9,8},{10,11... | collective-permute-start | bytes 2752520 | tf_op jit(solution)/shard_map/ppermute | solution.py:194
  93.6 20.9 %collective-permute-start.13 = (bf16[128,3584]{1,0:T(8,128)(2,1)S(1)}, bf16[128,3584]{1,0:T(8,128)(2,1)S(1)}, u32[]{:S(2)}, u32[]{:S(2)}) collective-permute-start(bf16[128,3584]{1,0:T(8,128)(2,1)S(1)} %collective-permute-done.7.mine_ref), channel_id=1, source_target_pairs={{0,4},{4,8},{8,12},{12,14},{14,10},{10,6},{6,2},{2,0},{1,3},{5,1},... | collective-permute-start | bytes 2752520 | tf_op jit(solution)/shard_map/ppermute | solution.py:194
  111.5 5.3 %collective-permute-start.25 = (bf16[128,3584]{1,0:T(8,128)(2,1)S(1)}, bf16[128,3584]{1,0:T(8,128)(2,1)S(1)}, u32[]{:S(2)}, u32[]{:S(2)}) collective-permute-start(bf16[128,3584]{1,0:T(8,128)(2,1)S(1)} %collective-permute-done.20.mine_ref), channel_id=1, source_target_pairs={{0,1},{1,0},{2,3},{3,2},{4,5},{5,4},{6,7},{7,6},{8,9},{9,8},{10,11... | collective-permute-start | bytes 2752520 | tf_op jit(solution)/shard_map/ppermute | solution.py:194
  111.5 20.3 %collective-permute-start.24 = (bf16[128,3584]{1,0:T(8,128)(2,1)S(1)}, bf16[128,3584]{1,0:T(8,128)(2,1)S(1)}, u32[]{:S(2)}, u32[]{:S(2)}) collective-permute-start(bf16[128,3584]{1,0:T(8,128)(2,1)S(1)} %collective-permute-done.11.mine_ref), channel_id=1, source_target_pairs={{0,4},{4,8},{8,12},{12,14},{14,10},{10,6},{6,2},{2,0},{1,3},{5,1},... | collective-permute-start | bytes 2752520 | tf_op jit(solution)/shard_map/ppermute | solution.py:194
  114.4 17.4 %collective-permute-start.19 = (bf16[128,3584]{1,0:T(8,128)(2,1)S(1)}, bf16[128,3584]{1,0:T(8,128)(2,1)S(1)}, u32[]{:S(2)}, u32[]{:S(2)}) collective-permute-start(bf16[128,3584]{1,0:T(8,128)(2,1)S(1)} %collective-permute-done.13.mine_ref), channel_id=1, source_target_pairs={{0,1},{1,0},{2,3},{3,2},{4,5},{5,4},{6,7},{7,6},{8,9},{9,8},{10,11... | collective-permute-start | bytes 2752520 | tf_op jit(solution)/shard_map/ppermute | solution.py:194
  115.0 20.9 %collective-permute-start.21 = (bf16[128,3584]{1,0:T(8,128)(2,1)S(1)}, bf16[128,3584]{1,0:T(8,128)(2,1)S(1)}, u32[]{:S(2)}, u32[]{:S(2)}) collective-permute-start(bf16[128,3584]{1,0:T(8,128)(2,1)S(1)} %collective-permute-done.20.mine_ref), channel_id=1, source_target_pairs={{4,0},{8,4},{12,8},{14,12},{10,14},{6,10},{2,6},{0,2},{3,1},{1,5},... | collective-permute-start | bytes 2752520 | tf_op jit(solution)/shard_map/ppermute | solution.py:194
  131.8 9.7 %collective-permute-start.26 = (bf16[128,3584]{1,0:T(8,128)(2,1)S(1)}, bf16[128,3584]{1,0:T(8,128)(2,1)}, u32[]{:S(2)}, u32[]{:S(2)}) collective-permute-start(bf16[128,3584]{1,0:T(8,128)(2,1)S(1)} %collective-permute-done.24.mine_ref), channel_id=1, source_target_pairs={{0,1},{1,0},{2,3},{3,2},{4,5},{5,4},{6,7},{7,6},{8,9},{9,8},{10,11... | collective-permute-start | bytes 2752520 | tf_op jit(solution)/shard_map/ppermute | solution.py:194
  131.8 19.7 %collective-permute-start.28 = (bf16[128,3584]{1,0:T(8,128)(2,1)S(1)}, bf16[128,3584]{1,0:T(8,128)(2,1)S(1)}, u32[]{:S(2)}, u32[]{:S(2)}) collective-permute-start(bf16[128,3584]{1,0:T(8,128)(2,1)S(1)} %collective-permute-done.24.mine_ref), channel_id=1, source_target_pairs={{0,4},{4,8},{8,12},{12,14},{14,10},{10,6},{6,2},{2,0},{1,3},{5,1},... | collective-permute-start | bytes 2752520 | tf_op jit(solution)/shard_map/ppermute | solution.py:194
  135.9 15.6 %collective-permute-start.23 = (bf16[128,3584]{1,0:T(8,128)(2,1)S(1)}, bf16[128,3584]{1,0:T(8,128)(2,1)}, u32[]{:S(2)}, u32[]{:S(2)}) collective-permute-start(bf16[128,3584]{1,0:T(8,128)(2,1)S(1)} %collective-permute-done.21.mine_ref), channel_id=1, source_target_pairs={{0,1},{1,0},{2,3},{3,2},{4,5},{5,4},{6,7},{7,6},{8,9},{9,8},{10,11... | collective-permute-start | bytes 2752520 | tf_op jit(solution)/shard_map/ppermute | solution.py:194
  136.5 20.0 %collective-permute-start.22 = (bf16[128,3584]{1,0:T(8,128)(2,1)S(1)}, bf16[128,3584]{1,0:T(8,128)(2,1)}, u32[]{:S(2)}, u32[]{:S(2)}) collective-permute-start(bf16[128,3584]{1,0:T(8,128)(2,1)S(1)} %collective-permute-done.21.mine_ref), channel_id=1, source_target_pairs={{4,0},{8,4},{12,8},{14,12},{10,14},{6,10},{2,6},{0,2},{3,1},{1,5},... | collective-permute-start | bytes 2752520 | tf_op jit(solution)/shard_map/ppermute | solution.py:194
  138.0 18.4 %all-to-all-start.1 = ((f32[16,16,128]{2,1,0:T(8,128)}), f32[16,16,128]{2,1,0:T(8,128)S(1)}, u32[]{:S(2)}, u32[]{:S(2)}) async-start(f32[16,16,128]{2,1,0:T(8,128)} %get-tuple-element.111), calls=%async_computation.1 | async-start | bytes 262144 | tf_op jit(solution)/shard_map/all_to_all | solution.py:229
  151.5 5.1 %collective-permute-start.29 = (bf16[128,3584]{1,0:T(8,128)(2,1)S(1)}, bf16[128,3584]{1,0:T(8,128)(2,1)S(1)}, u32[]{:S(2)}, u32[]{:S(2)}) collective-permute-start(bf16[128,3584]{1,0:T(8,128)(2,1)S(1)} %collective-permute-done.28.mine_ref), channel_id=1, source_target_pairs={{0,1},{1,0},{2,3},{3,2},{4,5},{5,4},{6,7},{7,6},{8,9},{9,8},{10,11... | collective-permute-start | bytes 2752520 | tf_op jit(solution)/shard_map/ppermute | solution.py:194
  156.5 3.6 %collective-permute-start.27 = (bf16[128,3584]{1,0:T(8,128)(2,1)}, bf16[128,3584]{1,0:T(8,128)(2,1)S(1)}, u32[]{:S(2)}, u32[]{:S(2)}) collective-permute-start(bf16[128,3584]{1,0:T(8,128)(2,1)} %collective-permute-done.22.mine_ref), channel_id=1, source_target_pairs={{0,1},{1,0},{2,3},{3,2},{4,5},{5,4},{6,7},{7,6},{8,9},{9,8},{10,11... | collective-permute-start | bytes 2752520 | tf_op jit(solution)/shard_map/ppermute | solution.py:194
  (13 other events, 54.4 us)

commit v7 on v6

--- a/solution.py
+++ b/solution.py
@@ -13,7 +13,6 @@
 HELD_BYTES = 1 << 25
 RING_BYTES = 1 << 26
 VMEM_BYTES = 24 << 20
-LAG = 4
 
 
 def ring_tables(peer_count):
@@ -31,7 +30,10 @@
     onward += [(2 * ring[i] + 1, 2 * ring[(i - 1) % chips] + 1) for i in range(chips)]
     swap = [(i, i ^ 1) for i in range(peer_count)]
     backward = [(b, a) for a, b in onward]
-    return sources, onward, backward, swap
+    target = dict(onward)
+    second = [(a, target[b]) for a, b in onward]
+    across = [(b, a ^ 1) for a, b in second]
+    return sources, onward, backward, swap, second, across
 
 
 def meta_kernel(owners_ref, blocks_ref, offsets_ref, values_ref, meta_ref):
@@ -57,7 +59,8 @@
     total_ref, bias_ref, lat_ref, pre_ref, acts_ref, bias_sum = refs[-6:]
     first, last = len(refs) == 6, bias_ref.shape[0] == 1
     bias_sum[...] = jnp.zeros_like(bias_sum) if first else refs[1][...]
-    lat_ref[...] = jnp.zeros_like(lat_ref) if first else refs[2][...]
+    if not last:
+        lat_ref[...] = jnp.zeros_like(lat_ref) if first else refs[2][...]
     latents, width = decoder_ref.shape
     tokens = mine_ref.shape[0]
     span = column_span(width)
@@ -91,7 +94,7 @@
                 dense_both.append(dense)
             pre_ref[block : block + 16, at] = jnp.concatenate(kept_both, axis=0).astype(jnp.bfloat16)
             acts_ref[block : block + 16, at] = jnp.concatenate(dense_both, axis=0).astype(jnp.bfloat16)
-        source = order_ref[tile]
+        source = tile if last else order_ref[tile]
         for k in range(per_block):
             lat_ref[source, k : k + 1, :] = jnp.sum(sums[k], axis=0, keepdims=True)
     for at in range(0, width, span):
@@ -131,7 +134,7 @@
     peer_count = lax.axis_size("lat")
     chips = peer_count // 2
     me = lax.axis_index("lat")
-    sources, onward, backward, swap = ring_tables(peer_count)
+    sources, onward, backward, swap, second, across = ring_tables(peer_count)
     order = jnp.asarray(sources)[me]
     own_t = owners.T
     whole = pl.BlockSpec(memory_space=pltpu.VMEM)
@@ -156,6 +159,7 @@
 
     def grad_step(hop, rows, totals, last):
         sums, lanes = (latent_count, width), (latent_count, token_count)
+        lat = (2 if last else peer_count, per_block, token_count)
         return pl.pallas_call(
             functools.partial(grad_kernel, per_block),
             in_specs=[scalars] + [whole] * (4 + len(totals)),
@@ -163,7 +167,7 @@
             out_shape=[
                 jax.ShapeDtypeStruct(sums, jnp.bfloat16) if last else pltpu.VMEM(sums, jnp.float32),
                 jax.ShapeDtypeStruct((1, latent_count), jnp.float32) if last else pltpu.VMEM(lanes, jnp.float32),
-                jax.ShapeDtypeStruct((peer_count, per_block, token_count), jnp.float32),
+                jax.ShapeDtypeStruct(lat, jnp.float32),
                 pltpu.VMEM((latent_count, step_tokens), jnp.bfloat16),
             ],
             scratch_shapes=[
@@ -193,61 +197,55 @@
     def send(rows, way, *first):
         return lax.ppermute(after(rows, *first) if first else rows, "lat", way)
 
-    half = chips // 2
-    later = [("inputs", 1)]
-    for hop in range(1, half):
-        later += [("inputs", hop + 1), ("inputs", -hop)]
-    turns = []
-    for hop in range(1, half + 1):
-        turns += [("grads", hop)] + ([("grads", -hop)] if hop < half else []) + [later.pop(0)]
-    turns += later
+    final, back = chips - 2, chips - 1
     pres, totals, encoder_grad = {}, (), None
 
-    def use(kind, hop, rows, last=False):
-        nonlocal totals, encoder_grad
-        if kind == "grads":
-            *totals, pres[hop] = grad_step(hop, rows, totals, last)
-            return totals[1]
+    def use_grads(hop, rows, last=False):
+        nonlocal totals
+        *totals, pres[hop] = grad_step(hop, rows, totals, last)
+
+    def use_inputs(hop, rows, last=False):
+        nonlocal encoder_grad
         encoder_grad = input_step(pres[hop], rows, encoder_grad, last)
-        return encoder_grad
-
-    held = {(kind, way): rows for kind, rows in (("grads", grad_recon), ("inputs", inputs)) for way in (True, False)}
-    own_grads, own_inputs = send(grad_recon, swap), send(inputs, swap, meta)
-    marks = []
-    last_grads = max(turn for turn, (kind, _) in enumerate(turns) if kind == "grads")
-    returned = None
-
-    def arrive(turn):
-        nonlocal returned
-        kind, hop = turns[turn]
-        last = turn in (last_grads, len(turns) - 1)
-        ready = (meta,) if turn < 2 else (marks[turn - 2],)
-        if turn == len(turns) - 1:
-            ready += (returned,)
-        marks.append(use(kind, hop % chips, (arrived[turn], send(arrived[turn], swap, *ready)), last))
-        if turn == last_grads:
-            returned = lax.all_to_all(totals[2], "lat", split_axis=0, concat_axis=0, tiled=True)
-
-    use("grads", 0, (grad_recon, own_grads))
-    use("inputs", 0, (inputs, own_inputs))
-    arrived = []
-    for turn, (kind, hop) in enumerate(turns):
-        if turn >= LAG:
-            arrive(turn - LAG)
-        ready = () if turn < 3 else (meta,) if turn < LAG else (marks[turn - LAG],)
-        rows = send(held[kind, hop > 0], onward if hop > 0 else backward, *ready)
-        held[kind, hop > 0] = rows
-        arrived.append(rows)
-    for turn in range(len(turns) - LAG, len(turns)):
-        arrive(turn)
-    latent_grads = pick_returned(after(returned, encoder_grad), own_t)
+
+    grad, grad_back = send(grad_recon, onward), send(grad_recon, backward)
+    inward, input_back = send(inputs, onward), send(inputs, backward)
+    own_theirs = send(grad_recon, swap)
+    meta = after(meta, grad, grad_back, inward)
+    grad_next = send(grad, onward)
+    use_grads(0, (grad_recon, own_theirs))
+    input_next = send(inward, onward, totals[1])
+    use_grads(1, (grad, send(grad, swap)))
+    use_grads(back, (grad_back, send(grad_back, swap)))
+    use_inputs(0, (inputs, send(inputs, swap)))
+    use_inputs(1, (inward, send(inward, swap)))
+    use_inputs(back, (input_back, send(input_back, swap)))
+    grad, inward = grad_next, input_next
+    grad_next = send(grad, onward, totals[1])
+    for hop in range(2, final):
+        use_grads(hop, (grad, send(grad, swap)))
+        input_next = send(inward, onward, totals[1])
+        use_inputs(hop, (inward, send(inward, swap)))
+        grad, inward = grad_next, input_next
+        if hop < final - 1:
+            grad_next = send(grad, onward, encoder_grad)
+    returned = lax.all_to_all(totals[2], "lat", split_axis=0, concat_axis=0, tiled=True)
+    totals = totals[:2]
+    use_grads(final, (grad, send(grad, swap)), True)
+    use_inputs(final, (inward, send(inward, swap, returned)), True)
+    lat = totals[2]
+    sent_back = lax.ppermute(lat[0], "lat", second), lax.ppermute(lat[1], "lat", across)
+    nearest = jnp.asarray(sources)[me, 2, 0]
+    latent_grads = pick_returned(returned, own_t, (nearest, nearest ^ 1), sent_back)
     return (totals[0], encoder_grad, totals[1].reshape(latent_count), latent_grads)
 
 
-def pick_returned(returned, own_t):
+def pick_returned(returned, own_t, more_owners=(), more=()):
     owner_id = jnp.arange(returned.shape[0], dtype=jnp.int32)[:, None, None, None]
-    picked = jnp.where(own_t[None, :, None, :] == owner_id, returned[:, None, :, :], 0.0)
-    return jnp.sum(picked, axis=0).reshape(-1, own_t.shape[1]).T
+    picked = jnp.sum(jnp.where(own_t[None, :, None, :] == owner_id, returned[:, None, :, :], 0.0), axis=0)
+    for owner, sent_back in zip(more_owners, more):
+        picked += jnp.where(own_t[:, None, :] == owner, sent_back[None], 0.0)
+    return picked.reshape(-1, own_t.shape[1]).T
 
 
 def build_kernel(block_count, per_block, me_ref, meta_ref, acts_ref, cols_ref):

time: 165 us -> 182 us (1.10)
  waiting for transfers between devices: 85.6 us -> 98.7 us
    all_to_all x1, waiting for transfers between devices: 0.68 us -> 6.07 us  [by_ring(): lax.all_to_all(totals[2], 'lat', split_axis=0, concat_axis=0, tiled=True)]
    ppermute x30, waiting for transfers between devices: 68.5 us -> 72.8 us  [send(): return lax.ppermute(after(rows, *first) if first else rows, 'lat', way)]
    ppermute x0 -> x2, starting transfers between devices: none -> 2.84 us  [the longest x1 2.11 us: by_ring(): lax.ppermute(lat[1], 'lat', across)]
    pallas_call x8, Pallas kernels: 26.4 us -> 28.4 us  [grad_step(): pl.pallas_call(functools.partial(grad_kernel, per_block), in_specs=[scala...]
    unnamed x26 -> x30, local copies, waits for them, and re-layouts: 11.4 us -> 11.2 us
  transfers between devices with their start and end apart: 32 -> 34, of which waited for: 11 -> 15; matrix products, arithmetic and copies ran while one was open for 0% -> 2% of each run, Pallas kernels for 23% -> 22%
where the time goes in v7:
time: 182 us; the launch traced here: 181 us
  waiting for transfers between devices  98.7 us (54%)
  Pallas kernels  42.5 us (23%)
  starting transfers between devices  23.8 us (13%)
  local copies, waits for them, and re-layouts  13.1 us (7%)
    ppermute x30, waiting for transfers between devices, send(): return lax.ppermute(after(rows, *first) if first else rows, 'lat', way)  72.8 us
    pallas_call x8, Pallas kernels, grad_step(): pl.pallas_call(functools.partial(grad_kernel, per_block), in_specs=[scala...  28.4 us
    all_to_all x1, waiting for transfers between devices, by_ring(): meta = lax.all_to_all(meta, 'lat', split_axis=0, concat_axis=0, tiled=True)  18 us
    pallas_call x8, Pallas kernels, input_step(): pl.pallas_call(input_kernel, in_specs=[whole] * (3 + len(totals)), out_sp...  13.4 us
    ppermute x30, starting transfers between devices, send(): return lax.ppermute(after(rows, *first) if first else rows, 'lat', way)  12.4 us
    unnamed x30, local copies, waits for them, and re-layouts  11.2 us
    all_to_all x1, waiting for transfers between devices, by_ring(): lax.all_to_all(totals[2], 'lat', split_axis=0, concat_axis=0, tiled=True)  6.07 us
    all_to_all x1, starting transfers between devices, by_ring(): meta = lax.all_to_all(meta, 'lat', split_axis=0, concat_axis=0, tiled=True)  5.07 us
  transfers between devices with their start and end apart: 34, of which 15 were waited for; matrix products, arithmetic and copies ran while one was open for 2% of the time, Pallas kernels for 22%

profile of v7, /device:TPU:0, one launch (start us, length us, event | category | flops | bytes accessed | tf_op | source)
XLA Modules:
  0.0 181.0 jit_solution(12728177636909121148)
XLA Ops:
  0.6 3.1 %collective-permute-start = (bf16[128,3584]{1,0:T(8,128)(2,1)}, bf16[128,3584]{1,0:T(8,128)(2,1)}, u32[]{:S(2)}, u32[]{:S(2)}) collective-permute-start(bf16[128,3584]{1,0:T(8,128)(2,1)} %mine_ref.2), channel_id=1, source_target_pairs={{0,4},{4,8},{8,12},{12,14},{14,10},{10,6},{6,2},{2,0},{1,3},{5,1},... | collective-permute-start | bytes 2752520 | tf_op jit(solution)/shard_map/ppermute | solution.py:198
  3.7 2.0 %collective-permute-start.2 = (bf16[128,3584]{1,0:T(8,128)(2,1)}, bf16[128,3584]{1,0:T(8,128)(2,1)S(1)}, u32[]{:S(2)}, u32[]{:S(2)}) collective-permute-start(bf16[128,3584]{1,0:T(8,128)(2,1)} %mine_ref.3), channel_id=1, source_target_pairs={{0,4},{4,8},{8,12},{12,14},{14,10},{10,6},{6,2},{2,0},{1,3},{5,1},... | collective-permute-start | bytes 2752520 | tf_op jit(solution)/shard_map/ppermute | solution.py:198
  5.7 18.9 %collective-permute-done.mine_ref = bf16[128,3584]{1,0:T(8,128)(2,1)} collective-permute-done((bf16[128,3584]{1,0:T(8,128)(2,1)}, bf16[128,3584]{1,0:T(8,128)(2,1)}, u32[]{:S(2)}, u32[]{:S(2)}) %collective-permute-start) | collective-permute-done | bytes 917536 | tf_op jit(solution)/shard_map/ppermute | solution.py:198
  30.9 5.1 %all-to-all-start = ((bf16[16,32,128]{2,1,0:T(8,128)(2,1)}), bf16[16,32,128]{2,1,0:T(8,128)(2,1)S(1)}, u32[]{:S(2)}, u32[]{:S(2)}) async-start(bf16[16,32,128]{2,1,0:T(8,128)(2,1)} %meta.1), calls=%async_computation | async-start | bytes 262144 | tf_op jit(solution)/shard_map/all_to_all | solution.py:155
  36.6 2.0 %collective-permute-start.11 = (bf16[128,3584]{1,0:T(8,128)(2,1)}, bf16[128,3584]{1,0:T(8,128)(2,1)S(1)}, u32[]{:S(2)}, u32[]{:S(2)}) collective-permute-start(bf16[128,3584]{1,0:T(8,128)(2,1)} %mine_ref.3), channel_id=1, source_target_pairs={{4,0},{8,4},{12,8},{14,12},{10,14},{6,10},{2,6},{0,2},{3,1},{1,5},... | collective-permute-start | bytes 2752520 | tf_op jit(solution)/shard_map/ppermute | solution.py:198
  38.6 18.0 %all-to-all-done.meta_ref = bf16[16,32,128]{2,1,0:T(8,128)(2,1)S(1)} async-done(((bf16[16,32,128]{2,1,0:T(8,128)(2,1)}), bf16[16,32,128]{2,1,0:T(8,128)(2,1)S(1)}, u32[]{:S(2)}, u32[]{:S(2)}) %all-to-all-start) | async-done | bytes 131104 | tf_op jit(solution)/shard_map/all_to_all | solution.py:155
  59.3 3.4 %grad_step.8 = (f32[256,3584]{1,0:T(8,128)S(1)}, f32[256,128]{1,0:T(8,128)S(1)}, f32[16,16,128]{2,1,0:T(8,128)S(1)}, bf16[256,256]{1,0:T(8,128)(2,1)S(1)}) custom-call(s32[2]{0:T(128)S(1)} %get-tuple-element.96.order_ref, bf16[16,32,128]{2,1,0:T(8,128)(2,1)S(1)} %all-to-all-done.meta_ref, bf16[256,3584]{1,0:T(8,128)(2,1)S(1)} %copy-done.6, ...), custom_call_target="tpu_custom_call" | custom-call | flops 1 | bytes 1 | tf_op jit(solution)/shard_map/grad_step/pallas_call | solution.py:163
  63.4 3.8 %grad_step.9 = (f32[256,3584]{1,0:T(8,128)S(1)}, f32[256,128]{1,0:T(8,128)S(1)}, f32[16,16,128]{2,1,0:T(8,128)S(1)}, bf16[256,256]{1,0:T(8,128)(2,1)S(1)}) custom-call(s32[2]{0:T(128)S(1)} %get-tuple-element.97.order_ref, bf16[16,32,128]{2,1,0:T(8,128)(2,1)S(1)} %all-to-all-done.meta_ref, ...), custom_call_target="tpu_custom_call", output_to_operand_aliasing={{0}: (5, {}), {1}: (6, {})} | custom-call | flops 1 | bytes 1 | tf_op jit(solution)/shard_map/grad_step/pallas_call | solution.py:163
  67.2 3.8 %grad_step.10 = (f32[256,3584]{1,0:T(8,128)S(1)}, f32[256,128]{1,0:T(8,128)S(1)}, f32[16,16,128]{2,1,0:T(8,128)S(1)}, bf16[256,256]{1,0:T(8,128)(2,1)S(1)}) custom-call(s32[2]{0:T(128)S(1)} %get-tuple-element.98.order_ref, bf16[16,32,128]{2,1,0:T(8,128)(2,1)S(1)} %all-to-all-done.meta_ref, ...), custom_call_target="tpu_custom_call", output_to_operand_aliasing={{0}: (5, {}), {1}: (6, {})} | custom-call | flops 1 | bytes 1 | tf_op jit(solution)/shard_map/grad_step/pallas_call | solution.py:163
  71.2 1.6 collective-permute-start.13
  72.9 3.3 %collective-permute-done.9.mine_ref = bf16[128,3584]{1,0:T(8,128)(2,1)S(1)} collective-permute-done((bf16[128,3584]{1,0:T(8,128)(2,1)S(1)}, bf16[128,3584]{1,0:T(8,128)(2,1)S(1)}, u32[]{:S(2)}, u32[]{:S(2)}) %collective-permute-start.9) | collective-permute-done | bytes 917536 | tf_op jit(solution)/shard_map/ppermute | solution.py:198
  76.7 2.9 %grad_step.11 = (f32[256,3584]{1,0:T(8,128)S(1)}, f32[256,128]{1,0:T(8,128)S(1)}, f32[16,16,128]{2,1,0:T(8,128)S(1)}, bf16[256,256]{1,0:T(8,128)(2,1)S(1)}) custom-call(s32[2]{0:T(128)S(1)} %get-tuple-element.95.order_ref, bf16[16,32,128]{2,1,0:T(8,128)(2,1)S(1)} %all-to-all-done.meta_ref, ...), custom_call_target="tpu_custom_call", output_to_operand_aliasing={{0}: (5, {}), {1}: (6, {})} | custom-call | flops 1 | bytes 1 | tf_op jit(solution)/shard_map/grad_step/pallas_call | solution.py:163
  79.8 6.2 %collective-permute-done.7.mine_ref = bf16[128,3584]{1,0:T(8,128)(2,1)S(1)} collective-permute-done((bf16[128,3584]{1,0:T(8,128)(2,1)S(1)}, bf16[128,3584]{1,0:T(8,128)(2,1)S(1)}, u32[]{:S(2)}, u32[]{:S(2)}) %collective-permute-start.7) | collective-permute-done | bytes 917536 | tf_op jit(solution)/shard_map/ppermute | solution.py:198
  91.0 4.8 %collective-permute-done.17.mine_ref = bf16[128,3584]{1,0:T(8,128)(2,1)S(1)} collective-permute-done((bf16[128,3584]{1,0:T(8,128)(2,1)S(1)}, bf16[128,3584]{1,0:T(8,128)(2,1)S(1)}, u32[]{:S(2)}, u32[]{:S(2)}) %collective-permute-start.17) | collective-permute-done | bytes 917536 | tf_op jit(solution)/shard_map/ppermute | solution.py:198
  95.8 2.9 %grad_step.12 = (f32[256,3584]{1,0:T(8,128)S(1)}, f32[256,128]{1,0:T(8,128)S(1)}, f32[16,16,128]{2,1,0:T(8,128)S(1)}, bf16[256,256]{1,0:T(8,128)(2,1)S(1)}) custom-call(s32[2]{0:T(128)S(1)} %get-tuple-element.94.order_ref, bf16[16,32,128]{2,1,0:T(8,128)(2,1)S(1)} %all-to-all-done.meta_ref, ...), custom_call_target="tpu_custom_call", output_to_operand_aliasing={{0}: (5, {}), {1}: (6, {})} | custom-call | flops 1 | bytes 1 | tf_op jit(solution)/shard_map/grad_step/pallas_call | solution.py:163
  98.8 6.9 %collective-permute-done.15.mine_ref = bf16[128,3584]{1,0:T(8,128)(2,1)S(1)} collective-permute-done((bf16[128,3584]{1,0:T(8,128)(2,1)S(1)}, bf16[128,3584]{1,0:T(8,128)(2,1)S(1)}, u32[]{:S(2)}, u32[]{:S(2)}) %collective-permute-start.15) | collective-permute-done | bytes 917536 | tf_op jit(solution)/shard_map/ppermute | solution.py:198
  107.1 8.4 %collective-permute-done.21.mine_ref = bf16[128,3584]{1,0:T(8,128)(2,1)S(1)} collective-permute-done((bf16[128,3584]{1,0:T(8,128)(2,1)S(1)}, bf16[128,3584]{1,0:T(8,128)(2,1)S(1)}, u32[]{:S(2)}, u32[]{:S(2)}) %collective-permute-start.21) | collective-permute-done | bytes 917536 | tf_op jit(solution)/shard_map/ppermute | solution.py:198
  115.5 2.9 %grad_step.13 = (f32[256,3584]{1,0:T(8,128)S(1)}, f32[256,128]{1,0:T(8,128)S(1)}, f32[16,16,128]{2,1,0:T(8,128)S(1)}, bf16[256,256]{1,0:T(8,128)(2,1)S(1)}) custom-call(s32[2]{0:T(128)S(1)} %get-tuple-element.93.order_ref, bf16[16,32,128]{2,1,0:T(8,128)(2,1)S(1)} %all-to-all-done.meta_ref, ...), custom_call_target="tpu_custom_call", output_to_operand_aliasing={{0}: (5, {}), {1}: (6, {})} | custom-call | flops 1 | bytes 1 | tf_op jit(solution)/shard_map/grad_step/pallas_call | solution.py:163
  118.4 6.9 %collective-permute-done.19.mine_ref = bf16[128,3584]{1,0:T(8,128)(2,1)S(1)} collective-permute-done((bf16[128,3584]{1,0:T(8,128)(2,1)S(1)}, bf16[128,3584]{1,0:T(8,128)(2,1)S(1)}, u32[]{:S(2)}, u32[]{:S(2)}) %collective-permute-start.19) | collective-permute-done | bytes 917536 | tf_op jit(solution)/shard_map/ppermute | solution.py:198
  127.8 3.5 %grad_step.14 = (f32[256,3584]{1,0:T(8,128)S(1)}, f32[256,128]{1,0:T(8,128)S(1)}, f32[16,16,128]{2,1,0:T(8,128)}, bf16[256,256]{1,0:T(8,128)(2,1)S(1)}) custom-call(s32[2]{0:T(128)S(1)} %get-tuple-element.92.order_ref, bf16[16,32,128]{2,1,0:T(8,128)(2,1)S(1)} %all-to-all-done.meta_ref, ...), custom_call_target="tpu_custom_call", output_to_operand_aliasing={{0}: (5, {}), {1}: (6, {})} | custom-call | flops 1 | bytes 1 | tf_op jit(solution)/shard_map/grad_step/pallas_call | solution.py:163
  131.3 1.8 copy-done.4
  133.1 5.6 %collective-permute-done.26.mine_ref = bf16[128,3584]{1,0:T(8,128)(2,1)S(1)} collective-permute-done((bf16[128,3584]{1,0:T(8,128)(2,1)S(1)}, bf16[128,3584]{1,0:T(8,128)(2,1)S(1)}, u32[]{:S(2)}, u32[]{:S(2)}) %collective-permute-start.26) | collective-permute-done | bytes 917536 | tf_op jit(solution)/shard_map/ppermute | solution.py:198
  138.7 9.9 %collective-permute-done.23.mine_ref = bf16[128,3584]{1,0:T(8,128)(2,1)} collective-permute-done((bf16[128,3584]{1,0:T(8,128)(2,1)S(1)}, bf16[128,3584]{1,0:T(8,128)(2,1)}, u32[]{:S(2)}, u32[]{:S(2)}) %collective-permute-start.23) | collective-permute-done | bytes 917536 | tf_op jit(solution)/shard_map/ppermute | solution.py:198
  148.7 3.5 %all-to-all-start.1 = ((f32[16,16,128]{2,1,0:T(8,128)}), f32[16,16,128]{2,1,0:T(8,128)S(1)}, u32[]{:S(2)}, u32[]{:S(2)}) async-start(f32[16,16,128]{2,1,0:T(8,128)} %get-tuple-element.85), calls=%async_computation.1 | async-start | bytes 262144 | tf_op jit(solution)/shard_map/all_to_all | solution.py:232
  154.0 6.1 %all-to-all-done.1 = f32[16,16,128]{2,1,0:T(8,128)S(1)} async-done(((f32[16,16,128]{2,1,0:T(8,128)}), f32[16,16,128]{2,1,0:T(8,128)S(1)}, u32[]{:S(2)}, u32[]{:S(2)}) %all-to-all-start.1) | async-done | bytes 131104 | tf_op jit(solution)/shard_map/all_to_all | solution.py:232
  160.9 2.0 %copy-done.1 = f32[3584,256]{1,0:T(8,128)S(1)} copy-done((f32[3584,256]{1,0:T(8,128)S(1)}, f32[3584,256]{1,0:T(8,128)}, u32[]{:S(2)}) %copy-start.1) | copy-done | bytes 3670040
  163.0 2.6 %input_step.14.refs_0_ = f32[3584,256]{1,0:T(8,128)S(1)} custom-call(bf16[256,256]{1,0:T(8,128)(2,1)S(1)} %get-tuple-element.87.pre_ref, bf16[128,3584]{1,0:T(8,128)(2,1)S(1)} %collective-permute-done.26.mine_ref, bf16[128,3584]{1,0:T(8,128)(2,1)} %collective-permute-done.29.theirs_ref, f32[3584,256]{1,0:T(8,128)S(1)} %copy-done.1), custom_call_target="tpu_custom_call", output_to_operand_aliasing={{}: (3, {})} | custom-call | flops 1 | bytes 1 | tf_op jit(solution)/shard_map/input_step/pallas_call | solution.py:186
  165.6 1.8 copy-done.2
  167.4 5.1 %grad_step.15 = (bf16[256,3584]{1,0:T(8,128)(2,1)}, f32[1,256]{1,0:T(1,128)}, f32[2,16,128]{2,1,0:T(8,128)S(1)}, bf16[256,256]{1,0:T(8,128)(2,1)S(1)}) custom-call(s32[2]{0:T(128)S(1)} %get-tuple-element.99.order_ref, bf16[16,32,128]{2,1,0:T(8,128)(2,1)S(1)} %all-to-all-done.meta_ref, bf16[256,3584]{1,0:T(8,128)(2,1)S(1)} %copy-done.7, ...), custom_call_target="tpu_custom_call" | custom-call | flops 1 | bytes 1 | tf_op jit(solution)/shard_map/grad_step/pallas_call | solution.py:163
  173.3 2.1 %collective-permute-start.31 = (f32[16,128]{1,0:T(8,128)S(1)}, f32[16,128]{1,0:T(8,128)S(1)}, u32[]{:S(2)}, u32[]{:S(2)}) collective-permute-start(f32[16,128]{1,0:T(8,128)S(1)} %get-tuple-element.91), channel_id=1, source_target_pairs={{8,1},{12,5},{14,9},{10,13},{6,15},{2,11},{0,7},{4,3},{7,0},{3,4},... | collective-permute-start | bytes 24584 | tf_op jit(solution)/shard_map/ppermute | solution.py:237
  175.5 1.6 collective-permute-done.30
  177.9 3.1 %input_step.15 = bf16[3584,256]{1,0:T(8,128)(2,1)} custom-call(bf16[256,256]{1,0:T(8,128)(2,1)S(1)} %get-tuple-element.82.pre_ref, bf16[128,3584]{1,0:T(8,128)(2,1)} %collective-permute-done.27.mine_ref, bf16[128,3584]{1,0:T(8,128)(2,1)S(1)} %collective-permute-done.28.theirs_ref, f32[3584,256]{1,0:T(8,128)S(1)} %copy-done.3), custom_call_target="tpu_custom_call" | custom-call | flops 1 | bytes 1 | tf_op jit(solution)/shard_map/input_step/pallas_call | solution.py:186
  (91 shorter events, 23.7 us)
Async XLA Ops:
  0.6 24.0 %collective-permute-start = (bf16[128,3584]{1,0:T(8,128)(2,1)}, bf16[128,3584]{1,0:T(8,128)(2,1)}, u32[]{:S(2)}, u32[]{:S(2)}) collective-permute-start(bf16[128,3584]{1,0:T(8,128)(2,1)} %mine_ref.2), channel_id=1, source_target_pairs={{0,4},{4,8},{8,12},{12,14},{14,10},{10,6},{6,2},{2,0},{1,3},{5,1},... | collective-permute-start | bytes 2752520 | tf_op jit(solution)/shard_map/ppermute | solution.py:198
  3.7 23.6 %collective-permute-start.1 = (bf16[128,3584]{1,0:T(8,128)(2,1)}, bf16[128,3584]{1,0:T(8,128)(2,1)}, u32[]{:S(2)}, u32[]{:S(2)}) collective-permute-start(bf16[128,3584]{1,0:T(8,128)(2,1)} %mine_ref.2), channel_id=1, source_target_pairs={{4,0},{8,4},{12,8},{14,12},{10,14},{6,10},{2,6},{0,2},{3,1},{1,5},... | collective-permute-start | bytes 2752520 | tf_op jit(solution)/shard_map/ppermute | solution.py:198
  3.7 32.9 %collective-permute-start.2 = (bf16[128,3584]{1,0:T(8,128)(2,1)}, bf16[128,3584]{1,0:T(8,128)(2,1)S(1)}, u32[]{:S(2)}, u32[]{:S(2)}) collective-permute-start(bf16[128,3584]{1,0:T(8,128)(2,1)} %mine_ref.3), channel_id=1, source_target_pairs={{0,4},{4,8},{8,12},{12,14},{14,10},{10,6},{6,2},{2,0},{1,3},{5,1},... | collective-permute-start | bytes 2752520 | tf_op jit(solution)/shard_map/ppermute | solution.py:198
  5.7 50.9 %collective-permute-start.6 = (bf16[128,3584]{1,0:T(8,128)(2,1)}, bf16[128,3584]{1,0:T(8,128)(2,1)}, u32[]{:S(2)}, u32[]{:S(2)}) collective-permute-start(bf16[128,3584]{1,0:T(8,128)(2,1)} %mine_ref.2), channel_id=1, source_target_pairs={{0,1},{1,0},{2,3},{3,2},{4,5},{5,4},{6,7},{7,6},{8,9},{9,8},{10,11... | collective-permute-start | bytes 2752520 | tf_op jit(solution)/shard_map/ppermute | solution.py:198
  24.6 38.2 %collective-permute-start.3 = (bf16[128,3584]{1,0:T(8,128)(2,1)}, bf16[128,3584]{1,0:T(8,128)(2,1)S(1)}, u32[]{:S(2)}, u32[]{:S(2)}) collective-permute-start(bf16[128,3584]{1,0:T(8,128)(2,1)} %collective-permute-done.mine_ref), channel_id=1, source_target_pairs={{0,4},{4,8},{8,12},{12,14},{14,10},{10,6},{6,2},{2,0},{1,3},{5,1},... | collective-permute-start | bytes 2752520 | tf_op jit(solution)/shard_map/ppermute | solution.py:198
  26.2 36.7 %collective-permute-start.5 = (bf16[128,3584]{1,0:T(8,128)(2,1)}, bf16[128,3584]{1,0:T(8,128)(2,1)}, u32[]{:S(2)}, u32[]{:S(2)}) collective-permute-start(bf16[128,3584]{1,0:T(8,128)(2,1)} %collective-permute-done.mine_ref), channel_id=1, source_target_pairs={{0,1},{1,0},{2,3},{3,2},{4,5},{5,4},{6,7},{7,6},{8,9},{9,8},{10,11... | collective-permute-start | bytes 2752520 | tf_op jit(solution)/shard_map/ppermute | solution.py:198
  27.3 39.9 %collective-permute-start.4 = (bf16[128,3584]{1,0:T(8,128)(2,1)}, bf16[128,3584]{1,0:T(8,128)(2,1)}, u32[]{:S(2)}, u32[]{:S(2)}) collective-permute-start(bf16[128,3584]{1,0:T(8,128)(2,1)} %collective-permute-done.1.mine_ref), channel_id=1, source_target_pairs={{0,1},{1,0},{2,3},{3,2},{4,5},{5,4},{6,7},{7,6},{8,9},{9,8},{10,11... | collective-permute-start | bytes 2752520 | tf_op jit(solution)/shard_map/ppermute | solution.py:198
  30.9 25.8 %all-to-all-start = ((bf16[16,32,128]{2,1,0:T(8,128)(2,1)}), bf16[16,32,128]{2,1,0:T(8,128)(2,1)S(1)}, u32[]{:S(2)}, u32[]{:S(2)}) async-start(bf16[16,32,128]{2,1,0:T(8,128)(2,1)} %meta.1), calls=%async_computation | async-start | bytes 262144 | tf_op jit(solution)/shard_map/all_to_all | solution.py:155
  36.6 34.6 %collective-permute-start.11 = (bf16[128,3584]{1,0:T(8,128)(2,1)}, bf16[128,3584]{1,0:T(8,128)(2,1)S(1)}, u32[]{:S(2)}, u32[]{:S(2)}) collective-permute-start(bf16[128,3584]{1,0:T(8,128)(2,1)} %mine_ref.3), channel_id=1, source_target_pairs={{4,0},{8,4},{12,8},{14,12},{10,14},{6,10},{2,6},{0,2},{3,1},{1,5},... | collective-permute-start | bytes 2752520 | tf_op jit(solution)/shard_map/ppermute | solution.py:198
  62.7 13.4 %collective-permute-start.9 = (bf16[128,3584]{1,0:T(8,128)(2,1)S(1)}, bf16[128,3584]{1,0:T(8,128)(2,1)S(1)}, u32[]{:S(2)}, u32[]{:S(2)}) collective-permute-start(bf16[128,3584]{1,0:T(8,128)(2,1)S(1)} %collective-permute-done.2.mine_ref), channel_id=1, source_target_pairs={{0,4},{4,8},{8,12},{12,14},{14,10},{10,6},{6,2},{2,0},{1,3},{5,1},... | collective-permute-start | bytes 2752520 | tf_op jit(solution)/shard_map/ppermute | solution.py:198
  62.8 13.4 %collective-permute-start.8 = (bf16[128,3584]{1,0:T(8,128)(2,1)S(1)}, bf16[128,3584]{1,0:T(8,128)(2,1)S(1)}, u32[]{:S(2)}, u32[]{:S(2)}) collective-permute-start(bf16[128,3584]{1,0:T(8,128)(2,1)S(1)} %collective-permute-done.3.mine_ref), channel_id=1, source_target_pairs={{0,1},{1,0},{2,3},{3,2},{4,5},{5,4},{6,7},{7,6},{8,9},{9,8},{10,11... | collective-permute-start | bytes 2752520 | tf_op jit(solution)/shard_map/ppermute | solution.py:198
  62.9 16.7 %collective-permute-start.14 = (bf16[128,3584]{1,0:T(8,128)(2,1)S(1)}, bf16[128,3584]{1,0:T(8,128)(2,1)S(1)}, u32[]{:S(2)}, u32[]{:S(2)}) collective-permute-start(bf16[128,3584]{1,0:T(8,128)(2,1)S(1)} %copy-done.9), channel_id=1, source_target_pairs={{0,1},{1,0},{2,3},{3,2},{4,5},{5,4},{6,7},{7,6},{8,9},{9,8},{10,11... | collective-permute-start | bytes 2752520 | tf_op jit(solution)/shard_map/ppermute | solution.py:198
  71.1 14.9 %collective-permute-start.7 = (bf16[128,3584]{1,0:T(8,128)(2,1)S(1)}, bf16[128,3584]{1,0:T(8,128)(2,1)S(1)}, u32[]{:S(2)}, u32[]{:S(2)}) collective-permute-start(bf16[128,3584]{1,0:T(8,128)(2,1)S(1)} %collective-permute-done.3.mine_ref), channel_id=1, source_target_pairs={{0,4},{4,8},{8,12},{12,14},{14,10},{10,6},{6,2},{2,0},{1,3},{5,1},... | collective-permute-start | bytes 2752520 | tf_op jit(solution)/shard_map/ppermute | solution.py:198
  71.2 15.5 %collective-permute-start.13 = (bf16[128,3584]{1,0:T(8,128)(2,1)S(1)}, bf16[128,3584]{1,0:T(8,128)(2,1)S(1)}, u32[]{:S(2)}, u32[]{:S(2)}) collective-permute-start(bf16[128,3584]{1,0:T(8,128)(2,1)S(1)} %collective-permute-done.2.mine_ref), channel_id=1, source_target_pairs={{0,1},{1,0},{2,3},{3,2},{4,5},{5,4},{6,7},{7,6},{8,9},{9,8},{10,11... | collective-permute-start | bytes 2752520 | tf_op jit(solution)/shard_map/ppermute | solution.py:198
  76.2 11.9 %collective-permute-start.12 = (bf16[128,3584]{1,0:T(8,128)(2,1)S(1)}, bf16[128,3584]{1,0:T(8,128)(2,1)S(1)}, u32[]{:S(2)}, u32[]{:S(2)}) collective-permute-start(bf16[128,3584]{1,0:T(8,128)(2,1)S(1)} %collective-permute-done.11.mine_ref), channel_id=1, source_target_pairs={{0,1},{1,0},{2,3},{3,2},{4,5},{5,4},{6,7},{7,6},{8,9},{9,8},{10,11... | collective-permute-start | bytes 2752520 | tf_op jit(solution)/shard_map/ppermute | solution.py:198
  76.2 13.3 %collective-permute-start.10 = (bf16[128,3584]{1,0:T(8,128)(2,1)S(1)}, bf16[128,3584]{1,0:T(8,128)(2,1)S(1)}, u32[]{:S(2)}, u32[]{:S(2)}) collective-permute-start(bf16[128,3584]{1,0:T(8,128)(2,1)S(1)} %collective-permute-done.9.mine_ref), channel_id=1, source_target_pairs={{0,1},{1,0},{2,3},{3,2},{4,5},{5,4},{6,7},{7,6},{8,9},{9,8},{10,11... | collective-permute-start | bytes 2752520 | tf_op jit(solution)/shard_map/ppermute | solution.py:198
  79.6 16.2 %collective-permute-start.17 = (bf16[128,3584]{1,0:T(8,128)(2,1)S(1)}, bf16[128,3584]{1,0:T(8,128)(2,1)S(1)}, u32[]{:S(2)}, u32[]{:S(2)}) collective-permute-start(bf16[128,3584]{1,0:T(8,128)(2,1)S(1)} %collective-permute-done.9.mine_ref), channel_id=1, source_target_pairs={{0,4},{4,8},{8,12},{12,14},{14,10},{10,6},{6,2},{2,0},{1,3},{5,1},... | collective-permute-start | bytes 2752520 | tf_op jit(solution)/shard_map/ppermute | solution.py:198
  86.0 9.8 %collective-permute-start.16 = (bf16[128,3584]{1,0:T(8,128)(2,1)S(1)}, bf16[128,3584]{1,0:T(8,128)(2,1)S(1)}, u32[]{:S(2)}, u32[]{:S(2)}) collective-permute-start(bf16[128,3584]{1,0:T(8,128)(2,1)S(1)} %collective-permute-done.7.mine_ref), channel_id=1, source_target_pairs={{0,1},{1,0},{2,3},{3,2},{4,5},{5,4},{6,7},{7,6},{8,9},{9,8},{10,11... | collective-permute-start | bytes 2752520 | tf_op jit(solution)/shard_map/ppermute | solution.py:198
  90.9 14.7 %collective-permute-start.15 = (bf16[128,3584]{1,0:T(8,128)(2,1)S(1)}, bf16[128,3584]{1,0:T(8,128)(2,1)S(1)}, u32[]{:S(2)}, u32[]{:S(2)}) collective-permute-start(bf16[128,3584]{1,0:T(8,128)(2,1)S(1)} %collective-permute-done.7.mine_ref), channel_id=1, source_target_pairs={{0,4},{4,8},{8,12},{12,14},{14,10},{10,6},{6,2},{2,0},{1,3},{5,1},... | collective-permute-start | bytes 2752520 | tf_op jit(solution)/shard_map/ppermute | solution.py:198
  95.8 9.8 %collective-permute-start.18 = (bf16[128,3584]{1,0:T(8,128)(2,1)S(1)}, bf16[128,3584]{1,0:T(8,128)(2,1)S(1)}, u32[]{:S(2)}, u32[]{:S(2)}) collective-permute-start(bf16[128,3584]{1,0:T(8,128)(2,1)S(1)} %collective-permute-done.17.mine_ref), channel_id=1, source_target_pairs={{0,1},{1,0},{2,3},{3,2},{4,5},{5,4},{6,7},{7,6},{8,9},{9,8},{10,11... | collective-permute-start | bytes 2752520 | tf_op jit(solution)/shard_map/ppermute | solution.py:198
  98.7 16.8 %collective-permute-start.21 = (bf16[128,3584]{1,0:T(8,128)(2,1)S(1)}, bf16[128,3584]{1,0:T(8,128)(2,1)S(1)}, u32[]{:S(2)}, u32[]{:S(2)}) collective-permute-start(bf16[128,3584]{1,0:T(8,128)(2,1)S(1)} %collective-permute-done.17.mine_ref), channel_id=1, source_target_pairs={{0,4},{4,8},{8,12},{12,14},{14,10},{10,6},{6,2},{2,0},{1,3},{5,1},... | collective-permute-start | bytes 2752520 | tf_op jit(solution)/shard_map/ppermute | solution.py:198
  105.7 9.8 %collective-permute-start.20 = (bf16[128,3584]{1,0:T(8,128)(2,1)S(1)}, bf16[128,3584]{1,0:T(8,128)(2,1)S(1)}, u32[]{:S(2)}, u32[]{:S(2)}) collective-permute-start(bf16[128,3584]{1,0:T(8,128)(2,1)S(1)} %collective-permute-done.15.mine_ref), channel_id=1, source_target_pairs={{0,1},{1,0},{2,3},{3,2},{4,5},{5,4},{6,7},{7,6},{8,9},{9,8},{10,11... | collective-permute-start | bytes 2752520 | tf_op jit(solution)/shard_map/ppermute | solution.py:198
  107.1 18.3 %collective-permute-start.19 = (bf16[128,3584]{1,0:T(8,128)(2,1)S(1)}, bf16[128,3584]{1,0:T(8,128)(2,1)S(1)}, u32[]{:S(2)}, u32[]{:S(2)}) collective-permute-start(bf16[128,3584]{1,0:T(8,128)(2,1)S(1)} %collective-permute-done.15.mine_ref), channel_id=1, source_target_pairs={{0,4},{4,8},{8,12},{12,14},{14,10},{10,6},{6,2},{2,0},{1,3},{5,1},... | collective-permute-start | bytes 2752520 | tf_op jit(solution)/shard_map/ppermute | solution.py:198
  115.5 9.8 %collective-permute-start.22 = (bf16[128,3584]{1,0:T(8,128)(2,1)S(1)}, bf16[128,3584]{1,0:T(8,128)(2,1)S(1)}, u32[]{:S(2)}, u32[]{:S(2)}) collective-permute-start(bf16[128,3584]{1,0:T(8,128)(2,1)S(1)} %collective-permute-done.21.mine_ref), channel_id=1, source_target_pairs={{0,1},{1,0},{2,3},{3,2},{4,5},{5,4},{6,7},{7,6},{8,9},{9,8},{10,11... | collective-permute-start | bytes 2752520 | tf_op jit(solution)/shard_map/ppermute | solution.py:198
  125.3 13.4 %collective-permute-start.26 = (bf16[128,3584]{1,0:T(8,128)(2,1)S(1)}, bf16[128,3584]{1,0:T(8,128)(2,1)S(1)}, u32[]{:S(2)}, u32[]{:S(2)}) collective-permute-start(bf16[128,3584]{1,0:T(8,128)(2,1)S(1)} %collective-permute-done.21.mine_ref), channel_id=1, source_target_pairs={{0,4},{4,8},{8,12},{12,14},{14,10},{10,6},{6,2},{2,0},{1,3},{5,1},... | collective-permute-start | bytes 2752520 | tf_op jit(solution)/shard_map/ppermute | solution.py:198
  126.8 21.9 %collective-permute-start.23 = (bf16[128,3584]{1,0:T(8,128)(2,1)S(1)}, bf16[128,3584]{1,0:T(8,128)(2,1)}, u32[]{:S(2)}, u32[]{:S(2)}) collective-permute-start(bf16[128,3584]{1,0:T(8,128)(2,1)S(1)} %collective-permute-done.19.mine_ref), channel_id=1, source_target_pairs={{0,4},{4,8},{8,12},{12,14},{14,10},{10,6},{6,2},{2,0},{1,3},{5,1},... | collective-permute-start | bytes 2752520 | tf_op jit(solution)/shard_map/ppermute | solution.py:198
  138.7 21.4 %collective-permute-start.27 = (bf16[128,3584]{1,0:T(8,128)(2,1)S(1)}, bf16[128,3584]{1,0:T(8,128)(2,1)}, u32[]{:S(2)}, u32[]{:S(2)}) collective-permute-start(bf16[128,3584]{1,0:T(8,128)(2,1)S(1)} %collective-permute-done.26.mine_ref), channel_id=1, source_target_pairs={{0,4},{4,8},{8,12},{12,14},{14,10},{10,6},{6,2},{2,0},{1,3},{5,1},... | collective-permute-start | bytes 2752520 | tf_op jit(solution)/shard_map/ppermute | solution.py:198
  138.7 22.2 %collective-permute-start.29 = (bf16[128,3584]{1,0:T(8,128)(2,1)S(1)}, bf16[128,3584]{1,0:T(8,128)(2,1)}, u32[]{:S(2)}, u32[]{:S(2)}) collective-permute-start(bf16[128,3584]{1,0:T(8,128)(2,1)S(1)} %collective-permute-done.26.mine_ref), channel_id=1, source_target_pairs={{0,1},{1,0},{2,3},{3,2},{4,5},{5,4},{6,7},{7,6},{8,9},{9,8},{10,11... | collective-permute-start | bytes 2752520 | tf_op jit(solution)/shard_map/ppermute | solution.py:198
  148.7 18.8 %collective-permute-start.24 = (bf16[128,3584]{1,0:T(8,128)(2,1)}, bf16[128,3584]{1,0:T(8,128)(2,1)}, u32[]{:S(2)}, u32[]{:S(2)}) collective-permute-start(bf16[128,3584]{1,0:T(8,128)(2,1)} %collective-permute-done.23.mine_ref), channel_id=1, source_target_pairs={{0,1},{1,0},{2,3},{3,2},{4,5},{5,4},{6,7},{7,6},{8,9},{9,8},{10,11... | collective-permute-start | bytes 2752520 | tf_op jit(solution)/shard_map/ppermute | solution.py:198
  148.7 11.4 %all-to-all-start.1 = ((f32[16,16,128]{2,1,0:T(8,128)}), f32[16,16,128]{2,1,0:T(8,128)S(1)}, u32[]{:S(2)}, u32[]{:S(2)}) async-start(f32[16,16,128]{2,1,0:T(8,128)} %get-tuple-element.85), calls=%async_computation.1 | async-start | bytes 262144 | tf_op jit(solution)/shard_map/all_to_all | solution.py:232
  160.1 17.8 %collective-permute-start.28 = (bf16[128,3584]{1,0:T(8,128)(2,1)}, bf16[128,3584]{1,0:T(8,128)(2,1)S(1)}, u32[]{:S(2)}, u32[]{:S(2)}) collective-permute-start(bf16[128,3584]{1,0:T(8,128)(2,1)} %collective-permute-done.27.mine_ref), channel_id=1, source_target_pairs={{0,1},{1,0},{2,3},{3,2},{4,5},{5,4},{6,7},{7,6},{8,9},{9,8},{10,11... | collective-permute-start | bytes 2752520 | tf_op jit(solution)/shard_map/ppermute | solution.py:198
  172.6 4.5 %collective-permute-start.30 = (f32[16,128]{1,0:T(8,128)S(1)}, f32[16,128]{1,0:T(8,128)S(1)}, u32[]{:S(2)}, u32[]{:S(2)}) collective-permute-start(f32[16,128]{1,0:T(8,128)S(1)} %get-tuple-element.90), channel_id=1, source_target_pairs={{0,8},{4,12},{8,14},{12,10},{14,6},{10,2},{6,0},{2,4},{1,7},{5,3},... | collective-permute-start | bytes 24584 | tf_op jit(solution)/shard_map/ppermute | solution.py:237
  (17 other events, 79.5 us)

commit v8 on v6

--- a/solution.py
+++ b/solution.py
@@ -34,26 +34,22 @@
     return sources, onward, backward, swap
 
 
-def meta_kernel(owners_ref, blocks_ref, offsets_ref, values_ref, meta_ref):
+def extend_kernel(rows_ref, owners_ref, blocks_ref, offsets_ref, values_ref, out_ref):
+    width = rows_ref.shape[1]
     count, per_block, tokens = offsets_ref.shape
-    columns = [
-        (jnp.broadcast_to(blocks_ref[i : i + 1, :], (per_block, tokens)) * BLOCK + offsets_ref[i]).astype(jnp.float32)
-        for i in range(count)
-    ]
-    values = [values_ref[i].astype(jnp.float32) for i in range(count)]
-    named = [jnp.broadcast_to(owners_ref[i : i + 1, :], (per_block, tokens)) for i in range(count)]
-    for owner in range(meta_ref.shape[0]):
-        told_columns = jnp.full((per_block, tokens), -1.0, jnp.float32)
-        told_values = jnp.zeros((per_block, tokens), jnp.float32)
-        for i in range(count):
-            mine = named[i] == owner
-            told_columns = jnp.where(mine, columns[i], told_columns)
-            told_values = jnp.where(mine, values[i], told_values)
-        meta_ref[owner, :per_block, :] = told_columns.astype(jnp.bfloat16)
-        meta_ref[owner, per_block:, :] = told_values.astype(jnp.bfloat16)
-
-
-def grad_kernel(per_block, order_ref, meta_ref, decoder_ref, mine_ref, theirs_ref, *refs):
+    pairs = count * per_block
+    out_ref[:, :width] = rows_ref[...]
+    out_ref[:, width:] = jnp.zeros((out_ref.shape[0], out_ref.shape[1] - width), jnp.bfloat16)
+    for i in range(count):
+        at = slice(i * per_block, (i + 1) * per_block)
+        columns = jnp.broadcast_to(blocks_ref[i : i + 1, :], (per_block, tokens)) * BLOCK + offsets_ref[i]
+        out_ref[at, width : width + tokens] = columns.astype(jnp.float32).astype(jnp.bfloat16)
+        out_ref[pairs + at.start : pairs + at.stop, width : width + tokens] = values_ref[i]
+    named = jnp.concatenate([owners_ref[...], jnp.zeros((16 - count, tokens), jnp.int32)], axis=0)
+    out_ref[:16, width + tokens :] = named.astype(jnp.float32).astype(jnp.bfloat16)
+
+
+def grad_kernel(count, per_block, order_ref, decoder_ref, mine_ref, theirs_ref, *refs):
     total_ref, bias_ref, lat_ref, pre_ref, acts_ref, bias_sum = refs[-6:]
     first, last = len(refs) == 6, bias_ref.shape[0] == 1
     bias_sum[...] = jnp.zeros_like(bias_sum) if first else refs[1][...]
@@ -69,9 +65,16 @@
         )
     row = lax.broadcasted_iota(jnp.int32, (8, tokens), 0)
     for tile in range(2):
-        meta = meta_ref[order_ref[tile]].astype(jnp.float32)
-        columns = [jnp.broadcast_to(meta[k : k + 1], (8, tokens)).astype(jnp.int32) for k in range(per_block)]
-        values = [jnp.broadcast_to(meta[per_block + k : per_block + k + 1], (8, tokens)) for k in range(per_block)]
+        entries = (mine_ref, theirs_ref)[tile][:, width : width + tokens].astype(jnp.float32)
+        named = (mine_ref, theirs_ref)[tile][:16, width + tokens :].astype(jnp.float32).astype(jnp.int32)
+        told_columns = jnp.full((per_block, tokens), -1.0, jnp.float32)
+        told_values = jnp.zeros((per_block, tokens), jnp.float32)
+        for i in range(count):
+            own = jnp.broadcast_to(named[i : i + 1], (per_block, tokens)) == order_ref[2]
+            told_columns = jnp.where(own, entries[i * per_block : (i + 1) * per_block], told_columns)
+            told_values = jnp.where(own, entries[(count + i) * per_block : (count + i + 1) * per_block], told_values)
+        columns = [jnp.broadcast_to(told_columns[k : k + 1], (8, tokens)).astype(jnp.int32) for k in range(per_block)]
+        values = [jnp.broadcast_to(told_values[k : k + 1], (8, tokens)) for k in range(per_block)]
         sums = [jnp.zeros((8, tokens), jnp.float32) for _ in range(per_block)]
         at = slice(tile * tokens, (tile + 1) * tokens)
         for block in range(0, latents, 16):
@@ -132,7 +135,7 @@
     chips = peer_count // 2
     me = lax.axis_index("lat")
     sources, onward, backward, swap = ring_tables(peer_count)
-    order = jnp.asarray(sources)[me]
+    order = jnp.concatenate([jnp.asarray(sources)[me], jnp.full((chips, 1), me, jnp.int32)], axis=1)
     own_t = owners.T
     whole = pl.BlockSpec(memory_space=pltpu.VMEM)
     scalars = pl.BlockSpec(memory_space=pltpu.SMEM)
@@ -140,16 +143,15 @@
     light = pl.CostEstimate(flops=1, bytes_accessed=1, transcendentals=0)
     params = pltpu.CompilerParams(vmem_limit_bytes=VMEM_BYTES)
 
-    meta = pl.pallas_call(
-        meta_kernel,
-        in_specs=[whole] * 4,
+    extended = pl.pallas_call(
+        extend_kernel,
+        in_specs=[whole] * 5,
         out_specs=whole,
-        out_shape=jax.ShapeDtypeStruct((peer_count, 2 * per_block, token_count), jnp.bfloat16),
+        out_shape=jax.ShapeDtypeStruct((token_count, width + 2 * token_count), jnp.bfloat16),
         compiler_params=params,
         cost_estimate=light,
-        name="meta",
-    )(own_t, local_blocks.T, offsets.transpose(1, 2, 0), act_values.transpose(1, 2, 0))
-    meta = lax.all_to_all(meta, "lat", split_axis=0, concat_axis=0, tiled=True)
+        name="extend",
+    )(grad_recon, own_t, local_blocks.T, offsets.transpose(1, 2, 0), act_values.transpose(1, 2, 0))
 
     def near(value):
         return pltpu.with_memory_space_constraint(value, pltpu.VMEM)
@@ -157,8 +159,8 @@
     def grad_step(hop, rows, totals, last):
         sums, lanes = (latent_count, width), (latent_count, token_count)
         return pl.pallas_call(
-            functools.partial(grad_kernel, per_block),
-            in_specs=[scalars] + [whole] * (4 + len(totals)),
+            functools.partial(grad_kernel, block_count, per_block),
+            in_specs=[scalars] + [whole] * (3 + len(totals)),
             out_specs=[whole] * 4,
             out_shape=[
                 jax.ShapeDtypeStruct(sums, jnp.bfloat16) if last else pltpu.VMEM(sums, jnp.float32),
@@ -170,11 +172,11 @@
                 pltpu.VMEM((latent_count, step_tokens), jnp.bfloat16),
                 pltpu.VMEM(lanes, jnp.float32),
             ],
-            input_output_aliases={} if last or not totals else {5: 0, 6: 1},
+            input_output_aliases={} if last or not totals else {4: 0, 5: 1},
             compiler_params=params,
             cost_estimate=light,
             name="grad_step",
-        )(order[hop], near(meta), near(decoder), near(rows[0]), near(rows[1]), *map(near, totals))
+        )(order[hop], near(decoder), near(rows[0]), near(rows[1]), *map(near, totals))
 
     def input_step(pre, rows, total, last):
         sums = (width, latent_count)
@@ -193,14 +195,11 @@
     def send(rows, way, *first):
         return lax.ppermute(after(rows, *first) if first else rows, "lat", way)
 
-    half = chips // 2
-    later = [("inputs", 1)]
-    for hop in range(1, half):
-        later += [("inputs", hop + 1), ("inputs", -hop)]
-    turns = []
-    for hop in range(1, half + 1):
-        turns += [("grads", hop)] + ([("grads", -hop)] if hop < half else []) + [later.pop(0)]
-    turns += later
+    turns = [("grads", 1), ("grads", -1)]
+    input_hops = [1, -1, *range(2, chips - 3), -2, chips - 3]
+    for hop in range(2, chips - 1):
+        turns += [("grads", hop), ("inputs", input_hops.pop(0))]
+    turns += [("inputs", hop) for hop in input_hops]
     pres, totals, encoder_grad = {}, (), None
 
     def use(kind, hop, rows, last=False):
@@ -211,8 +210,8 @@
         encoder_grad = input_step(pres[hop], rows, encoder_grad, last)
         return encoder_grad
 
-    held = {(kind, way): rows for kind, rows in (("grads", grad_recon), ("inputs", inputs)) for way in (True, False)}
-    own_grads, own_inputs = send(grad_recon, swap), send(inputs, swap, meta)
+    held = {(kind, way): rows for kind, rows in (("grads", extended), ("inputs", inputs)) for way in (True, False)}
+    own_grads, own_inputs = send(extended, swap), send(inputs, swap)
     marks = []
     last_grads = max(turn for turn, (kind, _) in enumerate(turns) if kind == "grads")
     returned = None
@@ -221,25 +220,25 @@
         nonlocal returned
         kind, hop = turns[turn]
         last = turn in (last_grads, len(turns) - 1)
-        ready = (meta,) if turn < 2 else (marks[turn - 2],)
+        ready = () if turn < 2 else (marks[turn - 2],)
         if turn == len(turns) - 1:
             ready += (returned,)
         marks.append(use(kind, hop % chips, (arrived[turn], send(arrived[turn], swap, *ready)), last))
         if turn == last_grads:
             returned = lax.all_to_all(totals[2], "lat", split_axis=0, concat_axis=0, tiled=True)
 
-    use("grads", 0, (grad_recon, own_grads))
+    use("grads", 0, (extended, own_grads))
     use("inputs", 0, (inputs, own_inputs))
     arrived = []
     for turn, (kind, hop) in enumerate(turns):
-        if turn >= LAG:
-            arrive(turn - LAG)
-        ready = () if turn < 3 else (meta,) if turn < LAG else (marks[turn - LAG],)
+        while len(marks) < (turn - 2 if turn == len(turns) - 1 else turn - LAG + 1):
+            arrive(len(marks))
+        ready = (marks[-1],) if marks else ()
         rows = send(held[kind, hop > 0], onward if hop > 0 else backward, *ready)
         held[kind, hop > 0] = rows
         arrived.append(rows)
-    for turn in range(len(turns) - LAG, len(turns)):
-        arrive(turn)
+    while len(marks) < len(turns):
+        arrive(len(marks))
     latent_grads = pick_returned(after(returned, encoder_grad), own_t)
     return (totals[0], encoder_grad, totals[1].reshape(latent_count), latent_grads)
 
@@ -383,10 +382,14 @@
     return (decoder_grad, jnp.concatenate(encoder_parts, axis=0), bias_grad, latent_grads)
 
 
-def per_device(grad_recon, *others):
-    row_bytes = lax.axis_size("lat") * grad_recon.size * grad_recon.dtype.itemsize
-    way = by_ring if 2 * row_bytes <= RING_BYTES and lax.axis_size("lat") % 4 == 0 else by_gather
-    return way(grad_recon, *others)
+def per_device(grad_recon, inputs, decoder, owners, local_blocks, offsets, act_values):
+    peer_count = lax.axis_size("lat")
+    token_count = grad_recon.shape[0]
+    entries = offsets.shape[1] * offsets.shape[2]
+    small = 2 * peer_count * grad_recon.size * grad_recon.dtype.itemsize <= RING_BYTES
+    fits = token_count == BLOCK and 2 * entries <= token_count and offsets.shape[2] == 16 and offsets.shape[1] <= 16
+    way = by_ring if small and fits and peer_count % 4 == 0 and peer_count >= 16 else by_gather
+    return way(grad_recon, inputs, decoder, owners, local_blocks, offsets, act_values)
 
 
 def solution(mesh):

time: 165 us -> 190 us (1.15)
  waiting for transfers between devices: 85.6 us -> 107 us
  starting transfers between devices: 23.2 us -> 28.4 us
  Pallas kernels: 41.4 us -> 39 us
    ppermute x30, waiting for transfers between devices: 68.5 us -> 97.7 us  [send(): return lax.ppermute(after(rows, *first) if first else rows, 'lat', way)]
    all_to_all x1 -> x0, waiting for transfers between devices: 16.4 us -> none  [by_ring(): meta = lax.all_to_all(meta, 'lat', split_axis=0, concat_axis=0, tiled=True)]
    all_to_all x1, waiting for transfers between devices: 0.68 us -> 9.68 us  [arrive(): lax.all_to_all(totals[2], 'lat', split_axis=0, concat_axis=0, tiled=True)]
    ppermute x30, starting transfers between devices: 13.3 us -> 22.1 us  [send(): return lax.ppermute(after(rows, *first) if first else rows, 'lat', way)]
    all_to_all x1 -> x0, starting transfers between devices: 6.36 us -> none  [by_ring(): meta = lax.all_to_all(meta, 'lat', split_axis=0, concat_axis=0, tiled=True)]
    all_to_all x1, starting transfers between devices: 3.51 us -> 6.35 us  [arrive(): lax.all_to_all(totals[2], 'lat', split_axis=0, concat_axis=0, tiled=True)]
  transfers between devices with their start and end apart: 32 -> 31, of which waited for: 11 -> 12; matrix products, arithmetic and copies ran while one was open for 0% -> 1% of each run, Pallas kernels for 23% -> 19%
where the time goes in v8:
time: 190 us; the launch traced here: 189 us
  waiting for transfers between devices  107 us (56%)
  Pallas kernels  39 us (21%)
  starting transfers between devices  28.4 us (15%)
  local copies, waits for them, and re-layouts  12.3 us (6%)
    ppermute x30, waiting for transfers between devices, send(): return lax.ppermute(after(rows, *first) if first else rows, 'lat', way)  97.7 us
    pallas_call x8, Pallas kernels, grad_step(): pl.pallas_call(functools.partial(grad_kernel, block_count, per_block), in...  25.7 us
    ppermute x30, starting transfers between devices, send(): return lax.ppermute(after(rows, *first) if first else rows, 'lat', way)  22.1 us
    pallas_call x8, Pallas kernels, input_step(): pl.pallas_call(input_kernel, in_specs=[whole] * (3 + len(totals)), out_sp...  13.2 us
    unnamed x26, local copies, waits for them, and re-layouts  11.4 us
    all_to_all x1, waiting for transfers between devices, arrive(): lax.all_to_all(totals[2], 'lat', split_axis=0, concat_axis=0, tiled=True)  9.68 us
    all_to_all x1, starting transfers between devices, arrive(): lax.all_to_all(totals[2], 'lat', split_axis=0, concat_axis=0, tiled=True)  6.35 us
  transfers between devices with their start and end apart: 31, of which 12 were waited for; matrix products, arithmetic and copies ran while one was open for 1% of the time, Pallas kernels for 19%

profile of v8, /device:TPU:0, one launch (start us, length us, event | category | flops | bytes accessed | tf_op | source)
XLA Modules:
  0.0 188.8 jit_solution(12281018526782606617)
XLA Ops:
  4.7 3.1 %collective-permute-start = (bf16[128,3840]{1,0:T(8,128)(2,1)S(1)}, bf16[128,3840]{1,0:T(8,128)(2,1)}, u32[]{:S(2)}, u32[]{:S(2)}) collective-permute-start(bf16[128,3840]{1,0:T(8,128)(2,1)S(1)} %extend.1.mine_ref), channel_id=1, source_target_pairs={{0,4},{4,8},{8,12},{12,14},{14,10},{10,6},{6,2},{2,0},{1,3},{5,1},... | collective-permute-start | bytes 2949128 | tf_op jit(solution)/shard_map/ppermute | solution.py:196
  7.8 22.1 %collective-permute-done.mine_ref = bf16[128,3840]{1,0:T(8,128)(2,1)} collective-permute-done((bf16[128,3840]{1,0:T(8,128)(2,1)S(1)}, bf16[128,3840]{1,0:T(8,128)(2,1)}, u32[]{:S(2)}, u32[]{:S(2)}) %collective-permute-start) | collective-permute-done | bytes 983072 | tf_op jit(solution)/shard_map/ppermute | solution.py:196
  29.9 1.6 collective-permute-start.1
  33.6 1.5 copy-done.4
  35.1 3.3 %grad_step.8 = (f32[256,3584]{1,0:T(8,128)S(1)}, f32[256,128]{1,0:T(8,128)S(1)}, f32[16,16,128]{2,1,0:T(8,128)S(1)}, bf16[256,256]{1,0:T(8,128)(2,1)S(1)}) custom-call(s32[3]{0:T(128)S(1)} %get-tuple-element.104.order_ref, bf16[256,3584]{1,0:T(8,128)(2,1)S(1)} %copy-done.4, bf16[128,3840]{1,0:T(8,128)(2,1)S(1)} %extend.1.mine_ref, ...), custom_call_target="tpu_custom_call" | custom-call | flops 1 | bytes 1 | tf_op jit(solution)/shard_map/grad_step/pallas_call | solution.py:161
  38.4 3.9 %grad_step.9 = (f32[256,3584]{1,0:T(8,128)S(1)}, f32[256,128]{1,0:T(8,128)S(1)}, f32[16,16,128]{2,1,0:T(8,128)S(1)}, bf16[256,256]{1,0:T(8,128)(2,1)S(1)}) custom-call(s32[3]{0:T(128)S(1)} %get-tuple-element.103.order_ref, bf16[256,3584]{1,0:T(8,128)(2,1)S(1)} %copy-done.4, ...), custom_call_target="tpu_custom_call", output_to_operand_aliasing={{0}: (4, {}), {1}: (5, {})} | custom-call | flops 1 | bytes 1 | tf_op jit(solution)/shard_map/grad_step/pallas_call | solution.py:161
  42.4 2.2 %collective-permute-done.1.mine_ref = bf16[128,3840]{1,0:T(8,128)(2,1)S(1)} collective-permute-done((bf16[128,3840]{1,0:T(8,128)(2,1)}, bf16[128,3840]{1,0:T(8,128)(2,1)S(1)}, u32[]{:S(2)}, u32[]{:S(2)}) %collective-permute-start.1) | collective-permute-done | bytes 983072 | tf_op jit(solution)/shard_map/ppermute | solution.py:196
  45.8 1.7 collective-permute-start.15
  47.5 2.9 %grad_step.10 = (f32[256,3584]{1,0:T(8,128)S(1)}, f32[256,128]{1,0:T(8,128)S(1)}, f32[16,16,128]{2,1,0:T(8,128)S(1)}, bf16[256,256]{1,0:T(8,128)(2,1)S(1)}) custom-call(s32[3]{0:T(128)S(1)} %get-tuple-element.106.order_ref, bf16[256,3584]{1,0:T(8,128)(2,1)S(1)} %copy-done.4, ...), custom_call_target="tpu_custom_call", output_to_operand_aliasing={{0}: (4, {}), {1}: (5, {})} | custom-call | flops 1 | bytes 1 | tf_op jit(solution)/shard_map/grad_step/pallas_call | solution.py:161
  50.4 18.2 %collective-permute-done.15.mine_ref = bf16[128,3584]{1,0:T(8,128)(2,1)S(1)} collective-permute-done((bf16[128,3584]{1,0:T(8,128)(2,1)S(1)}, bf16[128,3584]{1,0:T(8,128)(2,1)S(1)}, u32[]{:S(2)}, u32[]{:S(2)}) %collective-permute-start.15) | collective-permute-done | bytes 917536 | tf_op jit(solution)/shard_map/ppermute | solution.py:196
  68.5 2.9 %grad_step.11 = (f32[256,3584]{1,0:T(8,128)S(1)}, f32[256,128]{1,0:T(8,128)S(1)}, f32[16,16,128]{2,1,0:T(8,128)S(1)}, bf16[256,256]{1,0:T(8,128)(2,1)S(1)}) custom-call(s32[3]{0:T(128)S(1)} %get-tuple-element.105.order_ref, bf16[256,3584]{1,0:T(8,128)(2,1)S(1)} %copy-done.4, ...), custom_call_target="tpu_custom_call", output_to_operand_aliasing={{0}: (4, {}), {1}: (5, {})} | custom-call | flops 1 | bytes 1 | tf_op jit(solution)/shard_map/grad_step/pallas_call | solution.py:161
  73.7 1.6 collective-permute-start.19
  75.3 2.9 %grad_step.12 = (f32[256,3584]{1,0:T(8,128)S(1)}, f32[256,128]{1,0:T(8,128)S(1)}, f32[16,16,128]{2,1,0:T(8,128)S(1)}, bf16[256,256]{1,0:T(8,128)(2,1)S(1)}) custom-call(s32[3]{0:T(128)S(1)} %get-tuple-element.107.order_ref, bf16[256,3584]{1,0:T(8,128)(2,1)S(1)} %copy-done.4, ...), custom_call_target="tpu_custom_call", output_to_operand_aliasing={{0}: (4, {}), {1}: (5, {})} | custom-call | flops 1 | bytes 1 | tf_op jit(solution)/shard_map/grad_step/pallas_call | solution.py:161
  78.2 16.2 %collective-permute-done.8.mine_ref = bf16[128,3840]{1,0:T(8,128)(2,1)S(1)} collective-permute-done((bf16[128,3840]{1,0:T(8,128)(2,1)S(1)}, bf16[128,3840]{1,0:T(8,128)(2,1)S(1)}, u32[]{:S(2)}, u32[]{:S(2)}) %collective-permute-start.8) | collective-permute-done | bytes 983072 | tf_op jit(solution)/shard_map/ppermute | solution.py:196
  94.4 1.7 collective-permute-start.10
  96.8 1.4 input_step.9.refs_0_
  100.2 2.9 %grad_step.13 = (f32[256,3584]{1,0:T(8,128)S(1)}, f32[256,128]{1,0:T(8,128)S(1)}, f32[16,16,128]{2,1,0:T(8,128)S(1)}, bf16[256,256]{1,0:T(8,128)(2,1)S(1)}) custom-call(s32[3]{0:T(128)S(1)} %get-tuple-element.108.order_ref, bf16[256,3584]{1,0:T(8,128)(2,1)S(1)} %copy-done.5, ...), custom_call_target="tpu_custom_call", output_to_operand_aliasing={{0}: (4, {}), {1}: (5, {})} | custom-call | flops 1 | bytes 1 | tf_op jit(solution)/shard_map/grad_step/pallas_call | solution.py:161
  103.1 5.9 %collective-permute-done.10.mine_ref = bf16[128,3840]{1,0:T(8,128)(2,1)S(1)} collective-permute-done((bf16[128,3840]{1,0:T(8,128)(2,1)S(1)}, bf16[128,3840]{1,0:T(8,128)(2,1)S(1)}, u32[]{:S(2)}, u32[]{:S(2)}) %collective-permute-start.10) | collective-permute-done | bytes 983072 | tf_op jit(solution)/shard_map/ppermute | solution.py:196
  111.6 7.2 %collective-permute-done.18.mine_ref = bf16[128,3584]{1,0:T(8,128)(2,1)S(1)} collective-permute-done((bf16[128,3584]{1,0:T(8,128)(2,1)S(1)}, bf16[128,3584]{1,0:T(8,128)(2,1)S(1)}, u32[]{:S(2)}, u32[]{:S(2)}) %collective-permute-start.18) | collective-permute-done | bytes 917536 | tf_op jit(solution)/shard_map/ppermute | solution.py:196
  120.1 2.9 %grad_step.14 = (f32[256,3584]{1,0:T(8,128)S(1)}, f32[256,128]{1,0:T(8,128)S(1)}, f32[16,16,128]{2,1,0:T(8,128)S(1)}, bf16[256,256]{1,0:T(8,128)(2,1)S(1)}) custom-call(s32[3]{0:T(128)S(1)} %get-tuple-element.102.order_ref, bf16[256,3584]{1,0:T(8,128)(2,1)S(1)} %copy-done.5, ...), custom_call_target="tpu_custom_call", output_to_operand_aliasing={{0}: (4, {}), {1}: (5, {})} | custom-call | flops 1 | bytes 1 | tf_op jit(solution)/shard_map/grad_step/pallas_call | solution.py:161
  122.9 6.4 %collective-permute-done.12.mine_ref = bf16[128,3840]{1,0:T(8,128)(2,1)S(1)} collective-permute-done((bf16[128,3840]{1,0:T(8,128)(2,1)S(1)}, bf16[128,3840]{1,0:T(8,128)(2,1)S(1)}, u32[]{:S(2)}, u32[]{:S(2)}) %collective-permute-start.12) | collective-permute-done | bytes 983072 | tf_op jit(solution)/shard_map/ppermute | solution.py:196
  130.7 8.4 %collective-permute-done.21.mine_ref = bf16[128,3584]{1,0:T(8,128)(2,1)S(1)} collective-permute-done((bf16[128,3584]{1,0:T(8,128)(2,1)S(1)}, bf16[128,3584]{1,0:T(8,128)(2,1)S(1)}, u32[]{:S(2)}, u32[]{:S(2)}) %collective-permute-start.21) | collective-permute-done | bytes 917536 | tf_op jit(solution)/shard_map/ppermute | solution.py:196
  143.0 9.5 %collective-permute-done.23.mine_ref = bf16[128,3584]{1,0:T(8,128)(2,1)S(1)} collective-permute-done((bf16[128,3584]{1,0:T(8,128)(2,1)S(1)}, bf16[128,3584]{1,0:T(8,128)(2,1)S(1)}, u32[]{:S(2)}, u32[]{:S(2)}) %collective-permute-start.23) | collective-permute-done | bytes 917536 | tf_op jit(solution)/shard_map/ppermute | solution.py:196
  152.5 2.0 %collective-permute-start.28 = (bf16[128,3584]{1,0:T(8,128)(2,1)S(1)}, bf16[128,3584]{1,0:T(8,128)(2,1)S(1)}, u32[]{:S(2)}, u32[]{:S(2)}) collective-permute-start(bf16[128,3584]{1,0:T(8,128)(2,1)S(1)} %collective-permute-done.19.mine_ref), channel_id=1, source_target_pairs={{4,0},{8,4},{12,8},{14,12},{10,14},{6,10},{2,6},{0,2},{3,1},{1,5},... | collective-permute-start | bytes 2752520 | tf_op jit(solution)/shard_map/ppermute | solution.py:196
  154.6 4.1 %grad_step.15 = (bf16[256,3584]{1,0:T(8,128)(2,1)}, f32[1,256]{1,0:T(1,128)}, f32[16,16,128]{2,1,0:T(8,128)}, bf16[256,256]{1,0:T(8,128)(2,1)S(1)}) custom-call(s32[3]{0:T(128)S(1)} %get-tuple-element.109.order_ref, bf16[256,3584]{1,0:T(8,128)(2,1)S(1)} %copy-done.5, bf16[128,3840]{1,0:T(8,128)(2,1)S(1)} %collective-permute-done.12.mine_ref, ...), custom_call_target="tpu_custom_call" | custom-call | flops 1 | bytes 1 | tf_op jit(solution)/shard_map/grad_step/pallas_call | solution.py:161
  158.6 6.3 %all-to-all-start = ((f32[16,16,128]{2,1,0:T(8,128)}), f32[16,16,128]{2,1,0:T(8,128)S(1)}, u32[]{:S(2)}, u32[]{:S(2)}) async-start(f32[16,16,128]{2,1,0:T(8,128)} %get-tuple-element.96), calls=%async_computation | async-start | bytes 262144 | tf_op jit(solution)/shard_map/all_to_all | solution.py:228
  165.0 2.0 %copy-done.1 = f32[3584,256]{1,0:T(8,128)S(1)} copy-done((f32[3584,256]{1,0:T(8,128)S(1)}, f32[3584,256]{1,0:T(8,128)}, u32[]{:S(2)}) %copy-start.1) | copy-done | bytes 3670040
  167.1 2.5 %input_step.13.refs_0_ = f32[3584,256]{1,0:T(8,128)S(1)} custom-call(bf16[256,256]{1,0:T(8,128)(2,1)S(1)} %get-tuple-element.93.pre_ref, bf16[128,3584]{1,0:T(8,128)(2,1)S(1)} %collective-permute-done.23.mine_ref, bf16[128,3584]{1,0:T(8,128)(2,1)} %collective-permute-done.26.theirs_ref, f32[3584,256]{1,0:T(8,128)S(1)} %copy-done.1), custom_call_target="tpu_custom_call", output_to_operand_aliasing={{}: (3, {})} | custom-call | flops 1 | bytes 1 | tf_op jit(solution)/shard_map/input_step/pallas_call | solution.py:184
  169.6 1.8 copy-done.2
  171.8 9.7 %all-to-all-done = f32[16,16,128]{2,1,0:T(8,128)S(1)} async-done(((f32[16,16,128]{2,1,0:T(8,128)}), f32[16,16,128]{2,1,0:T(8,128)S(1)}, u32[]{:S(2)}, u32[]{:S(2)}) %all-to-all-start) | async-done | bytes 131104 | tf_op jit(solution)/shard_map/all_to_all | solution.py:228
  181.6 2.0 %copy-done.3 = f32[3584,256]{1,0:T(8,128)S(1)} copy-done((f32[3584,256]{1,0:T(8,128)S(1)}, f32[3584,256]{1,0:T(8,128)}, u32[]{:S(2)}) %copy-start.3) | copy-done | bytes 3670040
  185.0 3.1 %input_step.15 = bf16[3584,256]{1,0:T(8,128)(2,1)} custom-call(bf16[256,256]{1,0:T(8,128)(2,1)S(1)} %get-tuple-element.80.pre_ref, bf16[128,3584]{1,0:T(8,128)(2,1)} %collective-permute-done.24.mine_ref, bf16[128,3584]{1,0:T(8,128)(2,1)S(1)} %collective-permute-done.27.theirs_ref, f32[3584,256]{1,0:T(8,128)S(1)} %input_step.14.refs_0_), custom_call_target="tpu_custom_call" | custom-call | flops 1 | bytes 1 | tf_op jit(solution)/shard_map/input_step/pallas_call | solution.py:184
  (77 shorter events, 24.2 us)
Async XLA Ops:
  4.7 25.2 %collective-permute-start = (bf16[128,3840]{1,0:T(8,128)(2,1)S(1)}, bf16[128,3840]{1,0:T(8,128)(2,1)}, u32[]{:S(2)}, u32[]{:S(2)}) collective-permute-start(bf16[128,3840]{1,0:T(8,128)(2,1)S(1)} %extend.1.mine_ref), channel_id=1, source_target_pairs={{0,4},{4,8},{8,12},{12,14},{14,10},{10,6},{6,2},{2,0},{1,3},{5,1},... | collective-permute-start | bytes 2949128 | tf_op jit(solution)/shard_map/ppermute | solution.py:196
  7.8 24.6 %collective-permute-start.6 = (bf16[128,3840]{1,0:T(8,128)(2,1)S(1)}, bf16[128,3840]{1,0:T(8,128)(2,1)S(1)}, u32[]{:S(2)}, u32[]{:S(2)}) collective-permute-start(bf16[128,3840]{1,0:T(8,128)(2,1)S(1)} %extend.1.mine_ref), channel_id=1, source_target_pairs={{4,0},{8,4},{12,8},{14,12},{10,14},{6,10},{2,6},{0,2},{3,1},{1,5},... | collective-permute-start | bytes 2949128 | tf_op jit(solution)/shard_map/ppermute | solution.py:196
  7.8 25.8 %collective-permute-start.3 = (bf16[128,3840]{1,0:T(8,128)(2,1)S(1)}, bf16[128,3840]{1,0:T(8,128)(2,1)}, u32[]{:S(2)}, u32[]{:S(2)}) collective-permute-start(bf16[128,3840]{1,0:T(8,128)(2,1)S(1)} %extend.1.mine_ref), channel_id=1, source_target_pairs={{0,1},{1,0},{2,3},{3,2},{4,5},{5,4},{6,7},{7,6},{8,9},{9,8},{10,11... | collective-permute-start | bytes 2949128 | tf_op jit(solution)/shard_map/ppermute | solution.py:196
  29.9 8.5 %collective-permute-start.2 = (bf16[128,3840]{1,0:T(8,128)(2,1)}, bf16[128,3840]{1,0:T(8,128)(2,1)}, u32[]{:S(2)}, u32[]{:S(2)}) collective-permute-start(bf16[128,3840]{1,0:T(8,128)(2,1)} %collective-permute-done.mine_ref), channel_id=1, source_target_pairs={{0,1},{1,0},{2,3},{3,2},{4,5},{5,4},{6,7},{7,6},{8,9},{9,8},{10,11... | collective-permute-start | bytes 2949128 | tf_op jit(solution)/shard_map/ppermute | solution.py:196
  29.9 14.7 %collective-permute-start.1 = (bf16[128,3840]{1,0:T(8,128)(2,1)}, bf16[128,3840]{1,0:T(8,128)(2,1)S(1)}, u32[]{:S(2)}, u32[]{:S(2)}) collective-permute-start(bf16[128,3840]{1,0:T(8,128)(2,1)} %collective-permute-done.mine_ref), channel_id=1, source_target_pairs={{0,4},{4,8},{8,12},{12,14},{14,10},{10,6},{6,2},{2,0},{1,3},{5,1},... | collective-permute-start | bytes 2949128 | tf_op jit(solution)/shard_map/ppermute | solution.py:196
  32.5 15.0 %collective-permute-start.7 = (bf16[128,3840]{1,0:T(8,128)(2,1)S(1)}, bf16[128,3840]{1,0:T(8,128)(2,1)S(1)}, u32[]{:S(2)}, u32[]{:S(2)}) collective-permute-start(bf16[128,3840]{1,0:T(8,128)(2,1)S(1)} %collective-permute-done.6.mine_ref), channel_id=1, source_target_pairs={{0,1},{1,0},{2,3},{3,2},{4,5},{5,4},{6,7},{7,6},{8,9},{9,8},{10,11... | collective-permute-start | bytes 2949128 | tf_op jit(solution)/shard_map/ppermute | solution.py:196
  44.6 23.9 %collective-permute-start.5 = (bf16[128,3840]{1,0:T(8,128)(2,1)S(1)}, bf16[128,3840]{1,0:T(8,128)(2,1)S(1)}, u32[]{:S(2)}, u32[]{:S(2)}) collective-permute-start(bf16[128,3840]{1,0:T(8,128)(2,1)S(1)} %collective-permute-done.1.mine_ref), channel_id=1, source_target_pairs={{0,1},{1,0},{2,3},{3,2},{4,5},{5,4},{6,7},{7,6},{8,9},{9,8},{10,11... | collective-permute-start | bytes 2949128 | tf_op jit(solution)/shard_map/ppermute | solution.py:196
  44.6 26.8 %collective-permute-start.4 = (bf16[128,3840]{1,0:T(8,128)(2,1)S(1)}, bf16[128,3840]{1,0:T(8,128)(2,1)S(1)}, u32[]{:S(2)}, u32[]{:S(2)}) collective-permute-start(bf16[128,3840]{1,0:T(8,128)(2,1)S(1)} %collective-permute-done.1.mine_ref), channel_id=1, source_target_pairs={{0,4},{4,8},{8,12},{12,14},{14,10},{10,6},{6,2},{2,0},{1,3},{5,1},... | collective-permute-start | bytes 2949128 | tf_op jit(solution)/shard_map/ppermute | solution.py:196
  45.8 22.7 %collective-permute-start.15 = (bf16[128,3584]{1,0:T(8,128)(2,1)S(1)}, bf16[128,3584]{1,0:T(8,128)(2,1)S(1)}, u32[]{:S(2)}, u32[]{:S(2)}) collective-permute-start(bf16[128,3584]{1,0:T(8,128)(2,1)S(1)} %copy-done.7), channel_id=1, source_target_pairs={{0,4},{4,8},{8,12},{12,14},{14,10},{10,6},{6,2},{2,0},{1,3},{5,1},... | collective-permute-start | bytes 2752520 | tf_op jit(solution)/shard_map/ppermute | solution.py:196
  71.4 3.9 %collective-permute-start.9 = (bf16[128,3840]{1,0:T(8,128)(2,1)S(1)}, bf16[128,3840]{1,0:T(8,128)(2,1)S(1)}, u32[]{:S(2)}, u32[]{:S(2)}) collective-permute-start(bf16[128,3840]{1,0:T(8,128)(2,1)S(1)} %collective-permute-done.4.mine_ref), channel_id=1, source_target_pairs={{0,1},{1,0},{2,3},{3,2},{4,5},{5,4},{6,7},{7,6},{8,9},{9,8},{10,11... | collective-permute-start | bytes 2949128 | tf_op jit(solution)/shard_map/ppermute | solution.py:196
  71.5 22.9 %collective-permute-start.8 = (bf16[128,3840]{1,0:T(8,128)(2,1)S(1)}, bf16[128,3840]{1,0:T(8,128)(2,1)S(1)}, u32[]{:S(2)}, u32[]{:S(2)}) collective-permute-start(bf16[128,3840]{1,0:T(8,128)(2,1)S(1)} %collective-permute-done.4.mine_ref), channel_id=1, source_target_pairs={{0,4},{4,8},{8,12},{12,14},{14,10},{10,6},{6,2},{2,0},{1,3},{5,1},... | collective-permute-start | bytes 2949128 | tf_op jit(solution)/shard_map/ppermute | solution.py:196
  72.7 23.4 %collective-permute-start.17 = (bf16[128,3584]{1,0:T(8,128)(2,1)S(1)}, bf16[128,3584]{1,0:T(8,128)(2,1)S(1)}, u32[]{:S(2)}, u32[]{:S(2)}) collective-permute-start(bf16[128,3584]{1,0:T(8,128)(2,1)S(1)} %copy-done.7), channel_id=1, source_target_pairs={{0,1},{1,0},{2,3},{3,2},{4,5},{5,4},{6,7},{7,6},{8,9},{9,8},{10,11... | collective-permute-start | bytes 2752520 | tf_op jit(solution)/shard_map/ppermute | solution.py:196
  73.7 23.1 %collective-permute-start.16 = (bf16[128,3584]{1,0:T(8,128)(2,1)S(1)}, bf16[128,3584]{1,0:T(8,128)(2,1)S(1)}, u32[]{:S(2)}, u32[]{:S(2)}) collective-permute-start(bf16[128,3584]{1,0:T(8,128)(2,1)S(1)} %collective-permute-done.15.mine_ref), channel_id=1, source_target_pairs={{0,1},{1,0},{2,3},{3,2},{4,5},{5,4},{6,7},{7,6},{8,9},{9,8},{10,11... | collective-permute-start | bytes 2752520 | tf_op jit(solution)/shard_map/ppermute | solution.py:196
  73.7 24.5 %collective-permute-start.19 = (bf16[128,3584]{1,0:T(8,128)(2,1)S(1)}, bf16[128,3584]{1,0:T(8,128)(2,1)S(1)}, u32[]{:S(2)}, u32[]{:S(2)}) collective-permute-start(bf16[128,3584]{1,0:T(8,128)(2,1)S(1)} %copy-done.7), channel_id=1, source_target_pairs={{4,0},{8,4},{12,8},{14,12},{10,14},{6,10},{2,6},{0,2},{3,1},{1,5},... | collective-permute-start | bytes 2752520 | tf_op jit(solution)/shard_map/ppermute | solution.py:196
  94.4 5.8 %collective-permute-start.11 = (bf16[128,3840]{1,0:T(8,128)(2,1)S(1)}, bf16[128,3840]{1,0:T(8,128)(2,1)S(1)}, u32[]{:S(2)}, u32[]{:S(2)}) collective-permute-start(bf16[128,3840]{1,0:T(8,128)(2,1)S(1)} %collective-permute-done.8.mine_ref), channel_id=1, source_target_pairs={{0,1},{1,0},{2,3},{3,2},{4,5},{5,4},{6,7},{7,6},{8,9},{9,8},{10,11... | collective-permute-start | bytes 2949128 | tf_op jit(solution)/shard_map/ppermute | solution.py:196
  94.4 14.6 %collective-permute-start.10 = (bf16[128,3840]{1,0:T(8,128)(2,1)S(1)}, bf16[128,3840]{1,0:T(8,128)(2,1)S(1)}, u32[]{:S(2)}, u32[]{:S(2)}) collective-permute-start(bf16[128,3840]{1,0:T(8,128)(2,1)S(1)} %collective-permute-done.8.mine_ref), channel_id=1, source_target_pairs={{0,4},{4,8},{8,12},{12,14},{14,10},{10,6},{6,2},{2,0},{1,3},{5,1},... | collective-permute-start | bytes 2949128 | tf_op jit(solution)/shard_map/ppermute | solution.py:196
  98.2 12.0 %collective-permute-start.20 = (bf16[128,3584]{1,0:T(8,128)(2,1)S(1)}, bf16[128,3584]{1,0:T(8,128)(2,1)S(1)}, u32[]{:S(2)}, u32[]{:S(2)}) collective-permute-start(bf16[128,3584]{1,0:T(8,128)(2,1)S(1)} %collective-permute-done.19.mine_ref), channel_id=1, source_target_pairs={{0,1},{1,0},{2,3},{3,2},{4,5},{5,4},{6,7},{7,6},{8,9},{9,8},{10,11... | collective-permute-start | bytes 2752520 | tf_op jit(solution)/shard_map/ppermute | solution.py:196
  99.3 19.5 %collective-permute-start.18 = (bf16[128,3584]{1,0:T(8,128)(2,1)S(1)}, bf16[128,3584]{1,0:T(8,128)(2,1)S(1)}, u32[]{:S(2)}, u32[]{:S(2)}) collective-permute-start(bf16[128,3584]{1,0:T(8,128)(2,1)S(1)} %collective-permute-done.15.mine_ref), channel_id=1, source_target_pairs={{0,4},{4,8},{8,12},{12,14},{14,10},{10,6},{6,2},{2,0},{1,3},{5,1},... | collective-permute-start | bytes 2752520 | tf_op jit(solution)/shard_map/ppermute | solution.py:196
  108.9 11.1 %collective-permute-start.13 = (bf16[128,3840]{1,0:T(8,128)(2,1)S(1)}, bf16[128,3840]{1,0:T(8,128)(2,1)S(1)}, u32[]{:S(2)}, u32[]{:S(2)}) collective-permute-start(bf16[128,3840]{1,0:T(8,128)(2,1)S(1)} %collective-permute-done.10.mine_ref), channel_id=1, source_target_pairs={{0,1},{1,0},{2,3},{3,2},{4,5},{5,4},{6,7},{7,6},{8,9},{9,8},{10,11... | collective-permute-start | bytes 2949128 | tf_op jit(solution)/shard_map/ppermute | solution.py:196
  109.0 20.4 %collective-permute-start.12 = (bf16[128,3840]{1,0:T(8,128)(2,1)S(1)}, bf16[128,3840]{1,0:T(8,128)(2,1)S(1)}, u32[]{:S(2)}, u32[]{:S(2)}) collective-permute-start(bf16[128,3840]{1,0:T(8,128)(2,1)S(1)} %collective-permute-done.10.mine_ref), channel_id=1, source_target_pairs={{0,4},{4,8},{8,12},{12,14},{14,10},{10,6},{6,2},{2,0},{1,3},{5,1},... | collective-permute-start | bytes 2949128 | tf_op jit(solution)/shard_map/ppermute | solution.py:196
  118.8 10.5 %collective-permute-start.22 = (bf16[128,3584]{1,0:T(8,128)(2,1)S(1)}, bf16[128,3584]{1,0:T(8,128)(2,1)S(1)}, u32[]{:S(2)}, u32[]{:S(2)}) collective-permute-start(bf16[128,3584]{1,0:T(8,128)(2,1)S(1)} %collective-permute-done.18.mine_ref), channel_id=1, source_target_pairs={{0,1},{1,0},{2,3},{3,2},{4,5},{5,4},{6,7},{7,6},{8,9},{9,8},{10,11... | collective-permute-start | bytes 2752520 | tf_op jit(solution)/shard_map/ppermute | solution.py:196
  118.8 20.4 %collective-permute-start.21 = (bf16[128,3584]{1,0:T(8,128)(2,1)S(1)}, bf16[128,3584]{1,0:T(8,128)(2,1)S(1)}, u32[]{:S(2)}, u32[]{:S(2)}) collective-permute-start(bf16[128,3584]{1,0:T(8,128)(2,1)S(1)} %collective-permute-done.18.mine_ref), channel_id=1, source_target_pairs={{0,4},{4,8},{8,12},{12,14},{14,10},{10,6},{6,2},{2,0},{1,3},{5,1},... | collective-permute-start | bytes 2752520 | tf_op jit(solution)/shard_map/ppermute | solution.py:196
  129.3 25.3 %collective-permute-start.14 = (bf16[128,3840]{1,0:T(8,128)(2,1)S(1)}, bf16[128,3840]{1,0:T(8,128)(2,1)S(1)}, u32[]{:S(2)}, u32[]{:S(2)}) collective-permute-start(bf16[128,3840]{1,0:T(8,128)(2,1)S(1)} %collective-permute-done.12.mine_ref), channel_id=1, source_target_pairs={{0,1},{1,0},{2,3},{3,2},{4,5},{5,4},{6,7},{7,6},{8,9},{9,8},{10,11... | collective-permute-start | bytes 2949128 | tf_op jit(solution)/shard_map/ppermute | solution.py:196
  139.1 2.5 %collective-permute-start.25 = (bf16[128,3584]{1,0:T(8,128)(2,1)S(1)}, bf16[128,3584]{1,0:T(8,128)(2,1)S(1)}, u32[]{:S(2)}, u32[]{:S(2)}) collective-permute-start(bf16[128,3584]{1,0:T(8,128)(2,1)S(1)} %collective-permute-done.21.mine_ref), channel_id=1, source_target_pairs={{0,1},{1,0},{2,3},{3,2},{4,5},{5,4},{6,7},{7,6},{8,9},{9,8},{10,11... | collective-permute-start | bytes 2752520 | tf_op jit(solution)/shard_map/ppermute | solution.py:196
  139.1 13.4 %collective-permute-start.23 = (bf16[128,3584]{1,0:T(8,128)(2,1)S(1)}, bf16[128,3584]{1,0:T(8,128)(2,1)S(1)}, u32[]{:S(2)}, u32[]{:S(2)}) collective-permute-start(bf16[128,3584]{1,0:T(8,128)(2,1)S(1)} %collective-permute-done.21.mine_ref), channel_id=1, source_target_pairs={{0,4},{4,8},{8,12},{12,14},{14,10},{10,6},{6,2},{2,0},{1,3},{5,1},... | collective-permute-start | bytes 2752520 | tf_op jit(solution)/shard_map/ppermute | solution.py:196
  143.0 15.6 %copy-start = (f32[3584,256]{1,0:T(8,128)}, f32[3584,256]{1,0:T(8,128)S(1)}, u32[]{:S(2)}) copy-start(f32[3584,256]{1,0:T(8,128)S(1)} %input_step.12.refs_0_) | copy-start | bytes 11010052
  152.5 12.5 %collective-permute-start.26 = (bf16[128,3584]{1,0:T(8,128)(2,1)S(1)}, bf16[128,3584]{1,0:T(8,128)(2,1)}, u32[]{:S(2)}, u32[]{:S(2)}) collective-permute-start(bf16[128,3584]{1,0:T(8,128)(2,1)S(1)} %collective-permute-done.23.mine_ref), channel_id=1, source_target_pairs={{0,1},{1,0},{2,3},{3,2},{4,5},{5,4},{6,7},{7,6},{8,9},{9,8},{10,11... | collective-permute-start | bytes 2752520 | tf_op jit(solution)/shard_map/ppermute | solution.py:196
  152.5 19.3 %collective-permute-start.28 = (bf16[128,3584]{1,0:T(8,128)(2,1)S(1)}, bf16[128,3584]{1,0:T(8,128)(2,1)S(1)}, u32[]{:S(2)}, u32[]{:S(2)}) collective-permute-start(bf16[128,3584]{1,0:T(8,128)(2,1)S(1)} %collective-permute-done.19.mine_ref), channel_id=1, source_target_pairs={{4,0},{8,4},{12,8},{14,12},{10,14},{6,10},{2,6},{0,2},{3,1},{1,5},... | collective-permute-start | bytes 2752520 | tf_op jit(solution)/shard_map/ppermute | solution.py:196
  158.6 22.9 %collective-permute-start.24 = (bf16[128,3584]{1,0:T(8,128)(2,1)S(1)}, bf16[128,3584]{1,0:T(8,128)(2,1)}, u32[]{:S(2)}, u32[]{:S(2)}) collective-permute-start(bf16[128,3584]{1,0:T(8,128)(2,1)S(1)} %collective-permute-done.23.mine_ref), channel_id=1, source_target_pairs={{0,4},{4,8},{8,12},{12,14},{14,10},{10,6},{6,2},{2,0},{1,3},{5,1},... | collective-permute-start | bytes 2752520 | tf_op jit(solution)/shard_map/ppermute | solution.py:196
  158.6 22.9 %all-to-all-start = ((f32[16,16,128]{2,1,0:T(8,128)}), f32[16,16,128]{2,1,0:T(8,128)S(1)}, u32[]{:S(2)}, u32[]{:S(2)}) async-start(f32[16,16,128]{2,1,0:T(8,128)} %get-tuple-element.96), calls=%async_computation | async-start | bytes 262144 | tf_op jit(solution)/shard_map/all_to_all | solution.py:228
  171.8 9.7 %collective-permute-start.29 = (bf16[128,3584]{1,0:T(8,128)(2,1)S(1)}, bf16[128,3584]{1,0:T(8,128)(2,1)S(1)}, u32[]{:S(2)}, u32[]{:S(2)}) collective-permute-start(bf16[128,3584]{1,0:T(8,128)(2,1)S(1)} %collective-permute-done.28.mine_ref), channel_id=1, source_target_pairs={{0,1},{1,0},{2,3},{3,2},{4,5},{5,4},{6,7},{7,6},{8,9},{9,8},{10,11... | collective-permute-start | bytes 2752520 | tf_op jit(solution)/shard_map/ppermute | solution.py:196
  181.5 3.5 %collective-permute-start.27 = (bf16[128,3584]{1,0:T(8,128)(2,1)}, bf16[128,3584]{1,0:T(8,128)(2,1)S(1)}, u32[]{:S(2)}, u32[]{:S(2)}) collective-permute-start(bf16[128,3584]{1,0:T(8,128)(2,1)} %collective-permute-done.24.mine_ref), channel_id=1, source_target_pairs={{0,1},{1,0},{2,3},{3,2},{4,5},{5,4},{6,7},{7,6},{8,9},{9,8},{10,11... | collective-permute-start | bytes 2752520 | tf_op jit(solution)/shard_map/ppermute | solution.py:196
  (12 other events, 36.6 us)

commit v9 on v6

--- a/solution.py
+++ b/solution.py
@@ -18,39 +18,113 @@
 
 def ring_tables(peer_count):
     chips = peer_count // 2
+    half = chips // 2
     ring = [chip for chip in range(chips) if chip % 2 == 0] + [chip for chip in reversed(range(chips)) if chip % 2]
     place = {chip: spot for spot, chip in enumerate(ring)}
     sources = np.zeros((peer_count, chips, 2), np.int32)
+    ways = np.zeros((peer_count, peer_count + 2), np.int32)
     for device in range(peer_count):
         chip, core = divmod(device, 2)
         sign = 1 - 2 * core
         for hop in range(chips):
             behind, ahead = ring[(place[chip] - sign * hop) % chips], ring[(place[chip] + sign * hop) % chips]
             sources[device, hop] = (2 * behind + core, 2 * ahead + 1 - core)
+            ways[device, 2 * ahead : 2 * ahead + 2] = 0 if hop == 0 else 1 if hop <= half else 2
+            if hop in (half, half + 1):
+                ways[device, peer_count + hop - half] = ahead
     onward = [(2 * ring[i], 2 * ring[(i + 1) % chips]) for i in range(chips)]
     onward += [(2 * ring[i] + 1, 2 * ring[(i - 1) % chips] + 1) for i in range(chips)]
+    backward = [(b, a) for a, b in onward]
     swap = [(i, i ^ 1) for i in range(peer_count)]
-    backward = [(b, a) for a, b in onward]
-    return sources, onward, backward, swap
-
-
-def meta_kernel(owners_ref, blocks_ref, offsets_ref, values_ref, meta_ref):
+    return sources, ways, onward, backward, swap
+
+
+def one_hot(spots):
+    count = spots.shape[1]
+    row = lax.broadcasted_iota(jnp.int32, (count, count), 0)
+    return jnp.where(row == jnp.broadcast_to(spots, (count, count)), 1.0, 0.0).astype(jnp.bfloat16)
+
+
+def spread_kernel(ways_ref, *refs):
+    sources, refs = refs[:6], refs[6:]
+    meta_ref, orders_ref, *chains = refs[:6]
+    held, sems = refs[6:12], refs[12]
+    copies = [pltpu.make_async_copy(source, kept, sems.at[i]) for i, (source, kept) in enumerate(zip(sources, held))]
+    for copy in copies:
+        copy.start()
+    owners_ref, blocks_ref, offsets_ref, values_ref = held[:4]
+    peers = meta_ref.shape[0]
     count, per_block, tokens = offsets_ref.shape
+    token = lax.broadcasted_iota(jnp.int32, (8, tokens), 1)
+    up_to = jnp.where(
+        lax.broadcasted_iota(jnp.int32, (tokens, tokens), 0) <= lax.broadcasted_iota(jnp.int32, (tokens, tokens), 1), 1.0, 0.0
+    ).astype(jnp.bfloat16)
+    copies[0].wait()
+    owners = owners_ref[...]
+    orders_ref[0] = one_hot(token[:1])
+    for way in range(2):
+        named = jnp.max(jnp.where((owners >> 1) == ways_ref[peers + way], 1.0, 0.0), axis=0, keepdims=True)
+        named = jnp.broadcast_to(named, (8, tokens))
+        before = jnp.dot(named.astype(jnp.bfloat16), up_to, preferred_element_type=jnp.float32).astype(jnp.int32)
+        total = jnp.max(before, axis=1, keepdims=True)
+        spots = jnp.where(named > 0, before - 1, total + token - before)
+        orders_ref[way + 1] = one_hot(spots[:1])
+    for copy in copies[1:4]:
+        copy.wait()
     columns = [
         (jnp.broadcast_to(blocks_ref[i : i + 1, :], (per_block, tokens)) * BLOCK + offsets_ref[i]).astype(jnp.float32)
         for i in range(count)
     ]
     values = [values_ref[i].astype(jnp.float32) for i in range(count)]
     named = [jnp.broadcast_to(owners_ref[i : i + 1, :], (per_block, tokens)) for i in range(count)]
-    for owner in range(meta_ref.shape[0]):
+    for owner in range(peers):
         told_columns = jnp.full((per_block, tokens), -1.0, jnp.float32)
         told_values = jnp.zeros((per_block, tokens), jnp.float32)
         for i in range(count):
             mine = named[i] == owner
             told_columns = jnp.where(mine, columns[i], told_columns)
             told_values = jnp.where(mine, values[i], told_values)
-        meta_ref[owner, :per_block, :] = told_columns.astype(jnp.bfloat16)
-        meta_ref[owner, per_block:, :] = told_values.astype(jnp.bfloat16)
+        told = jnp.concatenate([told_columns, told_values], axis=0).astype(jnp.bfloat16)
+        told = lax.dot_general(
+            told, orders_ref[ways_ref[owner]], (((1,), (1,)), ((), ())), preferred_element_type=jnp.float32
+        )
+        meta_ref[owner] = told.astype(jnp.bfloat16)
+    for i, rows_ref in enumerate(held[4:]):
+        copies[4 + i].wait()
+        width = rows_ref.shape[1]
+        span = column_span(width)
+        for at in range(0, width, span):
+            for way in range(2):
+                moved = jnp.dot(orders_ref[way + 1], rows_ref[:, at : at + span], preferred_element_type=jnp.float32)
+                chains[2 * i + way][:, at : at + span] = moved.astype(jnp.bfloat16)
+
+
+def pick_kernel(ways_ref, owners_ref, orders_ref, returned_ref, out_ref):
+    peers, per_block, tokens = returned_ref.shape
+    count = owners_ref.shape[0]
+    out_ref[...] = jnp.zeros_like(out_ref)
+    for owner in range(peers):
+        rest, pieces = returned_ref[owner], []
+        for _ in range(3):
+            pieces.append(rest.astype(jnp.bfloat16))
+            rest = rest - pieces[-1].astype(jnp.float32)
+        back = jnp.dot(
+            jnp.concatenate(pieces, axis=0), orders_ref[ways_ref[owner]], preferred_element_type=jnp.float32
+        )
+        back = back[:per_block] + back[per_block : 2 * per_block] + back[2 * per_block :]
+        for i in range(count):
+            mine = jnp.broadcast_to(owners_ref[i : i + 1, :], (per_block, tokens)) == owner
+            at = slice(i * per_block, (i + 1) * per_block)
+            out_ref[at, :] = jnp.where(mine, back, out_ref[at, :])
+
+
+def both_rows(mine_ref, theirs_ref, at, tokens):
+    parts = []
+    for rows_ref in (mine_ref, theirs_ref):
+        parts.append(rows_ref[:, at])
+        if rows_ref.shape[0] < tokens:
+            parts.append(jnp.zeros((tokens - rows_ref.shape[0], parts[-1].shape[1]), jnp.bfloat16))
+    return jnp.concatenate(parts, axis=0)
 
 
 def grad_kernel(per_block, order_ref, meta_ref, decoder_ref, mine_ref, theirs_ref, *refs):
@@ -59,11 +133,11 @@
     bias_sum[...] = jnp.zeros_like(bias_sum) if first else refs[1][...]
     lat_ref[...] = jnp.zeros_like(lat_ref) if first else refs[2][...]
     latents, width = decoder_ref.shape
-    tokens = mine_ref.shape[0]
+    tokens = meta_ref.shape[2]
     span = column_span(width)
     products = jnp.zeros((latents, 2 * tokens), jnp.float32)
     for at in range(0, width, span):
-        rows = jnp.concatenate([mine_ref[:, at : at + span], theirs_ref[:, at : at + span]], axis=0)
+        rows = both_rows(mine_ref, theirs_ref, slice(at, at + span), tokens)
         products += lax.dot_general(
             decoder_ref[:, at : at + span], rows, (((1,), (1,)), ((), ())), preferred_element_type=jnp.float32
         )
@@ -95,7 +169,7 @@
         for k in range(per_block):
             lat_ref[source, k : k + 1, :] = jnp.sum(sums[k], axis=0, keepdims=True)
     for at in range(0, width, span):
-        rows = jnp.concatenate([mine_ref[:, at : at + span], theirs_ref[:, at : at + span]], axis=0)
+        rows = both_rows(mine_ref, theirs_ref, slice(at, at + span), tokens)
         term = jnp.dot(acts_ref[...], rows, preferred_element_type=jnp.float32)
         if not first:
             term += refs[0][:, at : at + span]
@@ -108,7 +182,7 @@
     width = mine_ref.shape[1]
     span = column_span(width)
     for at in range(0, width, span):
-        rows = jnp.concatenate([mine_ref[:, at : at + span], theirs_ref[:, at : at + span]], axis=0)
+        rows = both_rows(mine_ref, theirs_ref, slice(at, at + span), pre_ref.shape[1] // 2)
         term = lax.dot_general(rows, pre_ref[...], (((0,), (1,)), ((), ())), preferred_element_type=jnp.float32)
         if len(refs) == 2:
             term += refs[0][at : at + span, :]
@@ -131,8 +205,10 @@
     peer_count = lax.axis_size("lat")
     chips = peer_count // 2
     me = lax.axis_index("lat")
-    sources, onward, backward, swap = ring_tables(peer_count)
-    order = jnp.asarray(sources)[me]
+    sources, ways, onward, backward, swap = ring_tables(peer_count)
+    order, ways = jnp.asarray(sources)[me], jnp.asarray(ways)[me]
+    capacity = (3 * token_count * block_count + 2 * peer_count - 1) // (2 * peer_count)
+    needed = min(token_count, -(-2 * capacity // 16) * 16)
     own_t = owners.T
     whole = pl.BlockSpec(memory_space=pltpu.VMEM)
     scalars = pl.BlockSpec(memory_space=pltpu.SMEM)
@@ -140,15 +216,22 @@
     light = pl.CostEstimate(flops=1, bytes_accessed=1, transcendentals=0)
     params = pltpu.CompilerParams(vmem_limit_bytes=VMEM_BYTES)
 
-    meta = pl.pallas_call(
-        meta_kernel,
-        in_specs=[whole] * 4,
-        out_specs=whole,
-        out_shape=jax.ShapeDtypeStruct((peer_count, 2 * per_block, token_count), jnp.bfloat16),
+    arrays = (own_t, local_blocks.T, offsets.transpose(1, 2, 0), act_values.transpose(1, 2, 0), grad_recon, inputs)
+    rows_shape = (token_count, width)
+    meta, orders, *chains = pl.pallas_call(
+        spread_kernel,
+        in_specs=[scalars] + [pl.BlockSpec(memory_space=pltpu.HBM)] * len(arrays),
+        out_specs=[whole] * 6,
+        out_shape=[
+            jax.ShapeDtypeStruct((peer_count, 2 * per_block, token_count), jnp.bfloat16),
+            jax.ShapeDtypeStruct((3, token_count, token_count), jnp.bfloat16),
+            *[pltpu.VMEM(rows_shape, jnp.bfloat16)] * 4,
+        ],
+        scratch_shapes=[pltpu.VMEM(array.shape, array.dtype) for array in arrays] + [pltpu.SemaphoreType.DMA((6,))],
         compiler_params=params,
         cost_estimate=light,
-        name="meta",
-    )(own_t, local_blocks.T, offsets.transpose(1, 2, 0), act_values.transpose(1, 2, 0))
+        name="spread",
+    )(ways, *[pltpu.with_memory_space_constraint(array, pltpu.HBM) for array in arrays])
     meta = lax.all_to_all(meta, "lat", split_axis=0, concat_axis=0, tiled=True)
 
     def near(value):
@@ -211,22 +294,31 @@
         encoder_grad = input_step(pres[hop], rows, encoder_grad, last)
         return encoder_grad
 
-    held = {(kind, way): rows for kind, rows in (("grads", grad_recon), ("inputs", inputs)) for way in (True, False)}
+    held = dict(zip([("grads", True), ("grads", False), ("inputs", True), ("inputs", False)], chains))
     own_grads, own_inputs = send(grad_recon, swap), send(inputs, swap, meta)
     marks = []
     last_grads = max(turn for turn, (kind, _) in enumerate(turns) if kind == "grads")
-    returned = None
+    latent_grads = None
 
     def arrive(turn):
-        nonlocal returned
+        nonlocal latent_grads
         kind, hop = turns[turn]
         last = turn in (last_grads, len(turns) - 1)
         ready = (meta,) if turn < 2 else (marks[turn - 2],)
         if turn == len(turns) - 1:
-            ready += (returned,)
+            ready += (latent_grads,)
         marks.append(use(kind, hop % chips, (arrived[turn], send(arrived[turn], swap, *ready)), last))
         if turn == last_grads:
             returned = lax.all_to_all(totals[2], "lat", split_axis=0, concat_axis=0, tiled=True)
+            latent_grads = pl.pallas_call(
+                pick_kernel,
+                in_specs=[scalars] + [whole] * 3,
+                out_specs=whole,
+                out_shape=jax.ShapeDtypeStruct((block_count * per_block, token_count), jnp.float32),
+                compiler_params=params,
+                cost_estimate=light,
+                name="pick",
+            )(ways, own_t, orders, returned)
 
     use("grads", 0, (grad_recon, own_grads))
     use("inputs", 0, (inputs, own_inputs))
@@ -235,13 +327,15 @@
         if turn >= LAG:
             arrive(turn - LAG)
         ready = () if turn < 3 else (meta,) if turn < LAG else (marks[turn - LAG],)
-        rows = send(held[kind, hop > 0], onward if hop > 0 else backward, *ready)
+        rows = held[kind, hop > 0]
+        if hop in (half, 1 - half):
+            rows = rows[:needed]
+        rows = send(rows, onward if hop > 0 else backward, *ready)
         held[kind, hop > 0] = rows
         arrived.append(rows)
     for turn in range(len(turns) - LAG, len(turns)):
         arrive(turn)
-    latent_grads = pick_returned(after(returned, encoder_grad), own_t)
-    return (totals[0], encoder_grad, totals[1].reshape(latent_count), latent_grads)
+    return (totals[0], encoder_grad, totals[1].reshape(latent_count), latent_grads.T)
 
 
 def pick_returned(returned, own_t):
@@ -383,10 +477,12 @@
     return (decoder_grad, jnp.concatenate(encoder_parts, axis=0), bias_grad, latent_grads)
 
 
-def per_device(grad_recon, *others):
-    row_bytes = lax.axis_size("lat") * grad_recon.size * grad_recon.dtype.itemsize
-    way = by_ring if 2 * row_bytes <= RING_BYTES and lax.axis_size("lat") % 4 == 0 else by_gather
-    return way(grad_recon, *others)
+def per_device(grad_recon, inputs, decoder, owners, local_blocks, offsets, act_values):
+    peer_count = lax.axis_size("lat")
+    small = 2 * peer_count * grad_recon.size * grad_recon.dtype.itemsize <= RING_BYTES
+    fits = grad_recon.shape[0] == BLOCK and offsets.shape[2] == 16 and decoder.shape[0] <= 256
+    way = by_ring if small and fits and peer_count % 4 == 0 and peer_count >= 8 else by_gather
+    return way(grad_recon, inputs, decoder, owners, local_blocks, offsets, act_values)
 
 
 def solution(mesh):

time: 165 us -> 171 us (1.036)
  blocking collectives: 0 us -> 17.6 us
  local copies, waits for them, and re-layouts: 12.1 us -> 5.22 us
    all_to_all x0 -> x1, blocking collectives: none -> 17.6 us  [arrive(): lax.all_to_all(totals[2], 'lat', split_axis=0, concat_axis=0, tiled=True)]
    unnamed x26 -> x16, local copies, waits for them, and re-layouts: 11.4 us -> 3.64 us
    pallas_call x1 -> x2, Pallas kernels: 0.71 us -> 5.32 us  [the longest x1 3.86 us: by_ring(): pl.pallas_call(spread_kernel, in_specs=[scalars] + [pl.BlockSpec(memory_s...]
    ppermute x30, waiting for transfers between devices: 68.5 us -> 64.5 us  [send(): return lax.ppermute(after(rows, *first) if first else rows, 'lat', way)]
    all_to_all x1, waiting for transfers between devices: 16.4 us -> 20 us  [by_ring(): meta = lax.all_to_all(meta, 'lat', split_axis=0, concat_axis=0, tiled=True)]
    all_to_all x1 -> x0, starting transfers between devices: 3.51 us -> none  [arrive(): lax.all_to_all(totals[2], 'lat', split_axis=0, concat_axis=0, tiled=True)]
    pallas_call x8, Pallas kernels: 14.3 us -> 10.9 us  [input_step(): pl.pallas_call(input_kernel, in_specs=[whole] * (3 + len(totals)), out_sp...]
    ppermute x30, starting transfers between devices: 13.3 us -> 16.4 us  [send(): return lax.ppermute(after(rows, *first) if first else rows, 'lat', way)]
  transfers between devices with their start and end apart: 32 -> 31, of which waited for: 11 -> 10; matrix products, arithmetic and copies ran while one was open for 0% -> 1% of each run, Pallas kernels for 23% -> 20%
where the time goes in v9:
time: 171 us; the launch traced here: 170 us
  waiting for transfers between devices  84.4 us (49%)
  Pallas kernels  40.3 us (24%)
  starting transfers between devices  21.9 us (13%)
  blocking collectives  17.6 us (10%)
  local copies, waits for them, and re-layouts  5.22 us (3%)
    ppermute x30, waiting for transfers between devices, send(): return lax.ppermute(after(rows, *first) if first else rows, 'lat', way)  64.5 us
    pallas_call x8, Pallas kernels, grad_step(): pl.pallas_call(functools.partial(grad_kernel, per_block), in_specs=[scala...  24.1 us
    all_to_all x1, waiting for transfers between devices, by_ring(): meta = lax.all_to_all(meta, 'lat', split_axis=0, concat_axis=0, tiled=True)  20 us
    all_to_all x1, blocking collectives, arrive(): lax.all_to_all(totals[2], 'lat', split_axis=0, concat_axis=0, tiled=True)  17.6 us
    ppermute x30, starting transfers between devices, send(): return lax.ppermute(after(rows, *first) if first else rows, 'lat', way)  16.4 us
    pallas_call x8, Pallas kernels, input_step(): pl.pallas_call(input_kernel, in_specs=[whole] * (3 + len(totals)), out_sp...  10.9 us
    all_to_all x1, starting transfers between devices, by_ring(): meta = lax.all_to_all(meta, 'lat', split_axis=0, concat_axis=0, tiled=True)  5.52 us
    pallas_call x1, Pallas kernels, by_ring(): pl.pallas_call(spread_kernel, in_specs=[scalars] + [pl.BlockSpec(memory_s...  3.86 us
  transfers between devices with their start and end apart: 31, of which 10 were waited for; matrix products, arithmetic and copies ran while one was open for 1% of the time, Pallas kernels for 20%

profile of v9, /device:TPU:0, one launch (start us, length us, event | category | flops | bytes accessed | tf_op | source)
XLA Modules:
  0.0 170.4 jit_solution(10095396833732015145)
XLA Ops:
  1.3 3.9 %spread.1 = (bf16[16,32,128]{2,1,0:T(8,128)(2,1)}, bf16[3,128,128]{2,1,0:T(8,128)(2,1)S(1)}, bf16[128,3584]{1,0:T(8,128)(2,1)}, bf16[128,3584]{1,0:T(8,128)(2,1)...) custom-call(s32[18]{0:T(128)S(1)} %dynamic-slice_bitcast_fusion.ways_ref, s32[4,128]{1,0:T(4,128)} %bitcast.24, ...), custom_call_target="tpu_custom_call" | custom-call | flops 1 | bytes 1 | tf_op jit(solution)/shard_map/spread/pallas_call | solution.py:221
  6.2 3.0 %collective-permute-start = (bf16[128,3584]{1,0:T(8,128)(2,1)}, bf16[128,3584]{1,0:T(8,128)(2,1)S(1)}, u32[]{:S(2)}, u32[]{:S(2)}) collective-permute-start(bf16[128,3584]{1,0:T(8,128)(2,1)} %get-tuple-element.68), channel_id=1, source_target_pairs={{0,4},{4,8},{8,12},{12,14},{14,10},{10,6},{6,2},{2,0},{1,3},{5,1},... | collective-permute-start | bytes 2752520 | tf_op jit(solution)/shard_map/ppermute | solution.py:277
  10.0 5.5 %all-to-all-start = ((bf16[16,32,128]{2,1,0:T(8,128)(2,1)}), bf16[16,32,128]{2,1,0:T(8,128)(2,1)S(1)}, u32[]{:S(2)}, u32[]{:S(2)}) async-start(bf16[16,32,128]{2,1,0:T(8,128)(2,1)} %get-tuple-element.67), calls=%async_computation | async-start | bytes 262144 | tf_op jit(solution)/shard_map/all_to_all | solution.py:235
  16.0 20.0 %all-to-all-done.meta_ref = bf16[16,32,128]{2,1,0:T(8,128)(2,1)S(1)} async-done(((bf16[16,32,128]{2,1,0:T(8,128)(2,1)}), bf16[16,32,128]{2,1,0:T(8,128)(2,1)S(1)}, u32[]{:S(2)}, u32[]{:S(2)}) %all-to-all-start) | async-done | bytes 131104 | tf_op jit(solution)/shard_map/all_to_all | solution.py:235
  36.5 1.7 %collective-permute-start.1 = (bf16[128,3584]{1,0:T(8,128)(2,1)S(1)}, bf16[128,3584]{1,0:T(8,128)(2,1)S(1)}, u32[]{:S(2)}, u32[]{:S(2)}) collective-permute-start(bf16[128,3584]{1,0:T(8,128)(2,1)S(1)} %collective-permute-done.mine_ref), channel_id=1, source_target_pairs={{0,4},{4,8},{8,12},{12,14},{14,10},{10,6},{6,2},{2,0},{1,3},{5,1},... | collective-permute-start | bytes 2752520 | tf_op jit(solution)/shard_map/ppermute | solution.py:277
  39.1 1.5 copy-done
  41.8 2.7 %grad_step.8 = (f32[256,3584]{1,0:T(8,128)S(1)}, f32[256,128]{1,0:T(8,128)S(1)}, f32[16,16,128]{2,1,0:T(8,128)S(1)}, bf16[256,256]{1,0:T(8,128)(2,1)S(1)}) custom-call(s32[2]{0:T(128)S(1)} %get-tuple-element.135.order_ref, bf16[16,32,128]{2,1,0:T(8,128)(2,1)S(1)} %all-to-all-done.meta_ref, bf16[256,3584]{1,0:T(8,128)(2,1)S(1)} %copy-done, ...), custom_call_target="tpu_custom_call" | custom-call | flops 1 | bytes 1 | tf_op jit(solution)/shard_map/grad_step/pallas_call | solution.py:242
  44.4 2.9 %grad_step.9 = (f32[256,3584]{1,0:T(8,128)S(1)}, f32[256,128]{1,0:T(8,128)S(1)}, f32[16,16,128]{2,1,0:T(8,128)S(1)}, bf16[256,256]{1,0:T(8,128)(2,1)S(1)}) custom-call(s32[2]{0:T(128)S(1)} %get-tuple-element.136.order_ref, bf16[16,32,128]{2,1,0:T(8,128)(2,1)S(1)} %all-to-all-done.meta_ref, ...), custom_call_target="tpu_custom_call", output_to_operand_aliasing={{0}: (5, {}), {1}: (6, {})} | custom-call | flops 1 | bytes 1 | tf_op jit(solution)/shard_map/grad_step/pallas_call | solution.py:242
  47.3 2.3 %collective-permute-done.4.mine_ref = bf16[128,3584]{1,0:T(8,128)(2,1)S(1)} collective-permute-done((bf16[128,3584]{1,0:T(8,128)(2,1)}, bf16[128,3584]{1,0:T(8,128)(2,1)S(1)}, u32[]{:S(2)}, u32[]{:S(2)}) %collective-permute-start.4) | collective-permute-done | bytes 917536 | tf_op jit(solution)/shard_map/ppermute | solution.py:277
  49.7 2.9 %grad_step.10 = (f32[256,3584]{1,0:T(8,128)S(1)}, f32[256,128]{1,0:T(8,128)S(1)}, f32[16,16,128]{2,1,0:T(8,128)S(1)}, bf16[256,256]{1,0:T(8,128)(2,1)S(1)}) custom-call(s32[2]{0:T(128)S(1)} %get-tuple-element.133.order_ref, bf16[16,32,128]{2,1,0:T(8,128)(2,1)S(1)} %all-to-all-done.meta_ref, ...), custom_call_target="tpu_custom_call", output_to_operand_aliasing={{0}: (5, {}), {1}: (6, {})} | custom-call | flops 1 | bytes 1 | tf_op jit(solution)/shard_map/grad_step/pallas_call | solution.py:242
  52.6 13.6 %collective-permute-done.1.mine_ref = bf16[128,3584]{1,0:T(8,128)(2,1)S(1)} collective-permute-done((bf16[128,3584]{1,0:T(8,128)(2,1)S(1)}, bf16[128,3584]{1,0:T(8,128)(2,1)S(1)}, u32[]{:S(2)}, u32[]{:S(2)}) %collective-permute-start.1) | collective-permute-done | bytes 917536 | tf_op jit(solution)/shard_map/ppermute | solution.py:277
  66.9 1.4 input_step.9.refs_0_
  69.1 1.5 collective-permute-start.7
  70.6 2.9 %grad_step.11 = (f32[256,3584]{1,0:T(8,128)S(1)}, f32[256,128]{1,0:T(8,128)S(1)}, f32[16,16,128]{2,1,0:T(8,128)S(1)}, bf16[256,256]{1,0:T(8,128)(2,1)S(1)}) custom-call(s32[2]{0:T(128)S(1)} %get-tuple-element.134.order_ref, bf16[16,32,128]{2,1,0:T(8,128)(2,1)S(1)} %all-to-all-done.meta_ref, ...), custom_call_target="tpu_custom_call", output_to_operand_aliasing={{0}: (5, {}), {1}: (6, {})} | custom-call | flops 1 | bytes 1 | tf_op jit(solution)/shard_map/grad_step/pallas_call | solution.py:242
  73.5 6.1 %collective-permute-done.11.mine_ref = bf16[128,3584]{1,0:T(8,128)(2,1)S(1)} collective-permute-done((bf16[128,3584]{1,0:T(8,128)(2,1)S(1)}, bf16[128,3584]{1,0:T(8,128)(2,1)S(1)}, u32[]{:S(2)}, u32[]{:S(2)}) %collective-permute-start.11) | collective-permute-done | bytes 917536 | tf_op jit(solution)/shard_map/ppermute | solution.py:277
  79.7 2.9 %grad_step.12 = (f32[256,3584]{1,0:T(8,128)S(1)}, f32[256,128]{1,0:T(8,128)S(1)}, f32[16,16,128]{2,1,0:T(8,128)S(1)}, bf16[256,256]{1,0:T(8,128)(2,1)S(1)}) custom-call(s32[2]{0:T(128)S(1)} %get-tuple-element.130.order_ref, bf16[16,32,128]{2,1,0:T(8,128)(2,1)S(1)} %all-to-all-done.meta_ref, ...), custom_call_target="tpu_custom_call", output_to_operand_aliasing={{0}: (5, {}), {1}: (6, {})} | custom-call | flops 1 | bytes 1 | tf_op jit(solution)/shard_map/grad_step/pallas_call | solution.py:242
  82.6 13.3 %collective-permute-done.7.mine_ref = bf16[128,3584]{1,0:T(8,128)(2,1)S(1)} collective-permute-done((bf16[128,3584]{1,0:T(8,128)(2,1)S(1)}, bf16[128,3584]{1,0:T(8,128)(2,1)S(1)}, u32[]{:S(2)}, u32[]{:S(2)}) %collective-permute-start.7) | collective-permute-done | bytes 917536 | tf_op jit(solution)/shard_map/ppermute | solution.py:277
  96.0 1.4 input_step.10.refs_0_
  98.0 1.6 collective-permute-start.13
  99.6 2.9 %grad_step.13 = (f32[256,3584]{1,0:T(8,128)S(1)}, f32[256,128]{1,0:T(8,128)S(1)}, f32[16,16,128]{2,1,0:T(8,128)S(1)}, bf16[256,256]{1,0:T(8,128)(2,1)S(1)}) custom-call(s32[2]{0:T(128)S(1)} %get-tuple-element.131.order_ref, bf16[16,32,128]{2,1,0:T(8,128)(2,1)S(1)} %all-to-all-done.meta_ref, ...), custom_call_target="tpu_custom_call", output_to_operand_aliasing={{0}: (5, {}), {1}: (6, {})} | custom-call | flops 1 | bytes 1 | tf_op jit(solution)/shard_map/grad_step/pallas_call | solution.py:242
  102.5 14.3 %collective-permute-done.20.mine_ref = bf16[128,3584]{1,0:T(8,128)(2,1)S(1)} collective-permute-done((bf16[128,3584]{1,0:T(8,128)(2,1)S(1)}, bf16[128,3584]{1,0:T(8,128)(2,1)S(1)}, u32[]{:S(2)}, u32[]{:S(2)}) %collective-permute-start.20) | collective-permute-done | bytes 917536 | tf_op jit(solution)/shard_map/ppermute | solution.py:277
  116.7 2.9 %grad_step.14 = (f32[256,3584]{1,0:T(8,128)S(1)}, f32[256,128]{1,0:T(8,128)S(1)}, f32[16,16,128]{2,1,0:T(8,128)S(1)}, bf16[256,256]{1,0:T(8,128)(2,1)S(1)}) custom-call(s32[2]{0:T(128)S(1)} %get-tuple-element.132.order_ref, bf16[16,32,128]{2,1,0:T(8,128)(2,1)S(1)} %all-to-all-done.meta_ref, ...), custom_call_target="tpu_custom_call", output_to_operand_aliasing={{0}: (5, {}), {1}: (6, {})} | custom-call | flops 1 | bytes 1 | tf_op jit(solution)/shard_map/grad_step/pallas_call | solution.py:242
  119.7 2.3 %collective-permute-start.21 = (bf16[128,3584]{1,0:T(8,128)(2,1)S(1)}, bf16[128,3584]{1,0:T(8,128)(2,1)S(1)}, u32[]{:S(2)}, u32[]{:S(2)}) collective-permute-start(bf16[128,3584]{1,0:T(8,128)(2,1)S(1)} %collective-permute-done.20.mine_ref), channel_id=1, source_target_pairs={{4,0},{8,4},{12,8},{14,12},{10,14},{6,10},{2,6},{0,2},{3,1},{1,5},... | collective-permute-start | bytes 2752520 | tf_op jit(solution)/shard_map/ppermute | solution.py:277
  122.0 1.4 input_step.11.refs_0_
  123.4 13.8 %collective-permute-done.24.mine_ref = bf16[128,3584]{1,0:T(8,128)(2,1)S(1)} collective-permute-done((bf16[128,3584]{1,0:T(8,128)(2,1)S(1)}, bf16[128,3584]{1,0:T(8,128)(2,1)S(1)}, u32[]{:S(2)}, u32[]{:S(2)}) %collective-permute-start.24) | collective-permute-done | bytes 917536 | tf_op jit(solution)/shard_map/ppermute | solution.py:277
  137.1 4.0 %grad_step.15 = (bf16[256,3584]{1,0:T(8,128)(2,1)}, f32[1,256]{1,0:T(1,128)}, f32[16,16,128]{2,1,0:T(8,128)S(1)}, bf16[256,256]{1,0:T(8,128)(2,1)S(1)}) custom-call(s32[2]{0:T(128)S(1)} %get-tuple-element.137.order_ref, bf16[16,32,128]{2,1,0:T(8,128)(2,1)S(1)} %all-to-all-done.meta_ref, bf16[256,3584]{1,0:T(8,128)(2,1)S(1)} %copy-done.1, ...), custom_call_target="tpu_custom_call" | custom-call | flops 1 | bytes 1 | tf_op jit(solution)/shard_map/grad_step/pallas_call | solution.py:242
  141.8 2.1 %collective-permute-start.22 = (bf16[96,3584]{1,0:T(8,128)(2,1)S(1)}, bf16[96,3584]{1,0:T(8,128)(2,1)S(1)}, u32[]{:S(2)}, u32[]{:S(2)}) collective-permute-start(bf16[96,3584]{1,0:T(8,128)(2,1)S(1)} %slice.58), channel_id=1, source_target_pairs={{4,0},{8,4},{12,8},{14,12},{10,14},{6,10},{2,6},{0,2},{3,1},{1,5},... | collective-permute-start | bytes 2064392 | tf_op jit(solution)/shard_map/ppermute | solution.py:277
  143.9 17.6 %all_to_all.10.returned_ref = f32[16,16,128]{2,1,0:T(8,128)S(1)} all-to-all(f32[16,16,128]{2,1,0:T(8,128)S(1)} %get-tuple-element.125), channel_id=1, replica_groups=mesh['groups'=2,'lat'=16] {'lat'}, dimensions={0} | all-to-all | bytes 262144 | tf_op jit(solution)/shard_map/all_to_all | solution.py:312
  161.5 1.5 pick.1
  163.0 1.4 input_step.12.refs_0_
  164.8 1.4 input_step.13.refs_0_
  168.4 2.0 %input_step.15 = bf16[3584,256]{1,0:T(8,128)(2,1)} custom-call(bf16[256,256]{1,0:T(8,128)(2,1)S(1)} %get-tuple-element.111.pre_ref, bf16[96,3584]{1,0:T(8,128)(2,1)S(1)} %collective-permute-done.22.mine_ref, bf16[96,3584]{1,0:T(8,128)(2,1)S(1)} %collective-permute-done.27.theirs_ref, f32[3584,256]{1,0:T(8,128)S(1)} %input_step.14.refs_0_), custom_call_target="tpu_custom_call" | custom-call | flops 1 | bytes 1 | tf_op jit(solution)/shard_map/input_step/pallas_call | solution.py:265
  (72 shorter events, 11.1 us)
Async XLA Ops:
  6.2 29.8 %collective-permute-start = (bf16[128,3584]{1,0:T(8,128)(2,1)}, bf16[128,3584]{1,0:T(8,128)(2,1)S(1)}, u32[]{:S(2)}, u32[]{:S(2)}) collective-permute-start(bf16[128,3584]{1,0:T(8,128)(2,1)} %get-tuple-element.68), channel_id=1, source_target_pairs={{0,4},{4,8},{8,12},{12,14},{14,10},{10,6},{6,2},{2,0},{1,3},{5,1},... | collective-permute-start | bytes 2752520 | tf_op jit(solution)/shard_map/ppermute | solution.py:277
  9.2 26.9 %collective-permute-start.8 = (bf16[128,3584]{1,0:T(8,128)(2,1)}, bf16[128,3584]{1,0:T(8,128)(2,1)S(1)}, u32[]{:S(2)}, u32[]{:S(2)}) collective-permute-start(bf16[128,3584]{1,0:T(8,128)(2,1)} %get-tuple-element.80), channel_id=1, source_target_pairs={{4,0},{8,4},{12,8},{14,12},{10,14},{6,10},{2,6},{0,2},{3,1},{1,5},... | collective-permute-start | bytes 2752520 | tf_op jit(solution)/shard_map/ppermute | solution.py:277
  10.0 25.9 %all-to-all-start = ((bf16[16,32,128]{2,1,0:T(8,128)(2,1)}), bf16[16,32,128]{2,1,0:T(8,128)(2,1)S(1)}, u32[]{:S(2)}, u32[]{:S(2)}) async-start(bf16[16,32,128]{2,1,0:T(8,128)(2,1)} %get-tuple-element.67), calls=%async_computation | async-start | bytes 262144 | tf_op jit(solution)/shard_map/all_to_all | solution.py:235
  15.6 23.3 %collective-permute-start.3 = (bf16[128,3584]{1,0:T(8,128)(2,1)}, bf16[128,3584]{1,0:T(8,128)(2,1)S(1)}, u32[]{:S(2)}, u32[]{:S(2)}) collective-permute-start(bf16[128,3584]{1,0:T(8,128)(2,1)} %mine_ref.2), channel_id=1, source_target_pairs={{0,1},{1,0},{2,3},{3,2},{4,5},{5,4},{6,7},{7,6},{8,9},{9,8},{10,11... | collective-permute-start | bytes 2752520 | tf_op jit(solution)/shard_map/ppermute | solution.py:277
  35.9 8.5 %collective-permute-start.2 = (bf16[128,3584]{1,0:T(8,128)(2,1)S(1)}, bf16[128,3584]{1,0:T(8,128)(2,1)S(1)}, u32[]{:S(2)}, u32[]{:S(2)}) collective-permute-start(bf16[128,3584]{1,0:T(8,128)(2,1)S(1)} %collective-permute-done.mine_ref), channel_id=1, source_target_pairs={{0,1},{1,0},{2,3},{3,2},{4,5},{5,4},{6,7},{7,6},{8,9},{9,8},{10,11... | collective-permute-start | bytes 2752520 | tf_op jit(solution)/shard_map/ppermute | solution.py:277
  36.0 13.6 %collective-permute-start.4 = (bf16[128,3584]{1,0:T(8,128)(2,1)}, bf16[128,3584]{1,0:T(8,128)(2,1)S(1)}, u32[]{:S(2)}, u32[]{:S(2)}) collective-permute-start(bf16[128,3584]{1,0:T(8,128)(2,1)} %copy-done.7), channel_id=1, source_target_pairs={{0,4},{4,8},{8,12},{12,14},{14,10},{10,6},{6,2},{2,0},{1,3},{5,1},... | collective-permute-start | bytes 2752520 | tf_op jit(solution)/shard_map/ppermute | solution.py:277
  36.1 13.5 %collective-permute-start.9 = (bf16[128,3584]{1,0:T(8,128)(2,1)S(1)}, bf16[128,3584]{1,0:T(8,128)(2,1)S(1)}, u32[]{:S(2)}, u32[]{:S(2)}) collective-permute-start(bf16[128,3584]{1,0:T(8,128)(2,1)S(1)} %collective-permute-done.8.mine_ref), channel_id=1, source_target_pairs={{0,1},{1,0},{2,3},{3,2},{4,5},{5,4},{6,7},{7,6},{8,9},{9,8},{10,11... | collective-permute-start | bytes 2752520 | tf_op jit(solution)/shard_map/ppermute | solution.py:277
  36.5 29.7 %collective-permute-start.1 = (bf16[128,3584]{1,0:T(8,128)(2,1)S(1)}, bf16[128,3584]{1,0:T(8,128)(2,1)S(1)}, u32[]{:S(2)}, u32[]{:S(2)}) collective-permute-start(bf16[128,3584]{1,0:T(8,128)(2,1)S(1)} %collective-permute-done.mine_ref), channel_id=1, source_target_pairs={{0,4},{4,8},{8,12},{12,14},{14,10},{10,6},{6,2},{2,0},{1,3},{5,1},... | collective-permute-start | bytes 2752520 | tf_op jit(solution)/shard_map/ppermute | solution.py:277
  38.9 27.3 %collective-permute-start.6 = (bf16[128,3584]{1,0:T(8,128)(2,1)}, bf16[128,3584]{1,0:T(8,128)(2,1)S(1)}, u32[]{:S(2)}, u32[]{:S(2)}) collective-permute-start(bf16[128,3584]{1,0:T(8,128)(2,1)} %mine_ref.3), channel_id=1, source_target_pairs={{0,1},{1,0},{2,3},{3,2},{4,5},{5,4},{6,7},{7,6},{8,9},{9,8},{10,11... | collective-permute-start | bytes 2752520 | tf_op jit(solution)/shard_map/ppermute | solution.py:277
  49.7 17.2 %collective-permute-start.5 = (bf16[128,3584]{1,0:T(8,128)(2,1)S(1)}, bf16[128,3584]{1,0:T(8,128)(2,1)S(1)}, u32[]{:S(2)}, u32[]{:S(2)}) collective-permute-start(bf16[128,3584]{1,0:T(8,128)(2,1)S(1)} %collective-permute-done.4.mine_ref), channel_id=1, source_target_pairs={{0,1},{1,0},{2,3},{3,2},{4,5},{5,4},{6,7},{7,6},{8,9},{9,8},{10,11... | collective-permute-start | bytes 2752520 | tf_op jit(solution)/shard_map/ppermute | solution.py:277
  49.7 19.1 %collective-permute-start.14 = (bf16[128,3584]{1,0:T(8,128)(2,1)S(1)}, bf16[128,3584]{1,0:T(8,128)(2,1)S(1)}, u32[]{:S(2)}, u32[]{:S(2)}) collective-permute-start(bf16[128,3584]{1,0:T(8,128)(2,1)S(1)} %collective-permute-done.8.mine_ref), channel_id=1, source_target_pairs={{4,0},{8,4},{12,8},{14,12},{10,14},{6,10},{2,6},{0,2},{3,1},{1,5},... | collective-permute-start | bytes 2752520 | tf_op jit(solution)/shard_map/ppermute | solution.py:277
  66.1 4.5 %collective-permute-start.10 = (bf16[128,3584]{1,0:T(8,128)(2,1)S(1)}, bf16[128,3584]{1,0:T(8,128)(2,1)S(1)}, u32[]{:S(2)}, u32[]{:S(2)}) collective-permute-start(bf16[128,3584]{1,0:T(8,128)(2,1)S(1)} %collective-permute-done.1.mine_ref), channel_id=1, source_target_pairs={{0,1},{1,0},{2,3},{3,2},{4,5},{5,4},{6,7},{7,6},{8,9},{9,8},{10,11... | collective-permute-start | bytes 2752520 | tf_op jit(solution)/shard_map/ppermute | solution.py:277
  66.1 13.4 %collective-permute-start.11 = (bf16[128,3584]{1,0:T(8,128)(2,1)S(1)}, bf16[128,3584]{1,0:T(8,128)(2,1)S(1)}, u32[]{:S(2)}, u32[]{:S(2)}) collective-permute-start(bf16[128,3584]{1,0:T(8,128)(2,1)S(1)} %collective-permute-done.4.mine_ref), channel_id=1, source_target_pairs={{0,4},{4,8},{8,12},{12,14},{14,10},{10,6},{6,2},{2,0},{1,3},{5,1},... | collective-permute-start | bytes 2752520 | tf_op jit(solution)/shard_map/ppermute | solution.py:277
  68.7 10.9 %collective-permute-start.17 = (bf16[128,3584]{1,0:T(8,128)(2,1)S(1)}, bf16[128,3584]{1,0:T(8,128)(2,1)S(1)}, u32[]{:S(2)}, u32[]{:S(2)}) collective-permute-start(bf16[128,3584]{1,0:T(8,128)(2,1)S(1)} %collective-permute-done.14.mine_ref), channel_id=1, source_target_pairs={{0,1},{1,0},{2,3},{3,2},{4,5},{5,4},{6,7},{7,6},{8,9},{9,8},{10,11... | collective-permute-start | bytes 2752520 | tf_op jit(solution)/shard_map/ppermute | solution.py:277
  69.1 26.8 %collective-permute-start.7 = (bf16[128,3584]{1,0:T(8,128)(2,1)S(1)}, bf16[128,3584]{1,0:T(8,128)(2,1)S(1)}, u32[]{:S(2)}, u32[]{:S(2)}) collective-permute-start(bf16[128,3584]{1,0:T(8,128)(2,1)S(1)} %collective-permute-done.1.mine_ref), channel_id=1, source_target_pairs={{0,4},{4,8},{8,12},{12,14},{14,10},{10,6},{6,2},{2,0},{1,3},{5,1},... | collective-permute-start | bytes 2752520 | tf_op jit(solution)/shard_map/ppermute | solution.py:277
  79.5 16.4 %collective-permute-start.12 = (bf16[128,3584]{1,0:T(8,128)(2,1)S(1)}, bf16[128,3584]{1,0:T(8,128)(2,1)S(1)}, u32[]{:S(2)}, u32[]{:S(2)}) collective-permute-start(bf16[128,3584]{1,0:T(8,128)(2,1)S(1)} %collective-permute-done.11.mine_ref), channel_id=1, source_target_pairs={{0,1},{1,0},{2,3},{3,2},{4,5},{5,4},{6,7},{7,6},{8,9},{9,8},{10,11... | collective-permute-start | bytes 2752520 | tf_op jit(solution)/shard_map/ppermute | solution.py:277
  79.6 17.8 %collective-permute-start.15 = (bf16[96,3584]{1,0:T(8,128)(2,1)S(1)}, bf16[96,3584]{1,0:T(8,128)(2,1)S(1)}, u32[]{:S(2)}, u32[]{:S(2)}) collective-permute-start(bf16[96,3584]{1,0:T(8,128)(2,1)S(1)} %slice.57), channel_id=1, source_target_pairs={{4,0},{8,4},{12,8},{14,12},{10,14},{6,10},{2,6},{0,2},{3,1},{1,5},... | collective-permute-start | bytes 2064392 | tf_op jit(solution)/shard_map/ppermute | solution.py:277
  95.9 3.6 %collective-permute-start.18 = (bf16[128,3584]{1,0:T(8,128)(2,1)S(1)}, bf16[128,3584]{1,0:T(8,128)(2,1)S(1)}, u32[]{:S(2)}, u32[]{:S(2)}) collective-permute-start(bf16[128,3584]{1,0:T(8,128)(2,1)S(1)} %collective-permute-done.7.mine_ref), channel_id=1, source_target_pairs={{0,1},{1,0},{2,3},{3,2},{4,5},{5,4},{6,7},{7,6},{8,9},{9,8},{10,11... | collective-permute-start | bytes 2752520 | tf_op jit(solution)/shard_map/ppermute | solution.py:277
  95.9 20.8 %collective-permute-start.20 = (bf16[128,3584]{1,0:T(8,128)(2,1)S(1)}, bf16[128,3584]{1,0:T(8,128)(2,1)S(1)}, u32[]{:S(2)}, u32[]{:S(2)}) collective-permute-start(bf16[128,3584]{1,0:T(8,128)(2,1)S(1)} %copy-done.6), channel_id=1, source_target_pairs={{4,0},{8,4},{12,8},{14,12},{10,14},{6,10},{2,6},{0,2},{3,1},{1,5},... | collective-permute-start | bytes 2752520 | tf_op jit(solution)/shard_map/ppermute | solution.py:277
  97.4 19.4 %collective-permute-start.16 = (bf16[96,3584]{1,0:T(8,128)(2,1)S(1)}, bf16[96,3584]{1,0:T(8,128)(2,1)S(1)}, u32[]{:S(2)}, u32[]{:S(2)}) collective-permute-start(bf16[96,3584]{1,0:T(8,128)(2,1)S(1)} %collective-permute-done.15.mine_ref), channel_id=1, source_target_pairs={{0,1},{1,0},{2,3},{3,2},{4,5},{5,4},{6,7},{7,6},{8,9},{9,8},{10,11... | collective-permute-start | bytes 2064392 | tf_op jit(solution)/shard_map/ppermute | solution.py:277
  98.0 24.0 %collective-permute-start.13 = (bf16[96,3584]{1,0:T(8,128)(2,1)S(1)}, bf16[96,3584]{1,0:T(8,128)(2,1)S(1)}, u32[]{:S(2)}, u32[]{:S(2)}) collective-permute-start(bf16[96,3584]{1,0:T(8,128)(2,1)S(1)} %slice.56), channel_id=1, source_target_pairs={{0,4},{4,8},{8,12},{12,14},{14,10},{10,6},{6,2},{2,0},{1,3},{5,1},... | collective-permute-start | bytes 2064392 | tf_op jit(solution)/shard_map/ppermute | solution.py:277
  116.7 5.3 %collective-permute-start.25 = (bf16[128,3584]{1,0:T(8,128)(2,1)S(1)}, bf16[128,3584]{1,0:T(8,128)(2,1)S(1)}, u32[]{:S(2)}, u32[]{:S(2)}) collective-permute-start(bf16[128,3584]{1,0:T(8,128)(2,1)S(1)} %collective-permute-done.20.mine_ref), channel_id=1, source_target_pairs={{0,1},{1,0},{2,3},{3,2},{4,5},{5,4},{6,7},{7,6},{8,9},{9,8},{10,11... | collective-permute-start | bytes 2752520 | tf_op jit(solution)/shard_map/ppermute | solution.py:277
  116.7 20.4 %collective-permute-start.24 = (bf16[128,3584]{1,0:T(8,128)(2,1)S(1)}, bf16[128,3584]{1,0:T(8,128)(2,1)S(1)}, u32[]{:S(2)}, u32[]{:S(2)}) collective-permute-start(bf16[128,3584]{1,0:T(8,128)(2,1)S(1)} %collective-permute-done.11.mine_ref), channel_id=1, source_target_pairs={{0,4},{4,8},{8,12},{12,14},{14,10},{10,6},{6,2},{2,0},{1,3},{5,1},... | collective-permute-start | bytes 2752520 | tf_op jit(solution)/shard_map/ppermute | solution.py:277
  119.7 21.5 %collective-permute-start.21 = (bf16[128,3584]{1,0:T(8,128)(2,1)S(1)}, bf16[128,3584]{1,0:T(8,128)(2,1)S(1)}, u32[]{:S(2)}, u32[]{:S(2)}) collective-permute-start(bf16[128,3584]{1,0:T(8,128)(2,1)S(1)} %collective-permute-done.20.mine_ref), channel_id=1, source_target_pairs={{4,0},{8,4},{12,8},{14,12},{10,14},{6,10},{2,6},{0,2},{3,1},{1,5},... | collective-permute-start | bytes 2752520 | tf_op jit(solution)/shard_map/ppermute | solution.py:277
  122.0 15.2 %collective-permute-start.19 = (bf16[96,3584]{1,0:T(8,128)(2,1)S(1)}, bf16[96,3584]{1,0:T(8,128)(2,1)S(1)}, u32[]{:S(2)}, u32[]{:S(2)}) collective-permute-start(bf16[96,3584]{1,0:T(8,128)(2,1)S(1)} %collective-permute-done.13.mine_ref), channel_id=1, source_target_pairs={{0,1},{1,0},{2,3},{3,2},{4,5},{5,4},{6,7},{7,6},{8,9},{9,8},{10,11... | collective-permute-start | bytes 2064392 | tf_op jit(solution)/shard_map/ppermute | solution.py:277
  137.1 25.8 %collective-permute-start.26 = (bf16[128,3584]{1,0:T(8,128)(2,1)S(1)}, bf16[128,3584]{1,0:T(8,128)(2,1)S(1)}, u32[]{:S(2)}, u32[]{:S(2)}) collective-permute-start(bf16[128,3584]{1,0:T(8,128)(2,1)S(1)} %collective-permute-done.24.mine_ref), channel_id=1, source_target_pairs={{0,1},{1,0},{2,3},{3,2},{4,5},{5,4},{6,7},{7,6},{8,9},{9,8},{10,11... | collective-permute-start | bytes 2752520 | tf_op jit(solution)/shard_map/ppermute | solution.py:277
  137.1 24.4 %copy-start.4 = (s32[128,4]{0,1:T(4,128)S(1)}, s32[128,4]{0,1:T(4,128)}, u32[]{:S(2)}) copy-start(s32[128,4]{0,1:T(4,128)} %param.12) | copy-start | bytes 6148
  141.2 23.6 %collective-permute-start.23 = (bf16[128,3584]{1,0:T(8,128)(2,1)S(1)}, bf16[128,3584]{1,0:T(8,128)(2,1)S(1)}, u32[]{:S(2)}, u32[]{:S(2)}) collective-permute-start(bf16[128,3584]{1,0:T(8,128)(2,1)S(1)} %collective-permute-done.21.mine_ref), channel_id=1, source_target_pairs={{0,1},{1,0},{2,3},{3,2},{4,5},{5,4},{6,7},{7,6},{8,9},{9,8},{10,11... | collective-permute-start | bytes 2752520 | tf_op jit(solution)/shard_map/ppermute | solution.py:277
  141.7 22.6 %collective-permute-start.28 = (bf16[96,3584]{1,0:T(8,128)(2,1)S(1)}, bf16[96,3584]{1,0:T(8,128)(2,1)S(1)}, u32[]{:S(2)}, u32[]{:S(2)}) collective-permute-start(bf16[96,3584]{1,0:T(8,128)(2,1)S(1)} %slice.59), channel_id=1, source_target_pairs={{0,4},{4,8},{8,12},{12,14},{14,10},{10,6},{6,2},{2,0},{1,3},{5,1},... | collective-permute-start | bytes 2064392 | tf_op jit(solution)/shard_map/ppermute | solution.py:277
  141.8 24.3 %collective-permute-start.22 = (bf16[96,3584]{1,0:T(8,128)(2,1)S(1)}, bf16[96,3584]{1,0:T(8,128)(2,1)S(1)}, u32[]{:S(2)}, u32[]{:S(2)}) collective-permute-start(bf16[96,3584]{1,0:T(8,128)(2,1)S(1)} %slice.58), channel_id=1, source_target_pairs={{4,0},{8,4},{12,8},{14,12},{10,14},{6,10},{2,6},{0,2},{3,1},{1,5},... | collective-permute-start | bytes 2064392 | tf_op jit(solution)/shard_map/ppermute | solution.py:277
  164.4 2.2 %collective-permute-start.29 = (bf16[96,3584]{1,0:T(8,128)(2,1)S(1)}, bf16[96,3584]{1,0:T(8,128)(2,1)S(1)}, u32[]{:S(2)}, u32[]{:S(2)}) collective-permute-start(bf16[96,3584]{1,0:T(8,128)(2,1)S(1)} %collective-permute-done.28.mine_ref), channel_id=1, source_target_pairs={{0,1},{1,0},{2,3},{3,2},{4,5},{5,4},{6,7},{7,6},{8,9},{9,8},{10,11... | collective-permute-start | bytes 2064392 | tf_op jit(solution)/shard_map/ppermute | solution.py:277
  166.2 2.2 %collective-permute-start.27 = (bf16[96,3584]{1,0:T(8,128)(2,1)S(1)}, bf16[96,3584]{1,0:T(8,128)(2,1)S(1)}, u32[]{:S(2)}, u32[]{:S(2)}) collective-permute-start(bf16[96,3584]{1,0:T(8,128)(2,1)S(1)} %collective-permute-done.22.mine_ref), channel_id=1, source_target_pairs={{0,1},{1,0},{2,3},{3,2},{4,5},{5,4},{6,7},{7,6},{8,9},{9,8},{10,11... | collective-permute-start | bytes 2064392 | tf_op jit(solution)/shard_map/ppermute | solution.py:277
  (7 other events, 43.1 us)

commit v10 on v6

--- a/solution.py
+++ b/solution.py
@@ -13,7 +13,8 @@
 HELD_BYTES = 1 << 25
 RING_BYTES = 1 << 26
 VMEM_BYTES = 24 << 20
-LAG = 4
+LAG = 5
+EARLY = 1
 
 
 def ring_tables(peer_count):
@@ -221,7 +222,7 @@
         nonlocal returned
         kind, hop = turns[turn]
         last = turn in (last_grads, len(turns) - 1)
-        ready = (meta,) if turn < 2 else (marks[turn - 2],)
+        ready = (meta,) if turn < 3 else (marks[turn - 3],)
         if turn == len(turns) - 1:
             ready += (returned,)
         marks.append(use(kind, hop % chips, (arrived[turn], send(arrived[turn], swap, *ready)), last))
@@ -232,14 +233,14 @@
     use("inputs", 0, (inputs, own_inputs))
     arrived = []
     for turn, (kind, hop) in enumerate(turns):
-        if turn >= LAG:
-            arrive(turn - LAG)
-        ready = () if turn < 3 else (meta,) if turn < LAG else (marks[turn - LAG],)
+        while len(marks) < (last_grads + 1 if turn >= len(turns) - EARLY else turn - LAG + 1):
+            arrive(len(marks))
+        ready = () if turn < 3 else (meta,) if turn < max(LAG, 4) else (marks[-1],)
         rows = send(held[kind, hop > 0], onward if hop > 0 else backward, *ready)
         held[kind, hop > 0] = rows
         arrived.append(rows)
-    for turn in range(len(turns) - LAG, len(turns)):
-        arrive(turn)
+    while len(marks) < len(turns):
+        arrive(len(marks))
     latent_grads = pick_returned(after(returned, encoder_grad), own_t)
     return (totals[0], encoder_grad, totals[1].reshape(latent_count), latent_grads)
 

time: 165 us -> 176 us (1.067)
  blocking collectives: 0 us -> 31.8 us
  waiting for transfers between devices: 85.6 us -> 61.2 us
  Pallas kernels: 41.4 us -> 43.7 us
  local copies, waits for them, and re-layouts: 12.1 us -> 14.2 us
    all_to_all x0 -> x1, blocking collectives: none -> 31.8 us  [by_ring(): meta = lax.all_to_all(meta, 'lat', split_axis=0, concat_axis=0, tiled=True)]
    all_to_all x1 -> x0, waiting for transfers between devices: 16.4 us -> none  [by_ring(): meta = lax.all_to_all(meta, 'lat', split_axis=0, concat_axis=0, tiled=True)]
    ppermute x30, waiting for transfers between devices: 68.5 us -> 60.9 us  [send(): return lax.ppermute(after(rows, *first) if first else rows, 'lat', way)]
    all_to_all x1 -> x0, starting transfers between devices: 6.36 us -> none  [by_ring(): meta = lax.all_to_all(meta, 'lat', split_axis=0, concat_axis=0, tiled=True)]
    ppermute x30, starting transfers between devices: 13.3 us -> 17.6 us  [send(): return lax.ppermute(after(rows, *first) if first else rows, 'lat', way)]
    pallas_call x8, Pallas kernels: 14.3 us -> 17.7 us  [input_step(): pl.pallas_call(input_kernel, in_specs=[whole] * (3 + len(totals)), out_sp...]
    unnamed x26 -> x32, local copies, waits for them, and re-layouts: 11.4 us -> 13.5 us
  transfers between devices with their start and end apart: 32 -> 31, of which waited for: 11 -> 8; matrix products, arithmetic and copies ran while one was open for 0% -> 0% of each run, Pallas kernels for 23% -> 23%
where the time goes in v10:
time: 176 us; the launch traced here: 175 us
  waiting for transfers between devices  61.2 us (35%)
  Pallas kernels  43.7 us (25%)
  blocking collectives  31.8 us (18%)
  starting transfers between devices  21.8 us (12%)
  local copies, waits for them, and re-layouts  14.2 us (8%)
    ppermute x30, waiting for transfers between devices, send(): return lax.ppermute(after(rows, *first) if first else rows, 'lat', way)  60.9 us
    all_to_all x1, blocking collectives, by_ring(): meta = lax.all_to_all(meta, 'lat', split_axis=0, concat_axis=0, tiled=True)  31.8 us
    pallas_call x8, Pallas kernels, grad_step(): pl.pallas_call(functools.partial(grad_kernel, per_block), in_specs=[scala...  26 us
    pallas_call x8, Pallas kernels, input_step(): pl.pallas_call(input_kernel, in_specs=[whole] * (3 + len(totals)), out_sp...  17.7 us
    ppermute x30, starting transfers between devices, send(): return lax.ppermute(after(rows, *first) if first else rows, 'lat', way)  17.6 us
    unnamed x32, local copies, waits for them, and re-layouts  13.5 us
    all_to_all x1, starting transfers between devices, arrive(): lax.all_to_all(totals[2], 'lat', split_axis=0, concat_axis=0, tiled=True)  4.17 us
  transfers between devices with their start and end apart: 31, of which 8 were waited for; matrix products, arithmetic and copies ran while one was open for 0% of the time, Pallas kernels for 23%

profile of v10, /device:TPU:0, one launch (start us, length us, event | category | flops | bytes accessed | tf_op | source)
XLA Modules:
  0.0 175.3 jit_solution(12341306589664401447)
XLA Ops:
  0.6 3.1 %collective-permute-start = (bf16[128,3584]{1,0:T(8,128)(2,1)}, bf16[128,3584]{1,0:T(8,128)(2,1)}, u32[]{:S(2)}, u32[]{:S(2)}) collective-permute-start(bf16[128,3584]{1,0:T(8,128)(2,1)} %mine_ref.2), channel_id=1, source_target_pairs={{0,4},{4,8},{8,12},{12,14},{14,10},{10,6},{6,2},{2,0},{1,3},{5,1},... | collective-permute-start | bytes 2752520 | tf_op jit(solution)/shard_map/ppermute | solution.py:195
  3.7 2.0 %collective-permute-start.13 = (bf16[128,3584]{1,0:T(8,128)(2,1)}, bf16[128,3584]{1,0:T(8,128)(2,1)S(1)}, u32[]{:S(2)}, u32[]{:S(2)}) collective-permute-start(bf16[128,3584]{1,0:T(8,128)(2,1)} %mine_ref.3), channel_id=1, source_target_pairs={{0,4},{4,8},{8,12},{12,14},{14,10},{10,6},{6,2},{2,0},{1,3},{5,1},... | collective-permute-start | bytes 2752520 | tf_op jit(solution)/shard_map/ppermute | solution.py:195
  8.6 31.8 %all_to_all.10.meta_ref = bf16[16,32,128]{2,1,0:T(8,128)(2,1)S(1)} all-to-all(bf16[16,32,128]{2,1,0:T(8,128)(2,1)S(1)} %meta.1), channel_id=1, replica_groups=mesh['groups'=2,'lat'=16] {'lat'}, dimensions={0} | all-to-all | bytes 262144 | tf_op jit(solution)/shard_map/all_to_all | solution.py:153
  48.0 2.7 %grad_step.8 = (f32[256,3584]{1,0:T(8,128)S(1)}, f32[256,128]{1,0:T(8,128)S(1)}, f32[16,16,128]{2,1,0:T(8,128)S(1)}, bf16[256,256]{1,0:T(8,128)(2,1)S(1)}) custom-call(s32[2]{0:T(128)S(1)} %get-tuple-element.120.order_ref, bf16[16,32,128]{2,1,0:T(8,128)(2,1)S(1)} %all_to_all.10.meta_ref, bf16[256,3584]{1,0:T(8,128)(2,1)S(1)} %copy-done.4, ...), custom_call_target="tpu_custom_call" | custom-call | flops 1 | bytes 1 | tf_op jit(solution)/shard_map/grad_step/pallas_call | solution.py:160
  51.2 3.8 %grad_step.9 = (f32[256,3584]{1,0:T(8,128)S(1)}, f32[256,128]{1,0:T(8,128)S(1)}, f32[16,16,128]{2,1,0:T(8,128)S(1)}, bf16[256,256]{1,0:T(8,128)(2,1)S(1)}) custom-call(s32[2]{0:T(128)S(1)} %get-tuple-element.121.order_ref, bf16[16,32,128]{2,1,0:T(8,128)(2,1)S(1)} %all_to_all.10.meta_ref, ...), custom_call_target="tpu_custom_call", output_to_operand_aliasing={{0}: (5, {}), {1}: (6, {})} | custom-call | flops 1 | bytes 1 | tf_op jit(solution)/shard_map/grad_step/pallas_call | solution.py:160
  55.1 8.1 %collective-permute-done.1.mine_ref = bf16[128,3584]{1,0:T(8,128)(2,1)S(1)} collective-permute-done((bf16[128,3584]{1,0:T(8,128)(2,1)}, bf16[128,3584]{1,0:T(8,128)(2,1)S(1)}, u32[]{:S(2)}, u32[]{:S(2)}) %collective-permute-start.1) | collective-permute-done | bytes 917536 | tf_op jit(solution)/shard_map/ppermute | solution.py:195
  63.2 3.9 %grad_step.10 = (f32[256,3584]{1,0:T(8,128)S(1)}, f32[256,128]{1,0:T(8,128)S(1)}, f32[16,16,128]{2,1,0:T(8,128)S(1)}, bf16[256,256]{1,0:T(8,128)(2,1)S(1)}) custom-call(s32[2]{0:T(128)S(1)} %get-tuple-element.122.order_ref, bf16[16,32,128]{2,1,0:T(8,128)(2,1)S(1)} %all_to_all.10.meta_ref, ...), custom_call_target="tpu_custom_call", output_to_operand_aliasing={{0}: (5, {}), {1}: (6, {})} | custom-call | flops 1 | bytes 1 | tf_op jit(solution)/shard_map/grad_step/pallas_call | solution.py:160
  67.3 2.1 %collective-permute-start.8 = (bf16[128,3584]{1,0:T(8,128)(2,1)S(1)}, bf16[128,3584]{1,0:T(8,128)(2,1)S(1)}, u32[]{:S(2)}, u32[]{:S(2)}) collective-permute-start(bf16[128,3584]{1,0:T(8,128)(2,1)S(1)} %collective-permute-done.7.mine_ref), channel_id=1, source_target_pairs={{0,1},{1,0},{2,3},{3,2},{4,5},{5,4},{6,7},{7,6},{8,9},{9,8},{10,11... | collective-permute-start | bytes 2752520 | tf_op jit(solution)/shard_map/ppermute | solution.py:195
  69.4 1.9 %input_step.8.refs_0_ = f32[3584,256]{1,0:T(8,128)S(1)} custom-call(bf16[256,256]{1,0:T(8,128)(2,1)S(1)} %get-tuple-element.86.pre_ref, bf16[128,3584]{1,0:T(8,128)(2,1)S(1)} %copy-done.7, bf16[128,3584]{1,0:T(8,128)(2,1)} %collective-permute-done.15.theirs_ref), custom_call_target="tpu_custom_call" | custom-call | flops 1 | bytes 1 | tf_op jit(solution)/shard_map/input_step/pallas_call | solution.py:183
  73.3 4.2 %collective-permute-done.21.mine_ref = bf16[128,3584]{1,0:T(8,128)(2,1)S(1)} collective-permute-done((bf16[128,3584]{1,0:T(8,128)(2,1)S(1)}, bf16[128,3584]{1,0:T(8,128)(2,1)S(1)}, u32[]{:S(2)}, u32[]{:S(2)}) %collective-permute-start.21) | collective-permute-done | bytes 917536 | tf_op jit(solution)/shard_map/ppermute | solution.py:195
  77.5 2.9 %grad_step.11 = (f32[256,3584]{1,0:T(8,128)S(1)}, f32[256,128]{1,0:T(8,128)S(1)}, f32[16,16,128]{2,1,0:T(8,128)S(1)}, bf16[256,256]{1,0:T(8,128)(2,1)S(1)}) custom-call(s32[2]{0:T(128)S(1)} %get-tuple-element.118.order_ref, bf16[16,32,128]{2,1,0:T(8,128)(2,1)S(1)} %all_to_all.10.meta_ref, ...), custom_call_target="tpu_custom_call", output_to_operand_aliasing={{0}: (5, {}), {1}: (6, {})} | custom-call | flops 1 | bytes 1 | tf_op jit(solution)/shard_map/grad_step/pallas_call | solution.py:160
  80.4 15.8 %collective-permute-done.6.mine_ref = bf16[128,3584]{1,0:T(8,128)(2,1)S(1)} collective-permute-done((bf16[128,3584]{1,0:T(8,128)(2,1)S(1)}, bf16[128,3584]{1,0:T(8,128)(2,1)S(1)}, u32[]{:S(2)}, u32[]{:S(2)}) %collective-permute-start.6) | collective-permute-done | bytes 917536 | tf_op jit(solution)/shard_map/ppermute | solution.py:195
  96.2 2.9 %grad_step.12 = (f32[256,3584]{1,0:T(8,128)S(1)}, f32[256,128]{1,0:T(8,128)S(1)}, f32[16,16,128]{2,1,0:T(8,128)S(1)}, bf16[256,256]{1,0:T(8,128)(2,1)S(1)}) custom-call(s32[2]{0:T(128)S(1)} %get-tuple-element.119.order_ref, bf16[16,32,128]{2,1,0:T(8,128)(2,1)S(1)} %all_to_all.10.meta_ref, ...), custom_call_target="tpu_custom_call", output_to_operand_aliasing={{0}: (5, {}), {1}: (6, {})} | custom-call | flops 1 | bytes 1 | tf_op jit(solution)/shard_map/grad_step/pallas_call | solution.py:160
  99.2 2.0 %collective-permute-start.18 = (bf16[128,3584]{1,0:T(8,128)(2,1)S(1)}, bf16[128,3584]{1,0:T(8,128)(2,1)S(1)}, u32[]{:S(2)}, u32[]{:S(2)}) collective-permute-start(bf16[128,3584]{1,0:T(8,128)(2,1)S(1)} %copy-done.7), channel_id=1, source_target_pairs={{4,0},{8,4},{12,8},{14,12},{10,14},{6,10},{2,6},{0,2},{3,1},{1,5},... | collective-permute-start | bytes 2752520 | tf_op jit(solution)/shard_map/ppermute | solution.py:195
  102.9 2.9 %grad_step.13 = (f32[256,3584]{1,0:T(8,128)S(1)}, f32[256,128]{1,0:T(8,128)S(1)}, f32[16,16,128]{2,1,0:T(8,128)S(1)}, bf16[256,256]{1,0:T(8,128)(2,1)S(1)}) custom-call(s32[2]{0:T(128)S(1)} %get-tuple-element.117.order_ref, bf16[16,32,128]{2,1,0:T(8,128)(2,1)S(1)} %all_to_all.10.meta_ref, ...), custom_call_target="tpu_custom_call", output_to_operand_aliasing={{0}: (5, {}), {1}: (6, {})} | custom-call | flops 1 | bytes 1 | tf_op jit(solution)/shard_map/grad_step/pallas_call | solution.py:160
  105.8 16.2 %collective-permute-done.10.mine_ref = bf16[128,3584]{1,0:T(8,128)(2,1)S(1)} collective-permute-done((bf16[128,3584]{1,0:T(8,128)(2,1)S(1)}, bf16[128,3584]{1,0:T(8,128)(2,1)S(1)}, u32[]{:S(2)}, u32[]{:S(2)}) %collective-permute-start.10) | collective-permute-done | bytes 917536 | tf_op jit(solution)/shard_map/ppermute | solution.py:195
  122.4 2.1 %collective-permute-start.19 = (bf16[128,3584]{1,0:T(8,128)(2,1)S(1)}, bf16[128,3584]{1,0:T(8,128)(2,1)S(1)}, u32[]{:S(2)}, u32[]{:S(2)}) collective-permute-start(bf16[128,3584]{1,0:T(8,128)(2,1)S(1)} %collective-permute-done.18.mine_ref), channel_id=1, source_target_pairs={{4,0},{8,4},{12,8},{14,12},{10,14},{6,10},{2,6},{0,2},{3,1},{1,5},... | collective-permute-start | bytes 2752520 | tf_op jit(solution)/shard_map/ppermute | solution.py:195
  124.5 2.9 %grad_step.14 = (f32[256,3584]{1,0:T(8,128)S(1)}, f32[256,128]{1,0:T(8,128)S(1)}, f32[16,16,128]{2,1,0:T(8,128)S(1)}, bf16[256,256]{1,0:T(8,128)(2,1)S(1)}) custom-call(s32[2]{0:T(128)S(1)} %get-tuple-element.116.order_ref, bf16[16,32,128]{2,1,0:T(8,128)(2,1)S(1)} %all_to_all.10.meta_ref, ...), custom_call_target="tpu_custom_call", output_to_operand_aliasing={{0}: (5, {}), {1}: (6, {})} | custom-call | flops 1 | bytes 1 | tf_op jit(solution)/shard_map/grad_step/pallas_call | solution.py:160
  127.4 11.1 %collective-permute-done.23.mine_ref = bf16[128,3584]{1,0:T(8,128)(2,1)S(1)} collective-permute-done((bf16[128,3584]{1,0:T(8,128)(2,1)S(1)}, bf16[128,3584]{1,0:T(8,128)(2,1)S(1)}, u32[]{:S(2)}, u32[]{:S(2)}) %collective-permute-start.23) | collective-permute-done | bytes 917536 | tf_op jit(solution)/shard_map/ppermute | solution.py:195
  138.5 4.1 %grad_step.15 = (bf16[256,3584]{1,0:T(8,128)(2,1)}, f32[1,256]{1,0:T(1,128)}, f32[16,16,128]{2,1,0:T(8,128)S(1)}, bf16[256,256]{1,0:T(8,128)(2,1)S(1)}) custom-call(s32[2]{0:T(128)S(1)} %get-tuple-element.123.order_ref, bf16[16,32,128]{2,1,0:T(8,128)(2,1)S(1)} %all_to_all.10.meta_ref, bf16[256,3584]{1,0:T(8,128)(2,1)S(1)} %copy-done.5, ...), custom_call_target="tpu_custom_call" | custom-call | flops 1 | bytes 1 | tf_op jit(solution)/shard_map/grad_step/pallas_call | solution.py:160
  142.6 2.0 %collective-permute-start.20 = (bf16[128,3584]{1,0:T(8,128)(2,1)S(1)}, bf16[128,3584]{1,0:T(8,128)(2,1)}, u32[]{:S(2)}, u32[]{:S(2)}) collective-permute-start(bf16[128,3584]{1,0:T(8,128)(2,1)S(1)} %collective-permute-done.19.mine_ref), channel_id=1, source_target_pairs={{4,0},{8,4},{12,8},{14,12},{10,14},{6,10},{2,6},{0,2},{3,1},{1,5},... | collective-permute-start | bytes 2752520 | tf_op jit(solution)/shard_map/ppermute | solution.py:195
  144.6 4.2 %all-to-all-start.1 = ((f32[16,16,128]{2,1,0:T(8,128)}), f32[16,16,128]{2,1,0:T(8,128)}, u32[]{:S(2)}, u32[]{:S(2)}) async-start(f32[16,16,128]{2,1,0:T(8,128)} %copy-done.10), calls=%async_computation.1 | async-start | bytes 262144 | tf_op jit(solution)/shard_map/all_to_all | solution.py:230
  148.8 2.0 %copy-done.1 = f32[3584,256]{1,0:T(8,128)S(1)} copy-done((f32[3584,256]{1,0:T(8,128)S(1)}, f32[3584,256]{1,0:T(8,128)}, u32[]{:S(2)}) %copy-start.1) | copy-done | bytes 3670040
  150.8 2.5 %input_step.11.refs_0_ = f32[3584,256]{1,0:T(8,128)S(1)} custom-call(bf16[256,256]{1,0:T(8,128)(2,1)S(1)} %get-tuple-element.107.pre_ref, bf16[128,3584]{1,0:T(8,128)(2,1)S(1)} %collective-permute-done.18.mine_ref, bf16[128,3584]{1,0:T(8,128)(2,1)} %collective-permute-done.25.theirs_ref, f32[3584,256]{1,0:T(8,128)S(1)} %copy-done.1), custom_call_target="tpu_custom_call", output_to_operand_aliasing={{}: (3, {})} | custom-call | flops 1 | bytes 1 | tf_op jit(solution)/shard_map/input_step/pallas_call | solution.py:183
  153.6 5.1 %collective-permute-done.27.mine_ref = bf16[128,3584]{1,0:T(8,128)(2,1)} collective-permute-done((bf16[128,3584]{1,0:T(8,128)(2,1)S(1)}, bf16[128,3584]{1,0:T(8,128)(2,1)}, u32[]{:S(2)}, u32[]{:S(2)}) %collective-permute-start.27) | collective-permute-done | bytes 917536 | tf_op jit(solution)/shard_map/ppermute | solution.py:195
  158.7 2.5 %input_step.12.refs_0_ = f32[3584,256]{1,0:T(8,128)S(1)} custom-call(bf16[256,256]{1,0:T(8,128)(2,1)S(1)} %get-tuple-element.101.pre_ref, bf16[128,3584]{1,0:T(8,128)(2,1)S(1)} %collective-permute-done.23.mine_ref, bf16[128,3584]{1,0:T(8,128)(2,1)} %collective-permute-done.24.theirs_ref, ...), custom_call_target="tpu_custom_call", output_to_operand_aliasing={{}: (3, {})} | custom-call | flops 1 | bytes 1 | tf_op jit(solution)/shard_map/input_step/pallas_call | solution.py:183
  161.2 1.8 %copy-done.2 = f32[3584,256]{1,0:T(8,128)} copy-done((f32[3584,256]{1,0:T(8,128)}, f32[3584,256]{1,0:T(8,128)S(1)}, u32[]{:S(2)}) %copy-start.2) | copy-done | bytes 3670040
  163.5 2.0 %copy-done.3 = f32[3584,256]{1,0:T(8,128)S(1)} copy-done((f32[3584,256]{1,0:T(8,128)S(1)}, f32[3584,256]{1,0:T(8,128)}, u32[]{:S(2)}) %copy-start.3) | copy-done | bytes 3670040
  165.6 2.5 %input_step.13.refs_0_ = f32[3584,256]{1,0:T(8,128)S(1)} custom-call(bf16[256,256]{1,0:T(8,128)(2,1)S(1)} %get-tuple-element.113.pre_ref, bf16[128,3584]{1,0:T(8,128)(2,1)S(1)} %collective-permute-done.19.mine_ref, bf16[128,3584]{1,0:T(8,128)(2,1)} %collective-permute-done.29.theirs_ref, f32[3584,256]{1,0:T(8,128)S(1)} %copy-done.3), custom_call_target="tpu_custom_call", output_to_operand_aliasing={{}: (3, {})} | custom-call | flops 1 | bytes 1 | tf_op jit(solution)/shard_map/input_step/pallas_call | solution.py:183
  168.1 2.5 %input_step.14.refs_0_ = f32[3584,256]{1,0:T(8,128)S(1)} custom-call(bf16[256,256]{1,0:T(8,128)(2,1)S(1)} %get-tuple-element.111.pre_ref, bf16[128,3584]{1,0:T(8,128)(2,1)} %collective-permute-done.27.mine_ref, bf16[128,3584]{1,0:T(8,128)(2,1)S(1)} %collective-permute-done.28.theirs_ref, ...), custom_call_target="tpu_custom_call", output_to_operand_aliasing={{}: (3, {})} | custom-call | flops 1 | bytes 1 | tf_op jit(solution)/shard_map/input_step/pallas_call | solution.py:183
  170.6 3.1 %input_step.15 = bf16[3584,256]{1,0:T(8,128)(2,1)} custom-call(bf16[256,256]{1,0:T(8,128)(2,1)S(1)} %get-tuple-element.96.pre_ref, bf16[128,3584]{1,0:T(8,128)(2,1)} %collective-permute-done.20.mine_ref, bf16[128,3584]{1,0:T(8,128)(2,1)S(1)} %collective-permute-done.26.theirs_ref, f32[3584,256]{1,0:T(8,128)S(1)} %input_step.14.refs_0_), custom_call_target="tpu_custom_call" | custom-call | flops 1 | bytes 1 | tf_op jit(solution)/shard_map/input_step/pallas_call | solution.py:183
  173.7 1.6 select_reduce_fusion
  (84 shorter events, 16.2 us)
Async XLA Ops:
  0.6 39.8 %collective-permute-start = (bf16[128,3584]{1,0:T(8,128)(2,1)}, bf16[128,3584]{1,0:T(8,128)(2,1)}, u32[]{:S(2)}, u32[]{:S(2)}) collective-permute-start(bf16[128,3584]{1,0:T(8,128)(2,1)} %mine_ref.2), channel_id=1, source_target_pairs={{0,4},{4,8},{8,12},{12,14},{14,10},{10,6},{6,2},{2,0},{1,3},{5,1},... | collective-permute-start | bytes 2752520 | tf_op jit(solution)/shard_map/ppermute | solution.py:195
  3.7 36.8 %collective-permute-start.2 = (bf16[128,3584]{1,0:T(8,128)(2,1)}, bf16[128,3584]{1,0:T(8,128)(2,1)}, u32[]{:S(2)}, u32[]{:S(2)}) collective-permute-start(bf16[128,3584]{1,0:T(8,128)(2,1)} %mine_ref.2), channel_id=1, source_target_pairs={{4,0},{8,4},{12,8},{14,12},{10,14},{6,10},{2,6},{0,2},{3,1},{1,5},... | collective-permute-start | bytes 2752520 | tf_op jit(solution)/shard_map/ppermute | solution.py:195
  3.7 37.3 %collective-permute-start.5 = (bf16[128,3584]{1,0:T(8,128)(2,1)}, bf16[128,3584]{1,0:T(8,128)(2,1)S(1)}, u32[]{:S(2)}, u32[]{:S(2)}) collective-permute-start(bf16[128,3584]{1,0:T(8,128)(2,1)} %mine_ref.2), channel_id=1, source_target_pairs={{0,1},{1,0},{2,3},{3,2},{4,5},{5,4},{6,7},{7,6},{8,9},{9,8},{10,11... | collective-permute-start | bytes 2752520 | tf_op jit(solution)/shard_map/ppermute | solution.py:195
  3.7 39.7 %collective-permute-start.13 = (bf16[128,3584]{1,0:T(8,128)(2,1)}, bf16[128,3584]{1,0:T(8,128)(2,1)S(1)}, u32[]{:S(2)}, u32[]{:S(2)}) collective-permute-start(bf16[128,3584]{1,0:T(8,128)(2,1)} %mine_ref.3), channel_id=1, source_target_pairs={{0,4},{4,8},{8,12},{12,14},{14,10},{10,6},{6,2},{2,0},{1,3},{5,1},... | collective-permute-start | bytes 2752520 | tf_op jit(solution)/shard_map/ppermute | solution.py:195
  40.5 10.2 %collective-permute-start.4 = (bf16[128,3584]{1,0:T(8,128)(2,1)}, bf16[128,3584]{1,0:T(8,128)(2,1)}, u32[]{:S(2)}, u32[]{:S(2)}) collective-permute-start(bf16[128,3584]{1,0:T(8,128)(2,1)} %collective-permute-done.mine_ref), channel_id=1, source_target_pairs={{0,1},{1,0},{2,3},{3,2},{4,5},{5,4},{6,7},{7,6},{8,9},{9,8},{10,11... | collective-permute-start | bytes 2752520 | tf_op jit(solution)/shard_map/ppermute | solution.py:195
  40.5 22.7 %collective-permute-start.1 = (bf16[128,3584]{1,0:T(8,128)(2,1)}, bf16[128,3584]{1,0:T(8,128)(2,1)S(1)}, u32[]{:S(2)}, u32[]{:S(2)}) collective-permute-start(bf16[128,3584]{1,0:T(8,128)(2,1)} %collective-permute-done.mine_ref), channel_id=1, source_target_pairs={{0,4},{4,8},{8,12},{12,14},{14,10},{10,6},{6,2},{2,0},{1,3},{5,1},... | collective-permute-start | bytes 2752520 | tf_op jit(solution)/shard_map/ppermute | solution.py:195
  40.5 22.7 %collective-permute-start.3 = (bf16[128,3584]{1,0:T(8,128)(2,1)}, bf16[128,3584]{1,0:T(8,128)(2,1)}, u32[]{:S(2)}, u32[]{:S(2)}) collective-permute-start(bf16[128,3584]{1,0:T(8,128)(2,1)} %collective-permute-done.2.mine_ref), channel_id=1, source_target_pairs={{0,1},{1,0},{2,3},{3,2},{4,5},{5,4},{6,7},{7,6},{8,9},{9,8},{10,11... | collective-permute-start | bytes 2752520 | tf_op jit(solution)/shard_map/ppermute | solution.py:195
  41.9 25.2 %collective-permute-start.7 = (bf16[128,3584]{1,0:T(8,128)(2,1)}, bf16[128,3584]{1,0:T(8,128)(2,1)S(1)}, u32[]{:S(2)}, u32[]{:S(2)}) collective-permute-start(bf16[128,3584]{1,0:T(8,128)(2,1)} %collective-permute-done.2.mine_ref), channel_id=1, source_target_pairs={{4,0},{8,4},{12,8},{14,12},{10,14},{6,10},{2,6},{0,2},{3,1},{1,5},... | collective-permute-start | bytes 2752520 | tf_op jit(solution)/shard_map/ppermute | solution.py:195
  43.4 23.9 %collective-permute-start.15 = (bf16[128,3584]{1,0:T(8,128)(2,1)}, bf16[128,3584]{1,0:T(8,128)(2,1)}, u32[]{:S(2)}, u32[]{:S(2)}) collective-permute-start(bf16[128,3584]{1,0:T(8,128)(2,1)} %mine_ref.3), channel_id=1, source_target_pairs={{0,1},{1,0},{2,3},{3,2},{4,5},{5,4},{6,7},{7,6},{8,9},{9,8},{10,11... | collective-permute-start | bytes 2752520 | tf_op jit(solution)/shard_map/ppermute | solution.py:195
  50.7 20.6 %collective-permute-start.14 = (bf16[128,3584]{1,0:T(8,128)(2,1)S(1)}, bf16[128,3584]{1,0:T(8,128)(2,1)S(1)}, u32[]{:S(2)}, u32[]{:S(2)}) collective-permute-start(bf16[128,3584]{1,0:T(8,128)(2,1)S(1)} %collective-permute-done.13.mine_ref), channel_id=1, source_target_pairs={{0,1},{1,0},{2,3},{3,2},{4,5},{5,4},{6,7},{7,6},{8,9},{9,8},{10,11... | collective-permute-start | bytes 2752520 | tf_op jit(solution)/shard_map/ppermute | solution.py:195
  63.2 14.3 %collective-permute-start.21 = (bf16[128,3584]{1,0:T(8,128)(2,1)S(1)}, bf16[128,3584]{1,0:T(8,128)(2,1)S(1)}, u32[]{:S(2)}, u32[]{:S(2)}) collective-permute-start(bf16[128,3584]{1,0:T(8,128)(2,1)S(1)} %collective-permute-done.13.mine_ref), channel_id=1, source_target_pairs={{0,4},{4,8},{8,12},{12,14},{14,10},{10,6},{6,2},{2,0},{1,3},{5,1},... | collective-permute-start | bytes 2752520 | tf_op jit(solution)/shard_map/ppermute | solution.py:195
  63.2 14.3 %collective-permute-start.9 = (bf16[128,3584]{1,0:T(8,128)(2,1)S(1)}, bf16[128,3584]{1,0:T(8,128)(2,1)S(1)}, u32[]{:S(2)}, u32[]{:S(2)}) collective-permute-start(bf16[128,3584]{1,0:T(8,128)(2,1)S(1)} %collective-permute-done.1.mine_ref), channel_id=1, source_target_pairs={{0,1},{1,0},{2,3},{3,2},{4,5},{5,4},{6,7},{7,6},{8,9},{9,8},{10,11... | collective-permute-start | bytes 2752520 | tf_op jit(solution)/shard_map/ppermute | solution.py:195
  63.2 6.2 %copy-start.7 = (bf16[128,3584]{1,0:T(8,128)(2,1)S(1)}, bf16[128,3584]{1,0:T(8,128)(2,1)}, u32[]{:S(2)}) copy-start(bf16[128,3584]{1,0:T(8,128)(2,1)} %mine_ref.3) | copy-start | bytes 2752516
  67.1 29.1 %collective-permute-start.6 = (bf16[128,3584]{1,0:T(8,128)(2,1)S(1)}, bf16[128,3584]{1,0:T(8,128)(2,1)S(1)}, u32[]{:S(2)}, u32[]{:S(2)}) collective-permute-start(bf16[128,3584]{1,0:T(8,128)(2,1)S(1)} %collective-permute-done.1.mine_ref), channel_id=1, source_target_pairs={{0,4},{4,8},{8,12},{12,14},{14,10},{10,6},{6,2},{2,0},{1,3},{5,1},... | collective-permute-start | bytes 2752520 | tf_op jit(solution)/shard_map/ppermute | solution.py:195
  67.3 28.9 %collective-permute-start.8 = (bf16[128,3584]{1,0:T(8,128)(2,1)S(1)}, bf16[128,3584]{1,0:T(8,128)(2,1)S(1)}, u32[]{:S(2)}, u32[]{:S(2)}) collective-permute-start(bf16[128,3584]{1,0:T(8,128)(2,1)S(1)} %collective-permute-done.7.mine_ref), channel_id=1, source_target_pairs={{0,1},{1,0},{2,3},{3,2},{4,5},{5,4},{6,7},{7,6},{8,9},{9,8},{10,11... | collective-permute-start | bytes 2752520 | tf_op jit(solution)/shard_map/ppermute | solution.py:195
  72.7 28.5 %collective-permute-start.16 = (bf16[128,3584]{1,0:T(8,128)(2,1)S(1)}, bf16[128,3584]{1,0:T(8,128)(2,1)S(1)}, u32[]{:S(2)}, u32[]{:S(2)}) collective-permute-start(bf16[128,3584]{1,0:T(8,128)(2,1)S(1)} %collective-permute-done.7.mine_ref), channel_id=1, source_target_pairs={{4,0},{8,4},{12,8},{14,12},{10,14},{6,10},{2,6},{0,2},{3,1},{1,5},... | collective-permute-start | bytes 2752520 | tf_op jit(solution)/shard_map/ppermute | solution.py:195
  77.5 23.7 %collective-permute-start.22 = (bf16[128,3584]{1,0:T(8,128)(2,1)S(1)}, bf16[128,3584]{1,0:T(8,128)(2,1)S(1)}, u32[]{:S(2)}, u32[]{:S(2)}) collective-permute-start(bf16[128,3584]{1,0:T(8,128)(2,1)S(1)} %collective-permute-done.21.mine_ref), channel_id=1, source_target_pairs={{0,1},{1,0},{2,3},{3,2},{4,5},{5,4},{6,7},{7,6},{8,9},{9,8},{10,11... | collective-permute-start | bytes 2752520 | tf_op jit(solution)/shard_map/ppermute | solution.py:195
  96.2 6.7 %collective-permute-start.11 = (bf16[128,3584]{1,0:T(8,128)(2,1)S(1)}, bf16[128,3584]{1,0:T(8,128)(2,1)S(1)}, u32[]{:S(2)}, u32[]{:S(2)}) collective-permute-start(bf16[128,3584]{1,0:T(8,128)(2,1)S(1)} %collective-permute-done.6.mine_ref), channel_id=1, source_target_pairs={{0,1},{1,0},{2,3},{3,2},{4,5},{5,4},{6,7},{7,6},{8,9},{9,8},{10,11... | collective-permute-start | bytes 2752520 | tf_op jit(solution)/shard_map/ppermute | solution.py:195
  99.1 22.9 %collective-permute-start.10 = (bf16[128,3584]{1,0:T(8,128)(2,1)S(1)}, bf16[128,3584]{1,0:T(8,128)(2,1)S(1)}, u32[]{:S(2)}, u32[]{:S(2)}) collective-permute-start(bf16[128,3584]{1,0:T(8,128)(2,1)S(1)} %collective-permute-done.6.mine_ref), channel_id=1, source_target_pairs={{0,4},{4,8},{8,12},{12,14},{14,10},{10,6},{6,2},{2,0},{1,3},{5,1},... | collective-permute-start | bytes 2752520 | tf_op jit(solution)/shard_map/ppermute | solution.py:195
  99.2 23.2 %collective-permute-start.18 = (bf16[128,3584]{1,0:T(8,128)(2,1)S(1)}, bf16[128,3584]{1,0:T(8,128)(2,1)S(1)}, u32[]{:S(2)}, u32[]{:S(2)}) collective-permute-start(bf16[128,3584]{1,0:T(8,128)(2,1)S(1)} %copy-done.7), channel_id=1, source_target_pairs={{4,0},{8,4},{12,8},{14,12},{10,14},{6,10},{2,6},{0,2},{3,1},{1,5},... | collective-permute-start | bytes 2752520 | tf_op jit(solution)/shard_map/ppermute | solution.py:195
  101.2 23.3 %collective-permute-start.17 = (bf16[128,3584]{1,0:T(8,128)(2,1)S(1)}, bf16[128,3584]{1,0:T(8,128)(2,1)S(1)}, u32[]{:S(2)}, u32[]{:S(2)}) collective-permute-start(bf16[128,3584]{1,0:T(8,128)(2,1)S(1)} %collective-permute-done.16.mine_ref), channel_id=1, source_target_pairs={{0,1},{1,0},{2,3},{3,2},{4,5},{5,4},{6,7},{7,6},{8,9},{9,8},{10,11... | collective-permute-start | bytes 2752520 | tf_op jit(solution)/shard_map/ppermute | solution.py:195
  102.6 35.9 %collective-permute-start.23 = (bf16[128,3584]{1,0:T(8,128)(2,1)S(1)}, bf16[128,3584]{1,0:T(8,128)(2,1)S(1)}, u32[]{:S(2)}, u32[]{:S(2)}) collective-permute-start(bf16[128,3584]{1,0:T(8,128)(2,1)S(1)} %collective-permute-done.21.mine_ref), channel_id=1, source_target_pairs={{0,4},{4,8},{8,12},{12,14},{14,10},{10,6},{6,2},{2,0},{1,3},{5,1},... | collective-permute-start | bytes 2752520 | tf_op jit(solution)/shard_map/ppermute | solution.py:195
  122.0 16.5 %collective-permute-start.12 = (bf16[128,3584]{1,0:T(8,128)(2,1)S(1)}, bf16[128,3584]{1,0:T(8,128)(2,1)S(1)}, u32[]{:S(2)}, u32[]{:S(2)}) collective-permute-start(bf16[128,3584]{1,0:T(8,128)(2,1)S(1)} %collective-permute-done.10.mine_ref), channel_id=1, source_target_pairs={{0,1},{1,0},{2,3},{3,2},{4,5},{5,4},{6,7},{7,6},{8,9},{9,8},{10,11... | collective-permute-start | bytes 2752520 | tf_op jit(solution)/shard_map/ppermute | solution.py:195
  122.4 20.2 %collective-permute-start.19 = (bf16[128,3584]{1,0:T(8,128)(2,1)S(1)}, bf16[128,3584]{1,0:T(8,128)(2,1)S(1)}, u32[]{:S(2)}, u32[]{:S(2)}) collective-permute-start(bf16[128,3584]{1,0:T(8,128)(2,1)S(1)} %collective-permute-done.18.mine_ref), channel_id=1, source_target_pairs={{4,0},{8,4},{12,8},{14,12},{10,14},{6,10},{2,6},{0,2},{3,1},{1,5},... | collective-permute-start | bytes 2752520 | tf_op jit(solution)/shard_map/ppermute | solution.py:195
  124.5 24.3 %collective-permute-start.25 = (bf16[128,3584]{1,0:T(8,128)(2,1)S(1)}, bf16[128,3584]{1,0:T(8,128)(2,1)}, u32[]{:S(2)}, u32[]{:S(2)}) collective-permute-start(bf16[128,3584]{1,0:T(8,128)(2,1)S(1)} %collective-permute-done.18.mine_ref), channel_id=1, source_target_pairs={{0,1},{1,0},{2,3},{3,2},{4,5},{5,4},{6,7},{7,6},{8,9},{9,8},{10,11... | collective-permute-start | bytes 2752520 | tf_op jit(solution)/shard_map/ppermute | solution.py:195
  138.5 20.2 %collective-permute-start.24 = (bf16[128,3584]{1,0:T(8,128)(2,1)S(1)}, bf16[128,3584]{1,0:T(8,128)(2,1)}, u32[]{:S(2)}, u32[]{:S(2)}) collective-permute-start(bf16[128,3584]{1,0:T(8,128)(2,1)S(1)} %collective-permute-done.23.mine_ref), channel_id=1, source_target_pairs={{0,1},{1,0},{2,3},{3,2},{4,5},{5,4},{6,7},{7,6},{8,9},{9,8},{10,11... | collective-permute-start | bytes 2752520 | tf_op jit(solution)/shard_map/ppermute | solution.py:195
  138.5 20.2 %collective-permute-start.27 = (bf16[128,3584]{1,0:T(8,128)(2,1)S(1)}, bf16[128,3584]{1,0:T(8,128)(2,1)}, u32[]{:S(2)}, u32[]{:S(2)}) collective-permute-start(bf16[128,3584]{1,0:T(8,128)(2,1)S(1)} %collective-permute-done.23.mine_ref), channel_id=1, source_target_pairs={{0,4},{4,8},{8,12},{12,14},{14,10},{10,6},{6,2},{2,0},{1,3},{5,1},... | collective-permute-start | bytes 2752520 | tf_op jit(solution)/shard_map/ppermute | solution.py:195
  142.6 20.7 %collective-permute-start.20 = (bf16[128,3584]{1,0:T(8,128)(2,1)S(1)}, bf16[128,3584]{1,0:T(8,128)(2,1)}, u32[]{:S(2)}, u32[]{:S(2)}) collective-permute-start(bf16[128,3584]{1,0:T(8,128)(2,1)S(1)} %collective-permute-done.19.mine_ref), channel_id=1, source_target_pairs={{4,0},{8,4},{12,8},{14,12},{10,14},{6,10},{2,6},{0,2},{3,1},{1,5},... | collective-permute-start | bytes 2752520 | tf_op jit(solution)/shard_map/ppermute | solution.py:195
  144.6 18.6 %all-to-all-start.1 = ((f32[16,16,128]{2,1,0:T(8,128)}), f32[16,16,128]{2,1,0:T(8,128)}, u32[]{:S(2)}, u32[]{:S(2)}) async-start(f32[16,16,128]{2,1,0:T(8,128)} %copy-done.10), calls=%async_computation.1 | async-start | bytes 262144 | tf_op jit(solution)/shard_map/all_to_all | solution.py:230
  153.3 10.2 %collective-permute-start.29 = (bf16[128,3584]{1,0:T(8,128)(2,1)S(1)}, bf16[128,3584]{1,0:T(8,128)(2,1)}, u32[]{:S(2)}, u32[]{:S(2)}) collective-permute-start(bf16[128,3584]{1,0:T(8,128)(2,1)S(1)} %collective-permute-done.19.mine_ref), channel_id=1, source_target_pairs={{0,1},{1,0},{2,3},{3,2},{4,5},{5,4},{6,7},{7,6},{8,9},{9,8},{10,11... | collective-permute-start | bytes 2752520 | tf_op jit(solution)/shard_map/ppermute | solution.py:195
  158.7 9.4 %collective-permute-start.28 = (bf16[128,3584]{1,0:T(8,128)(2,1)}, bf16[128,3584]{1,0:T(8,128)(2,1)S(1)}, u32[]{:S(2)}, u32[]{:S(2)}) collective-permute-start(bf16[128,3584]{1,0:T(8,128)(2,1)} %collective-permute-done.27.mine_ref), channel_id=1, source_target_pairs={{0,1},{1,0},{2,3},{3,2},{4,5},{5,4},{6,7},{7,6},{8,9},{9,8},{10,11... | collective-permute-start | bytes 2752520 | tf_op jit(solution)/shard_map/ppermute | solution.py:195
  163.2 7.3 %collective-permute-start.26 = (bf16[128,3584]{1,0:T(8,128)(2,1)}, bf16[128,3584]{1,0:T(8,128)(2,1)S(1)}, u32[]{:S(2)}, u32[]{:S(2)}) collective-permute-start(bf16[128,3584]{1,0:T(8,128)(2,1)} %collective-permute-done.20.mine_ref), channel_id=1, source_target_pairs={{0,1},{1,0},{2,3},{3,2},{4,5},{5,4},{6,7},{7,6},{8,9},{9,8},{10,11... | collective-permute-start | bytes 2752520 | tf_op jit(solution)/shard_map/ppermute | solution.py:195
  (15 other events, 29.7 us)

commit v11 on v10

--- a/solution.py
+++ b/solution.py
@@ -13,8 +13,7 @@
 HELD_BYTES = 1 << 25
 RING_BYTES = 1 << 26
 VMEM_BYTES = 24 << 20
-LAG = 5
-EARLY = 1
+LAG = 4
 
 
 def ring_tables(peer_count):
@@ -32,7 +31,10 @@
     onward += [(2 * ring[i] + 1, 2 * ring[(i - 1) % chips] + 1) for i in range(chips)]
     swap = [(i, i ^ 1) for i in range(peer_count)]
     backward = [(b, a) for a, b in onward]
-    return sources, onward, backward, swap
+    target = dict(onward)
+    second = [(a, target[b]) for a, b in onward]
+    across = [(b, a ^ 1) for a, b in second]
+    return sources, onward, backward, swap, second, across
 
 
 def meta_kernel(owners_ref, blocks_ref, offsets_ref, values_ref, meta_ref):
@@ -58,7 +60,8 @@
     total_ref, bias_ref, lat_ref, pre_ref, acts_ref, bias_sum = refs[-6:]
     first, last = len(refs) == 6, bias_ref.shape[0] == 1
     bias_sum[...] = jnp.zeros_like(bias_sum) if first else refs[1][...]
-    lat_ref[...] = jnp.zeros_like(lat_ref) if first else refs[2][...]
+    if not last:
+        lat_ref[...] = jnp.zeros_like(lat_ref) if first else refs[2][...]
     latents, width = decoder_ref.shape
     tokens = mine_ref.shape[0]
     span = column_span(width)
@@ -92,7 +95,7 @@
                 dense_both.append(dense)
             pre_ref[block : block + 16, at] = jnp.concatenate(kept_both, axis=0).astype(jnp.bfloat16)
             acts_ref[block : block + 16, at] = jnp.concatenate(dense_both, axis=0).astype(jnp.bfloat16)
-        source = order_ref[tile]
+        source = tile if last else order_ref[tile]
         for k in range(per_block):
             lat_ref[source, k : k + 1, :] = jnp.sum(sums[k], axis=0, keepdims=True)
     for at in range(0, width, span):
@@ -104,8 +107,13 @@
     bias_ref[...] = jnp.sum(bias_sum[...].T, axis=0, keepdims=True) if last else bias_sum[...]
 
 
-def input_kernel(pre_ref, mine_ref, theirs_ref, *refs):
-    total_ref = refs[-1]
+def input_kernel(last, pre_ref, mine_ref, theirs_ref, *refs):
+    copies = []
+    if last:
+        out_ref, total_ref, sems = refs[-3:]
+        refs = refs[:-2]
+    else:
+        total_ref = refs[-1]
     width = mine_ref.shape[1]
     span = column_span(width)
     for at in range(0, width, span):
@@ -114,6 +122,12 @@
         if len(refs) == 2:
             term += refs[0][at : at + span, :]
         total_ref[at : at + span, :] = term.astype(total_ref.dtype)
+        if last:
+            here = pl.ds(at, span)
+            copies.append(pltpu.make_async_copy(total_ref.at[here], out_ref.at[here], sems.at[at // span]))
+            copies[-1].start()
+    for copy in copies:
+        copy.wait()
 
 
 def column_span(width):
@@ -132,7 +146,7 @@
     peer_count = lax.axis_size("lat")
     chips = peer_count // 2
     me = lax.axis_index("lat")
-    sources, onward, backward, swap = ring_tables(peer_count)
+    sources, onward, backward, swap, second, across = ring_tables(peer_count)
     order = jnp.asarray(sources)[me]
     own_t = owners.T
     whole = pl.BlockSpec(memory_space=pltpu.VMEM)
@@ -157,6 +171,7 @@
 
     def grad_step(hop, rows, totals, last):
         sums, lanes = (latent_count, width), (latent_count, token_count)
+        lat = (2 if last else peer_count, per_block, token_count)
         return pl.pallas_call(
             functools.partial(grad_kernel, per_block),
             in_specs=[scalars] + [whole] * (4 + len(totals)),
@@ -164,7 +179,7 @@
             out_shape=[
                 jax.ShapeDtypeStruct(sums, jnp.bfloat16) if last else pltpu.VMEM(sums, jnp.float32),
                 jax.ShapeDtypeStruct((1, latent_count), jnp.float32) if last else pltpu.VMEM(lanes, jnp.float32),
-                jax.ShapeDtypeStruct((peer_count, per_block, token_count), jnp.float32),
+                jax.ShapeDtypeStruct(lat, jnp.float32),
                 pltpu.VMEM((latent_count, step_tokens), jnp.bfloat16),
             ],
             scratch_shapes=[
@@ -181,10 +196,16 @@
         sums = (width, latent_count)
         totals = () if total is None else (total,)
         return pl.pallas_call(
-            input_kernel,
+            functools.partial(input_kernel, last),
             in_specs=[whole] * (3 + len(totals)),
-            out_specs=whole,
+            out_specs=pl.BlockSpec(memory_space=pl.ANY) if last else whole,
             out_shape=jax.ShapeDtypeStruct(sums, jnp.bfloat16) if last else pltpu.VMEM(sums, jnp.float32),
+            scratch_shapes=[
+                pltpu.VMEM(sums, jnp.bfloat16),
+                pltpu.SemaphoreType.DMA((width // column_span(width),)),
+            ]
+            if last
+            else [],
             input_output_aliases={3: 0} if totals and not last else {},
             compiler_params=params,
             cost_estimate=light,
@@ -194,14 +215,10 @@
     def send(rows, way, *first):
         return lax.ppermute(after(rows, *first) if first else rows, "lat", way)
 
-    half = chips // 2
-    later = [("inputs", 1)]
-    for hop in range(1, half):
-        later += [("inputs", hop + 1), ("inputs", -hop)]
-    turns = []
-    for hop in range(1, half + 1):
-        turns += [("grads", hop)] + ([("grads", -hop)] if hop < half else []) + [later.pop(0)]
-    turns += later
+    turns = [("grads", 1), ("grads", -1), ("inputs", 1)]
+    for hop in range(2, chips - 2):
+        turns += [("grads", hop), ("inputs", hop)]
+    turns += [("grads", chips - 2), ("inputs", -1), ("inputs", chips - 2)]
     pres, totals, encoder_grad = {}, (), None
 
     def use(kind, hop, rows, last=False):
@@ -219,36 +236,42 @@
     returned = None
 
     def arrive(turn):
-        nonlocal returned
+        nonlocal returned, totals
         kind, hop = turns[turn]
         last = turn in (last_grads, len(turns) - 1)
-        ready = (meta,) if turn < 3 else (marks[turn - 3],)
+        if turn == last_grads:
+            returned = lax.all_to_all(totals[2], "lat", split_axis=0, concat_axis=0, tiled=True)
+            totals = totals[:2]
+        ready = (meta,) if turn < 2 else (marks[turn - 2],)
         if turn == len(turns) - 1:
             ready += (returned,)
         marks.append(use(kind, hop % chips, (arrived[turn], send(arrived[turn], swap, *ready)), last))
-        if turn == last_grads:
-            returned = lax.all_to_all(totals[2], "lat", split_axis=0, concat_axis=0, tiled=True)
 
     use("grads", 0, (grad_recon, own_grads))
     use("inputs", 0, (inputs, own_inputs))
     arrived = []
     for turn, (kind, hop) in enumerate(turns):
-        while len(marks) < (last_grads + 1 if turn >= len(turns) - EARLY else turn - LAG + 1):
+        while len(marks) < turn - LAG + 1:
             arrive(len(marks))
-        ready = () if turn < 3 else (meta,) if turn < max(LAG, 4) else (marks[-1],)
+        ready = () if turn < 3 else (meta,) if turn < LAG else (marks[-1],)
         rows = send(held[kind, hop > 0], onward if hop > 0 else backward, *ready)
         held[kind, hop > 0] = rows
         arrived.append(rows)
     while len(marks) < len(turns):
         arrive(len(marks))
-    latent_grads = pick_returned(after(returned, encoder_grad), own_t)
+    lat = totals[2]
+    sent_back = lax.ppermute(lat[0], "lat", second), lax.ppermute(lat[1], "lat", across)
+    nearest = jnp.asarray(sources)[me, 2, 0]
+    latent_grads = pick_returned(after(returned, encoder_grad), own_t, (nearest, nearest ^ 1), sent_back)
     return (totals[0], encoder_grad, totals[1].reshape(latent_count), latent_grads)
 
 
-def pick_returned(returned, own_t):
+def pick_returned(returned, own_t, more_owners=(), more=()):
     owner_id = jnp.arange(returned.shape[0], dtype=jnp.int32)[:, None, None, None]
-    picked = jnp.where(own_t[None, :, None, :] == owner_id, returned[:, None, :, :], 0.0)
-    return jnp.sum(picked, axis=0).reshape(-1, own_t.shape[1]).T
+    picked = jnp.sum(jnp.where(own_t[None, :, None, :] == owner_id, returned[:, None, :, :], 0.0), axis=0)
+    for owner, sent_back in zip(more_owners, more):
+        picked += jnp.where(own_t[:, None, :] == owner, sent_back[None], 0.0)
+    return picked.reshape(-1, own_t.shape[1]).T
 
 
 def build_kernel(block_count, per_block, me_ref, meta_ref, acts_ref, cols_ref):

time: 176 us -> 173 us (0.983)
  blocking collectives: 31.8 us -> 0 us
  waiting for transfers between devices: 61.2 us -> 87.3 us
    all_to_all x1 -> x0, blocking collectives: 31.8 us -> none  [by_ring(): meta = lax.all_to_all(meta, 'lat', split_axis=0, concat_axis=0, tiled=True)]
    all_to_all x0 -> x1, waiting for transfers between devices: none -> 16.4 us  [by_ring(): meta = lax.all_to_all(meta, 'lat', split_axis=0, concat_axis=0, tiled=True)]
    ppermute x30, waiting for transfers between devices: 60.9 us -> 70.9 us  [send(): return lax.ppermute(after(rows, *first) if first else rows, 'lat', way)]
    ppermute x30, starting transfers between devices: 17.6 us -> 9.41 us  [send(): return lax.ppermute(after(rows, *first) if first else rows, 'lat', way)]
    all_to_all x0 -> x1, starting transfers between devices: none -> 6.36 us  [by_ring(): meta = lax.all_to_all(meta, 'lat', split_axis=0, concat_axis=0, tiled=True)]
    ppermute x0 -> x2, starting transfers between devices: none -> 2.93 us  [the longest x1 2.55 us: by_ring(): lax.ppermute(lat[1], 'lat', across)]
    pallas_call x8, Pallas kernels: 26 us -> 28.3 us  [grad_step(): pl.pallas_call(functools.partial(grad_kernel, per_block), in_specs=[scala...]
    pallas_call x8, Pallas kernels: 17.7 us -> 15.6 us  [input_step(): pl.pallas_call(functools.partial(input_kernel, last), in_specs=[whole] *...]
  transfers between devices with their start and end apart: 31 -> 34, of which waited for: 8 -> 11; matrix products, arithmetic and copies ran while one was open for 0% -> 2% of each run, Pallas kernels for 23% -> 26%
where the time goes in v11:
time: 173 us; the launch traced here: 172 us
  waiting for transfers between devices  87.3 us (50%)
  Pallas kernels  44.6 us (26%)
  starting transfers between devices  22.2 us (13%)
  local copies, waits for them, and re-layouts  15.1 us (9%)
    ppermute x30, waiting for transfers between devices, send(): return lax.ppermute(after(rows, *first) if first else rows, 'lat', way)  70.9 us
    pallas_call x8, Pallas kernels, grad_step(): pl.pallas_call(functools.partial(grad_kernel, per_block), in_specs=[scala...  28.3 us
    all_to_all x1, waiting for transfers between devices, by_ring(): meta = lax.all_to_all(meta, 'lat', split_axis=0, concat_axis=0, tiled=True)  16.4 us
    pallas_call x8, Pallas kernels, input_step(): pl.pallas_call(functools.partial(input_kernel, last), in_specs=[whole] *...  15.6 us
    unnamed x28, local copies, waits for them, and re-layouts  13.2 us
    ppermute x30, starting transfers between devices, send(): return lax.ppermute(after(rows, *first) if first else rows, 'lat', way)  9.41 us
    all_to_all x1, starting transfers between devices, by_ring(): meta = lax.all_to_all(meta, 'lat', split_axis=0, concat_axis=0, tiled=True)  6.36 us
    all_to_all x1, starting transfers between devices, arrive(): lax.all_to_all(totals[2], 'lat', split_axis=0, concat_axis=0, tiled=True)  3.51 us
  transfers between devices with their start and end apart: 34, of which 11 were waited for; matrix products, arithmetic and copies ran while one was open for 2% of the time, Pallas kernels for 26%

profile of v11, /device:TPU:0, one launch (start us, length us, event | category | flops | bytes accessed | tf_op | source)
XLA Modules:
  0.0 172.1 jit_solution(4282032580511652816)
XLA Ops:
  0.6 3.1 %collective-permute-start = (bf16[128,3584]{1,0:T(8,128)(2,1)}, bf16[128,3584]{1,0:T(8,128)(2,1)S(1)}, u32[]{:S(2)}, u32[]{:S(2)}) collective-permute-start(bf16[128,3584]{1,0:T(8,128)(2,1)} %mine_ref.2), channel_id=1, source_target_pairs={{0,4},{4,8},{8,12},{12,14},{14,10},{10,6},{6,2},{2,0},{1,3},{5,1},... | collective-permute-start | bytes 2752520 | tf_op jit(solution)/shard_map/ppermute | solution.py:216
  7.3 6.4 %all-to-all-start = ((bf16[16,32,128]{2,1,0:T(8,128)(2,1)}), bf16[16,32,128]{2,1,0:T(8,128)(2,1)S(1)}, u32[]{:S(2)}, u32[]{:S(2)}) async-start(bf16[16,32,128]{2,1,0:T(8,128)(2,1)} %meta.1), calls=%async_computation | async-start | bytes 262144 | tf_op jit(solution)/shard_map/all_to_all | solution.py:167
  14.0 16.4 %all-to-all-done.meta_ref = bf16[16,32,128]{2,1,0:T(8,128)(2,1)S(1)} async-done(((bf16[16,32,128]{2,1,0:T(8,128)(2,1)}), bf16[16,32,128]{2,1,0:T(8,128)(2,1)S(1)}, u32[]{:S(2)}, u32[]{:S(2)}) %all-to-all-start) | async-done | bytes 131104 | tf_op jit(solution)/shard_map/all_to_all | solution.py:167
  31.0 1.7 %collective-permute-start.1 = (bf16[128,3584]{1,0:T(8,128)(2,1)S(1)}, bf16[128,3584]{1,0:T(8,128)(2,1)}, u32[]{:S(2)}, u32[]{:S(2)}) collective-permute-start(bf16[128,3584]{1,0:T(8,128)(2,1)S(1)} %collective-permute-done.mine_ref), channel_id=1, source_target_pairs={{0,4},{4,8},{8,12},{12,14},{14,10},{10,6},{6,2},{2,0},{1,3},{5,1},... | collective-permute-start | bytes 2752520 | tf_op jit(solution)/shard_map/ppermute | solution.py:216
  36.3 3.3 %grad_step.8 = (f32[256,3584]{1,0:T(8,128)S(1)}, f32[256,128]{1,0:T(8,128)S(1)}, f32[16,16,128]{2,1,0:T(8,128)S(1)}, bf16[256,256]{1,0:T(8,128)(2,1)S(1)}) custom-call(s32[2]{0:T(128)S(1)} %get-tuple-element.110.order_ref, bf16[16,32,128]{2,1,0:T(8,128)(2,1)S(1)} %all-to-all-done.meta_ref, bf16[256,3584]{1,0:T(8,128)(2,1)S(1)} %copy-done.6, ...), custom_call_target="tpu_custom_call" | custom-call | flops 1 | bytes 1 | tf_op jit(solution)/shard_map/grad_step/pallas_call | solution.py:175
  39.6 3.5 %grad_step.9 = (f32[256,3584]{1,0:T(8,128)S(1)}, f32[256,128]{1,0:T(8,128)S(1)}, f32[16,16,128]{2,1,0:T(8,128)S(1)}, bf16[256,256]{1,0:T(8,128)(2,1)S(1)}) custom-call(s32[2]{0:T(128)S(1)} %get-tuple-element.111.order_ref, bf16[16,32,128]{2,1,0:T(8,128)(2,1)S(1)} %all-to-all-done.meta_ref, ...), custom_call_target="tpu_custom_call", output_to_operand_aliasing={{0}: (5, {}), {1}: (6, {})} | custom-call | flops 1 | bytes 1 | tf_op jit(solution)/shard_map/grad_step/pallas_call | solution.py:175
  44.3 3.5 %grad_step.10 = (f32[256,3584]{1,0:T(8,128)S(1)}, f32[256,128]{1,0:T(8,128)S(1)}, f32[16,16,128]{2,1,0:T(8,128)S(1)}, bf16[256,256]{1,0:T(8,128)(2,1)S(1)}) custom-call(s32[2]{0:T(128)S(1)} %get-tuple-element.112.order_ref, bf16[16,32,128]{2,1,0:T(8,128)(2,1)S(1)} %all-to-all-done.meta_ref, ...), custom_call_target="tpu_custom_call", output_to_operand_aliasing={{0}: (5, {}), {1}: (6, {})} | custom-call | flops 1 | bytes 1 | tf_op jit(solution)/shard_map/grad_step/pallas_call | solution.py:175
  47.8 6.3 %collective-permute-done.1.mine_ref = bf16[128,3584]{1,0:T(8,128)(2,1)} collective-permute-done((bf16[128,3584]{1,0:T(8,128)(2,1)S(1)}, bf16[128,3584]{1,0:T(8,128)(2,1)}, u32[]{:S(2)}, u32[]{:S(2)}) %collective-permute-start.1) | collective-permute-done | bytes 917536 | tf_op jit(solution)/shard_map/ppermute | solution.py:216
  54.2 1.9 %input_step.8.refs_0_ = f32[3584,256]{1,0:T(8,128)S(1)} custom-call(bf16[256,256]{1,0:T(8,128)(2,1)S(1)} %get-tuple-element.85.pre_ref, bf16[128,3584]{1,0:T(8,128)(2,1)} %mine_ref.3, bf16[128,3584]{1,0:T(8,128)(2,1)S(1)} %collective-permute-done.18.theirs_ref), custom_call_target="tpu_custom_call" | custom-call | flops 1 | bytes 1 | tf_op jit(solution)/shard_map/input_step/pallas_call | solution.py:198
  57.5 6.4 %collective-permute-done.16.mine_ref = bf16[128,3584]{1,0:T(8,128)(2,1)S(1)} collective-permute-done((bf16[128,3584]{1,0:T(8,128)(2,1)S(1)}, bf16[128,3584]{1,0:T(8,128)(2,1)S(1)}, u32[]{:S(2)}, u32[]{:S(2)}) %collective-permute-start.16) | collective-permute-done | bytes 917536 | tf_op jit(solution)/shard_map/ppermute | solution.py:216
  63.9 3.5 %grad_step.11 = (f32[256,3584]{1,0:T(8,128)S(1)}, f32[256,128]{1,0:T(8,128)S(1)}, f32[16,16,128]{2,1,0:T(8,128)S(1)}, bf16[256,256]{1,0:T(8,128)(2,1)S(1)}) custom-call(s32[2]{0:T(128)S(1)} %get-tuple-element.109.order_ref, bf16[16,32,128]{2,1,0:T(8,128)(2,1)S(1)} %all-to-all-done.meta_ref, ...), custom_call_target="tpu_custom_call", output_to_operand_aliasing={{0}: (5, {}), {1}: (6, {})} | custom-call | flops 1 | bytes 1 | tf_op jit(solution)/shard_map/grad_step/pallas_call | solution.py:175
  67.5 6.2 %collective-permute-done.6.mine_ref = bf16[128,3584]{1,0:T(8,128)(2,1)S(1)} collective-permute-done((bf16[128,3584]{1,0:T(8,128)(2,1)}, bf16[128,3584]{1,0:T(8,128)(2,1)S(1)}, u32[]{:S(2)}, u32[]{:S(2)}) %collective-permute-start.6) | collective-permute-done | bytes 917536 | tf_op jit(solution)/shard_map/ppermute | solution.py:216
  75.1 8.4 %collective-permute-done.19.mine_ref = bf16[128,3584]{1,0:T(8,128)(2,1)S(1)} collective-permute-done((bf16[128,3584]{1,0:T(8,128)(2,1)S(1)}, bf16[128,3584]{1,0:T(8,128)(2,1)S(1)}, u32[]{:S(2)}, u32[]{:S(2)}) %collective-permute-start.19) | collective-permute-done | bytes 917536 | tf_op jit(solution)/shard_map/ppermute | solution.py:216
  83.6 2.9 %grad_step.12 = (f32[256,3584]{1,0:T(8,128)S(1)}, f32[256,128]{1,0:T(8,128)S(1)}, f32[16,16,128]{2,1,0:T(8,128)S(1)}, bf16[256,256]{1,0:T(8,128)(2,1)S(1)}) custom-call(s32[2]{0:T(128)S(1)} %get-tuple-element.108.order_ref, bf16[16,32,128]{2,1,0:T(8,128)(2,1)S(1)} %all-to-all-done.meta_ref, ...), custom_call_target="tpu_custom_call", output_to_operand_aliasing={{0}: (5, {}), {1}: (6, {})} | custom-call | flops 1 | bytes 1 | tf_op jit(solution)/shard_map/grad_step/pallas_call | solution.py:175
  86.5 6.8 %collective-permute-done.8.mine_ref = bf16[128,3584]{1,0:T(8,128)(2,1)S(1)} collective-permute-done((bf16[128,3584]{1,0:T(8,128)(2,1)S(1)}, bf16[128,3584]{1,0:T(8,128)(2,1)S(1)}, u32[]{:S(2)}, u32[]{:S(2)}) %collective-permute-start.8) | collective-permute-done | bytes 917536 | tf_op jit(solution)/shard_map/ppermute | solution.py:216
  94.8 8.4 %collective-permute-done.21.mine_ref = bf16[128,3584]{1,0:T(8,128)(2,1)S(1)} collective-permute-done((bf16[128,3584]{1,0:T(8,128)(2,1)S(1)}, bf16[128,3584]{1,0:T(8,128)(2,1)S(1)}, u32[]{:S(2)}, u32[]{:S(2)}) %collective-permute-start.21) | collective-permute-done | bytes 917536 | tf_op jit(solution)/shard_map/ppermute | solution.py:216
  103.3 2.9 %grad_step.13 = (f32[256,3584]{1,0:T(8,128)S(1)}, f32[256,128]{1,0:T(8,128)S(1)}, f32[16,16,128]{2,1,0:T(8,128)S(1)}, bf16[256,256]{1,0:T(8,128)(2,1)S(1)}) custom-call(s32[2]{0:T(128)S(1)} %get-tuple-element.107.order_ref, bf16[16,32,128]{2,1,0:T(8,128)(2,1)S(1)} %all-to-all-done.meta_ref, ...), custom_call_target="tpu_custom_call", output_to_operand_aliasing={{0}: (5, {}), {1}: (6, {})} | custom-call | flops 1 | bytes 1 | tf_op jit(solution)/shard_map/grad_step/pallas_call | solution.py:175
  106.2 6.8 %collective-permute-done.10.mine_ref = bf16[128,3584]{1,0:T(8,128)(2,1)S(1)} collective-permute-done((bf16[128,3584]{1,0:T(8,128)(2,1)S(1)}, bf16[128,3584]{1,0:T(8,128)(2,1)S(1)}, u32[]{:S(2)}, u32[]{:S(2)}) %collective-permute-start.10) | collective-permute-done | bytes 917536 | tf_op jit(solution)/shard_map/ppermute | solution.py:216
  114.5 2.2 %collective-permute-start.27 = (bf16[128,3584]{1,0:T(8,128)(2,1)}, bf16[128,3584]{1,0:T(8,128)(2,1)S(1)}, u32[]{:S(2)}, u32[]{:S(2)}) collective-permute-start(bf16[128,3584]{1,0:T(8,128)(2,1)} %mine_ref.3), channel_id=1, source_target_pairs={{4,0},{8,4},{12,8},{14,12},{10,14},{6,10},{2,6},{0,2},{3,1},{1,5},... | collective-permute-start | bytes 2752520 | tf_op jit(solution)/shard_map/ppermute | solution.py:216
  116.7 11.0 %collective-permute-done.23.mine_ref = bf16[128,3584]{1,0:T(8,128)(2,1)} collective-permute-done((bf16[128,3584]{1,0:T(8,128)(2,1)S(1)}, bf16[128,3584]{1,0:T(8,128)(2,1)}, u32[]{:S(2)}, u32[]{:S(2)}) %collective-permute-start.23) | collective-permute-done | bytes 917536 | tf_op jit(solution)/shard_map/ppermute | solution.py:216
  127.7 3.6 %grad_step.14 = (f32[256,3584]{1,0:T(8,128)S(1)}, f32[256,128]{1,0:T(8,128)S(1)}, f32[16,16,128]{2,1,0:T(8,128)}, bf16[256,256]{1,0:T(8,128)(2,1)S(1)}) custom-call(s32[2]{0:T(128)S(1)} %get-tuple-element.106.order_ref, bf16[16,32,128]{2,1,0:T(8,128)(2,1)S(1)} %all-to-all-done.meta_ref, ...), custom_call_target="tpu_custom_call", output_to_operand_aliasing={{0}: (5, {}), {1}: (6, {})} | custom-call | flops 1 | bytes 1 | tf_op jit(solution)/shard_map/grad_step/pallas_call | solution.py:175
  131.3 1.8 %copy-done.4 = f32[256,3584]{1,0:T(8,128)} copy-done((f32[256,3584]{1,0:T(8,128)}, f32[256,3584]{1,0:T(8,128)S(1)}, u32[]{:S(2)}) %copy-start.4) | copy-done | bytes 3670040
  133.1 9.5 %collective-permute-done.12.mine_ref = bf16[128,3584]{1,0:T(8,128)(2,1)} collective-permute-done((bf16[128,3584]{1,0:T(8,128)(2,1)S(1)}, bf16[128,3584]{1,0:T(8,128)(2,1)}, u32[]{:S(2)}, u32[]{:S(2)}) %collective-permute-start.12) | collective-permute-done | bytes 917536 | tf_op jit(solution)/shard_map/ppermute | solution.py:216
  142.7 3.5 %all-to-all-start.1 = ((f32[16,16,128]{2,1,0:T(8,128)}), f32[16,16,128]{2,1,0:T(8,128)S(1)}, u32[]{:S(2)}, u32[]{:S(2)}) async-start(f32[16,16,128]{2,1,0:T(8,128)} %get-tuple-element.94), calls=%async_computation.1 | async-start | bytes 262144 | tf_op jit(solution)/shard_map/all_to_all | solution.py:243
  146.2 2.0 %copy-done.1 = f32[3584,256]{1,0:T(8,128)S(1)} copy-done((f32[3584,256]{1,0:T(8,128)S(1)}, f32[3584,256]{1,0:T(8,128)}, u32[]{:S(2)}) %copy-start.1) | copy-done | bytes 3670040
  148.3 2.9 %input_step.13.refs_0_ = f32[3584,256]{1,0:T(8,128)S(1)} custom-call(bf16[256,256]{1,0:T(8,128)(2,1)S(1)} %get-tuple-element.99.pre_ref, bf16[128,3584]{1,0:T(8,128)(2,1)} %collective-permute-done.23.mine_ref, bf16[128,3584]{1,0:T(8,128)(2,1)} %collective-permute-done.28.theirs_ref, f32[3584,256]{1,0:T(8,128)S(1)} %copy-done.1), custom_call_target="tpu_custom_call", output_to_operand_aliasing={{}: (3, {})} | custom-call | flops 1 | bytes 1 | tf_op jit(solution)/shard_map/input_step/pallas_call | solution.py:198
  151.2 1.8 %copy-done.2 = f32[3584,256]{1,0:T(8,128)} copy-done((f32[3584,256]{1,0:T(8,128)}, f32[3584,256]{1,0:T(8,128)S(1)}, u32[]{:S(2)}) %copy-start.2) | copy-done | bytes 3670040
  153.3 5.0 %grad_step.15 = (bf16[256,3584]{1,0:T(8,128)(2,1)}, f32[1,256]{1,0:T(1,128)}, f32[2,16,128]{2,1,0:T(8,128)S(1)}, bf16[256,256]{1,0:T(8,128)(2,1)S(1)}) custom-call(s32[2]{0:T(128)S(1)} %get-tuple-element.113.order_ref, bf16[16,32,128]{2,1,0:T(8,128)(2,1)S(1)} %all-to-all-done.meta_ref, bf16[256,3584]{1,0:T(8,128)(2,1)S(1)} %copy-done.7, ...), custom_call_target="tpu_custom_call" | custom-call | flops 1 | bytes 1 | tf_op jit(solution)/shard_map/grad_step/pallas_call | solution.py:175
  161.1 2.6 %collective-permute-start.31 = (f32[16,128]{1,0:T(8,128)S(1)}, f32[16,128]{1,0:T(8,128)S(1)}, u32[]{:S(2)}, u32[]{:S(2)}) collective-permute-start(f32[16,128]{1,0:T(8,128)S(1)} %get-tuple-element.105), channel_id=1, source_target_pairs={{8,1},{12,5},{14,9},{10,13},{6,15},{2,11},{0,7},{4,3},{7,0},{3,4},... | collective-permute-start | bytes 24584 | tf_op jit(solution)/shard_map/ppermute | solution.py:263
  164.0 2.0 %copy-done.3 = f32[3584,256]{1,0:T(8,128)S(1)} copy-done((f32[3584,256]{1,0:T(8,128)S(1)}, f32[3584,256]{1,0:T(8,128)}, u32[]{:S(2)}) %copy-start.3) | copy-done | bytes 3670040
  166.1 2.5 %input_step.14.refs_0_ = f32[3584,256]{1,0:T(8,128)S(1)} custom-call(bf16[256,256]{1,0:T(8,128)(2,1)S(1)} %get-tuple-element.96.pre_ref, bf16[128,3584]{1,0:T(8,128)(2,1)S(1)} %collective-permute-done.27.mine_ref, bf16[128,3584]{1,0:T(8,128)(2,1)} %collective-permute-done.29.theirs_ref, f32[3584,256]{1,0:T(8,128)S(1)} %copy-done.3), custom_call_target="tpu_custom_call", output_to_operand_aliasing={{}: (3, {})} | custom-call | flops 1 | bytes 1 | tf_op jit(solution)/shard_map/input_step/pallas_call | solution.py:198
  168.6 2.8 %input_step.15 = bf16[3584,256]{1,0:T(8,128)(2,1)} custom-call(bf16[256,256]{1,0:T(8,128)(2,1)S(1)} %get-tuple-element.82.pre_ref, bf16[128,3584]{1,0:T(8,128)(2,1)} %collective-permute-done.24.mine_ref, bf16[128,3584]{1,0:T(8,128)(2,1)S(1)} %collective-permute-done.25.theirs_ref, f32[3584,256]{1,0:T(8,128)S(1)} %input_step.14.refs_0_), custom_call_target="tpu_custom_call" | custom-call | flops 1 | bytes 1 | tf_op jit(solution)/shard_map/input_step/pallas_call | solution.py:198
  (89 shorter events, 18.9 us)
Async XLA Ops:
  0.6 29.8 %collective-permute-start = (bf16[128,3584]{1,0:T(8,128)(2,1)}, bf16[128,3584]{1,0:T(8,128)(2,1)S(1)}, u32[]{:S(2)}, u32[]{:S(2)}) collective-permute-start(bf16[128,3584]{1,0:T(8,128)(2,1)} %mine_ref.2), channel_id=1, source_target_pairs={{0,4},{4,8},{8,12},{12,14},{14,10},{10,6},{6,2},{2,0},{1,3},{5,1},... | collective-permute-start | bytes 2752520 | tf_op jit(solution)/shard_map/ppermute | solution.py:216
  3.7 27.0 %collective-permute-start.2 = (bf16[128,3584]{1,0:T(8,128)(2,1)}, bf16[128,3584]{1,0:T(8,128)(2,1)S(1)}, u32[]{:S(2)}, u32[]{:S(2)}) collective-permute-start(bf16[128,3584]{1,0:T(8,128)(2,1)} %mine_ref.2), channel_id=1, source_target_pairs={{4,0},{8,4},{12,8},{14,12},{10,14},{6,10},{2,6},{0,2},{3,1},{1,5},... | collective-permute-start | bytes 2752520 | tf_op jit(solution)/shard_map/ppermute | solution.py:216
  7.3 23.2 %all-to-all-start = ((bf16[16,32,128]{2,1,0:T(8,128)(2,1)}), bf16[16,32,128]{2,1,0:T(8,128)(2,1)S(1)}, u32[]{:S(2)}, u32[]{:S(2)}) async-start(bf16[16,32,128]{2,1,0:T(8,128)(2,1)} %meta.1), calls=%async_computation | async-start | bytes 262144 | tf_op jit(solution)/shard_map/all_to_all | solution.py:167
  13.6 19.8 %collective-permute-start.5 = (bf16[128,3584]{1,0:T(8,128)(2,1)}, bf16[128,3584]{1,0:T(8,128)(2,1)}, u32[]{:S(2)}, u32[]{:S(2)}) collective-permute-start(bf16[128,3584]{1,0:T(8,128)(2,1)} %mine_ref.2), channel_id=1, source_target_pairs={{0,1},{1,0},{2,3},{3,2},{4,5},{5,4},{6,7},{7,6},{8,9},{9,8},{10,11... | collective-permute-start | bytes 2752520 | tf_op jit(solution)/shard_map/ppermute | solution.py:216
  30.6 13.6 %collective-permute-start.15 = (bf16[128,3584]{1,0:T(8,128)(2,1)}, bf16[128,3584]{1,0:T(8,128)(2,1)S(1)}, u32[]{:S(2)}, u32[]{:S(2)}) collective-permute-start(bf16[128,3584]{1,0:T(8,128)(2,1)} %mine_ref.3), channel_id=1, source_target_pairs={{0,4},{4,8},{8,12},{12,14},{14,10},{10,6},{6,2},{2,0},{1,3},{5,1},... | collective-permute-start | bytes 2752520 | tf_op jit(solution)/shard_map/ppermute | solution.py:216
  30.7 13.6 %collective-permute-start.3 = (bf16[128,3584]{1,0:T(8,128)(2,1)S(1)}, bf16[128,3584]{1,0:T(8,128)(2,1)}, u32[]{:S(2)}, u32[]{:S(2)}) collective-permute-start(bf16[128,3584]{1,0:T(8,128)(2,1)S(1)} %collective-permute-done.2.mine_ref), channel_id=1, source_target_pairs={{0,1},{1,0},{2,3},{3,2},{4,5},{5,4},{6,7},{7,6},{8,9},{9,8},{10,11... | collective-permute-start | bytes 2752520 | tf_op jit(solution)/shard_map/ppermute | solution.py:216
  31.0 23.1 %collective-permute-start.1 = (bf16[128,3584]{1,0:T(8,128)(2,1)S(1)}, bf16[128,3584]{1,0:T(8,128)(2,1)}, u32[]{:S(2)}, u32[]{:S(2)}) collective-permute-start(bf16[128,3584]{1,0:T(8,128)(2,1)S(1)} %collective-permute-done.mine_ref), channel_id=1, source_target_pairs={{0,4},{4,8},{8,12},{12,14},{14,10},{10,6},{6,2},{2,0},{1,3},{5,1},... | collective-permute-start | bytes 2752520 | tf_op jit(solution)/shard_map/ppermute | solution.py:216
  33.4 20.8 %collective-permute-start.18 = (bf16[128,3584]{1,0:T(8,128)(2,1)}, bf16[128,3584]{1,0:T(8,128)(2,1)S(1)}, u32[]{:S(2)}, u32[]{:S(2)}) collective-permute-start(bf16[128,3584]{1,0:T(8,128)(2,1)} %mine_ref.3), channel_id=1, source_target_pairs={{0,1},{1,0},{2,3},{3,2},{4,5},{5,4},{6,7},{7,6},{8,9},{9,8},{10,11... | collective-permute-start | bytes 2752520 | tf_op jit(solution)/shard_map/ppermute | solution.py:216
  44.2 19.7 %collective-permute-start.16 = (bf16[128,3584]{1,0:T(8,128)(2,1)S(1)}, bf16[128,3584]{1,0:T(8,128)(2,1)S(1)}, u32[]{:S(2)}, u32[]{:S(2)}) collective-permute-start(bf16[128,3584]{1,0:T(8,128)(2,1)S(1)} %collective-permute-done.15.mine_ref), channel_id=1, source_target_pairs={{0,4},{4,8},{8,12},{12,14},{14,10},{10,6},{6,2},{2,0},{1,3},{5,1},... | collective-permute-start | bytes 2752520 | tf_op jit(solution)/shard_map/ppermute | solution.py:216
  44.3 11.8 %collective-permute-start.17 = (bf16[128,3584]{1,0:T(8,128)(2,1)S(1)}, bf16[128,3584]{1,0:T(8,128)(2,1)S(1)}, u32[]{:S(2)}, u32[]{:S(2)}) collective-permute-start(bf16[128,3584]{1,0:T(8,128)(2,1)S(1)} %collective-permute-done.15.mine_ref), channel_id=1, source_target_pairs={{0,1},{1,0},{2,3},{3,2},{4,5},{5,4},{6,7},{7,6},{8,9},{9,8},{10,11... | collective-permute-start | bytes 2752520 | tf_op jit(solution)/shard_map/ppermute | solution.py:216
  54.1 9.8 %collective-permute-start.7 = (bf16[128,3584]{1,0:T(8,128)(2,1)}, bf16[128,3584]{1,0:T(8,128)(2,1)S(1)}, u32[]{:S(2)}, u32[]{:S(2)}) collective-permute-start(bf16[128,3584]{1,0:T(8,128)(2,1)} %collective-permute-done.1.mine_ref), channel_id=1, source_target_pairs={{0,1},{1,0},{2,3},{3,2},{4,5},{5,4},{6,7},{7,6},{8,9},{9,8},{10,11... | collective-permute-start | bytes 2752520 | tf_op jit(solution)/shard_map/ppermute | solution.py:216
  54.1 19.6 %collective-permute-start.6 = (bf16[128,3584]{1,0:T(8,128)(2,1)}, bf16[128,3584]{1,0:T(8,128)(2,1)S(1)}, u32[]{:S(2)}, u32[]{:S(2)}) collective-permute-start(bf16[128,3584]{1,0:T(8,128)(2,1)} %collective-permute-done.1.mine_ref), channel_id=1, source_target_pairs={{0,4},{4,8},{8,12},{12,14},{14,10},{10,6},{6,2},{2,0},{1,3},{5,1},... | collective-permute-start | bytes 2752520 | tf_op jit(solution)/shard_map/ppermute | solution.py:216
  63.8 19.7 %collective-permute-start.19 = (bf16[128,3584]{1,0:T(8,128)(2,1)S(1)}, bf16[128,3584]{1,0:T(8,128)(2,1)S(1)}, u32[]{:S(2)}, u32[]{:S(2)}) collective-permute-start(bf16[128,3584]{1,0:T(8,128)(2,1)S(1)} %collective-permute-done.16.mine_ref), channel_id=1, source_target_pairs={{0,4},{4,8},{8,12},{12,14},{14,10},{10,6},{6,2},{2,0},{1,3},{5,1},... | collective-permute-start | bytes 2752520 | tf_op jit(solution)/shard_map/ppermute | solution.py:216
  63.9 9.8 %collective-permute-start.20 = (bf16[128,3584]{1,0:T(8,128)(2,1)S(1)}, bf16[128,3584]{1,0:T(8,128)(2,1)S(1)}, u32[]{:S(2)}, u32[]{:S(2)}) collective-permute-start(bf16[128,3584]{1,0:T(8,128)(2,1)S(1)} %collective-permute-done.16.mine_ref), channel_id=1, source_target_pairs={{0,1},{1,0},{2,3},{3,2},{4,5},{5,4},{6,7},{7,6},{8,9},{9,8},{10,11... | collective-permute-start | bytes 2752520 | tf_op jit(solution)/shard_map/ppermute | solution.py:216
  73.7 9.9 %collective-permute-start.9 = (bf16[128,3584]{1,0:T(8,128)(2,1)S(1)}, bf16[128,3584]{1,0:T(8,128)(2,1)S(1)}, u32[]{:S(2)}, u32[]{:S(2)}) collective-permute-start(bf16[128,3584]{1,0:T(8,128)(2,1)S(1)} %collective-permute-done.6.mine_ref), channel_id=1, source_target_pairs={{0,1},{1,0},{2,3},{3,2},{4,5},{5,4},{6,7},{7,6},{8,9},{9,8},{10,11... | collective-permute-start | bytes 2752520 | tf_op jit(solution)/shard_map/ppermute | solution.py:216
  73.7 19.7 %collective-permute-start.8 = (bf16[128,3584]{1,0:T(8,128)(2,1)S(1)}, bf16[128,3584]{1,0:T(8,128)(2,1)S(1)}, u32[]{:S(2)}, u32[]{:S(2)}) collective-permute-start(bf16[128,3584]{1,0:T(8,128)(2,1)S(1)} %collective-permute-done.6.mine_ref), channel_id=1, source_target_pairs={{0,4},{4,8},{8,12},{12,14},{14,10},{10,6},{6,2},{2,0},{1,3},{5,1},... | collective-permute-start | bytes 2752520 | tf_op jit(solution)/shard_map/ppermute | solution.py:216
  83.5 19.7 %collective-permute-start.21 = (bf16[128,3584]{1,0:T(8,128)(2,1)S(1)}, bf16[128,3584]{1,0:T(8,128)(2,1)S(1)}, u32[]{:S(2)}, u32[]{:S(2)}) collective-permute-start(bf16[128,3584]{1,0:T(8,128)(2,1)S(1)} %collective-permute-done.19.mine_ref), channel_id=1, source_target_pairs={{0,4},{4,8},{8,12},{12,14},{14,10},{10,6},{6,2},{2,0},{1,3},{5,1},... | collective-permute-start | bytes 2752520 | tf_op jit(solution)/shard_map/ppermute | solution.py:216
  83.6 9.8 %collective-permute-start.22 = (bf16[128,3584]{1,0:T(8,128)(2,1)S(1)}, bf16[128,3584]{1,0:T(8,128)(2,1)S(1)}, u32[]{:S(2)}, u32[]{:S(2)}) collective-permute-start(bf16[128,3584]{1,0:T(8,128)(2,1)S(1)} %collective-permute-done.19.mine_ref), channel_id=1, source_target_pairs={{0,1},{1,0},{2,3},{3,2},{4,5},{5,4},{6,7},{7,6},{8,9},{9,8},{10,11... | collective-permute-start | bytes 2752520 | tf_op jit(solution)/shard_map/ppermute | solution.py:216
  93.3 9.9 %collective-permute-start.11 = (bf16[128,3584]{1,0:T(8,128)(2,1)S(1)}, bf16[128,3584]{1,0:T(8,128)(2,1)S(1)}, u32[]{:S(2)}, u32[]{:S(2)}) collective-permute-start(bf16[128,3584]{1,0:T(8,128)(2,1)S(1)} %collective-permute-done.8.mine_ref), channel_id=1, source_target_pairs={{0,1},{1,0},{2,3},{3,2},{4,5},{5,4},{6,7},{7,6},{8,9},{9,8},{10,11... | collective-permute-start | bytes 2752520 | tf_op jit(solution)/shard_map/ppermute | solution.py:216
  93.3 19.7 %collective-permute-start.10 = (bf16[128,3584]{1,0:T(8,128)(2,1)S(1)}, bf16[128,3584]{1,0:T(8,128)(2,1)S(1)}, u32[]{:S(2)}, u32[]{:S(2)}) collective-permute-start(bf16[128,3584]{1,0:T(8,128)(2,1)S(1)} %collective-permute-done.8.mine_ref), channel_id=1, source_target_pairs={{0,4},{4,8},{8,12},{12,14},{14,10},{10,6},{6,2},{2,0},{1,3},{5,1},... | collective-permute-start | bytes 2752520 | tf_op jit(solution)/shard_map/ppermute | solution.py:216
  103.2 9.9 %collective-permute-start.26 = (bf16[128,3584]{1,0:T(8,128)(2,1)S(1)}, bf16[128,3584]{1,0:T(8,128)(2,1)S(1)}, u32[]{:S(2)}, u32[]{:S(2)}) collective-permute-start(bf16[128,3584]{1,0:T(8,128)(2,1)S(1)} %collective-permute-done.21.mine_ref), channel_id=1, source_target_pairs={{0,1},{1,0},{2,3},{3,2},{4,5},{5,4},{6,7},{7,6},{8,9},{9,8},{10,11... | collective-permute-start | bytes 2752520 | tf_op jit(solution)/shard_map/ppermute | solution.py:216
  103.2 24.5 %collective-permute-start.23 = (bf16[128,3584]{1,0:T(8,128)(2,1)S(1)}, bf16[128,3584]{1,0:T(8,128)(2,1)}, u32[]{:S(2)}, u32[]{:S(2)}) collective-permute-start(bf16[128,3584]{1,0:T(8,128)(2,1)S(1)} %collective-permute-done.21.mine_ref), channel_id=1, source_target_pairs={{0,4},{4,8},{8,12},{12,14},{14,10},{10,6},{6,2},{2,0},{1,3},{5,1},... | collective-permute-start | bytes 2752520 | tf_op jit(solution)/shard_map/ppermute | solution.py:216
  113.0 14.7 %collective-permute-start.13 = (bf16[128,3584]{1,0:T(8,128)(2,1)S(1)}, bf16[128,3584]{1,0:T(8,128)(2,1)S(1)}, u32[]{:S(2)}, u32[]{:S(2)}) collective-permute-start(bf16[128,3584]{1,0:T(8,128)(2,1)S(1)} %collective-permute-done.10.mine_ref), channel_id=1, source_target_pairs={{0,1},{1,0},{2,3},{3,2},{4,5},{5,4},{6,7},{7,6},{8,9},{9,8},{10,11... | collective-permute-start | bytes 2752520 | tf_op jit(solution)/shard_map/ppermute | solution.py:216
  113.0 29.6 %collective-permute-start.12 = (bf16[128,3584]{1,0:T(8,128)(2,1)S(1)}, bf16[128,3584]{1,0:T(8,128)(2,1)}, u32[]{:S(2)}, u32[]{:S(2)}) collective-permute-start(bf16[128,3584]{1,0:T(8,128)(2,1)S(1)} %collective-permute-done.10.mine_ref), channel_id=1, source_target_pairs={{0,4},{4,8},{8,12},{12,14},{14,10},{10,6},{6,2},{2,0},{1,3},{5,1},... | collective-permute-start | bytes 2752520 | tf_op jit(solution)/shard_map/ppermute | solution.py:216
  114.5 38.5 %collective-permute-start.27 = (bf16[128,3584]{1,0:T(8,128)(2,1)}, bf16[128,3584]{1,0:T(8,128)(2,1)S(1)}, u32[]{:S(2)}, u32[]{:S(2)}) collective-permute-start(bf16[128,3584]{1,0:T(8,128)(2,1)} %mine_ref.3), channel_id=1, source_target_pairs={{4,0},{8,4},{12,8},{14,12},{10,14},{6,10},{2,6},{0,2},{3,1},{1,5},... | collective-permute-start | bytes 2752520 | tf_op jit(solution)/shard_map/ppermute | solution.py:216
  127.7 18.5 %collective-permute-start.28 = (bf16[128,3584]{1,0:T(8,128)(2,1)}, bf16[128,3584]{1,0:T(8,128)(2,1)}, u32[]{:S(2)}, u32[]{:S(2)}) collective-permute-start(bf16[128,3584]{1,0:T(8,128)(2,1)} %collective-permute-done.23.mine_ref), channel_id=1, source_target_pairs={{0,1},{1,0},{2,3},{3,2},{4,5},{5,4},{6,7},{7,6},{8,9},{9,8},{10,11... | collective-permute-start | bytes 2752520 | tf_op jit(solution)/shard_map/ppermute | solution.py:216
  142.6 10.7 %collective-permute-start.14 = (bf16[128,3584]{1,0:T(8,128)(2,1)}, bf16[128,3584]{1,0:T(8,128)(2,1)}, u32[]{:S(2)}, u32[]{:S(2)}) collective-permute-start(bf16[128,3584]{1,0:T(8,128)(2,1)} %collective-permute-done.12.mine_ref), channel_id=1, source_target_pairs={{0,1},{1,0},{2,3},{3,2},{4,5},{5,4},{6,7},{7,6},{8,9},{9,8},{10,11... | collective-permute-start | bytes 2752520 | tf_op jit(solution)/shard_map/ppermute | solution.py:216
  142.6 15.7 %collective-permute-start.24 = (bf16[128,3584]{1,0:T(8,128)(2,1)}, bf16[128,3584]{1,0:T(8,128)(2,1)}, u32[]{:S(2)}, u32[]{:S(2)}) collective-permute-start(bf16[128,3584]{1,0:T(8,128)(2,1)} %collective-permute-done.23.mine_ref), channel_id=1, source_target_pairs={{0,4},{4,8},{8,12},{12,14},{14,10},{10,6},{6,2},{2,0},{1,3},{5,1},... | collective-permute-start | bytes 2752520 | tf_op jit(solution)/shard_map/ppermute | solution.py:216
  142.7 15.6 %all-to-all-start.1 = ((f32[16,16,128]{2,1,0:T(8,128)}), f32[16,16,128]{2,1,0:T(8,128)S(1)}, u32[]{:S(2)}, u32[]{:S(2)}) async-start(f32[16,16,128]{2,1,0:T(8,128)} %get-tuple-element.94), calls=%async_computation.1 | async-start | bytes 262144 | tf_op jit(solution)/shard_map/all_to_all | solution.py:243
  153.0 11.1 %collective-permute-start.29 = (bf16[128,3584]{1,0:T(8,128)(2,1)S(1)}, bf16[128,3584]{1,0:T(8,128)(2,1)}, u32[]{:S(2)}, u32[]{:S(2)}) collective-permute-start(bf16[128,3584]{1,0:T(8,128)(2,1)S(1)} %collective-permute-done.27.mine_ref), channel_id=1, source_target_pairs={{0,1},{1,0},{2,3},{3,2},{4,5},{5,4},{6,7},{7,6},{8,9},{9,8},{10,11... | collective-permute-start | bytes 2752520 | tf_op jit(solution)/shard_map/ppermute | solution.py:216
  158.3 10.3 %collective-permute-start.25 = (bf16[128,3584]{1,0:T(8,128)(2,1)}, bf16[128,3584]{1,0:T(8,128)(2,1)S(1)}, u32[]{:S(2)}, u32[]{:S(2)}) collective-permute-start(bf16[128,3584]{1,0:T(8,128)(2,1)} %collective-permute-done.24.mine_ref), channel_id=1, source_target_pairs={{0,1},{1,0},{2,3},{3,2},{4,5},{5,4},{6,7},{7,6},{8,9},{9,8},{10,11... | collective-permute-start | bytes 2752520 | tf_op jit(solution)/shard_map/ppermute | solution.py:216
  161.1 10.4 %collective-permute-start.31 = (f32[16,128]{1,0:T(8,128)S(1)}, f32[16,128]{1,0:T(8,128)S(1)}, u32[]{:S(2)}, u32[]{:S(2)}) collective-permute-start(f32[16,128]{1,0:T(8,128)S(1)} %get-tuple-element.105), channel_id=1, source_target_pairs={{8,1},{12,5},{14,9},{10,13},{6,15},{2,11},{0,7},{4,3},{7,0},{3,4},... | collective-permute-start | bytes 24584 | tf_op jit(solution)/shard_map/ppermute | solution.py:263
  (16 other events, 66.9 us)

commit v12 on v6

--- a/solution.py
+++ b/solution.py
@@ -34,7 +34,14 @@
     return sources, onward, backward, swap
 
 
-def meta_kernel(owners_ref, blocks_ref, offsets_ref, values_ref, meta_ref):
+def meta_kernel(*refs):
+    sources, meta_ref, held, sems = refs[:4], refs[4], refs[5:9], refs[9]
+    copies = [pltpu.make_async_copy(source, kept, sems.at[i]) for i, (source, kept) in enumerate(zip(sources, held))]
+    for copy in copies:
+        copy.start()
+    for copy in copies:
+        copy.wait()
+    owners_ref, blocks_ref, offsets_ref, values_ref = held
     count, per_block, tokens = offsets_ref.shape
     columns = [
         (jnp.broadcast_to(blocks_ref[i : i + 1, :], (per_block, tokens)) * BLOCK + offsets_ref[i]).astype(jnp.float32)
@@ -115,6 +122,25 @@
         total_ref[at : at + span, :] = term.astype(total_ref.dtype)
 
 
+def last_input_kernel(pre_ref, mine_ref, theirs_ref, part_ref, total_ref, out_ref, held_ref, made_ref, in_sems, out_sems):
+    width = mine_ref.shape[1]
+    span = column_span(width)
+    parts = [pl.ds(at, span) for at in range(0, width, span)]
+    copies_in = [pltpu.make_async_copy(total_ref.at[p], held_ref.at[p], in_sems.at[i]) for i, p in enumerate(parts)]
+    copies_out = [pltpu.make_async_copy(made_ref.at[p], out_ref.at[p], out_sems.at[i]) for i, p in enumerate(parts)]
+    for copy in copies_in:
+        copy.start()
+    for i, at in enumerate(range(0, width, span)):
+        rows = jnp.concatenate([mine_ref[:, at : at + span], theirs_ref[:, at : at + span]], axis=0)
+        term = lax.dot_general(rows, pre_ref[...], (((0,), (1,)), ((), ())), preferred_element_type=jnp.float32)
+        term += part_ref[at : at + span, :]
+        copies_in[i].wait()
+        made_ref[at : at + span, :] = (term + held_ref[at : at + span, :]).astype(made_ref.dtype)
+        copies_out[i].start()
+    for copy in copies_out:
+        copy.wait()
+
+
 def column_span(width):
     return 512 if width % 512 == 0 else BLOCK
 
@@ -140,15 +166,17 @@
     light = pl.CostEstimate(flops=1, bytes_accessed=1, transcendentals=0)
     params = pltpu.CompilerParams(vmem_limit_bytes=VMEM_BYTES)
 
+    entries = (own_t, local_blocks.T, offsets.transpose(1, 2, 0), act_values.transpose(1, 2, 0))
     meta = pl.pallas_call(
         meta_kernel,
-        in_specs=[whole] * 4,
+        in_specs=[pl.BlockSpec(memory_space=pltpu.HBM)] * 4,
         out_specs=whole,
         out_shape=jax.ShapeDtypeStruct((peer_count, 2 * per_block, token_count), jnp.bfloat16),
+        scratch_shapes=[pltpu.VMEM(array.shape, array.dtype) for array in entries] + [pltpu.SemaphoreType.DMA((4,))],
         compiler_params=params,
         cost_estimate=light,
         name="meta",
-    )(own_t, local_blocks.T, offsets.transpose(1, 2, 0), act_values.transpose(1, 2, 0))
+    )(*[pltpu.with_memory_space_constraint(array, pltpu.HBM) for array in entries])
     meta = lax.all_to_all(meta, "lat", split_axis=0, concat_axis=0, tiled=True)
 
     def near(value):
@@ -176,19 +204,38 @@
             name="grad_step",
         )(order[hop], near(meta), near(decoder), near(rows[0]), near(rows[1]), *map(near, totals))
 
-    def input_step(pre, rows, total, last):
+    def input_step(pre, rows, total):
         sums = (width, latent_count)
         totals = () if total is None else (total,)
         return pl.pallas_call(
             input_kernel,
             in_specs=[whole] * (3 + len(totals)),
             out_specs=whole,
-            out_shape=jax.ShapeDtypeStruct(sums, jnp.bfloat16) if last else pltpu.VMEM(sums, jnp.float32),
-            input_output_aliases={3: 0} if totals and not last else {},
+            out_shape=pltpu.VMEM(sums, jnp.float32),
+            input_output_aliases={3: 0} if totals else {},
             compiler_params=params,
             cost_estimate=light,
             name="input_step",
         )(near(pre), near(rows[0]), near(rows[1]), *map(near, totals))
+
+    def last_input_step(pre, rows, part, total):
+        sums, far = (width, latent_count), pl.BlockSpec(memory_space=pltpu.HBM)
+        count = width // column_span(width)
+        return pl.pallas_call(
+            last_input_kernel,
+            in_specs=[whole] * 4 + [far],
+            out_specs=far,
+            out_shape=jax.ShapeDtypeStruct(sums, jnp.bfloat16),
+            scratch_shapes=[
+                pltpu.VMEM(sums, jnp.float32),
+                pltpu.VMEM(sums, jnp.bfloat16),
+                pltpu.SemaphoreType.DMA((count,)),
+                pltpu.SemaphoreType.DMA((count,)),
+            ],
+            compiler_params=params,
+            cost_estimate=light,
+            name="last_input_step",
+        )(near(pre), near(rows[0]), near(rows[1]), near(part), pltpu.with_memory_space_constraint(total, pltpu.HBM))
 
     def send(rows, way, *first):
         return lax.ppermute(after(rows, *first) if first else rows, "lat", way)
@@ -203,12 +250,20 @@
     turns += later
     pres, totals, encoder_grad = {}, (), None
 
-    def use(kind, hop, rows, last=False):
-        nonlocal totals, encoder_grad
+    encoder_part = None
+
+    def use(kind, hop, rows, left=len(turns)):
+        nonlocal totals, encoder_grad, encoder_part
         if kind == "grads":
-            *totals, pres[hop] = grad_step(hop, rows, totals, last)
+            *totals, pres[hop] = grad_step(hop, rows, totals, left == 0)
             return totals[1]
-        encoder_grad = input_step(pres[hop], rows, encoder_grad, last)
+        if left == 0:
+            encoder_grad = last_input_step(pres[hop], rows, encoder_part, encoder_grad)
+        elif left == 1:
+            encoder_part = input_step(pres[hop], rows, None)
+            return encoder_part
+        else:
+            encoder_grad = input_step(pres[hop], rows, encoder_grad)
         return encoder_grad
 
     held = {(kind, way): rows for kind, rows in (("grads", grad_recon), ("inputs", inputs)) for way in (True, False)}
@@ -220,11 +275,11 @@
     def arrive(turn):
         nonlocal returned
         kind, hop = turns[turn]
-        last = turn in (last_grads, len(turns) - 1)
+        left = 0 if turn == last_grads else len(turns) - 1 - turn
         ready = (meta,) if turn < 2 else (marks[turn - 2],)
         if turn == len(turns) - 1:
             ready += (returned,)
-        marks.append(use(kind, hop % chips, (arrived[turn], send(arrived[turn], swap, *ready)), last))
+        marks.append(use(kind, hop % chips, (arrived[turn], send(arrived[turn], swap, *ready)), left))
         if turn == last_grads:
             returned = lax.all_to_all(totals[2], "lat", split_axis=0, concat_axis=0, tiled=True)
 

time: 165 us -> 165 us (level)
  local copies, waits for them, and re-layouts: 12.1 us -> 7.23 us
  waiting for transfers between devices: 85.6 us -> 88.2 us
  Pallas kernels: 41.4 us -> 43.6 us
    pallas_call x1 -> x2, Pallas kernels: 0.71 us -> 6.59 us  [the longest x1 5.06 us: last_input_step(): pl.pallas_call(last_input_kernel, in_specs=[whole] * 4 + [far], out_specs...]
    unnamed x26 -> x16, local copies, waits for them, and re-layouts: 11.4 us -> 6.53 us
    pallas_call x8 -> x7, Pallas kernels: 14.3 us -> 10.6 us  [input_step(): pl.pallas_call(input_kernel, in_specs=[whole] * (3 + len(totals)), out_sp...]
    all_to_all x1, waiting for transfers between devices: 16.4 us -> 18.4 us  [by_ring(): meta = lax.all_to_all(meta, 'lat', split_axis=0, concat_axis=0, tiled=True)]
  transfers between devices with their start and end apart: 32 -> 32, of which waited for: 11 -> 12; matrix products, arithmetic and copies ran while one was open for 0% -> 0% of each run, Pallas kernels for 23% -> 23%
where the time goes in v12:
time: 165 us
  waiting for transfers between devices  88.2 us (53%)
  Pallas kernels  43.6 us (26%)
  starting transfers between devices  24.1 us (15%)
  local copies, waits for them, and re-layouts  7.23 us (4%)
    ppermute x30, waiting for transfers between devices, send(): return lax.ppermute(after(rows, *first) if first else rows, 'lat', way)  69 us
    pallas_call x8, Pallas kernels, grad_step(): pl.pallas_call(functools.partial(grad_kernel, per_block), in_specs=[scala...  26.4 us
    all_to_all x1, waiting for transfers between devices, by_ring(): meta = lax.all_to_all(meta, 'lat', split_axis=0, concat_axis=0, tiled=True)  18.4 us
    ppermute x30, starting transfers between devices, send(): return lax.ppermute(after(rows, *first) if first else rows, 'lat', way)  14.2 us
    pallas_call x7, Pallas kernels, input_step(): pl.pallas_call(input_kernel, in_specs=[whole] * (3 + len(totals)), out_sp...  10.6 us
    unnamed x16, local copies, waits for them, and re-layouts  6.53 us
    all_to_all x1, starting transfers between devices, by_ring(): meta = lax.all_to_all(meta, 'lat', split_axis=0, concat_axis=0, tiled=True)  6.37 us
    pallas_call x1, Pallas kernels, last_input_step(): pl.pallas_call(last_input_kernel, in_specs=[whole] * 4 + [far], out_specs...  5.06 us
  transfers between devices with their start and end apart: 32, of which 12 were waited for; matrix products, arithmetic and copies ran while one was open for 0% of the time, Pallas kernels for 23%

profile of v12, /device:TPU:0, one launch (start us, length us, event | category | flops | bytes accessed | tf_op | source)
XLA Modules:
  0.0 164.7 jit_solution(537702378722781931)
XLA Ops:
  0.6 3.1 %collective-permute-start = (bf16[128,3584]{1,0:T(8,128)(2,1)}, bf16[128,3584]{1,0:T(8,128)(2,1)}, u32[]{:S(2)}, u32[]{:S(2)}) collective-permute-start(bf16[128,3584]{1,0:T(8,128)(2,1)} %mine_ref.2), channel_id=1, source_target_pairs={{0,4},{4,8},{8,12},{12,14},{14,10},{10,6},{6,2},{2,0},{1,3},{5,1},... | collective-permute-start | bytes 2752520 | tf_op jit(solution)/shard_map/ppermute | solution.py:241
  3.7 1.5 meta.1
  5.3 6.4 %all-to-all-start = ((bf16[16,32,128]{2,1,0:T(8,128)(2,1)}), bf16[16,32,128]{2,1,0:T(8,128)(2,1)S(1)}, u32[]{:S(2)}, u32[]{:S(2)}) async-start(bf16[16,32,128]{2,1,0:T(8,128)(2,1)} %meta.1), calls=%async_computation | async-start | bytes 262144 | tf_op jit(solution)/shard_map/all_to_all | solution.py:180
  12.0 18.4 %all-to-all-done.meta_ref = bf16[16,32,128]{2,1,0:T(8,128)(2,1)S(1)} async-done(((bf16[16,32,128]{2,1,0:T(8,128)(2,1)}), bf16[16,32,128]{2,1,0:T(8,128)(2,1)S(1)}, u32[]{:S(2)}, u32[]{:S(2)}) %all-to-all-start) | async-done | bytes 131104 | tf_op jit(solution)/shard_map/all_to_all | solution.py:180
  31.0 1.7 %collective-permute-start.1 = (bf16[128,3584]{1,0:T(8,128)(2,1)}, bf16[128,3584]{1,0:T(8,128)(2,1)S(1)}, u32[]{:S(2)}, u32[]{:S(2)}) collective-permute-start(bf16[128,3584]{1,0:T(8,128)(2,1)} %collective-permute-done.mine_ref), channel_id=1, source_target_pairs={{0,4},{4,8},{8,12},{12,14},{14,10},{10,6},{6,2},{2,0},{1,3},{5,1},... | collective-permute-start | bytes 2752520 | tf_op jit(solution)/shard_map/ppermute | solution.py:241
  33.6 1.5 copy-done.3
  36.3 3.3 %grad_step.8 = (f32[256,3584]{1,0:T(8,128)S(1)}, f32[256,128]{1,0:T(8,128)S(1)}, f32[16,16,128]{2,1,0:T(8,128)S(1)}, bf16[256,256]{1,0:T(8,128)(2,1)S(1)}) custom-call(s32[2]{0:T(128)S(1)} %get-tuple-element.121.order_ref, bf16[16,32,128]{2,1,0:T(8,128)(2,1)S(1)} %all-to-all-done.meta_ref, bf16[256,3584]{1,0:T(8,128)(2,1)S(1)} %copy-done.3, ...), custom_call_target="tpu_custom_call" | custom-call | flops 1 | bytes 1 | tf_op jit(solution)/shard_map/grad_step/pallas_call | solution.py:187
  39.6 3.8 %grad_step.9 = (f32[256,3584]{1,0:T(8,128)S(1)}, f32[256,128]{1,0:T(8,128)S(1)}, f32[16,16,128]{2,1,0:T(8,128)S(1)}, bf16[256,256]{1,0:T(8,128)(2,1)S(1)}) custom-call(s32[2]{0:T(128)S(1)} %get-tuple-element.122.order_ref, bf16[16,32,128]{2,1,0:T(8,128)(2,1)S(1)} %all-to-all-done.meta_ref, ...), custom_call_target="tpu_custom_call", output_to_operand_aliasing={{0}: (5, {}), {1}: (6, {})} | custom-call | flops 1 | bytes 1 | tf_op jit(solution)/shard_map/grad_step/pallas_call | solution.py:187
  44.2 3.6 %grad_step.10 = (f32[256,3584]{1,0:T(8,128)S(1)}, f32[256,128]{1,0:T(8,128)S(1)}, f32[16,16,128]{2,1,0:T(8,128)S(1)}, bf16[256,256]{1,0:T(8,128)(2,1)S(1)}) custom-call(s32[2]{0:T(128)S(1)} %get-tuple-element.119.order_ref, bf16[16,32,128]{2,1,0:T(8,128)(2,1)S(1)} %all-to-all-done.meta_ref, ...), custom_call_target="tpu_custom_call", output_to_operand_aliasing={{0}: (5, {}), {1}: (6, {})} | custom-call | flops 1 | bytes 1 | tf_op jit(solution)/shard_map/grad_step/pallas_call | solution.py:187
  47.8 12.8 %collective-permute-done.1.mine_ref = bf16[128,3584]{1,0:T(8,128)(2,1)S(1)} collective-permute-done((bf16[128,3584]{1,0:T(8,128)(2,1)}, bf16[128,3584]{1,0:T(8,128)(2,1)S(1)}, u32[]{:S(2)}, u32[]{:S(2)}) %collective-permute-start.1) | collective-permute-done | bytes 917536 | tf_op jit(solution)/shard_map/ppermute | solution.py:241
  61.4 1.4 input_step.8.refs_0_
  63.7 1.5 collective-permute-start.7
  65.1 2.9 %grad_step.11 = (f32[256,3584]{1,0:T(8,128)S(1)}, f32[256,128]{1,0:T(8,128)S(1)}, f32[16,16,128]{2,1,0:T(8,128)S(1)}, bf16[256,256]{1,0:T(8,128)(2,1)S(1)}) custom-call(s32[2]{0:T(128)S(1)} %get-tuple-element.120.order_ref, bf16[16,32,128]{2,1,0:T(8,128)(2,1)S(1)} %all-to-all-done.meta_ref, ...), custom_call_target="tpu_custom_call", output_to_operand_aliasing={{0}: (5, {}), {1}: (6, {})} | custom-call | flops 1 | bytes 1 | tf_op jit(solution)/shard_map/grad_step/pallas_call | solution.py:187
  68.0 6.0 %collective-permute-done.11.mine_ref = bf16[128,3584]{1,0:T(8,128)(2,1)S(1)} collective-permute-done((bf16[128,3584]{1,0:T(8,128)(2,1)S(1)}, bf16[128,3584]{1,0:T(8,128)(2,1)S(1)}, u32[]{:S(2)}, u32[]{:S(2)}) %collective-permute-start.11) | collective-permute-done | bytes 917536 | tf_op jit(solution)/shard_map/ppermute | solution.py:241
  74.1 2.9 %grad_step.12 = (f32[256,3584]{1,0:T(8,128)S(1)}, f32[256,128]{1,0:T(8,128)S(1)}, f32[16,16,128]{2,1,0:T(8,128)S(1)}, bf16[256,256]{1,0:T(8,128)(2,1)S(1)}) custom-call(s32[2]{0:T(128)S(1)} %get-tuple-element.116.order_ref, bf16[16,32,128]{2,1,0:T(8,128)(2,1)S(1)} %all-to-all-done.meta_ref, ...), custom_call_target="tpu_custom_call", output_to_operand_aliasing={{0}: (5, {}), {1}: (6, {})} | custom-call | flops 1 | bytes 1 | tf_op jit(solution)/shard_map/grad_step/pallas_call | solution.py:187
  77.0 13.6 %collective-permute-done.7.mine_ref = bf16[128,3584]{1,0:T(8,128)(2,1)S(1)} collective-permute-done((bf16[128,3584]{1,0:T(8,128)(2,1)S(1)}, bf16[128,3584]{1,0:T(8,128)(2,1)S(1)}, u32[]{:S(2)}, u32[]{:S(2)}) %collective-permute-start.7) | collective-permute-done | bytes 917536 | tf_op jit(solution)/shard_map/ppermute | solution.py:241
  90.6 1.4 input_step.9.refs_0_
  94.1 2.9 %grad_step.13 = (f32[256,3584]{1,0:T(8,128)S(1)}, f32[256,128]{1,0:T(8,128)S(1)}, f32[16,16,128]{2,1,0:T(8,128)S(1)}, bf16[256,256]{1,0:T(8,128)(2,1)S(1)}) custom-call(s32[2]{0:T(128)S(1)} %get-tuple-element.117.order_ref, bf16[16,32,128]{2,1,0:T(8,128)(2,1)S(1)} %all-to-all-done.meta_ref, ...), custom_call_target="tpu_custom_call", output_to_operand_aliasing={{0}: (5, {}), {1}: (6, {})} | custom-call | flops 1 | bytes 1 | tf_op jit(solution)/shard_map/grad_step/pallas_call | solution.py:187
  97.0 14.5 %collective-permute-done.20.mine_ref = bf16[128,3584]{1,0:T(8,128)(2,1)S(1)} collective-permute-done((bf16[128,3584]{1,0:T(8,128)(2,1)S(1)}, bf16[128,3584]{1,0:T(8,128)(2,1)S(1)}, u32[]{:S(2)}, u32[]{:S(2)}) %collective-permute-start.20) | collective-permute-done | bytes 917536 | tf_op jit(solution)/shard_map/ppermute | solution.py:241
  111.5 2.9 %grad_step.14 = (f32[256,3584]{1,0:T(8,128)S(1)}, f32[256,128]{1,0:T(8,128)S(1)}, f32[16,16,128]{2,1,0:T(8,128)S(1)}, bf16[256,256]{1,0:T(8,128)(2,1)S(1)}) custom-call(s32[2]{0:T(128)S(1)} %get-tuple-element.118.order_ref, bf16[16,32,128]{2,1,0:T(8,128)(2,1)S(1)} %all-to-all-done.meta_ref, ...), custom_call_target="tpu_custom_call", output_to_operand_aliasing={{0}: (5, {}), {1}: (6, {})} | custom-call | flops 1 | bytes 1 | tf_op jit(solution)/shard_map/grad_step/pallas_call | solution.py:187
  115.0 2.0 %collective-permute-start.21 = (bf16[128,3584]{1,0:T(8,128)(2,1)S(1)}, bf16[128,3584]{1,0:T(8,128)(2,1)S(1)}, u32[]{:S(2)}, u32[]{:S(2)}) collective-permute-start(bf16[128,3584]{1,0:T(8,128)(2,1)S(1)} %collective-permute-done.20.mine_ref), channel_id=1, source_target_pairs={{4,0},{8,4},{12,8},{14,12},{10,14},{6,10},{2,6},{0,2},{3,1},{1,5},... | collective-permute-start | bytes 2752520 | tf_op jit(solution)/shard_map/ppermute | solution.py:241
  117.0 1.4 input_step.10.refs_0_
  118.4 13.1 %collective-permute-done.24.mine_ref = bf16[128,3584]{1,0:T(8,128)(2,1)S(1)} collective-permute-done((bf16[128,3584]{1,0:T(8,128)(2,1)S(1)}, bf16[128,3584]{1,0:T(8,128)(2,1)S(1)}, u32[]{:S(2)}, u32[]{:S(2)}) %collective-permute-start.24) | collective-permute-done | bytes 917536 | tf_op jit(solution)/shard_map/ppermute | solution.py:241
  131.5 4.1 %grad_step.15 = (bf16[256,3584]{1,0:T(8,128)(2,1)}, f32[1,256]{1,0:T(1,128)}, f32[16,16,128]{2,1,0:T(8,128)}, bf16[256,256]{1,0:T(8,128)(2,1)S(1)}) custom-call(s32[2]{0:T(128)S(1)} %get-tuple-element.123.order_ref, bf16[16,32,128]{2,1,0:T(8,128)(2,1)S(1)} %all-to-all-done.meta_ref, bf16[256,3584]{1,0:T(8,128)(2,1)S(1)} %copy-done.4, ...), custom_call_target="tpu_custom_call" | custom-call | flops 1 | bytes 1 | tf_op jit(solution)/shard_map/grad_step/pallas_call | solution.py:187
  136.2 2.0 %collective-permute-start.22 = (bf16[128,3584]{1,0:T(8,128)(2,1)S(1)}, bf16[128,3584]{1,0:T(8,128)(2,1)}, u32[]{:S(2)}, u32[]{:S(2)}) collective-permute-start(bf16[128,3584]{1,0:T(8,128)(2,1)S(1)} %collective-permute-done.21.mine_ref), channel_id=1, source_target_pairs={{4,0},{8,4},{12,8},{14,12},{10,14},{6,10},{2,6},{0,2},{3,1},{1,5},... | collective-permute-start | bytes 2752520 | tf_op jit(solution)/shard_map/ppermute | solution.py:241
  138.2 3.5 %all-to-all-start.1 = ((f32[16,16,128]{2,1,0:T(8,128)}), f32[16,16,128]{2,1,0:T(8,128)S(1)}, u32[]{:S(2)}, u32[]{:S(2)}) async-start(f32[16,16,128]{2,1,0:T(8,128)} %get-tuple-element.111), calls=%async_computation.1 | async-start | bytes 262144 | tf_op jit(solution)/shard_map/all_to_all | solution.py:284
  141.7 2.0 %copy-done.1 = f32[3584,256]{1,0:T(8,128)S(1)} copy-done((f32[3584,256]{1,0:T(8,128)S(1)}, f32[3584,256]{1,0:T(8,128)}, u32[]{:S(2)}) %copy-start.1) | copy-done | bytes 3670040
  145.2 6.0 %collective-permute-done.28.mine_ref = bf16[128,3584]{1,0:T(8,128)(2,1)} collective-permute-done((bf16[128,3584]{1,0:T(8,128)(2,1)S(1)}, bf16[128,3584]{1,0:T(8,128)(2,1)}, u32[]{:S(2)}, u32[]{:S(2)}) %collective-permute-start.28) | collective-permute-done | bytes 917536 | tf_op jit(solution)/shard_map/ppermute | solution.py:241
  151.1 2.5 %input_step.12.total_ref = f32[3584,256]{1,0:T(8,128)S(1)} custom-call(bf16[256,256]{1,0:T(8,128)(2,1)S(1)} %get-tuple-element.105.pre_ref, bf16[128,3584]{1,0:T(8,128)(2,1)S(1)} %collective-permute-done.21.mine_ref, bf16[128,3584]{1,0:T(8,128)(2,1)} %collective-permute-done.23.theirs_ref, ...), custom_call_target="tpu_custom_call", output_to_operand_aliasing={{}: (3, {})} | custom-call | flops 1 | bytes 1 | tf_op jit(solution)/shard_map/input_step/pallas_call | solution.py:210
  153.7 1.8 %copy-done.2 = f32[3584,256]{1,0:T(8,128)} copy-done((f32[3584,256]{1,0:T(8,128)}, f32[3584,256]{1,0:T(8,128)S(1)}, u32[]{:S(2)}) %copy-start.2) | copy-done | bytes 3670040
  156.6 1.9 %input_step.13.part_ref = f32[3584,256]{1,0:T(8,128)S(1)} custom-call(bf16[256,256]{1,0:T(8,128)(2,1)S(1)} %get-tuple-element.113.pre_ref, bf16[128,3584]{1,0:T(8,128)(2,1)} %collective-permute-done.28.mine_ref, bf16[128,3584]{1,0:T(8,128)(2,1)S(1)} %collective-permute-done.29.theirs_ref), custom_call_target="tpu_custom_call" | custom-call | flops 1 | bytes 1 | tf_op jit(solution)/shard_map/input_step/pallas_call | solution.py:210
  158.9 5.1 %last_input_step.1 = bf16[3584,256]{1,0:T(8,128)(2,1)} custom-call(bf16[256,256]{1,0:T(8,128)(2,1)S(1)} %get-tuple-element.100.pre_ref, bf16[128,3584]{1,0:T(8,128)(2,1)} %collective-permute-done.22.mine_ref, bf16[128,3584]{1,0:T(8,128)(2,1)S(1)} %collective-permute-done.27.theirs_ref, f32[3584,256]{1,0:T(8,128)S(1)} %input_step.13.part_ref, ...), custom_call_target="tpu_custom_call" | custom-call | flops 1 | bytes 1 | tf_op jit(solution)/shard_map/last_input_step/pallas_call | solution.py:224
  (69 shorter events, 12.3 us)
Async XLA Ops:
  0.6 29.8 %collective-permute-start = (bf16[128,3584]{1,0:T(8,128)(2,1)}, bf16[128,3584]{1,0:T(8,128)(2,1)}, u32[]{:S(2)}, u32[]{:S(2)}) collective-permute-start(bf16[128,3584]{1,0:T(8,128)(2,1)} %mine_ref.2), channel_id=1, source_target_pairs={{0,4},{4,8},{8,12},{12,14},{14,10},{10,6},{6,2},{2,0},{1,3},{5,1},... | collective-permute-start | bytes 2752520 | tf_op jit(solution)/shard_map/ppermute | solution.py:241
  3.7 27.0 %collective-permute-start.8 = (bf16[128,3584]{1,0:T(8,128)(2,1)}, bf16[128,3584]{1,0:T(8,128)(2,1)S(1)}, u32[]{:S(2)}, u32[]{:S(2)}) collective-permute-start(bf16[128,3584]{1,0:T(8,128)(2,1)} %mine_ref.2), channel_id=1, source_target_pairs={{4,0},{8,4},{12,8},{14,12},{10,14},{6,10},{2,6},{0,2},{3,1},{1,5},... | collective-permute-start | bytes 2752520 | tf_op jit(solution)/shard_map/ppermute | solution.py:241
  5.3 25.2 %all-to-all-start = ((bf16[16,32,128]{2,1,0:T(8,128)(2,1)}), bf16[16,32,128]{2,1,0:T(8,128)(2,1)S(1)}, u32[]{:S(2)}, u32[]{:S(2)}) async-start(bf16[16,32,128]{2,1,0:T(8,128)(2,1)} %meta.1), calls=%async_computation | async-start | bytes 262144 | tf_op jit(solution)/shard_map/all_to_all | solution.py:180
  11.6 21.8 %collective-permute-start.3 = (bf16[128,3584]{1,0:T(8,128)(2,1)}, bf16[128,3584]{1,0:T(8,128)(2,1)}, u32[]{:S(2)}, u32[]{:S(2)}) collective-permute-start(bf16[128,3584]{1,0:T(8,128)(2,1)} %mine_ref.2), channel_id=1, source_target_pairs={{0,1},{1,0},{2,3},{3,2},{4,5},{5,4},{6,7},{7,6},{8,9},{9,8},{10,11... | collective-permute-start | bytes 2752520 | tf_op jit(solution)/shard_map/ppermute | solution.py:241
  30.5 9.1 %collective-permute-start.2 = (bf16[128,3584]{1,0:T(8,128)(2,1)}, bf16[128,3584]{1,0:T(8,128)(2,1)}, u32[]{:S(2)}, u32[]{:S(2)}) collective-permute-start(bf16[128,3584]{1,0:T(8,128)(2,1)} %collective-permute-done.mine_ref), channel_id=1, source_target_pairs={{0,1},{1,0},{2,3},{3,2},{4,5},{5,4},{6,7},{7,6},{8,9},{9,8},{10,11... | collective-permute-start | bytes 2752520 | tf_op jit(solution)/shard_map/ppermute | solution.py:241
  30.6 13.6 %collective-permute-start.4 = (bf16[128,3584]{1,0:T(8,128)(2,1)}, bf16[128,3584]{1,0:T(8,128)(2,1)S(1)}, u32[]{:S(2)}, u32[]{:S(2)}) collective-permute-start(bf16[128,3584]{1,0:T(8,128)(2,1)} %mine_ref.3), channel_id=1, source_target_pairs={{0,4},{4,8},{8,12},{12,14},{14,10},{10,6},{6,2},{2,0},{1,3},{5,1},... | collective-permute-start | bytes 2752520 | tf_op jit(solution)/shard_map/ppermute | solution.py:241
  30.7 13.6 %collective-permute-start.9 = (bf16[128,3584]{1,0:T(8,128)(2,1)S(1)}, bf16[128,3584]{1,0:T(8,128)(2,1)}, u32[]{:S(2)}, u32[]{:S(2)}) collective-permute-start(bf16[128,3584]{1,0:T(8,128)(2,1)S(1)} %collective-permute-done.8.mine_ref), channel_id=1, source_target_pairs={{0,1},{1,0},{2,3},{3,2},{4,5},{5,4},{6,7},{7,6},{8,9},{9,8},{10,11... | collective-permute-start | bytes 2752520 | tf_op jit(solution)/shard_map/ppermute | solution.py:241
  31.0 29.7 %collective-permute-start.1 = (bf16[128,3584]{1,0:T(8,128)(2,1)}, bf16[128,3584]{1,0:T(8,128)(2,1)S(1)}, u32[]{:S(2)}, u32[]{:S(2)}) collective-permute-start(bf16[128,3584]{1,0:T(8,128)(2,1)} %collective-permute-done.mine_ref), channel_id=1, source_target_pairs={{0,4},{4,8},{8,12},{12,14},{14,10},{10,6},{6,2},{2,0},{1,3},{5,1},... | collective-permute-start | bytes 2752520 | tf_op jit(solution)/shard_map/ppermute | solution.py:241
  33.4 27.3 %collective-permute-start.6 = (bf16[128,3584]{1,0:T(8,128)(2,1)}, bf16[128,3584]{1,0:T(8,128)(2,1)S(1)}, u32[]{:S(2)}, u32[]{:S(2)}) collective-permute-start(bf16[128,3584]{1,0:T(8,128)(2,1)} %mine_ref.3), channel_id=1, source_target_pairs={{0,1},{1,0},{2,3},{3,2},{4,5},{5,4},{6,7},{7,6},{8,9},{9,8},{10,11... | collective-permute-start | bytes 2752520 | tf_op jit(solution)/shard_map/ppermute | solution.py:241
  44.2 17.2 %collective-permute-start.5 = (bf16[128,3584]{1,0:T(8,128)(2,1)S(1)}, bf16[128,3584]{1,0:T(8,128)(2,1)S(1)}, u32[]{:S(2)}, u32[]{:S(2)}) collective-permute-start(bf16[128,3584]{1,0:T(8,128)(2,1)S(1)} %collective-permute-done.4.mine_ref), channel_id=1, source_target_pairs={{0,1},{1,0},{2,3},{3,2},{4,5},{5,4},{6,7},{7,6},{8,9},{9,8},{10,11... | collective-permute-start | bytes 2752520 | tf_op jit(solution)/shard_map/ppermute | solution.py:241
  44.2 19.1 %collective-permute-start.14 = (bf16[128,3584]{1,0:T(8,128)(2,1)S(1)}, bf16[128,3584]{1,0:T(8,128)(2,1)S(1)}, u32[]{:S(2)}, u32[]{:S(2)}) collective-permute-start(bf16[128,3584]{1,0:T(8,128)(2,1)S(1)} %collective-permute-done.8.mine_ref), channel_id=1, source_target_pairs={{4,0},{8,4},{12,8},{14,12},{10,14},{6,10},{2,6},{0,2},{3,1},{1,5},... | collective-permute-start | bytes 2752520 | tf_op jit(solution)/shard_map/ppermute | solution.py:241
  60.7 4.5 %collective-permute-start.10 = (bf16[128,3584]{1,0:T(8,128)(2,1)S(1)}, bf16[128,3584]{1,0:T(8,128)(2,1)S(1)}, u32[]{:S(2)}, u32[]{:S(2)}) collective-permute-start(bf16[128,3584]{1,0:T(8,128)(2,1)S(1)} %collective-permute-done.1.mine_ref), channel_id=1, source_target_pairs={{0,1},{1,0},{2,3},{3,2},{4,5},{5,4},{6,7},{7,6},{8,9},{9,8},{10,11... | collective-permute-start | bytes 2752520 | tf_op jit(solution)/shard_map/ppermute | solution.py:241
  60.7 13.4 %collective-permute-start.11 = (bf16[128,3584]{1,0:T(8,128)(2,1)S(1)}, bf16[128,3584]{1,0:T(8,128)(2,1)S(1)}, u32[]{:S(2)}, u32[]{:S(2)}) collective-permute-start(bf16[128,3584]{1,0:T(8,128)(2,1)S(1)} %collective-permute-done.4.mine_ref), channel_id=1, source_target_pairs={{0,4},{4,8},{8,12},{12,14},{14,10},{10,6},{6,2},{2,0},{1,3},{5,1},... | collective-permute-start | bytes 2752520 | tf_op jit(solution)/shard_map/ppermute | solution.py:241
  63.3 10.8 %collective-permute-start.17 = (bf16[128,3584]{1,0:T(8,128)(2,1)S(1)}, bf16[128,3584]{1,0:T(8,128)(2,1)S(1)}, u32[]{:S(2)}, u32[]{:S(2)}) collective-permute-start(bf16[128,3584]{1,0:T(8,128)(2,1)S(1)} %collective-permute-done.14.mine_ref), channel_id=1, source_target_pairs={{0,1},{1,0},{2,3},{3,2},{4,5},{5,4},{6,7},{7,6},{8,9},{9,8},{10,11... | collective-permute-start | bytes 2752520 | tf_op jit(solution)/shard_map/ppermute | solution.py:241
  63.7 26.9 %collective-permute-start.7 = (bf16[128,3584]{1,0:T(8,128)(2,1)S(1)}, bf16[128,3584]{1,0:T(8,128)(2,1)S(1)}, u32[]{:S(2)}, u32[]{:S(2)}) collective-permute-start(bf16[128,3584]{1,0:T(8,128)(2,1)S(1)} %collective-permute-done.1.mine_ref), channel_id=1, source_target_pairs={{0,4},{4,8},{8,12},{12,14},{14,10},{10,6},{6,2},{2,0},{1,3},{5,1},... | collective-permute-start | bytes 2752520 | tf_op jit(solution)/shard_map/ppermute | solution.py:241
  74.1 16.5 %collective-permute-start.12 = (bf16[128,3584]{1,0:T(8,128)(2,1)S(1)}, bf16[128,3584]{1,0:T(8,128)(2,1)S(1)}, u32[]{:S(2)}, u32[]{:S(2)}) collective-permute-start(bf16[128,3584]{1,0:T(8,128)(2,1)S(1)} %collective-permute-done.11.mine_ref), channel_id=1, source_target_pairs={{0,1},{1,0},{2,3},{3,2},{4,5},{5,4},{6,7},{7,6},{8,9},{9,8},{10,11... | collective-permute-start | bytes 2752520 | tf_op jit(solution)/shard_map/ppermute | solution.py:241
  74.1 19.2 %collective-permute-start.15 = (bf16[128,3584]{1,0:T(8,128)(2,1)S(1)}, bf16[128,3584]{1,0:T(8,128)(2,1)S(1)}, u32[]{:S(2)}, u32[]{:S(2)}) collective-permute-start(bf16[128,3584]{1,0:T(8,128)(2,1)S(1)} %collective-permute-done.14.mine_ref), channel_id=1, source_target_pairs={{4,0},{8,4},{12,8},{14,12},{10,14},{6,10},{2,6},{0,2},{3,1},{1,5},... | collective-permute-start | bytes 2752520 | tf_op jit(solution)/shard_map/ppermute | solution.py:241
  90.6 3.6 %collective-permute-start.18 = (bf16[128,3584]{1,0:T(8,128)(2,1)S(1)}, bf16[128,3584]{1,0:T(8,128)(2,1)S(1)}, u32[]{:S(2)}, u32[]{:S(2)}) collective-permute-start(bf16[128,3584]{1,0:T(8,128)(2,1)S(1)} %collective-permute-done.7.mine_ref), channel_id=1, source_target_pairs={{0,1},{1,0},{2,3},{3,2},{4,5},{5,4},{6,7},{7,6},{8,9},{9,8},{10,11... | collective-permute-start | bytes 2752520 | tf_op jit(solution)/shard_map/ppermute | solution.py:241
  90.6 20.9 %collective-permute-start.20 = (bf16[128,3584]{1,0:T(8,128)(2,1)S(1)}, bf16[128,3584]{1,0:T(8,128)(2,1)S(1)}, u32[]{:S(2)}, u32[]{:S(2)}) collective-permute-start(bf16[128,3584]{1,0:T(8,128)(2,1)S(1)} %copy-done.6), channel_id=1, source_target_pairs={{4,0},{8,4},{12,8},{14,12},{10,14},{6,10},{2,6},{0,2},{3,1},{1,5},... | collective-permute-start | bytes 2752520 | tf_op jit(solution)/shard_map/ppermute | solution.py:241
  93.3 18.2 %collective-permute-start.16 = (bf16[128,3584]{1,0:T(8,128)(2,1)S(1)}, bf16[128,3584]{1,0:T(8,128)(2,1)S(1)}, u32[]{:S(2)}, u32[]{:S(2)}) collective-permute-start(bf16[128,3584]{1,0:T(8,128)(2,1)S(1)} %collective-permute-done.15.mine_ref), channel_id=1, source_target_pairs={{0,1},{1,0},{2,3},{3,2},{4,5},{5,4},{6,7},{7,6},{8,9},{9,8},{10,11... | collective-permute-start | bytes 2752520 | tf_op jit(solution)/shard_map/ppermute | solution.py:241
  93.6 20.9 %collective-permute-start.13 = (bf16[128,3584]{1,0:T(8,128)(2,1)S(1)}, bf16[128,3584]{1,0:T(8,128)(2,1)S(1)}, u32[]{:S(2)}, u32[]{:S(2)}) collective-permute-start(bf16[128,3584]{1,0:T(8,128)(2,1)S(1)} %collective-permute-done.7.mine_ref), channel_id=1, source_target_pairs={{0,4},{4,8},{8,12},{12,14},{14,10},{10,6},{6,2},{2,0},{1,3},{5,1},... | collective-permute-start | bytes 2752520 | tf_op jit(solution)/shard_map/ppermute | solution.py:241
  111.5 20.1 %collective-permute-start.24 = (bf16[128,3584]{1,0:T(8,128)(2,1)S(1)}, bf16[128,3584]{1,0:T(8,128)(2,1)S(1)}, u32[]{:S(2)}, u32[]{:S(2)}) collective-permute-start(bf16[128,3584]{1,0:T(8,128)(2,1)S(1)} %collective-permute-done.11.mine_ref), channel_id=1, source_target_pairs={{0,4},{4,8},{8,12},{12,14},{14,10},{10,6},{6,2},{2,0},{1,3},{5,1},... | collective-permute-start | bytes 2752520 | tf_op jit(solution)/shard_map/ppermute | solution.py:241
  111.5 5.5 %collective-permute-start.25 = (bf16[128,3584]{1,0:T(8,128)(2,1)S(1)}, bf16[128,3584]{1,0:T(8,128)(2,1)S(1)}, u32[]{:S(2)}, u32[]{:S(2)}) collective-permute-start(bf16[128,3584]{1,0:T(8,128)(2,1)S(1)} %collective-permute-done.20.mine_ref), channel_id=1, source_target_pairs={{0,1},{1,0},{2,3},{3,2},{4,5},{5,4},{6,7},{7,6},{8,9},{9,8},{10,11... | collective-permute-start | bytes 2752520 | tf_op jit(solution)/shard_map/ppermute | solution.py:241
  114.4 17.1 %collective-permute-start.19 = (bf16[128,3584]{1,0:T(8,128)(2,1)S(1)}, bf16[128,3584]{1,0:T(8,128)(2,1)S(1)}, u32[]{:S(2)}, u32[]{:S(2)}) collective-permute-start(bf16[128,3584]{1,0:T(8,128)(2,1)S(1)} %collective-permute-done.13.mine_ref), channel_id=1, source_target_pairs={{0,1},{1,0},{2,3},{3,2},{4,5},{5,4},{6,7},{7,6},{8,9},{9,8},{10,11... | collective-permute-start | bytes 2752520 | tf_op jit(solution)/shard_map/ppermute | solution.py:241
  115.0 20.6 %collective-permute-start.21 = (bf16[128,3584]{1,0:T(8,128)(2,1)S(1)}, bf16[128,3584]{1,0:T(8,128)(2,1)S(1)}, u32[]{:S(2)}, u32[]{:S(2)}) collective-permute-start(bf16[128,3584]{1,0:T(8,128)(2,1)S(1)} %collective-permute-done.20.mine_ref), channel_id=1, source_target_pairs={{4,0},{8,4},{12,8},{14,12},{10,14},{6,10},{2,6},{0,2},{3,1},{1,5},... | collective-permute-start | bytes 2752520 | tf_op jit(solution)/shard_map/ppermute | solution.py:241
  131.5 19.6 %collective-permute-start.28 = (bf16[128,3584]{1,0:T(8,128)(2,1)S(1)}, bf16[128,3584]{1,0:T(8,128)(2,1)}, u32[]{:S(2)}, u32[]{:S(2)}) collective-permute-start(bf16[128,3584]{1,0:T(8,128)(2,1)S(1)} %collective-permute-done.24.mine_ref), channel_id=1, source_target_pairs={{0,4},{4,8},{8,12},{12,14},{14,10},{10,6},{6,2},{2,0},{1,3},{5,1},... | collective-permute-start | bytes 2752520 | tf_op jit(solution)/shard_map/ppermute | solution.py:241
  131.5 10.2 %collective-permute-start.26 = (bf16[128,3584]{1,0:T(8,128)(2,1)S(1)}, bf16[128,3584]{1,0:T(8,128)(2,1)S(1)}, u32[]{:S(2)}, u32[]{:S(2)}) collective-permute-start(bf16[128,3584]{1,0:T(8,128)(2,1)S(1)} %collective-permute-done.24.mine_ref), channel_id=1, source_target_pairs={{0,1},{1,0},{2,3},{3,2},{4,5},{5,4},{6,7},{7,6},{8,9},{9,8},{10,11... | collective-permute-start | bytes 2752520 | tf_op jit(solution)/shard_map/ppermute | solution.py:241
  135.6 15.5 %collective-permute-start.23 = (bf16[128,3584]{1,0:T(8,128)(2,1)S(1)}, bf16[128,3584]{1,0:T(8,128)(2,1)}, u32[]{:S(2)}, u32[]{:S(2)}) collective-permute-start(bf16[128,3584]{1,0:T(8,128)(2,1)S(1)} %collective-permute-done.21.mine_ref), channel_id=1, source_target_pairs={{0,1},{1,0},{2,3},{3,2},{4,5},{5,4},{6,7},{7,6},{8,9},{9,8},{10,11... | collective-permute-start | bytes 2752520 | tf_op jit(solution)/shard_map/ppermute | solution.py:241
  136.2 20.1 %collective-permute-start.22 = (bf16[128,3584]{1,0:T(8,128)(2,1)S(1)}, bf16[128,3584]{1,0:T(8,128)(2,1)}, u32[]{:S(2)}, u32[]{:S(2)}) collective-permute-start(bf16[128,3584]{1,0:T(8,128)(2,1)S(1)} %collective-permute-done.21.mine_ref), channel_id=1, source_target_pairs={{4,0},{8,4},{12,8},{14,12},{10,14},{6,10},{2,6},{0,2},{3,1},{1,5},... | collective-permute-start | bytes 2752520 | tf_op jit(solution)/shard_map/ppermute | solution.py:241
  138.2 18.0 %all-to-all-start.1 = ((f32[16,16,128]{2,1,0:T(8,128)}), f32[16,16,128]{2,1,0:T(8,128)S(1)}, u32[]{:S(2)}, u32[]{:S(2)}) async-start(f32[16,16,128]{2,1,0:T(8,128)} %get-tuple-element.111), calls=%async_computation.1 | async-start | bytes 262144 | tf_op jit(solution)/shard_map/all_to_all | solution.py:284
  151.1 5.5 %collective-permute-start.29 = (bf16[128,3584]{1,0:T(8,128)(2,1)}, bf16[128,3584]{1,0:T(8,128)(2,1)S(1)}, u32[]{:S(2)}, u32[]{:S(2)}) collective-permute-start(bf16[128,3584]{1,0:T(8,128)(2,1)} %collective-permute-done.28.mine_ref), channel_id=1, source_target_pairs={{0,1},{1,0},{2,3},{3,2},{4,5},{5,4},{6,7},{7,6},{8,9},{9,8},{10,11... | collective-permute-start | bytes 2752520 | tf_op jit(solution)/shard_map/ppermute | solution.py:241
  156.2 2.7 %collective-permute-start.27 = (bf16[128,3584]{1,0:T(8,128)(2,1)}, bf16[128,3584]{1,0:T(8,128)(2,1)S(1)}, u32[]{:S(2)}, u32[]{:S(2)}) collective-permute-start(bf16[128,3584]{1,0:T(8,128)(2,1)} %collective-permute-done.22.mine_ref), channel_id=1, source_target_pairs={{0,1},{1,0},{2,3},{3,2},{4,5},{5,4},{6,7},{7,6},{8,9},{9,8},{10,11... | collective-permute-start | bytes 2752520 | tf_op jit(solution)/shard_map/ppermute | solution.py:241
  (8 other events, 49.4 us)

commit v13 on v12

--- a/solution.py
+++ b/solution.py
@@ -31,7 +31,10 @@
     onward += [(2 * ring[i] + 1, 2 * ring[(i - 1) % chips] + 1) for i in range(chips)]
     swap = [(i, i ^ 1) for i in range(peer_count)]
     backward = [(b, a) for a, b in onward]
-    return sources, onward, backward, swap
+    target = dict(onward)
+    second = [(a, target[b]) for a, b in onward]
+    across = [(b, a ^ 1) for a, b in second]
+    return sources, onward, backward, swap, second, across
 
 
 def meta_kernel(*refs):
@@ -64,7 +67,8 @@
     total_ref, bias_ref, lat_ref, pre_ref, acts_ref, bias_sum = refs[-6:]
     first, last = len(refs) == 6, bias_ref.shape[0] == 1
     bias_sum[...] = jnp.zeros_like(bias_sum) if first else refs[1][...]
-    lat_ref[...] = jnp.zeros_like(lat_ref) if first else refs[2][...]
+    if not last:
+        lat_ref[...] = jnp.zeros_like(lat_ref) if first else refs[2][...]
     latents, width = decoder_ref.shape
     tokens = mine_ref.shape[0]
     span = column_span(width)
@@ -98,7 +102,7 @@
                 dense_both.append(dense)
             pre_ref[block : block + 16, at] = jnp.concatenate(kept_both, axis=0).astype(jnp.bfloat16)
             acts_ref[block : block + 16, at] = jnp.concatenate(dense_both, axis=0).astype(jnp.bfloat16)
-        source = order_ref[tile]
+        source = tile if last else order_ref[tile]
         for k in range(per_block):
             lat_ref[source, k : k + 1, :] = jnp.sum(sums[k], axis=0, keepdims=True)
     for at in range(0, width, span):
@@ -122,22 +126,32 @@
         total_ref[at : at + span, :] = term.astype(total_ref.dtype)
 
 
-def last_input_kernel(pre_ref, mine_ref, theirs_ref, part_ref, total_ref, out_ref, held_ref, made_ref, in_sems, out_sems):
+def late_input_kernel(pre_ref, mine_ref, theirs_ref, total_ref, out_ref, held_ref, sems):
     width = mine_ref.shape[1]
     span = column_span(width)
     parts = [pl.ds(at, span) for at in range(0, width, span)]
-    copies_in = [pltpu.make_async_copy(total_ref.at[p], held_ref.at[p], in_sems.at[i]) for i, p in enumerate(parts)]
-    copies_out = [pltpu.make_async_copy(made_ref.at[p], out_ref.at[p], out_sems.at[i]) for i, p in enumerate(parts)]
-    for copy in copies_in:
+    copies = [pltpu.make_async_copy(total_ref.at[p], held_ref.at[p], sems.at[i]) for i, p in enumerate(parts)]
+    for copy in copies:
         copy.start()
     for i, at in enumerate(range(0, width, span)):
         rows = jnp.concatenate([mine_ref[:, at : at + span], theirs_ref[:, at : at + span]], axis=0)
         term = lax.dot_general(rows, pre_ref[...], (((0,), (1,)), ((), ())), preferred_element_type=jnp.float32)
-        term += part_ref[at : at + span, :]
-        copies_in[i].wait()
-        made_ref[at : at + span, :] = (term + held_ref[at : at + span, :]).astype(made_ref.dtype)
-        copies_out[i].start()
-    for copy in copies_out:
+        copies[i].wait()
+        out_ref[at : at + span, :] = term + held_ref[at : at + span, :]
+
+
+def last_input_kernel(pre_ref, mine_ref, theirs_ref, total_ref, out_ref, made_ref, sems):
+    width = mine_ref.shape[1]
+    span = column_span(width)
+    copies = []
+    for i, at in enumerate(range(0, width, span)):
+        rows = jnp.concatenate([mine_ref[:, at : at + span], theirs_ref[:, at : at + span]], axis=0)
+        term = lax.dot_general(rows, pre_ref[...], (((0,), (1,)), ((), ())), preferred_element_type=jnp.float32)
+        made_ref[at : at + span, :] = (term + total_ref[at : at + span, :]).astype(made_ref.dtype)
+        here = pl.ds(at, span)
+        copies.append(pltpu.make_async_copy(made_ref.at[here], out_ref.at[here], sems.at[i]))
+        copies[-1].start()
+    for copy in copies:
         copy.wait()
 
 
@@ -157,7 +171,7 @@
     peer_count = lax.axis_size("lat")
     chips = peer_count // 2
     me = lax.axis_index("lat")
-    sources, onward, backward, swap = ring_tables(peer_count)
+    sources, onward, backward, swap, second, across = ring_tables(peer_count)
     order = jnp.asarray(sources)[me]
     own_t = owners.T
     whole = pl.BlockSpec(memory_space=pltpu.VMEM)
@@ -184,6 +198,7 @@
 
     def grad_step(hop, rows, totals, last):
         sums, lanes = (latent_count, width), (latent_count, token_count)
+        lat = (2 if last else peer_count, per_block, token_count)
         return pl.pallas_call(
             functools.partial(grad_kernel, per_block),
             in_specs=[scalars] + [whole] * (4 + len(totals)),
@@ -191,7 +206,7 @@
             out_shape=[
                 jax.ShapeDtypeStruct(sums, jnp.bfloat16) if last else pltpu.VMEM(sums, jnp.float32),
                 jax.ShapeDtypeStruct((1, latent_count), jnp.float32) if last else pltpu.VMEM(lanes, jnp.float32),
-                jax.ShapeDtypeStruct((peer_count, per_block, token_count), jnp.float32),
+                jax.ShapeDtypeStruct(lat, jnp.float32),
                 pltpu.VMEM((latent_count, step_tokens), jnp.bfloat16),
             ],
             scratch_shapes=[
@@ -218,50 +233,40 @@
             name="input_step",
         )(near(pre), near(rows[0]), near(rows[1]), *map(near, totals))
 
-    def last_input_step(pre, rows, part, total):
+    def late_input_step(pre, rows, total, last):
         sums, far = (width, latent_count), pl.BlockSpec(memory_space=pltpu.HBM)
-        count = width // column_span(width)
+        total = near(total) if last else pltpu.with_memory_space_constraint(total, pltpu.HBM)
         return pl.pallas_call(
-            last_input_kernel,
-            in_specs=[whole] * 4 + [far],
-            out_specs=far,
-            out_shape=jax.ShapeDtypeStruct(sums, jnp.bfloat16),
+            last_input_kernel if last else late_input_kernel,
+            in_specs=[whole] * 3 + [whole if last else far],
+            out_specs=far if last else whole,
+            out_shape=jax.ShapeDtypeStruct(sums, jnp.bfloat16) if last else pltpu.VMEM(sums, jnp.float32),
             scratch_shapes=[
-                pltpu.VMEM(sums, jnp.float32),
-                pltpu.VMEM(sums, jnp.bfloat16),
-                pltpu.SemaphoreType.DMA((count,)),
-                pltpu.SemaphoreType.DMA((count,)),
+                pltpu.VMEM(sums, jnp.bfloat16 if last else jnp.float32),
+                pltpu.SemaphoreType.DMA((width // column_span(width),)),
             ],
             compiler_params=params,
             cost_estimate=light,
-            name="last_input_step",
-        )(near(pre), near(rows[0]), near(rows[1]), near(part), pltpu.with_memory_space_constraint(total, pltpu.HBM))
+            name="late_input_step",
+        )(near(pre), near(rows[0]), near(rows[1]), total)
 
     def send(rows, way, *first):
         return lax.ppermute(after(rows, *first) if first else rows, "lat", way)
 
-    half = chips // 2
-    later = [("inputs", 1)]
-    for hop in range(1, half):
-        later += [("inputs", hop + 1), ("inputs", -hop)]
-    turns = []
-    for hop in range(1, half + 1):
-        turns += [("grads", hop)] + ([("grads", -hop)] if hop < half else []) + [later.pop(0)]
-    turns += later
+    turns = [("grads", 1), ("grads", -1)]
+    for hop in range(2, chips - 1):
+        turns += [("grads", hop), ("inputs", hop - 1)]
+    turns += [("inputs", -1), ("inputs", chips - 2)]
     pres, totals, encoder_grad = {}, (), None
 
-    encoder_part = None
 
     def use(kind, hop, rows, left=len(turns)):
-        nonlocal totals, encoder_grad, encoder_part
+        nonlocal totals, encoder_grad
         if kind == "grads":
             *totals, pres[hop] = grad_step(hop, rows, totals, left == 0)
             return totals[1]
-        if left == 0:
-            encoder_grad = last_input_step(pres[hop], rows, encoder_part, encoder_grad)
-        elif left == 1:
-            encoder_part = input_step(pres[hop], rows, None)
-            return encoder_part
+        if left < 2:
+            encoder_grad = late_input_step(pres[hop], rows, encoder_grad, left == 0)
         else:
             encoder_grad = input_step(pres[hop], rows, encoder_grad)
         return encoder_grad
@@ -273,15 +278,16 @@
     returned = None
 
     def arrive(turn):
-        nonlocal returned
+        nonlocal returned, totals
         kind, hop = turns[turn]
         left = 0 if turn == last_grads else len(turns) - 1 - turn
         ready = (meta,) if turn < 2 else (marks[turn - 2],)
         if turn == len(turns) - 1:
             ready += (returned,)
-        marks.append(use(kind, hop % chips, (arrived[turn], send(arrived[turn], swap, *ready)), left))
         if turn == last_grads:
             returned = lax.all_to_all(totals[2], "lat", split_axis=0, concat_axis=0, tiled=True)
+            totals = totals[:2]
+        marks.append(use(kind, hop % chips, (arrived[turn], send(arrived[turn], swap, *ready)), left))
 
     use("grads", 0, (grad_recon, own_grads))
     use("inputs", 0, (inputs, own_inputs))
@@ -289,20 +295,25 @@
     for turn, (kind, hop) in enumerate(turns):
         if turn >= LAG:
             arrive(turn - LAG)
-        ready = () if turn < 3 else (meta,) if turn < LAG else (marks[turn - LAG],)
+        ready = () if turn < 2 else (meta,) if turn < LAG else (marks[turn - LAG],)
         rows = send(held[kind, hop > 0], onward if hop > 0 else backward, *ready)
         held[kind, hop > 0] = rows
         arrived.append(rows)
     for turn in range(len(turns) - LAG, len(turns)):
         arrive(turn)
-    latent_grads = pick_returned(after(returned, encoder_grad), own_t)
+    lat = totals[2]
+    sent_back = lax.ppermute(lat[0], "lat", second), lax.ppermute(lat[1], "lat", across)
+    nearest = jnp.asarray(sources)[me, 2, 0]
+    latent_grads = pick_returned(after(returned, encoder_grad), own_t, (nearest, nearest ^ 1), sent_back)
     return (totals[0], encoder_grad, totals[1].reshape(latent_count), latent_grads)
 
 
-def pick_returned(returned, own_t):
+def pick_returned(returned, own_t, more_owners=(), more=()):
     owner_id = jnp.arange(returned.shape[0], dtype=jnp.int32)[:, None, None, None]
-    picked = jnp.where(own_t[None, :, None, :] == owner_id, returned[:, None, :, :], 0.0)
-    return jnp.sum(picked, axis=0).reshape(-1, own_t.shape[1]).T
+    picked = jnp.sum(jnp.where(own_t[None, :, None, :] == owner_id, returned[:, None, :, :], 0.0), axis=0)
+    for owner, sent_back in zip(more_owners, more):
+        picked += jnp.where(own_t[:, None, :] == owner, sent_back[None], 0.0)
+    return picked.reshape(-1, own_t.shape[1]).T
 
 
 def build_kernel(block_count, per_block, me_ref, meta_ref, acts_ref, cols_ref):

time: 165 us -> 169 us (1.024)
  starting transfers between devices: 24.1 us -> 20.8 us
  local copies, waits for them, and re-layouts: 7.23 us -> 10.2 us
  Pallas kernels: 43.6 us -> 45.7 us
    ppermute x30, starting transfers between devices: 14.2 us -> 7.31 us  [send(): return lax.ppermute(after(rows, *first) if first else rows, 'lat', way)]
    ppermute x0 -> x2, starting transfers between devices: none -> 2.99 us  [the longest x1 2.49 us: by_ring(): lax.ppermute(lat[1], 'lat', across)]
    unnamed x16 -> x18, local copies, waits for them, and re-layouts: 6.53 us -> 8.28 us
    pallas_call x1 -> x2, Pallas kernels: 5.06 us -> 6.08 us  [late_input_step(): pl.pallas_call(last_input_kernel if last else late_input_kernel, in_specs...]
    pallas_call x7 -> x6, Pallas kernels: 10.6 us -> 10.2 us  [input_step(): pl.pallas_call(input_kernel, in_specs=[whole] * (3 + len(totals)), out_sp...]
  transfers between devices with their start and end apart: 32 -> 34, of which waited for: 12 -> 11; matrix products, arithmetic and copies ran while one was open for 0% -> 2% of each run, Pallas kernels for 23% -> 27%
where the time goes in v13:
time: 169 us
  waiting for transfers between devices  88.1 us (52%)
  Pallas kernels  45.7 us (27%)
  starting transfers between devices  20.8 us (12%)
  local copies, waits for them, and re-layouts  10.2 us (6%)
  other arithmetic  2.27 us (1%)
    ppermute x30, waiting for transfers between devices, send(): return lax.ppermute(after(rows, *first) if first else rows, 'lat', way)  69.7 us
    pallas_call x8, Pallas kernels, grad_step(): pl.pallas_call(functools.partial(grad_kernel, per_block), in_specs=[scala...  27.9 us
    all_to_all x1, waiting for transfers between devices, by_ring(): meta = lax.all_to_all(meta, 'lat', split_axis=0, concat_axis=0, tiled=True)  18.4 us
    pallas_call x6, Pallas kernels, input_step(): pl.pallas_call(input_kernel, in_specs=[whole] * (3 + len(totals)), out_sp...  10.2 us
    unnamed x18, local copies, waits for them, and re-layouts  8.28 us
    ppermute x30, starting transfers between devices, send(): return lax.ppermute(after(rows, *first) if first else rows, 'lat', way)  7.31 us
    all_to_all x1, starting transfers between devices, by_ring(): meta = lax.all_to_all(meta, 'lat', split_axis=0, concat_axis=0, tiled=True)  6.37 us
    pallas_call x2, Pallas kernels, late_input_step(): pl.pallas_call(last_input_kernel if last else late_input_kernel, in_specs...  6.08 us
  transfers between devices with their start and end apart: 34, of which 11 were waited for; matrix products, arithmetic and copies ran while one was open for 2% of the time, Pallas kernels for 27%

profile of v13, /device:TPU:0, one launch (start us, length us, event | category | flops | bytes accessed | tf_op | source)
XLA Modules:
  0.0 168.7 jit_solution(13907232026630604135)
XLA Ops:
  0.6 3.1 %collective-permute-start = (bf16[128,3584]{1,0:T(8,128)(2,1)}, bf16[128,3584]{1,0:T(8,128)(2,1)}, u32[]{:S(2)}, u32[]{:S(2)}) collective-permute-start(bf16[128,3584]{1,0:T(8,128)(2,1)} %mine_ref.2), channel_id=1, source_target_pairs={{0,4},{4,8},{8,12},{12,14},{14,10},{10,6},{6,2},{2,0},{1,3},{5,1},... | collective-permute-start | bytes 2752520 | tf_op jit(solution)/shard_map/ppermute | solution.py:254
  3.7 1.5 meta.1
  5.3 6.4 %all-to-all-start = ((bf16[16,32,128]{2,1,0:T(8,128)(2,1)}), bf16[16,32,128]{2,1,0:T(8,128)(2,1)S(1)}, u32[]{:S(2)}, u32[]{:S(2)}) async-start(bf16[16,32,128]{2,1,0:T(8,128)(2,1)} %meta.1), calls=%async_computation | async-start | bytes 262144 | tf_op jit(solution)/shard_map/all_to_all | solution.py:194
  12.0 18.4 %all-to-all-done.meta_ref = bf16[16,32,128]{2,1,0:T(8,128)(2,1)S(1)} async-done(((bf16[16,32,128]{2,1,0:T(8,128)(2,1)}), bf16[16,32,128]{2,1,0:T(8,128)(2,1)S(1)}, u32[]{:S(2)}, u32[]{:S(2)}) %all-to-all-start) | async-done | bytes 131104 | tf_op jit(solution)/shard_map/all_to_all | solution.py:194
  31.0 1.7 %collective-permute-start.15 = (bf16[128,3584]{1,0:T(8,128)(2,1)}, bf16[128,3584]{1,0:T(8,128)(2,1)S(1)}, u32[]{:S(2)}, u32[]{:S(2)}) collective-permute-start(bf16[128,3584]{1,0:T(8,128)(2,1)} %mine_ref.3), channel_id=1, source_target_pairs={{0,4},{4,8},{8,12},{12,14},{14,10},{10,6},{6,2},{2,0},{1,3},{5,1},... | collective-permute-start | bytes 2752520 | tf_op jit(solution)/shard_map/ppermute | solution.py:254
  33.4 1.5 copy-done.5
  36.1 3.3 %grad_step.8 = (f32[256,3584]{1,0:T(8,128)S(1)}, f32[256,128]{1,0:T(8,128)S(1)}, f32[16,16,128]{2,1,0:T(8,128)S(1)}, bf16[256,256]{1,0:T(8,128)(2,1)S(1)}) custom-call(s32[2]{0:T(128)S(1)} %get-tuple-element.109.order_ref, bf16[16,32,128]{2,1,0:T(8,128)(2,1)S(1)} %all-to-all-done.meta_ref, bf16[256,3584]{1,0:T(8,128)(2,1)S(1)} %copy-done.5, ...), custom_call_target="tpu_custom_call" | custom-call | flops 1 | bytes 1 | tf_op jit(solution)/shard_map/grad_step/pallas_call | solution.py:202
  39.4 3.8 %grad_step.9 = (f32[256,3584]{1,0:T(8,128)S(1)}, f32[256,128]{1,0:T(8,128)S(1)}, f32[16,16,128]{2,1,0:T(8,128)S(1)}, bf16[256,256]{1,0:T(8,128)(2,1)S(1)}) custom-call(s32[2]{0:T(128)S(1)} %get-tuple-element.110.order_ref, bf16[16,32,128]{2,1,0:T(8,128)(2,1)S(1)} %all-to-all-done.meta_ref, ...), custom_call_target="tpu_custom_call", output_to_operand_aliasing={{0}: (5, {}), {1}: (6, {})} | custom-call | flops 1 | bytes 1 | tf_op jit(solution)/shard_map/grad_step/pallas_call | solution.py:202
  44.7 3.5 %grad_step.10 = (f32[256,3584]{1,0:T(8,128)S(1)}, f32[256,128]{1,0:T(8,128)S(1)}, f32[16,16,128]{2,1,0:T(8,128)S(1)}, bf16[256,256]{1,0:T(8,128)(2,1)S(1)}) custom-call(s32[2]{0:T(128)S(1)} %get-tuple-element.107.order_ref, bf16[16,32,128]{2,1,0:T(8,128)(2,1)S(1)} %all-to-all-done.meta_ref, ...), custom_call_target="tpu_custom_call", output_to_operand_aliasing={{0}: (5, {}), {1}: (6, {})} | custom-call | flops 1 | bytes 1 | tf_op jit(solution)/shard_map/grad_step/pallas_call | solution.py:202
  48.2 5.8 %collective-permute-done.15.mine_ref = bf16[128,3584]{1,0:T(8,128)(2,1)S(1)} collective-permute-done((bf16[128,3584]{1,0:T(8,128)(2,1)}, bf16[128,3584]{1,0:T(8,128)(2,1)S(1)}, u32[]{:S(2)}, u32[]{:S(2)}) %collective-permute-start.15) | collective-permute-done | bytes 917536 | tf_op jit(solution)/shard_map/ppermute | solution.py:254
  54.1 2.9 %grad_step.11 = (f32[256,3584]{1,0:T(8,128)S(1)}, f32[256,128]{1,0:T(8,128)S(1)}, f32[16,16,128]{2,1,0:T(8,128)S(1)}, bf16[256,256]{1,0:T(8,128)(2,1)S(1)}) custom-call(s32[2]{0:T(128)S(1)} %get-tuple-element.108.order_ref, bf16[16,32,128]{2,1,0:T(8,128)(2,1)S(1)} %all-to-all-done.meta_ref, ...), custom_call_target="tpu_custom_call", output_to_operand_aliasing={{0}: (5, {}), {1}: (6, {})} | custom-call | flops 1 | bytes 1 | tf_op jit(solution)/shard_map/grad_step/pallas_call | solution.py:202
  57.0 6.9 %collective-permute-done.4.mine_ref = bf16[128,3584]{1,0:T(8,128)(2,1)S(1)} collective-permute-done((bf16[128,3584]{1,0:T(8,128)(2,1)S(1)}, bf16[128,3584]{1,0:T(8,128)(2,1)S(1)}, u32[]{:S(2)}, u32[]{:S(2)}) %collective-permute-start.4) | collective-permute-done | bytes 917536 | tf_op jit(solution)/shard_map/ppermute | solution.py:254
  63.9 1.9 %input_step.6.refs_0_ = f32[3584,256]{1,0:T(8,128)S(1)} custom-call(bf16[256,256]{1,0:T(8,128)(2,1)S(1)} %get-tuple-element.85.pre_ref, bf16[128,3584]{1,0:T(8,128)(2,1)} %mine_ref.3, bf16[128,3584]{1,0:T(8,128)(2,1)S(1)} %collective-permute-done.18.theirs_ref), custom_call_target="tpu_custom_call" | custom-call | flops 1 | bytes 1 | tf_op jit(solution)/shard_map/input_step/pallas_call | solution.py:225
  67.2 6.5 %collective-permute-done.16.mine_ref = bf16[128,3584]{1,0:T(8,128)(2,1)S(1)} collective-permute-done((bf16[128,3584]{1,0:T(8,128)(2,1)S(1)}, bf16[128,3584]{1,0:T(8,128)(2,1)S(1)}, u32[]{:S(2)}, u32[]{:S(2)}) %collective-permute-start.16) | collective-permute-done | bytes 917536 | tf_op jit(solution)/shard_map/ppermute | solution.py:254
  73.8 2.9 %grad_step.12 = (f32[256,3584]{1,0:T(8,128)S(1)}, f32[256,128]{1,0:T(8,128)S(1)}, f32[16,16,128]{2,1,0:T(8,128)S(1)}, bf16[256,256]{1,0:T(8,128)(2,1)S(1)}) custom-call(s32[2]{0:T(128)S(1)} %get-tuple-element.106.order_ref, bf16[16,32,128]{2,1,0:T(8,128)(2,1)S(1)} %all-to-all-done.meta_ref, ...), custom_call_target="tpu_custom_call", output_to_operand_aliasing={{0}: (5, {}), {1}: (6, {})} | custom-call | flops 1 | bytes 1 | tf_op jit(solution)/shard_map/grad_step/pallas_call | solution.py:202
  76.7 6.8 %collective-permute-done.8.mine_ref = bf16[128,3584]{1,0:T(8,128)(2,1)S(1)} collective-permute-done((bf16[128,3584]{1,0:T(8,128)(2,1)S(1)}, bf16[128,3584]{1,0:T(8,128)(2,1)S(1)}, u32[]{:S(2)}, u32[]{:S(2)}) %collective-permute-start.8) | collective-permute-done | bytes 917536 | tf_op jit(solution)/shard_map/ppermute | solution.py:254
  85.0 8.3 %collective-permute-done.19.mine_ref = bf16[128,3584]{1,0:T(8,128)(2,1)S(1)} collective-permute-done((bf16[128,3584]{1,0:T(8,128)(2,1)S(1)}, bf16[128,3584]{1,0:T(8,128)(2,1)S(1)}, u32[]{:S(2)}, u32[]{:S(2)}) %collective-permute-start.19) | collective-permute-done | bytes 917536 | tf_op jit(solution)/shard_map/ppermute | solution.py:254
  93.4 2.9 %grad_step.13 = (f32[256,3584]{1,0:T(8,128)S(1)}, f32[256,128]{1,0:T(8,128)S(1)}, f32[16,16,128]{2,1,0:T(8,128)S(1)}, bf16[256,256]{1,0:T(8,128)(2,1)S(1)}) custom-call(s32[2]{0:T(128)S(1)} %get-tuple-element.105.order_ref, bf16[16,32,128]{2,1,0:T(8,128)(2,1)S(1)} %all-to-all-done.meta_ref, ...), custom_call_target="tpu_custom_call", output_to_operand_aliasing={{0}: (5, {}), {1}: (6, {})} | custom-call | flops 1 | bytes 1 | tf_op jit(solution)/shard_map/grad_step/pallas_call | solution.py:202
  96.3 6.8 %collective-permute-done.10.mine_ref = bf16[128,3584]{1,0:T(8,128)(2,1)S(1)} collective-permute-done((bf16[128,3584]{1,0:T(8,128)(2,1)S(1)}, bf16[128,3584]{1,0:T(8,128)(2,1)S(1)}, u32[]{:S(2)}, u32[]{:S(2)}) %collective-permute-start.10) | collective-permute-done | bytes 917536 | tf_op jit(solution)/shard_map/ppermute | solution.py:254
  104.6 8.4 %collective-permute-done.21.mine_ref = bf16[128,3584]{1,0:T(8,128)(2,1)S(1)} collective-permute-done((bf16[128,3584]{1,0:T(8,128)(2,1)S(1)}, bf16[128,3584]{1,0:T(8,128)(2,1)S(1)}, u32[]{:S(2)}, u32[]{:S(2)}) %collective-permute-start.21) | collective-permute-done | bytes 917536 | tf_op jit(solution)/shard_map/ppermute | solution.py:254
  113.1 3.6 %grad_step.14 = (f32[256,3584]{1,0:T(8,128)S(1)}, f32[256,128]{1,0:T(8,128)S(1)}, f32[16,16,128]{2,1,0:T(8,128)}, bf16[256,256]{1,0:T(8,128)(2,1)S(1)}) custom-call(s32[2]{0:T(128)S(1)} %get-tuple-element.104.order_ref, bf16[16,32,128]{2,1,0:T(8,128)(2,1)S(1)} %all-to-all-done.meta_ref, ...), custom_call_target="tpu_custom_call", output_to_operand_aliasing={{0}: (5, {}), {1}: (6, {})} | custom-call | flops 1 | bytes 1 | tf_op jit(solution)/shard_map/grad_step/pallas_call | solution.py:202
  116.6 6.3 %collective-permute-done.12.mine_ref = bf16[128,3584]{1,0:T(8,128)(2,1)} collective-permute-done((bf16[128,3584]{1,0:T(8,128)(2,1)S(1)}, bf16[128,3584]{1,0:T(8,128)(2,1)}, u32[]{:S(2)}, u32[]{:S(2)}) %collective-permute-start.12) | collective-permute-done | bytes 917536 | tf_op jit(solution)/shard_map/ppermute | solution.py:254
  124.4 1.8 %copy-done = f32[3584,256]{1,0:T(8,128)} copy-done((f32[3584,256]{1,0:T(8,128)}, f32[3584,256]{1,0:T(8,128)S(1)}, u32[]{:S(2)}) %copy-start) | copy-done | bytes 3670040
  126.1 13.0 %collective-permute-done.23.mine_ref = bf16[128,3584]{1,0:T(8,128)(2,1)} collective-permute-done((bf16[128,3584]{1,0:T(8,128)(2,1)S(1)}, bf16[128,3584]{1,0:T(8,128)(2,1)}, u32[]{:S(2)}, u32[]{:S(2)}) %collective-permute-start.23) | collective-permute-done | bytes 917536 | tf_op jit(solution)/shard_map/ppermute | solution.py:254
  139.1 4.2 %all-to-all-start.1 = ((f32[16,16,128]{2,1,0:T(8,128)}), f32[16,16,128]{2,1,0:T(8,128)}, u32[]{:S(2)}, u32[]{:S(2)}) async-start(f32[16,16,128]{2,1,0:T(8,128)} %get-tuple-element.94), calls=%async_computation.1 | async-start | bytes 262144 | tf_op jit(solution)/shard_map/all_to_all | solution.py:288
  143.3 2.0 %copy-done.4 = f32[256,3584]{1,0:T(8,128)S(1)} copy-done((f32[256,3584]{1,0:T(8,128)S(1)}, f32[256,3584]{1,0:T(8,128)}, u32[]{:S(2)}) %copy-start.4) | copy-done | bytes 3670040
  145.4 5.0 %grad_step.15 = (bf16[256,3584]{1,0:T(8,128)(2,1)}, f32[1,256]{1,0:T(1,128)}, f32[2,16,128]{2,1,0:T(8,128)S(1)}, bf16[256,256]{1,0:T(8,128)(2,1)S(1)}) custom-call(s32[2]{0:T(128)S(1)} %get-tuple-element.111.order_ref, bf16[16,32,128]{2,1,0:T(8,128)(2,1)S(1)} %all-to-all-done.meta_ref, bf16[256,3584]{1,0:T(8,128)(2,1)S(1)} %copy-done.6, ...), custom_call_target="tpu_custom_call" | custom-call | flops 1 | bytes 1 | tf_op jit(solution)/shard_map/grad_step/pallas_call | solution.py:202
  150.8 2.8 %input_step.11.total_ref = f32[3584,256]{1,0:T(8,128)S(1)} custom-call(bf16[256,256]{1,0:T(8,128)(2,1)S(1)} %get-tuple-element.93.pre_ref, bf16[128,3584]{1,0:T(8,128)(2,1)} %collective-permute-done.23.mine_ref, bf16[128,3584]{1,0:T(8,128)(2,1)} %collective-permute-done.26.theirs_ref, f32[3584,256]{1,0:T(8,128)S(1)} %copy-done.1), custom_call_target="tpu_custom_call", output_to_operand_aliasing={{}: (3, {})} | custom-call | flops 1 | bytes 1 | tf_op jit(solution)/shard_map/input_step/pallas_call | solution.py:225
  153.5 1.8 %copy-done.2 = f32[3584,256]{1,0:T(8,128)} copy-done((f32[3584,256]{1,0:T(8,128)}, f32[3584,256]{1,0:T(8,128)S(1)}, u32[]{:S(2)}) %copy-start.2) | copy-done | bytes 3670040
  158.0 2.5 %collective-permute-start.31 = (f32[16,128]{1,0:T(8,128)S(1)}, f32[16,128]{1,0:T(8,128)S(1)}, u32[]{:S(2)}, u32[]{:S(2)}) collective-permute-start(f32[16,128]{1,0:T(8,128)S(1)} %get-tuple-element.103), channel_id=1, source_target_pairs={{8,1},{12,5},{14,9},{10,13},{6,15},{2,11},{0,7},{4,3},{7,0},{3,4},... | collective-permute-start | bytes 24584 | tf_op jit(solution)/shard_map/ppermute | solution.py:305
  161.0 3.3 %late_input_step.2.total_ref = f32[3584,256]{1,0:T(8,128)S(1)} custom-call(bf16[256,256]{1,0:T(8,128)(2,1)S(1)} %get-tuple-element.96.pre_ref, bf16[128,3584]{1,0:T(8,128)(2,1)S(1)} %collective-permute-done.28.mine_ref, bf16[128,3584]{1,0:T(8,128)(2,1)S(1)} %collective-permute-done.29.theirs_ref, f32[3584,256]{1,0:T(8,128)} %copy-done.2), custom_call_target="tpu_custom_call" | custom-call | flops 1 | bytes 1 | tf_op jit(solution)/shard_map/late_input_step/pallas_call | solution.py:239
  164.3 2.8 %late_input_step.3 = bf16[3584,256]{1,0:T(8,128)(2,1)} custom-call(bf16[256,256]{1,0:T(8,128)(2,1)S(1)} %get-tuple-element.81.pre_ref, bf16[128,3584]{1,0:T(8,128)(2,1)} %collective-permute-done.25.mine_ref, bf16[128,3584]{1,0:T(8,128)(2,1)S(1)} %collective-permute-done.27.theirs_ref, f32[3584,256]{1,0:T(8,128)S(1)} %late_input_step.2.total_ref), custom_call_target="tpu_custom_call" | custom-call | flops 1 | bytes 1 | tf_op jit(solution)/shard_map/late_input_step/pallas_call | solution.py:239
  (79 shorter events, 14.9 us)
Async XLA Ops:
  0.6 29.8 %collective-permute-start = (bf16[128,3584]{1,0:T(8,128)(2,1)}, bf16[128,3584]{1,0:T(8,128)(2,1)}, u32[]{:S(2)}, u32[]{:S(2)}) collective-permute-start(bf16[128,3584]{1,0:T(8,128)(2,1)} %mine_ref.2), channel_id=1, source_target_pairs={{0,4},{4,8},{8,12},{12,14},{14,10},{10,6},{6,2},{2,0},{1,3},{5,1},... | collective-permute-start | bytes 2752520 | tf_op jit(solution)/shard_map/ppermute | solution.py:254
  3.7 27.0 %collective-permute-start.6 = (bf16[128,3584]{1,0:T(8,128)(2,1)}, bf16[128,3584]{1,0:T(8,128)(2,1)S(1)}, u32[]{:S(2)}, u32[]{:S(2)}) collective-permute-start(bf16[128,3584]{1,0:T(8,128)(2,1)} %mine_ref.2), channel_id=1, source_target_pairs={{4,0},{8,4},{12,8},{14,12},{10,14},{6,10},{2,6},{0,2},{3,1},{1,5},... | collective-permute-start | bytes 2752520 | tf_op jit(solution)/shard_map/ppermute | solution.py:254
  5.3 25.2 %all-to-all-start = ((bf16[16,32,128]{2,1,0:T(8,128)(2,1)}), bf16[16,32,128]{2,1,0:T(8,128)(2,1)S(1)}, u32[]{:S(2)}, u32[]{:S(2)}) async-start(bf16[16,32,128]{2,1,0:T(8,128)(2,1)} %meta.1), calls=%async_computation | async-start | bytes 262144 | tf_op jit(solution)/shard_map/all_to_all | solution.py:194
  11.6 21.8 %collective-permute-start.3 = (bf16[128,3584]{1,0:T(8,128)(2,1)}, bf16[128,3584]{1,0:T(8,128)(2,1)}, u32[]{:S(2)}, u32[]{:S(2)}) collective-permute-start(bf16[128,3584]{1,0:T(8,128)(2,1)} %mine_ref.2), channel_id=1, source_target_pairs={{0,1},{1,0},{2,3},{3,2},{4,5},{5,4},{6,7},{7,6},{8,9},{9,8},{10,11... | collective-permute-start | bytes 2752520 | tf_op jit(solution)/shard_map/ppermute | solution.py:254
  30.5 9.0 %collective-permute-start.2 = (bf16[128,3584]{1,0:T(8,128)(2,1)}, bf16[128,3584]{1,0:T(8,128)(2,1)}, u32[]{:S(2)}, u32[]{:S(2)}) collective-permute-start(bf16[128,3584]{1,0:T(8,128)(2,1)} %collective-permute-done.mine_ref), channel_id=1, source_target_pairs={{0,1},{1,0},{2,3},{3,2},{4,5},{5,4},{6,7},{7,6},{8,9},{9,8},{10,11... | collective-permute-start | bytes 2752520 | tf_op jit(solution)/shard_map/ppermute | solution.py:254
  30.6 13.6 %collective-permute-start.1 = (bf16[128,3584]{1,0:T(8,128)(2,1)}, bf16[128,3584]{1,0:T(8,128)(2,1)S(1)}, u32[]{:S(2)}, u32[]{:S(2)}) collective-permute-start(bf16[128,3584]{1,0:T(8,128)(2,1)} %collective-permute-done.mine_ref), channel_id=1, source_target_pairs={{0,4},{4,8},{8,12},{12,14},{14,10},{10,6},{6,2},{2,0},{1,3},{5,1},... | collective-permute-start | bytes 2752520 | tf_op jit(solution)/shard_map/ppermute | solution.py:254
  30.7 14.0 %collective-permute-start.7 = (bf16[128,3584]{1,0:T(8,128)(2,1)S(1)}, bf16[128,3584]{1,0:T(8,128)(2,1)}, u32[]{:S(2)}, u32[]{:S(2)}) collective-permute-start(bf16[128,3584]{1,0:T(8,128)(2,1)S(1)} %collective-permute-done.6.mine_ref), channel_id=1, source_target_pairs={{0,1},{1,0},{2,3},{3,2},{4,5},{5,4},{6,7},{7,6},{8,9},{9,8},{10,11... | collective-permute-start | bytes 2752520 | tf_op jit(solution)/shard_map/ppermute | solution.py:254
  31.0 23.0 %collective-permute-start.15 = (bf16[128,3584]{1,0:T(8,128)(2,1)}, bf16[128,3584]{1,0:T(8,128)(2,1)S(1)}, u32[]{:S(2)}, u32[]{:S(2)}) collective-permute-start(bf16[128,3584]{1,0:T(8,128)(2,1)} %mine_ref.3), channel_id=1, source_target_pairs={{0,4},{4,8},{8,12},{12,14},{14,10},{10,6},{6,2},{2,0},{1,3},{5,1},... | collective-permute-start | bytes 2752520 | tf_op jit(solution)/shard_map/ppermute | solution.py:254
  44.2 9.9 %collective-permute-start.5 = (bf16[128,3584]{1,0:T(8,128)(2,1)S(1)}, bf16[128,3584]{1,0:T(8,128)(2,1)S(1)}, u32[]{:S(2)}, u32[]{:S(2)}) collective-permute-start(bf16[128,3584]{1,0:T(8,128)(2,1)S(1)} %collective-permute-done.1.mine_ref), channel_id=1, source_target_pairs={{0,1},{1,0},{2,3},{3,2},{4,5},{5,4},{6,7},{7,6},{8,9},{9,8},{10,11... | collective-permute-start | bytes 2752520 | tf_op jit(solution)/shard_map/ppermute | solution.py:254
  44.2 19.7 %collective-permute-start.4 = (bf16[128,3584]{1,0:T(8,128)(2,1)S(1)}, bf16[128,3584]{1,0:T(8,128)(2,1)S(1)}, u32[]{:S(2)}, u32[]{:S(2)}) collective-permute-start(bf16[128,3584]{1,0:T(8,128)(2,1)S(1)} %collective-permute-done.1.mine_ref), channel_id=1, source_target_pairs={{0,4},{4,8},{8,12},{12,14},{14,10},{10,6},{6,2},{2,0},{1,3},{5,1},... | collective-permute-start | bytes 2752520 | tf_op jit(solution)/shard_map/ppermute | solution.py:254
  44.3 19.7 %collective-permute-start.18 = (bf16[128,3584]{1,0:T(8,128)(2,1)}, bf16[128,3584]{1,0:T(8,128)(2,1)S(1)}, u32[]{:S(2)}, u32[]{:S(2)}) collective-permute-start(bf16[128,3584]{1,0:T(8,128)(2,1)} %mine_ref.3), channel_id=1, source_target_pairs={{0,1},{1,0},{2,3},{3,2},{4,5},{5,4},{6,7},{7,6},{8,9},{9,8},{10,11... | collective-permute-start | bytes 2752520 | tf_op jit(solution)/shard_map/ppermute | solution.py:254
  54.0 11.8 %collective-permute-start.17 = (bf16[128,3584]{1,0:T(8,128)(2,1)S(1)}, bf16[128,3584]{1,0:T(8,128)(2,1)S(1)}, u32[]{:S(2)}, u32[]{:S(2)}) collective-permute-start(bf16[128,3584]{1,0:T(8,128)(2,1)S(1)} %collective-permute-done.15.mine_ref), channel_id=1, source_target_pairs={{0,1},{1,0},{2,3},{3,2},{4,5},{5,4},{6,7},{7,6},{8,9},{9,8},{10,11... | collective-permute-start | bytes 2752520 | tf_op jit(solution)/shard_map/ppermute | solution.py:254
  54.0 19.7 %collective-permute-start.16 = (bf16[128,3584]{1,0:T(8,128)(2,1)S(1)}, bf16[128,3584]{1,0:T(8,128)(2,1)S(1)}, u32[]{:S(2)}, u32[]{:S(2)}) collective-permute-start(bf16[128,3584]{1,0:T(8,128)(2,1)S(1)} %collective-permute-done.15.mine_ref), channel_id=1, source_target_pairs={{0,4},{4,8},{8,12},{12,14},{14,10},{10,6},{6,2},{2,0},{1,3},{5,1},... | collective-permute-start | bytes 2752520 | tf_op jit(solution)/shard_map/ppermute | solution.py:254
  63.8 9.9 %collective-permute-start.9 = (bf16[128,3584]{1,0:T(8,128)(2,1)S(1)}, bf16[128,3584]{1,0:T(8,128)(2,1)S(1)}, u32[]{:S(2)}, u32[]{:S(2)}) collective-permute-start(bf16[128,3584]{1,0:T(8,128)(2,1)S(1)} %collective-permute-done.4.mine_ref), channel_id=1, source_target_pairs={{0,1},{1,0},{2,3},{3,2},{4,5},{5,4},{6,7},{7,6},{8,9},{9,8},{10,11... | collective-permute-start | bytes 2752520 | tf_op jit(solution)/shard_map/ppermute | solution.py:254
  63.9 19.7 %collective-permute-start.8 = (bf16[128,3584]{1,0:T(8,128)(2,1)S(1)}, bf16[128,3584]{1,0:T(8,128)(2,1)S(1)}, u32[]{:S(2)}, u32[]{:S(2)}) collective-permute-start(bf16[128,3584]{1,0:T(8,128)(2,1)S(1)} %collective-permute-done.4.mine_ref), channel_id=1, source_target_pairs={{0,4},{4,8},{8,12},{12,14},{14,10},{10,6},{6,2},{2,0},{1,3},{5,1},... | collective-permute-start | bytes 2752520 | tf_op jit(solution)/shard_map/ppermute | solution.py:254
  73.7 9.9 %collective-permute-start.20 = (bf16[128,3584]{1,0:T(8,128)(2,1)S(1)}, bf16[128,3584]{1,0:T(8,128)(2,1)S(1)}, u32[]{:S(2)}, u32[]{:S(2)}) collective-permute-start(bf16[128,3584]{1,0:T(8,128)(2,1)S(1)} %collective-permute-done.16.mine_ref), channel_id=1, source_target_pairs={{0,1},{1,0},{2,3},{3,2},{4,5},{5,4},{6,7},{7,6},{8,9},{9,8},{10,11... | collective-permute-start | bytes 2752520 | tf_op jit(solution)/shard_map/ppermute | solution.py:254
  73.7 19.7 %collective-permute-start.19 = (bf16[128,3584]{1,0:T(8,128)(2,1)S(1)}, bf16[128,3584]{1,0:T(8,128)(2,1)S(1)}, u32[]{:S(2)}, u32[]{:S(2)}) collective-permute-start(bf16[128,3584]{1,0:T(8,128)(2,1)S(1)} %collective-permute-done.16.mine_ref), channel_id=1, source_target_pairs={{0,4},{4,8},{8,12},{12,14},{14,10},{10,6},{6,2},{2,0},{1,3},{5,1},... | collective-permute-start | bytes 2752520 | tf_op jit(solution)/shard_map/ppermute | solution.py:254
  83.5 9.9 %collective-permute-start.11 = (bf16[128,3584]{1,0:T(8,128)(2,1)S(1)}, bf16[128,3584]{1,0:T(8,128)(2,1)S(1)}, u32[]{:S(2)}, u32[]{:S(2)}) collective-permute-start(bf16[128,3584]{1,0:T(8,128)(2,1)S(1)} %collective-permute-done.8.mine_ref), channel_id=1, source_target_pairs={{0,1},{1,0},{2,3},{3,2},{4,5},{5,4},{6,7},{7,6},{8,9},{9,8},{10,11... | collective-permute-start | bytes 2752520 | tf_op jit(solution)/shard_map/ppermute | solution.py:254
  83.5 19.7 %collective-permute-start.10 = (bf16[128,3584]{1,0:T(8,128)(2,1)S(1)}, bf16[128,3584]{1,0:T(8,128)(2,1)S(1)}, u32[]{:S(2)}, u32[]{:S(2)}) collective-permute-start(bf16[128,3584]{1,0:T(8,128)(2,1)S(1)} %collective-permute-done.8.mine_ref), channel_id=1, source_target_pairs={{0,4},{4,8},{8,12},{12,14},{14,10},{10,6},{6,2},{2,0},{1,3},{5,1},... | collective-permute-start | bytes 2752520 | tf_op jit(solution)/shard_map/ppermute | solution.py:254
  93.3 9.9 %collective-permute-start.22 = (bf16[128,3584]{1,0:T(8,128)(2,1)S(1)}, bf16[128,3584]{1,0:T(8,128)(2,1)S(1)}, u32[]{:S(2)}, u32[]{:S(2)}) collective-permute-start(bf16[128,3584]{1,0:T(8,128)(2,1)S(1)} %collective-permute-done.19.mine_ref), channel_id=1, source_target_pairs={{0,1},{1,0},{2,3},{3,2},{4,5},{5,4},{6,7},{7,6},{8,9},{9,8},{10,11... | collective-permute-start | bytes 2752520 | tf_op jit(solution)/shard_map/ppermute | solution.py:254
  93.3 19.7 %collective-permute-start.21 = (bf16[128,3584]{1,0:T(8,128)(2,1)S(1)}, bf16[128,3584]{1,0:T(8,128)(2,1)S(1)}, u32[]{:S(2)}, u32[]{:S(2)}) collective-permute-start(bf16[128,3584]{1,0:T(8,128)(2,1)S(1)} %collective-permute-done.19.mine_ref), channel_id=1, source_target_pairs={{0,4},{4,8},{8,12},{12,14},{14,10},{10,6},{6,2},{2,0},{1,3},{5,1},... | collective-permute-start | bytes 2752520 | tf_op jit(solution)/shard_map/ppermute | solution.py:254
  103.2 9.9 %collective-permute-start.13 = (bf16[128,3584]{1,0:T(8,128)(2,1)S(1)}, bf16[128,3584]{1,0:T(8,128)(2,1)S(1)}, u32[]{:S(2)}, u32[]{:S(2)}) collective-permute-start(bf16[128,3584]{1,0:T(8,128)(2,1)S(1)} %collective-permute-done.10.mine_ref), channel_id=1, source_target_pairs={{0,1},{1,0},{2,3},{3,2},{4,5},{5,4},{6,7},{7,6},{8,9},{9,8},{10,11... | collective-permute-start | bytes 2752520 | tf_op jit(solution)/shard_map/ppermute | solution.py:254
  103.2 19.8 %collective-permute-start.12 = (bf16[128,3584]{1,0:T(8,128)(2,1)S(1)}, bf16[128,3584]{1,0:T(8,128)(2,1)}, u32[]{:S(2)}, u32[]{:S(2)}) collective-permute-start(bf16[128,3584]{1,0:T(8,128)(2,1)S(1)} %collective-permute-done.10.mine_ref), channel_id=1, source_target_pairs={{0,4},{4,8},{8,12},{12,14},{14,10},{10,6},{6,2},{2,0},{1,3},{5,1},... | collective-permute-start | bytes 2752520 | tf_op jit(solution)/shard_map/ppermute | solution.py:254
  113.0 9.9 %collective-permute-start.24 = (bf16[128,3584]{1,0:T(8,128)(2,1)S(1)}, bf16[128,3584]{1,0:T(8,128)(2,1)S(1)}, u32[]{:S(2)}, u32[]{:S(2)}) collective-permute-start(bf16[128,3584]{1,0:T(8,128)(2,1)S(1)} %collective-permute-done.21.mine_ref), channel_id=1, source_target_pairs={{0,1},{1,0},{2,3},{3,2},{4,5},{5,4},{6,7},{7,6},{8,9},{9,8},{10,11... | collective-permute-start | bytes 2752520 | tf_op jit(solution)/shard_map/ppermute | solution.py:254
  113.0 26.1 %collective-permute-start.23 = (bf16[128,3584]{1,0:T(8,128)(2,1)S(1)}, bf16[128,3584]{1,0:T(8,128)(2,1)}, u32[]{:S(2)}, u32[]{:S(2)}) collective-permute-start(bf16[128,3584]{1,0:T(8,128)(2,1)S(1)} %collective-permute-done.21.mine_ref), channel_id=1, source_target_pairs={{0,4},{4,8},{8,12},{12,14},{14,10},{10,6},{6,2},{2,0},{1,3},{5,1},... | collective-permute-start | bytes 2752520 | tf_op jit(solution)/shard_map/ppermute | solution.py:254
  122.9 20.4 %collective-permute-start.14 = (bf16[128,3584]{1,0:T(8,128)(2,1)}, bf16[128,3584]{1,0:T(8,128)(2,1)}, u32[]{:S(2)}, u32[]{:S(2)}) collective-permute-start(bf16[128,3584]{1,0:T(8,128)(2,1)} %collective-permute-done.12.mine_ref), channel_id=1, source_target_pairs={{0,1},{1,0},{2,3},{3,2},{4,5},{5,4},{6,7},{7,6},{8,9},{9,8},{10,11... | collective-permute-start | bytes 2752520 | tf_op jit(solution)/shard_map/ppermute | solution.py:254
  122.9 27.4 %collective-permute-start.28 = (bf16[128,3584]{1,0:T(8,128)(2,1)}, bf16[128,3584]{1,0:T(8,128)(2,1)S(1)}, u32[]{:S(2)}, u32[]{:S(2)}) collective-permute-start(bf16[128,3584]{1,0:T(8,128)(2,1)} %mine_ref.3), channel_id=1, source_target_pairs={{4,0},{8,4},{12,8},{14,12},{10,14},{6,10},{2,6},{0,2},{3,1},{1,5},... | collective-permute-start | bytes 2752520 | tf_op jit(solution)/shard_map/ppermute | solution.py:254
  139.1 11.6 %collective-permute-start.26 = (bf16[128,3584]{1,0:T(8,128)(2,1)}, bf16[128,3584]{1,0:T(8,128)(2,1)}, u32[]{:S(2)}, u32[]{:S(2)}) collective-permute-start(bf16[128,3584]{1,0:T(8,128)(2,1)} %collective-permute-done.23.mine_ref), channel_id=1, source_target_pairs={{0,1},{1,0},{2,3},{3,2},{4,5},{5,4},{6,7},{7,6},{8,9},{9,8},{10,11... | collective-permute-start | bytes 2752520 | tf_op jit(solution)/shard_map/ppermute | solution.py:254
  139.1 16.2 %collective-permute-start.25 = (bf16[128,3584]{1,0:T(8,128)(2,1)}, bf16[128,3584]{1,0:T(8,128)(2,1)}, u32[]{:S(2)}, u32[]{:S(2)}) collective-permute-start(bf16[128,3584]{1,0:T(8,128)(2,1)} %collective-permute-done.23.mine_ref), channel_id=1, source_target_pairs={{0,4},{4,8},{8,12},{12,14},{14,10},{10,6},{6,2},{2,0},{1,3},{5,1},... | collective-permute-start | bytes 2752520 | tf_op jit(solution)/shard_map/ppermute | solution.py:254
  139.1 16.2 %all-to-all-start.1 = ((f32[16,16,128]{2,1,0:T(8,128)}), f32[16,16,128]{2,1,0:T(8,128)}, u32[]{:S(2)}, u32[]{:S(2)}) async-start(f32[16,16,128]{2,1,0:T(8,128)} %get-tuple-element.94), calls=%async_computation.1 | async-start | bytes 262144 | tf_op jit(solution)/shard_map/all_to_all | solution.py:288
  150.3 10.6 %collective-permute-start.29 = (bf16[128,3584]{1,0:T(8,128)(2,1)S(1)}, bf16[128,3584]{1,0:T(8,128)(2,1)S(1)}, u32[]{:S(2)}, u32[]{:S(2)}) collective-permute-start(bf16[128,3584]{1,0:T(8,128)(2,1)S(1)} %collective-permute-done.28.mine_ref), channel_id=1, source_target_pairs={{0,1},{1,0},{2,3},{3,2},{4,5},{5,4},{6,7},{7,6},{8,9},{9,8},{10,11... | collective-permute-start | bytes 2752520 | tf_op jit(solution)/shard_map/ppermute | solution.py:254
  158.0 10.1 %collective-permute-start.31 = (f32[16,128]{1,0:T(8,128)S(1)}, f32[16,128]{1,0:T(8,128)S(1)}, u32[]{:S(2)}, u32[]{:S(2)}) collective-permute-start(f32[16,128]{1,0:T(8,128)S(1)} %get-tuple-element.103), channel_id=1, source_target_pairs={{8,1},{12,5},{14,9},{10,13},{6,15},{2,11},{0,7},{4,3},{7,0},{3,4},... | collective-permute-start | bytes 24584 | tf_op jit(solution)/shard_map/ppermute | solution.py:305
  (11 other events, 52.4 us)

commit v14 on v13

--- a/solution.py
+++ b/solution.py
@@ -31,10 +31,7 @@
     onward += [(2 * ring[i] + 1, 2 * ring[(i - 1) % chips] + 1) for i in range(chips)]
     swap = [(i, i ^ 1) for i in range(peer_count)]
     backward = [(b, a) for a, b in onward]
-    target = dict(onward)
-    second = [(a, target[b]) for a, b in onward]
-    across = [(b, a ^ 1) for a, b in second]
-    return sources, onward, backward, swap, second, across
+    return sources, onward, backward, swap
 
 
 def meta_kernel(*refs):
@@ -67,8 +64,7 @@
     total_ref, bias_ref, lat_ref, pre_ref, acts_ref, bias_sum = refs[-6:]
     first, last = len(refs) == 6, bias_ref.shape[0] == 1
     bias_sum[...] = jnp.zeros_like(bias_sum) if first else refs[1][...]
-    if not last:
-        lat_ref[...] = jnp.zeros_like(lat_ref) if first else refs[2][...]
+    lat_ref[...] = jnp.zeros_like(lat_ref) if first else refs[2][...]
     latents, width = decoder_ref.shape
     tokens = mine_ref.shape[0]
     span = column_span(width)
@@ -102,7 +98,7 @@
                 dense_both.append(dense)
             pre_ref[block : block + 16, at] = jnp.concatenate(kept_both, axis=0).astype(jnp.bfloat16)
             acts_ref[block : block + 16, at] = jnp.concatenate(dense_both, axis=0).astype(jnp.bfloat16)
-        source = tile if last else order_ref[tile]
+        source = order_ref[tile]
         for k in range(per_block):
             lat_ref[source, k : k + 1, :] = jnp.sum(sums[k], axis=0, keepdims=True)
     for at in range(0, width, span):
@@ -171,7 +167,7 @@
     peer_count = lax.axis_size("lat")
     chips = peer_count // 2
     me = lax.axis_index("lat")
-    sources, onward, backward, swap, second, across = ring_tables(peer_count)
+    sources, onward, backward, swap = ring_tables(peer_count)
     order = jnp.asarray(sources)[me]
     own_t = owners.T
     whole = pl.BlockSpec(memory_space=pltpu.VMEM)
@@ -198,7 +194,6 @@
 
     def grad_step(hop, rows, totals, last):
         sums, lanes = (latent_count, width), (latent_count, token_count)
-        lat = (2 if last else peer_count, per_block, token_count)
         return pl.pallas_call(
             functools.partial(grad_kernel, per_block),
             in_specs=[scalars] + [whole] * (4 + len(totals)),
@@ -206,7 +201,7 @@
             out_shape=[
                 jax.ShapeDtypeStruct(sums, jnp.bfloat16) if last else pltpu.VMEM(sums, jnp.float32),
                 jax.ShapeDtypeStruct((1, latent_count), jnp.float32) if last else pltpu.VMEM(lanes, jnp.float32),
-                jax.ShapeDtypeStruct(lat, jnp.float32),
+                jax.ShapeDtypeStruct((peer_count, per_block, token_count), jnp.float32),
                 pltpu.VMEM((latent_count, step_tokens), jnp.bfloat16),
             ],
             scratch_shapes=[
@@ -253,10 +248,14 @@
     def send(rows, way, *first):
         return lax.ppermute(after(rows, *first) if first else rows, "lat", way)
 
-    turns = [("grads", 1), ("grads", -1)]
-    for hop in range(2, chips - 1):
-        turns += [("grads", hop), ("inputs", hop - 1)]
-    turns += [("inputs", -1), ("inputs", chips - 2)]
+    half = chips // 2
+    later = [("inputs", 1)]
+    for hop in range(1, half):
+        later += [("inputs", hop + 1), ("inputs", -hop)]
+    turns = []
+    for hop in range(1, half + 1):
+        turns += [("grads", hop)] + ([("grads", -hop)] if hop < half else []) + [later.pop(0)]
+    turns += later
     pres, totals, encoder_grad = {}, (), None
 
 
@@ -278,16 +277,15 @@
     returned = None
 
     def arrive(turn):
-        nonlocal returned, totals
+        nonlocal returned
         kind, hop = turns[turn]
         left = 0 if turn == last_grads else len(turns) - 1 - turn
         ready = (meta,) if turn < 2 else (marks[turn - 2],)
         if turn == len(turns) - 1:
             ready += (returned,)
+        marks.append(use(kind, hop % chips, (arrived[turn], send(arrived[turn], swap, *ready)), left))
         if turn == last_grads:
             returned = lax.all_to_all(totals[2], "lat", split_axis=0, concat_axis=0, tiled=True)
-            totals = totals[:2]
-        marks.append(use(kind, hop % chips, (arrived[turn], send(arrived[turn], swap, *ready)), left))
 
     use("grads", 0, (grad_recon, own_grads))
     use("inputs", 0, (inputs, own_inputs))
@@ -295,25 +293,20 @@
     for turn, (kind, hop) in enumerate(turns):
         if turn >= LAG:
             arrive(turn - LAG)
-        ready = () if turn < 2 else (meta,) if turn < LAG else (marks[turn - LAG],)
+        ready = () if turn < 3 else (meta,) if turn < LAG else (marks[turn - LAG],)
         rows = send(held[kind, hop > 0], onward if hop > 0 else backward, *ready)
         held[kind, hop > 0] = rows
         arrived.append(rows)
     for turn in range(len(turns) - LAG, len(turns)):
         arrive(turn)
-    lat = totals[2]
-    sent_back = lax.ppermute(lat[0], "lat", second), lax.ppermute(lat[1], "lat", across)
-    nearest = jnp.asarray(sources)[me, 2, 0]
-    latent_grads = pick_returned(after(returned, encoder_grad), own_t, (nearest, nearest ^ 1), sent_back)
+    latent_grads = pick_returned(after(returned, encoder_grad), own_t)
     return (totals[0], encoder_grad, totals[1].reshape(latent_count), latent_grads)
 
 
-def pick_returned(returned, own_t, more_owners=(), more=()):
+def pick_returned(returned, own_t):
     owner_id = jnp.arange(returned.shape[0], dtype=jnp.int32)[:, None, None, None]
-    picked = jnp.sum(jnp.where(own_t[None, :, None, :] == owner_id, returned[:, None, :, :], 0.0), axis=0)
-    for owner, sent_back in zip(more_owners, more):
-        picked += jnp.where(own_t[:, None, :] == owner, sent_back[None], 0.0)
-    return picked.reshape(-1, own_t.shape[1]).T
+    picked = jnp.where(own_t[None, :, None, :] == owner_id, returned[:, None, :, :], 0.0)
+    return jnp.sum(picked, axis=0).reshape(-1, own_t.shape[1]).T
 
 
 def build_kernel(block_count, per_block, me_ref, meta_ref, acts_ref, cols_ref):

time: 169 us -> 164 us (0.970)
  local copies, waits for them, and re-layouts: 10.2 us -> 7.23 us
  starting transfers between devices: 20.8 us -> 23.2 us
  Pallas kernels: 45.7 us -> 43.8 us
    ppermute x30, starting transfers between devices: 7.31 us -> 13.3 us  [send(): return lax.ppermute(after(rows, *first) if first else rows, 'lat', way)]
    ppermute x2 -> x0, starting transfers between devices: 2.99 us -> none  [the longest x1 2.49 us: by_ring(): lax.ppermute(lat[1], 'lat', across)]
    unnamed x18 -> x16, local copies, waits for them, and re-layouts: 8.28 us -> 6.53 us
  transfers between devices with their start and end apart: 34 -> 32, of which waited for: 11 -> 11; matrix products, arithmetic and copies ran while one was open for 2% -> 0% of each run, Pallas kernels for 27% -> 25%
where the time goes in v14:
time: 164 us; the launch traced here: 163 us
  waiting for transfers between devices  87.5 us (53%)
  Pallas kernels  43.8 us (27%)
  starting transfers between devices  23.2 us (14%)
  local copies, waits for them, and re-layouts  7.23 us (4%)
    ppermute x30, waiting for transfers between devices, send(): return lax.ppermute(after(rows, *first) if first else rows, 'lat', way)  68.5 us
    pallas_call x8, Pallas kernels, grad_step(): pl.pallas_call(functools.partial(grad_kernel, per_block), in_specs=[scala...  26.4 us
    all_to_all x1, waiting for transfers between devices, by_ring(): meta = lax.all_to_all(meta, 'lat', split_axis=0, concat_axis=0, tiled=True)  18.4 us
    ppermute x30, starting transfers between devices, send(): return lax.ppermute(after(rows, *first) if first else rows, 'lat', way)  13.3 us
    pallas_call x6, Pallas kernels, input_step(): pl.pallas_call(input_kernel, in_specs=[whole] * (3 + len(totals)), out_sp...  9.83 us
    unnamed x16, local copies, waits for them, and re-layouts  6.53 us
    all_to_all x1, starting transfers between devices, by_ring(): meta = lax.all_to_all(meta, 'lat', split_axis=0, concat_axis=0, tiled=True)  6.37 us
    pallas_call x2, Pallas kernels, late_input_step(): pl.pallas_call(last_input_kernel if last else late_input_kernel, in_specs...  6.08 us
  transfers between devices with their start and end apart: 32, of which 11 were waited for; matrix products, arithmetic and copies ran while one was open for 0% of the time, Pallas kernels for 25%

profile of v14, /device:TPU:0, one launch (start us, length us, event | category | flops | bytes accessed | tf_op | source)
XLA Modules:
  0.0 163.4 jit_solution(15884873847108775571)
XLA Ops:
  0.6 3.1 %collective-permute-start = (bf16[128,3584]{1,0:T(8,128)(2,1)}, bf16[128,3584]{1,0:T(8,128)(2,1)}, u32[]{:S(2)}, u32[]{:S(2)}) collective-permute-start(bf16[128,3584]{1,0:T(8,128)(2,1)} %mine_ref.2), channel_id=1, source_target_pairs={{0,4},{4,8},{8,12},{12,14},{14,10},{10,6},{6,2},{2,0},{1,3},{5,1},... | collective-permute-start | bytes 2752520 | tf_op jit(solution)/shard_map/ppermute | solution.py:249
  3.7 1.5 meta.1
  5.3 6.4 %all-to-all-start = ((bf16[16,32,128]{2,1,0:T(8,128)(2,1)}), bf16[16,32,128]{2,1,0:T(8,128)(2,1)S(1)}, u32[]{:S(2)}, u32[]{:S(2)}) async-start(bf16[16,32,128]{2,1,0:T(8,128)(2,1)} %meta.1), calls=%async_computation | async-start | bytes 262144 | tf_op jit(solution)/shard_map/all_to_all | solution.py:190
  12.0 18.4 %all-to-all-done.meta_ref = bf16[16,32,128]{2,1,0:T(8,128)(2,1)S(1)} async-done(((bf16[16,32,128]{2,1,0:T(8,128)(2,1)}), bf16[16,32,128]{2,1,0:T(8,128)(2,1)S(1)}, u32[]{:S(2)}, u32[]{:S(2)}) %all-to-all-start) | async-done | bytes 131104 | tf_op jit(solution)/shard_map/all_to_all | solution.py:190
  31.0 1.7 %collective-permute-start.1 = (bf16[128,3584]{1,0:T(8,128)(2,1)}, bf16[128,3584]{1,0:T(8,128)(2,1)S(1)}, u32[]{:S(2)}, u32[]{:S(2)}) collective-permute-start(bf16[128,3584]{1,0:T(8,128)(2,1)} %collective-permute-done.mine_ref), channel_id=1, source_target_pairs={{0,4},{4,8},{8,12},{12,14},{14,10},{10,6},{6,2},{2,0},{1,3},{5,1},... | collective-permute-start | bytes 2752520 | tf_op jit(solution)/shard_map/ppermute | solution.py:249
  33.6 1.5 copy-done.3
  36.3 3.3 %grad_step.8 = (f32[256,3584]{1,0:T(8,128)S(1)}, f32[256,128]{1,0:T(8,128)S(1)}, f32[16,16,128]{2,1,0:T(8,128)S(1)}, bf16[256,256]{1,0:T(8,128)(2,1)S(1)}) custom-call(s32[2]{0:T(128)S(1)} %get-tuple-element.121.order_ref, bf16[16,32,128]{2,1,0:T(8,128)(2,1)S(1)} %all-to-all-done.meta_ref, bf16[256,3584]{1,0:T(8,128)(2,1)S(1)} %copy-done.3, ...), custom_call_target="tpu_custom_call" | custom-call | flops 1 | bytes 1 | tf_op jit(solution)/shard_map/grad_step/pallas_call | solution.py:197
  39.6 3.8 %grad_step.9 = (f32[256,3584]{1,0:T(8,128)S(1)}, f32[256,128]{1,0:T(8,128)S(1)}, f32[16,16,128]{2,1,0:T(8,128)S(1)}, bf16[256,256]{1,0:T(8,128)(2,1)S(1)}) custom-call(s32[2]{0:T(128)S(1)} %get-tuple-element.122.order_ref, bf16[16,32,128]{2,1,0:T(8,128)(2,1)S(1)} %all-to-all-done.meta_ref, ...), custom_call_target="tpu_custom_call", output_to_operand_aliasing={{0}: (5, {}), {1}: (6, {})} | custom-call | flops 1 | bytes 1 | tf_op jit(solution)/shard_map/grad_step/pallas_call | solution.py:197
  44.2 3.6 %grad_step.10 = (f32[256,3584]{1,0:T(8,128)S(1)}, f32[256,128]{1,0:T(8,128)S(1)}, f32[16,16,128]{2,1,0:T(8,128)S(1)}, bf16[256,256]{1,0:T(8,128)(2,1)S(1)}) custom-call(s32[2]{0:T(128)S(1)} %get-tuple-element.119.order_ref, bf16[16,32,128]{2,1,0:T(8,128)(2,1)S(1)} %all-to-all-done.meta_ref, ...), custom_call_target="tpu_custom_call", output_to_operand_aliasing={{0}: (5, {}), {1}: (6, {})} | custom-call | flops 1 | bytes 1 | tf_op jit(solution)/shard_map/grad_step/pallas_call | solution.py:197
  47.8 12.8 %collective-permute-done.1.mine_ref = bf16[128,3584]{1,0:T(8,128)(2,1)S(1)} collective-permute-done((bf16[128,3584]{1,0:T(8,128)(2,1)}, bf16[128,3584]{1,0:T(8,128)(2,1)S(1)}, u32[]{:S(2)}, u32[]{:S(2)}) %collective-permute-start.1) | collective-permute-done | bytes 917536 | tf_op jit(solution)/shard_map/ppermute | solution.py:249
  61.4 1.4 input_step.7.refs_0_
  63.7 1.5 collective-permute-start.7
  65.1 2.9 %grad_step.11 = (f32[256,3584]{1,0:T(8,128)S(1)}, f32[256,128]{1,0:T(8,128)S(1)}, f32[16,16,128]{2,1,0:T(8,128)S(1)}, bf16[256,256]{1,0:T(8,128)(2,1)S(1)}) custom-call(s32[2]{0:T(128)S(1)} %get-tuple-element.120.order_ref, bf16[16,32,128]{2,1,0:T(8,128)(2,1)S(1)} %all-to-all-done.meta_ref, ...), custom_call_target="tpu_custom_call", output_to_operand_aliasing={{0}: (5, {}), {1}: (6, {})} | custom-call | flops 1 | bytes 1 | tf_op jit(solution)/shard_map/grad_step/pallas_call | solution.py:197
  68.0 6.0 %collective-permute-done.11.mine_ref = bf16[128,3584]{1,0:T(8,128)(2,1)S(1)} collective-permute-done((bf16[128,3584]{1,0:T(8,128)(2,1)S(1)}, bf16[128,3584]{1,0:T(8,128)(2,1)S(1)}, u32[]{:S(2)}, u32[]{:S(2)}) %collective-permute-start.11) | collective-permute-done | bytes 917536 | tf_op jit(solution)/shard_map/ppermute | solution.py:249
  74.1 2.9 %grad_step.12 = (f32[256,3584]{1,0:T(8,128)S(1)}, f32[256,128]{1,0:T(8,128)S(1)}, f32[16,16,128]{2,1,0:T(8,128)S(1)}, bf16[256,256]{1,0:T(8,128)(2,1)S(1)}) custom-call(s32[2]{0:T(128)S(1)} %get-tuple-element.116.order_ref, bf16[16,32,128]{2,1,0:T(8,128)(2,1)S(1)} %all-to-all-done.meta_ref, ...), custom_call_target="tpu_custom_call", output_to_operand_aliasing={{0}: (5, {}), {1}: (6, {})} | custom-call | flops 1 | bytes 1 | tf_op jit(solution)/shard_map/grad_step/pallas_call | solution.py:197
  77.0 13.6 %collective-permute-done.7.mine_ref = bf16[128,3584]{1,0:T(8,128)(2,1)S(1)} collective-permute-done((bf16[128,3584]{1,0:T(8,128)(2,1)S(1)}, bf16[128,3584]{1,0:T(8,128)(2,1)S(1)}, u32[]{:S(2)}, u32[]{:S(2)}) %collective-permute-start.7) | collective-permute-done | bytes 917536 | tf_op jit(solution)/shard_map/ppermute | solution.py:249
  90.6 1.4 input_step.8.refs_0_
  94.1 2.9 %grad_step.13 = (f32[256,3584]{1,0:T(8,128)S(1)}, f32[256,128]{1,0:T(8,128)S(1)}, f32[16,16,128]{2,1,0:T(8,128)S(1)}, bf16[256,256]{1,0:T(8,128)(2,1)S(1)}) custom-call(s32[2]{0:T(128)S(1)} %get-tuple-element.117.order_ref, bf16[16,32,128]{2,1,0:T(8,128)(2,1)S(1)} %all-to-all-done.meta_ref, ...), custom_call_target="tpu_custom_call", output_to_operand_aliasing={{0}: (5, {}), {1}: (6, {})} | custom-call | flops 1 | bytes 1 | tf_op jit(solution)/shard_map/grad_step/pallas_call | solution.py:197
  97.0 14.5 %collective-permute-done.20.mine_ref = bf16[128,3584]{1,0:T(8,128)(2,1)S(1)} collective-permute-done((bf16[128,3584]{1,0:T(8,128)(2,1)S(1)}, bf16[128,3584]{1,0:T(8,128)(2,1)S(1)}, u32[]{:S(2)}, u32[]{:S(2)}) %collective-permute-start.20) | collective-permute-done | bytes 917536 | tf_op jit(solution)/shard_map/ppermute | solution.py:249
  111.5 2.9 %grad_step.14 = (f32[256,3584]{1,0:T(8,128)S(1)}, f32[256,128]{1,0:T(8,128)S(1)}, f32[16,16,128]{2,1,0:T(8,128)S(1)}, bf16[256,256]{1,0:T(8,128)(2,1)S(1)}) custom-call(s32[2]{0:T(128)S(1)} %get-tuple-element.118.order_ref, bf16[16,32,128]{2,1,0:T(8,128)(2,1)S(1)} %all-to-all-done.meta_ref, ...), custom_call_target="tpu_custom_call", output_to_operand_aliasing={{0}: (5, {}), {1}: (6, {})} | custom-call | flops 1 | bytes 1 | tf_op jit(solution)/shard_map/grad_step/pallas_call | solution.py:197
  115.0 1.8 %collective-permute-start.21 = (bf16[128,3584]{1,0:T(8,128)(2,1)S(1)}, bf16[128,3584]{1,0:T(8,128)(2,1)S(1)}, u32[]{:S(2)}, u32[]{:S(2)}) collective-permute-start(bf16[128,3584]{1,0:T(8,128)(2,1)S(1)} %collective-permute-done.20.mine_ref), channel_id=1, source_target_pairs={{4,0},{8,4},{12,8},{14,12},{10,14},{6,10},{2,6},{0,2},{3,1},{1,5},... | collective-permute-start | bytes 2752520 | tf_op jit(solution)/shard_map/ppermute | solution.py:249
  118.2 13.6 %collective-permute-done.24.mine_ref = bf16[128,3584]{1,0:T(8,128)(2,1)S(1)} collective-permute-done((bf16[128,3584]{1,0:T(8,128)(2,1)S(1)}, bf16[128,3584]{1,0:T(8,128)(2,1)S(1)}, u32[]{:S(2)}, u32[]{:S(2)}) %collective-permute-start.24) | collective-permute-done | bytes 917536 | tf_op jit(solution)/shard_map/ppermute | solution.py:249
  131.8 4.1 %grad_step.15 = (bf16[256,3584]{1,0:T(8,128)(2,1)}, f32[1,256]{1,0:T(1,128)}, f32[16,16,128]{2,1,0:T(8,128)}, bf16[256,256]{1,0:T(8,128)(2,1)S(1)}) custom-call(s32[2]{0:T(128)S(1)} %get-tuple-element.123.order_ref, bf16[16,32,128]{2,1,0:T(8,128)(2,1)S(1)} %all-to-all-done.meta_ref, bf16[256,3584]{1,0:T(8,128)(2,1)S(1)} %copy-done.4, ...), custom_call_target="tpu_custom_call" | custom-call | flops 1 | bytes 1 | tf_op jit(solution)/shard_map/grad_step/pallas_call | solution.py:197
  136.5 1.6 collective-permute-start.22
  138.0 3.5 %all-to-all-start.1 = ((f32[16,16,128]{2,1,0:T(8,128)}), f32[16,16,128]{2,1,0:T(8,128)S(1)}, u32[]{:S(2)}, u32[]{:S(2)}) async-start(f32[16,16,128]{2,1,0:T(8,128)} %get-tuple-element.111), calls=%async_computation.1 | async-start | bytes 262144 | tf_op jit(solution)/shard_map/all_to_all | solution.py:288
  141.6 2.0 %copy-done.1 = f32[3584,256]{1,0:T(8,128)S(1)} copy-done((f32[3584,256]{1,0:T(8,128)S(1)}, f32[3584,256]{1,0:T(8,128)}, u32[]{:S(2)}) %copy-start.1) | copy-done | bytes 3670040
  143.6 2.5 %input_step.10.refs_0_ = f32[3584,256]{1,0:T(8,128)S(1)} custom-call(bf16[256,256]{1,0:T(8,128)(2,1)S(1)} %get-tuple-element.106.pre_ref, bf16[128,3584]{1,0:T(8,128)(2,1)S(1)} %collective-permute-done.24.mine_ref, bf16[128,3584]{1,0:T(8,128)(2,1)} %collective-permute-done.26.theirs_ref, f32[3584,256]{1,0:T(8,128)S(1)} %copy-done.1), custom_call_target="tpu_custom_call", output_to_operand_aliasing={{}: (3, {})} | custom-call | flops 1 | bytes 1 | tf_op jit(solution)/shard_map/input_step/pallas_call | solution.py:220
  146.1 5.4 %collective-permute-done.28.mine_ref = bf16[128,3584]{1,0:T(8,128)(2,1)S(1)} collective-permute-done((bf16[128,3584]{1,0:T(8,128)(2,1)S(1)}, bf16[128,3584]{1,0:T(8,128)(2,1)S(1)}, u32[]{:S(2)}, u32[]{:S(2)}) %collective-permute-start.28) | collective-permute-done | bytes 917536 | tf_op jit(solution)/shard_map/ppermute | solution.py:249
  151.5 2.5 %input_step.11.total_ref = f32[3584,256]{1,0:T(8,128)S(1)} custom-call(bf16[256,256]{1,0:T(8,128)(2,1)S(1)} %get-tuple-element.105.pre_ref, bf16[128,3584]{1,0:T(8,128)(2,1)S(1)} %collective-permute-done.21.mine_ref, bf16[128,3584]{1,0:T(8,128)(2,1)} %collective-permute-done.23.theirs_ref, ...), custom_call_target="tpu_custom_call", output_to_operand_aliasing={{}: (3, {})} | custom-call | flops 1 | bytes 1 | tf_op jit(solution)/shard_map/input_step/pallas_call | solution.py:220
  154.0 1.8 %copy-done.2 = f32[3584,256]{1,0:T(8,128)} copy-done((f32[3584,256]{1,0:T(8,128)}, f32[3584,256]{1,0:T(8,128)S(1)}, u32[]{:S(2)}) %copy-start.2) | copy-done | bytes 3670040
  156.6 3.3 %late_input_step.2.total_ref = f32[3584,256]{1,0:T(8,128)S(1)} custom-call(bf16[256,256]{1,0:T(8,128)(2,1)S(1)} %get-tuple-element.113.pre_ref, bf16[128,3584]{1,0:T(8,128)(2,1)S(1)} %collective-permute-done.28.mine_ref, bf16[128,3584]{1,0:T(8,128)(2,1)S(1)} %collective-permute-done.29.theirs_ref, f32[3584,256]{1,0:T(8,128)} %copy-done.2), custom_call_target="tpu_custom_call" | custom-call | flops 1 | bytes 1 | tf_op jit(solution)/shard_map/late_input_step/pallas_call | solution.py:234
  159.9 2.8 %late_input_step.3 = bf16[3584,256]{1,0:T(8,128)(2,1)} custom-call(bf16[256,256]{1,0:T(8,128)(2,1)S(1)} %get-tuple-element.100.pre_ref, bf16[128,3584]{1,0:T(8,128)(2,1)} %collective-permute-done.22.mine_ref, bf16[128,3584]{1,0:T(8,128)(2,1)S(1)} %collective-permute-done.27.theirs_ref, f32[3584,256]{1,0:T(8,128)S(1)} %late_input_step.2.total_ref), custom_call_target="tpu_custom_call" | custom-call | flops 1 | bytes 1 | tf_op jit(solution)/shard_map/late_input_step/pallas_call | solution.py:234
  (69 shorter events, 11.5 us)
Async XLA Ops:
  0.6 29.8 %collective-permute-start = (bf16[128,3584]{1,0:T(8,128)(2,1)}, bf16[128,3584]{1,0:T(8,128)(2,1)}, u32[]{:S(2)}, u32[]{:S(2)}) collective-permute-start(bf16[128,3584]{1,0:T(8,128)(2,1)} %mine_ref.2), channel_id=1, source_target_pairs={{0,4},{4,8},{8,12},{12,14},{14,10},{10,6},{6,2},{2,0},{1,3},{5,1},... | collective-permute-start | bytes 2752520 | tf_op jit(solution)/shard_map/ppermute | solution.py:249
  3.7 27.0 %collective-permute-start.8 = (bf16[128,3584]{1,0:T(8,128)(2,1)}, bf16[128,3584]{1,0:T(8,128)(2,1)S(1)}, u32[]{:S(2)}, u32[]{:S(2)}) collective-permute-start(bf16[128,3584]{1,0:T(8,128)(2,1)} %mine_ref.2), channel_id=1, source_target_pairs={{4,0},{8,4},{12,8},{14,12},{10,14},{6,10},{2,6},{0,2},{3,1},{1,5},... | collective-permute-start | bytes 2752520 | tf_op jit(solution)/shard_map/ppermute | solution.py:249
  5.3 25.2 %all-to-all-start = ((bf16[16,32,128]{2,1,0:T(8,128)(2,1)}), bf16[16,32,128]{2,1,0:T(8,128)(2,1)S(1)}, u32[]{:S(2)}, u32[]{:S(2)}) async-start(bf16[16,32,128]{2,1,0:T(8,128)(2,1)} %meta.1), calls=%async_computation | async-start | bytes 262144 | tf_op jit(solution)/shard_map/all_to_all | solution.py:190
  11.6 21.8 %collective-permute-start.3 = (bf16[128,3584]{1,0:T(8,128)(2,1)}, bf16[128,3584]{1,0:T(8,128)(2,1)}, u32[]{:S(2)}, u32[]{:S(2)}) collective-permute-start(bf16[128,3584]{1,0:T(8,128)(2,1)} %mine_ref.2), channel_id=1, source_target_pairs={{0,1},{1,0},{2,3},{3,2},{4,5},{5,4},{6,7},{7,6},{8,9},{9,8},{10,11... | collective-permute-start | bytes 2752520 | tf_op jit(solution)/shard_map/ppermute | solution.py:249
  30.5 9.1 %collective-permute-start.2 = (bf16[128,3584]{1,0:T(8,128)(2,1)}, bf16[128,3584]{1,0:T(8,128)(2,1)}, u32[]{:S(2)}, u32[]{:S(2)}) collective-permute-start(bf16[128,3584]{1,0:T(8,128)(2,1)} %collective-permute-done.mine_ref), channel_id=1, source_target_pairs={{0,1},{1,0},{2,3},{3,2},{4,5},{5,4},{6,7},{7,6},{8,9},{9,8},{10,11... | collective-permute-start | bytes 2752520 | tf_op jit(solution)/shard_map/ppermute | solution.py:249
  30.6 13.6 %collective-permute-start.4 = (bf16[128,3584]{1,0:T(8,128)(2,1)}, bf16[128,3584]{1,0:T(8,128)(2,1)S(1)}, u32[]{:S(2)}, u32[]{:S(2)}) collective-permute-start(bf16[128,3584]{1,0:T(8,128)(2,1)} %mine_ref.3), channel_id=1, source_target_pairs={{0,4},{4,8},{8,12},{12,14},{14,10},{10,6},{6,2},{2,0},{1,3},{5,1},... | collective-permute-start | bytes 2752520 | tf_op jit(solution)/shard_map/ppermute | solution.py:249
  30.7 13.6 %collective-permute-start.9 = (bf16[128,3584]{1,0:T(8,128)(2,1)S(1)}, bf16[128,3584]{1,0:T(8,128)(2,1)}, u32[]{:S(2)}, u32[]{:S(2)}) collective-permute-start(bf16[128,3584]{1,0:T(8,128)(2,1)S(1)} %collective-permute-done.8.mine_ref), channel_id=1, source_target_pairs={{0,1},{1,0},{2,3},{3,2},{4,5},{5,4},{6,7},{7,6},{8,9},{9,8},{10,11... | collective-permute-start | bytes 2752520 | tf_op jit(solution)/shard_map/ppermute | solution.py:249
  31.0 29.7 %collective-permute-start.1 = (bf16[128,3584]{1,0:T(8,128)(2,1)}, bf16[128,3584]{1,0:T(8,128)(2,1)S(1)}, u32[]{:S(2)}, u32[]{:S(2)}) collective-permute-start(bf16[128,3584]{1,0:T(8,128)(2,1)} %collective-permute-done.mine_ref), channel_id=1, source_target_pairs={{0,4},{4,8},{8,12},{12,14},{14,10},{10,6},{6,2},{2,0},{1,3},{5,1},... | collective-permute-start | bytes 2752520 | tf_op jit(solution)/shard_map/ppermute | solution.py:249
  33.4 27.3 %collective-permute-start.6 = (bf16[128,3584]{1,0:T(8,128)(2,1)}, bf16[128,3584]{1,0:T(8,128)(2,1)S(1)}, u32[]{:S(2)}, u32[]{:S(2)}) collective-permute-start(bf16[128,3584]{1,0:T(8,128)(2,1)} %mine_ref.3), channel_id=1, source_target_pairs={{0,1},{1,0},{2,3},{3,2},{4,5},{5,4},{6,7},{7,6},{8,9},{9,8},{10,11... | collective-permute-start | bytes 2752520 | tf_op jit(solution)/shard_map/ppermute | solution.py:249
  44.2 17.2 %collective-permute-start.5 = (bf16[128,3584]{1,0:T(8,128)(2,1)S(1)}, bf16[128,3584]{1,0:T(8,128)(2,1)S(1)}, u32[]{:S(2)}, u32[]{:S(2)}) collective-permute-start(bf16[128,3584]{1,0:T(8,128)(2,1)S(1)} %collective-permute-done.4.mine_ref), channel_id=1, source_target_pairs={{0,1},{1,0},{2,3},{3,2},{4,5},{5,4},{6,7},{7,6},{8,9},{9,8},{10,11... | collective-permute-start | bytes 2752520 | tf_op jit(solution)/shard_map/ppermute | solution.py:249
  44.2 19.1 %collective-permute-start.14 = (bf16[128,3584]{1,0:T(8,128)(2,1)S(1)}, bf16[128,3584]{1,0:T(8,128)(2,1)S(1)}, u32[]{:S(2)}, u32[]{:S(2)}) collective-permute-start(bf16[128,3584]{1,0:T(8,128)(2,1)S(1)} %collective-permute-done.8.mine_ref), channel_id=1, source_target_pairs={{4,0},{8,4},{12,8},{14,12},{10,14},{6,10},{2,6},{0,2},{3,1},{1,5},... | collective-permute-start | bytes 2752520 | tf_op jit(solution)/shard_map/ppermute | solution.py:249
  60.7 4.5 %collective-permute-start.10 = (bf16[128,3584]{1,0:T(8,128)(2,1)S(1)}, bf16[128,3584]{1,0:T(8,128)(2,1)S(1)}, u32[]{:S(2)}, u32[]{:S(2)}) collective-permute-start(bf16[128,3584]{1,0:T(8,128)(2,1)S(1)} %collective-permute-done.1.mine_ref), channel_id=1, source_target_pairs={{0,1},{1,0},{2,3},{3,2},{4,5},{5,4},{6,7},{7,6},{8,9},{9,8},{10,11... | collective-permute-start | bytes 2752520 | tf_op jit(solution)/shard_map/ppermute | solution.py:249
  60.7 13.4 %collective-permute-start.11 = (bf16[128,3584]{1,0:T(8,128)(2,1)S(1)}, bf16[128,3584]{1,0:T(8,128)(2,1)S(1)}, u32[]{:S(2)}, u32[]{:S(2)}) collective-permute-start(bf16[128,3584]{1,0:T(8,128)(2,1)S(1)} %collective-permute-done.4.mine_ref), channel_id=1, source_target_pairs={{0,4},{4,8},{8,12},{12,14},{14,10},{10,6},{6,2},{2,0},{1,3},{5,1},... | collective-permute-start | bytes 2752520 | tf_op jit(solution)/shard_map/ppermute | solution.py:249
  63.3 10.8 %collective-permute-start.17 = (bf16[128,3584]{1,0:T(8,128)(2,1)S(1)}, bf16[128,3584]{1,0:T(8,128)(2,1)S(1)}, u32[]{:S(2)}, u32[]{:S(2)}) collective-permute-start(bf16[128,3584]{1,0:T(8,128)(2,1)S(1)} %collective-permute-done.14.mine_ref), channel_id=1, source_target_pairs={{0,1},{1,0},{2,3},{3,2},{4,5},{5,4},{6,7},{7,6},{8,9},{9,8},{10,11... | collective-permute-start | bytes 2752520 | tf_op jit(solution)/shard_map/ppermute | solution.py:249
  63.7 26.9 %collective-permute-start.7 = (bf16[128,3584]{1,0:T(8,128)(2,1)S(1)}, bf16[128,3584]{1,0:T(8,128)(2,1)S(1)}, u32[]{:S(2)}, u32[]{:S(2)}) collective-permute-start(bf16[128,3584]{1,0:T(8,128)(2,1)S(1)} %collective-permute-done.1.mine_ref), channel_id=1, source_target_pairs={{0,4},{4,8},{8,12},{12,14},{14,10},{10,6},{6,2},{2,0},{1,3},{5,1},... | collective-permute-start | bytes 2752520 | tf_op jit(solution)/shard_map/ppermute | solution.py:249
  74.1 16.5 %collective-permute-start.12 = (bf16[128,3584]{1,0:T(8,128)(2,1)S(1)}, bf16[128,3584]{1,0:T(8,128)(2,1)S(1)}, u32[]{:S(2)}, u32[]{:S(2)}) collective-permute-start(bf16[128,3584]{1,0:T(8,128)(2,1)S(1)} %collective-permute-done.11.mine_ref), channel_id=1, source_target_pairs={{0,1},{1,0},{2,3},{3,2},{4,5},{5,4},{6,7},{7,6},{8,9},{9,8},{10,11... | collective-permute-start | bytes 2752520 | tf_op jit(solution)/shard_map/ppermute | solution.py:249
  74.1 19.2 %collective-permute-start.15 = (bf16[128,3584]{1,0:T(8,128)(2,1)S(1)}, bf16[128,3584]{1,0:T(8,128)(2,1)S(1)}, u32[]{:S(2)}, u32[]{:S(2)}) collective-permute-start(bf16[128,3584]{1,0:T(8,128)(2,1)S(1)} %collective-permute-done.14.mine_ref), channel_id=1, source_target_pairs={{4,0},{8,4},{12,8},{14,12},{10,14},{6,10},{2,6},{0,2},{3,1},{1,5},... | collective-permute-start | bytes 2752520 | tf_op jit(solution)/shard_map/ppermute | solution.py:249
  90.6 3.6 %collective-permute-start.18 = (bf16[128,3584]{1,0:T(8,128)(2,1)S(1)}, bf16[128,3584]{1,0:T(8,128)(2,1)S(1)}, u32[]{:S(2)}, u32[]{:S(2)}) collective-permute-start(bf16[128,3584]{1,0:T(8,128)(2,1)S(1)} %collective-permute-done.7.mine_ref), channel_id=1, source_target_pairs={{0,1},{1,0},{2,3},{3,2},{4,5},{5,4},{6,7},{7,6},{8,9},{9,8},{10,11... | collective-permute-start | bytes 2752520 | tf_op jit(solution)/shard_map/ppermute | solution.py:249
  90.6 20.9 %collective-permute-start.20 = (bf16[128,3584]{1,0:T(8,128)(2,1)S(1)}, bf16[128,3584]{1,0:T(8,128)(2,1)S(1)}, u32[]{:S(2)}, u32[]{:S(2)}) collective-permute-start(bf16[128,3584]{1,0:T(8,128)(2,1)S(1)} %copy-done.6), channel_id=1, source_target_pairs={{4,0},{8,4},{12,8},{14,12},{10,14},{6,10},{2,6},{0,2},{3,1},{1,5},... | collective-permute-start | bytes 2752520 | tf_op jit(solution)/shard_map/ppermute | solution.py:249
  93.3 18.2 %collective-permute-start.16 = (bf16[128,3584]{1,0:T(8,128)(2,1)S(1)}, bf16[128,3584]{1,0:T(8,128)(2,1)S(1)}, u32[]{:S(2)}, u32[]{:S(2)}) collective-permute-start(bf16[128,3584]{1,0:T(8,128)(2,1)S(1)} %collective-permute-done.15.mine_ref), channel_id=1, source_target_pairs={{0,1},{1,0},{2,3},{3,2},{4,5},{5,4},{6,7},{7,6},{8,9},{9,8},{10,11... | collective-permute-start | bytes 2752520 | tf_op jit(solution)/shard_map/ppermute | solution.py:249
  93.6 20.9 %collective-permute-start.13 = (bf16[128,3584]{1,0:T(8,128)(2,1)S(1)}, bf16[128,3584]{1,0:T(8,128)(2,1)S(1)}, u32[]{:S(2)}, u32[]{:S(2)}) collective-permute-start(bf16[128,3584]{1,0:T(8,128)(2,1)S(1)} %collective-permute-done.7.mine_ref), channel_id=1, source_target_pairs={{0,4},{4,8},{8,12},{12,14},{14,10},{10,6},{6,2},{2,0},{1,3},{5,1},... | collective-permute-start | bytes 2752520 | tf_op jit(solution)/shard_map/ppermute | solution.py:249
  111.5 5.3 %collective-permute-start.25 = (bf16[128,3584]{1,0:T(8,128)(2,1)S(1)}, bf16[128,3584]{1,0:T(8,128)(2,1)S(1)}, u32[]{:S(2)}, u32[]{:S(2)}) collective-permute-start(bf16[128,3584]{1,0:T(8,128)(2,1)S(1)} %collective-permute-done.20.mine_ref), channel_id=1, source_target_pairs={{0,1},{1,0},{2,3},{3,2},{4,5},{5,4},{6,7},{7,6},{8,9},{9,8},{10,11... | collective-permute-start | bytes 2752520 | tf_op jit(solution)/shard_map/ppermute | solution.py:249
  111.5 20.3 %collective-permute-start.24 = (bf16[128,3584]{1,0:T(8,128)(2,1)S(1)}, bf16[128,3584]{1,0:T(8,128)(2,1)S(1)}, u32[]{:S(2)}, u32[]{:S(2)}) collective-permute-start(bf16[128,3584]{1,0:T(8,128)(2,1)S(1)} %collective-permute-done.11.mine_ref), channel_id=1, source_target_pairs={{0,4},{4,8},{8,12},{12,14},{14,10},{10,6},{6,2},{2,0},{1,3},{5,1},... | collective-permute-start | bytes 2752520 | tf_op jit(solution)/shard_map/ppermute | solution.py:249
  114.4 17.4 %collective-permute-start.19 = (bf16[128,3584]{1,0:T(8,128)(2,1)S(1)}, bf16[128,3584]{1,0:T(8,128)(2,1)S(1)}, u32[]{:S(2)}, u32[]{:S(2)}) collective-permute-start(bf16[128,3584]{1,0:T(8,128)(2,1)S(1)} %collective-permute-done.13.mine_ref), channel_id=1, source_target_pairs={{0,1},{1,0},{2,3},{3,2},{4,5},{5,4},{6,7},{7,6},{8,9},{9,8},{10,11... | collective-permute-start | bytes 2752520 | tf_op jit(solution)/shard_map/ppermute | solution.py:249
  115.0 20.9 %collective-permute-start.21 = (bf16[128,3584]{1,0:T(8,128)(2,1)S(1)}, bf16[128,3584]{1,0:T(8,128)(2,1)S(1)}, u32[]{:S(2)}, u32[]{:S(2)}) collective-permute-start(bf16[128,3584]{1,0:T(8,128)(2,1)S(1)} %collective-permute-done.20.mine_ref), channel_id=1, source_target_pairs={{4,0},{8,4},{12,8},{14,12},{10,14},{6,10},{2,6},{0,2},{3,1},{1,5},... | collective-permute-start | bytes 2752520 | tf_op jit(solution)/shard_map/ppermute | solution.py:249
  131.8 9.7 %collective-permute-start.26 = (bf16[128,3584]{1,0:T(8,128)(2,1)S(1)}, bf16[128,3584]{1,0:T(8,128)(2,1)}, u32[]{:S(2)}, u32[]{:S(2)}) collective-permute-start(bf16[128,3584]{1,0:T(8,128)(2,1)S(1)} %collective-permute-done.24.mine_ref), channel_id=1, source_target_pairs={{0,1},{1,0},{2,3},{3,2},{4,5},{5,4},{6,7},{7,6},{8,9},{9,8},{10,11... | collective-permute-start | bytes 2752520 | tf_op jit(solution)/shard_map/ppermute | solution.py:249
  131.8 19.7 %collective-permute-start.28 = (bf16[128,3584]{1,0:T(8,128)(2,1)S(1)}, bf16[128,3584]{1,0:T(8,128)(2,1)S(1)}, u32[]{:S(2)}, u32[]{:S(2)}) collective-permute-start(bf16[128,3584]{1,0:T(8,128)(2,1)S(1)} %collective-permute-done.24.mine_ref), channel_id=1, source_target_pairs={{0,4},{4,8},{8,12},{12,14},{14,10},{10,6},{6,2},{2,0},{1,3},{5,1},... | collective-permute-start | bytes 2752520 | tf_op jit(solution)/shard_map/ppermute | solution.py:249
  135.9 15.6 %collective-permute-start.23 = (bf16[128,3584]{1,0:T(8,128)(2,1)S(1)}, bf16[128,3584]{1,0:T(8,128)(2,1)}, u32[]{:S(2)}, u32[]{:S(2)}) collective-permute-start(bf16[128,3584]{1,0:T(8,128)(2,1)S(1)} %collective-permute-done.21.mine_ref), channel_id=1, source_target_pairs={{0,1},{1,0},{2,3},{3,2},{4,5},{5,4},{6,7},{7,6},{8,9},{9,8},{10,11... | collective-permute-start | bytes 2752520 | tf_op jit(solution)/shard_map/ppermute | solution.py:249
  136.5 20.0 %collective-permute-start.22 = (bf16[128,3584]{1,0:T(8,128)(2,1)S(1)}, bf16[128,3584]{1,0:T(8,128)(2,1)}, u32[]{:S(2)}, u32[]{:S(2)}) collective-permute-start(bf16[128,3584]{1,0:T(8,128)(2,1)S(1)} %collective-permute-done.21.mine_ref), channel_id=1, source_target_pairs={{4,0},{8,4},{12,8},{14,12},{10,14},{6,10},{2,6},{0,2},{3,1},{1,5},... | collective-permute-start | bytes 2752520 | tf_op jit(solution)/shard_map/ppermute | solution.py:249
  138.0 18.4 %all-to-all-start.1 = ((f32[16,16,128]{2,1,0:T(8,128)}), f32[16,16,128]{2,1,0:T(8,128)S(1)}, u32[]{:S(2)}, u32[]{:S(2)}) async-start(f32[16,16,128]{2,1,0:T(8,128)} %get-tuple-element.111), calls=%async_computation.1 | async-start | bytes 262144 | tf_op jit(solution)/shard_map/all_to_all | solution.py:288
  151.5 5.1 %collective-permute-start.29 = (bf16[128,3584]{1,0:T(8,128)(2,1)S(1)}, bf16[128,3584]{1,0:T(8,128)(2,1)S(1)}, u32[]{:S(2)}, u32[]{:S(2)}) collective-permute-start(bf16[128,3584]{1,0:T(8,128)(2,1)S(1)} %collective-permute-done.28.mine_ref), channel_id=1, source_target_pairs={{0,1},{1,0},{2,3},{3,2},{4,5},{5,4},{6,7},{7,6},{8,9},{9,8},{10,11... | collective-permute-start | bytes 2752520 | tf_op jit(solution)/shard_map/ppermute | solution.py:249
  156.5 3.4 %collective-permute-start.27 = (bf16[128,3584]{1,0:T(8,128)(2,1)}, bf16[128,3584]{1,0:T(8,128)(2,1)S(1)}, u32[]{:S(2)}, u32[]{:S(2)}) collective-permute-start(bf16[128,3584]{1,0:T(8,128)(2,1)} %collective-permute-done.22.mine_ref), channel_id=1, source_target_pairs={{0,1},{1,0},{2,3},{3,2},{4,5},{5,4},{6,7},{7,6},{8,9},{9,8},{10,11... | collective-permute-start | bytes 2752520 | tf_op jit(solution)/shard_map/ppermute | solution.py:249
  (8 other events, 49.6 us)
